TPU v7x, 256 devices: a whole 4x4x8 slice. The times are simulated.
256 devices in a mesh: dp: 16 (over x_lo, z), mp: 16 (over x_hi, y, core).
Axes of the slice: x: 4 (x_hi: 2, x_lo: 2; x = x_hi * 2 + x_lo), y: 4, z: 8, core: 2. Of those that a mesh axis runs over, the one named last changes fastest.
Arguments:
- x_in: bfloat16 [64, 8, 8, 3072], P('dp', None, None, 'mp'), may hold values from -6 to 6
- dw_weight: float32 [7, 7, 3072], P(None, None, 'mp'), may hold values from -0.875 to 0.875
- dw_bias: float32 [3072], P('mp'), may hold values from -3 to 3
- ln_gain: float32 [3072], replicated, may hold values from 0.3 to 3
- ln_bias: float32 [3072], replicated, may hold values from -3 to 3
- w_in: bfloat16 [3072, 12288], P(None, 'mp'), may hold values from -0.109375 to 0.109375
- b_in: float32 [12288], P('mp'), may hold values from -3 to 3
- w_out: bfloat16 [12288, 3072], P('mp'), may hold values from -0.0546875 to 0.0546875
- b_out: float32 [3072], P('mp'), may hold values from -3 to 3
- layer_scale: float32 [3072], P('mp'), may hold values from 0.2 to 2
- head_gain: float32 [3072], P('mp'), may hold values from 0.3 to 3
- head_bias: float32 [3072], P('mp'), may hold values from -3 to 3
- projection: bfloat16 [3072, 1024], P('mp'), may hold values from -0.109375 to 0.109375
- text_emb: float32 [64, 1024], P('dp'), may hold values from -6 to 6
- labels: int32 [64], P('dp'), may hold values from 0 to 63, each once
Outputs:
- grad_input: float32 [64, 8, 8, 3072], P('dp', None, None, 'mp')
- grad_text: float32 [64, 1024], P('dp')
Inputs may be any that keep to these rules, and one draw needn't show every extreme that they name: `labels`: a permutation: every text index appears exactly once.
All inputs are finite; a program needn't handle non-finite values.
Results may differ from a plain program's by a relative error of at most 0.028.
Values may be sent and summed in bfloat16 or wider, within the bound.
No kernel may reach another device: no remote copies, remote signals or barrier semaphores. Data moves between devices by JAX's collectives and lax.ppermute only.
A program may use at most 64 MiB of HBM per device.

v0:
```python
import jax
import jax.numpy as jnp
from jax import lax
from jax.sharding import PartitionSpec as P

eps = 1e-06
logit_scale = 20.0
loss_scale = 512.0
root_half = 0.7071067811865476
inv_root_two_pi = 0.3989422804014327


def from_behind(array, axis, by):
    length = lax.axis_size(axis)
    return lax.ppermute(array, axis, [(i, (i + by) % length) for i in range(length)])


def depthwise(source, kernel):
    extent = source.shape[1]
    reach = kernel.shape[0] // 2
    padded = jnp.pad(source, ((0, 0), (reach, reach), (reach, reach), (0, 0)))
    summed = jnp.zeros(source.shape, jnp.float32)
    for offset_row in range(kernel.shape[0]):
        for offset_col in range(kernel.shape[1]):
            summed = (
                summed
                + padded[:, offset_row : offset_row + extent, offset_col : offset_col + extent, :]
                * kernel[offset_row, offset_col]
            )
    return summed


def gelu_value(pre_act):
    return 0.5 * pre_act * (1.0 + jax.scipy.special.erf(pre_act * root_half))


def gelu_slope(pre_act):
    return (
        0.5 * (1.0 + jax.scipy.special.erf(pre_act * root_half))
        + pre_act * jnp.exp(-0.5 * pre_act * pre_act) * inv_root_two_pi
    )


def body(
    x_in,
    dw_weight,
    dw_bias,
    ln_gain,
    ln_bias,
    w_in,
    b_in,
    w_out,
    b_out,
    layer_scale,
    head_gain,
    head_bias,
    projection,
    text_emb,
    labels,
):
    highest = lax.Precision.HIGHEST
    images = x_in.shape[0]
    side_len = x_in.shape[1]
    shard_ch = x_in.shape[3]
    channels = w_in.shape[0]
    hidden_local = w_in.shape[1]
    positions = side_len * side_len
    all_rows = images * positions
    ch_start = lax.axis_index("mp") * shard_ch
    gain_local = lax.dynamic_slice_in_dim(ln_gain, ch_start, shard_ch, 0)
    bias_local = lax.dynamic_slice_in_dim(ln_bias, ch_start, shard_ch, 0)
    conv_out = (depthwise(x_in.astype(jnp.float32), dw_weight) + dw_bias).astype(jnp.bfloat16)
    conv_rows = conv_out.reshape(all_rows, shard_ch)
    conv_float = conv_rows.astype(jnp.float32)
    first_sum, second_sum = lax.psum(
        (jnp.sum(conv_float, axis=1), jnp.sum(conv_float * conv_float, axis=1)), "mp"
    )
    average = first_sum / channels
    inverse = lax.rsqrt(second_sum / channels - average * average + eps)
    centred = (conv_float - average[:, None]) * inverse[:, None]
    normed = (centred * gain_local + bias_local).astype(jnp.bfloat16)
    hidden_pre = (
        jnp.dot(
            lax.all_gather(normed, "mp", axis=1, tiled=True),
            w_in,
            preferred_element_type=jnp.float32,
        )
        + b_in
    )
    activation = gelu_value(hidden_pre).astype(jnp.bfloat16)
    mixed = lax.psum_scatter(
        jnp.dot(activation, w_out, preferred_element_type=jnp.float32).astype(jnp.bfloat16),
        "mp",
        scatter_dimension=1,
        tiled=True,
    ).astype(jnp.float32)
    mixed_mean = jnp.mean(mixed.reshape(images, positions, shard_ch), axis=1)
    input_mean = jnp.mean(x_in.astype(jnp.float32).reshape(images, positions, shard_ch), axis=1)
    pooled = input_mean + layer_scale * (mixed_mean + b_out)
    head_first, head_second = lax.psum(
        (jnp.sum(pooled, axis=1), jnp.sum(pooled * pooled, axis=1)), "mp"
    )
    head_mean = head_first / channels
    head_inverse = lax.rsqrt(head_second / channels - head_mean * head_mean + eps)
    head_centred = (pooled - head_mean[:, None]) * head_inverse[:, None]
    head_normed = (head_centred * head_gain + head_bias).astype(jnp.bfloat16)
    image_emb = lax.psum(jnp.dot(head_normed, projection, preferred_element_type=jnp.float32), "mp")
    image_len = jnp.sqrt(jnp.sum(image_emb * image_emb, axis=1, keepdims=True) + eps)
    image_unit = image_emb / image_len
    text_len = jnp.sqrt(jnp.sum(text_emb * text_emb, axis=1, keepdims=True) + eps)
    text_unit = text_emb / text_len
    pairs_local = text_emb.shape[0]
    emb_width = text_emb.shape[1]

    def block_logits(other_unit):
        return logit_scale * jnp.dot(image_unit, other_unit.T, precision=highest)

    def logit_grads(weights, row_total, col_total, columns):
        matched = (labels[:, None] == columns[None, :]).astype(jnp.float32)
        return loss_scale * (
            0.5 * (weights / row_total[:, None] + weights / col_total[None, :]) - matched
        )

    cycle_len = lax.axis_size("dp")
    home_idx = lax.axis_index("dp")

    def first_turn(turn_index, state):
        moving_unit, column_total, row_total = state
        weights = jnp.exp(block_logits(moving_unit))
        row_total = row_total + jnp.sum(weights, axis=1)
        column_total = column_total + jnp.sum(weights, axis=0)
        moving_unit, column_total = from_behind((moving_unit, column_total), "dp", 1)
        return (moving_unit, column_total, row_total)

    zero_rows = jnp.zeros((pairs_local,), jnp.float32)
    moved_unit, column_total, row_total = lax.fori_loop(
        0, cycle_len, first_turn, (text_unit, zero_rows, jnp.zeros((images,), jnp.float32))
    )

    def second_turn(turn_index, state):
        moving_unit, moving_total, moving_grad, image_grad = state
        weights = jnp.exp(block_logits(moving_unit))
        anchor = (home_idx - turn_index) % cycle_len
        columns = anchor * pairs_local + jnp.arange(pairs_local, dtype=jnp.int32)
        grad_logits = logit_grads(weights, row_total, moving_total, columns)
        image_grad = image_grad + logit_scale * jnp.dot(grad_logits, moving_unit, precision=highest)
        moving_grad = moving_grad + logit_scale * jnp.dot(
            grad_logits.T, image_unit, precision=highest
        )
        moving_unit, moving_total, moving_grad = from_behind(
            (moving_unit, moving_total, moving_grad), "dp", 1
        )
        return (moving_unit, moving_total, moving_grad, image_grad)

    zero_emb = jnp.zeros((pairs_local, emb_width), jnp.float32)
    outcome = lax.fori_loop(
        0,
        cycle_len,
        second_turn,
        (moved_unit, column_total, zero_emb, jnp.zeros((images, emb_width), jnp.float32)),
    )
    grad_text_unit = outcome[2]
    grad_image_unit = outcome[3]
    grad_text = (
        grad_text_unit - text_unit * jnp.sum(text_unit * grad_text_unit, axis=1, keepdims=True)
    ) / text_len
    grad_image = (
        (
            grad_image_unit
            - image_unit * jnp.sum(image_unit * grad_image_unit, axis=1, keepdims=True)
        )
        / image_len
    ).astype(jnp.bfloat16)
    grad_head = jnp.dot(grad_image, projection.T, preferred_element_type=jnp.float32)
    head_scaled = grad_head * head_gain
    back_first, back_second = lax.psum(
        (jnp.sum(head_scaled, axis=1), jnp.sum(head_scaled * head_centred, axis=1)), "mp"
    )
    grad_pooled = head_inverse[:, None] * (
        head_scaled
        - back_first[:, None] / channels
        - head_centred * back_second[:, None] / channels
    )
    grad_block = grad_pooled / positions
    grad_mixed = (grad_block * layer_scale).astype(jnp.bfloat16)
    mixed_whole = lax.all_gather(grad_mixed, "mp", axis=1, tiled=True)
    grad_act = jnp.dot(mixed_whole, w_out.T, preferred_element_type=jnp.float32)
    gelu_grad = gelu_slope(hidden_pre).reshape(images, positions, hidden_local)
    grad_pre = (
        (grad_act[:, None, :] * gelu_grad).reshape(all_rows, hidden_local).astype(jnp.bfloat16)
    )
    grad_part = jnp.dot(grad_pre, w_in.T, preferred_element_type=jnp.float32)
    grad_normed = lax.psum_scatter(
        grad_part.astype(jnp.bfloat16), "mp", scatter_dimension=1, tiled=True
    ).astype(jnp.float32)
    normed_scaled = grad_normed * gain_local
    sum_first, sum_second = lax.psum(
        (jnp.sum(normed_scaled, axis=1), jnp.sum(normed_scaled * centred, axis=1)), "mp"
    )
    grad_conv = inverse[:, None] * (
        normed_scaled - sum_first[:, None] / channels - centred * sum_second[:, None] / channels
    )
    grad_field = grad_conv.reshape(images, side_len, side_len, shard_ch)
    grad_input = grad_block[:, None, None, :] + depthwise(grad_field, dw_weight[::-1, ::-1])
    return (grad_input, grad_text)


def solution(mesh):
    return jax.shard_map(
        body,
        mesh=mesh,
        in_specs=(
            P("dp", None, None, "mp"),
            P(None, None, "mp"),
            P("mp"),
            P(),
            P(),
            P(None, "mp"),
            P("mp"),
            P("mp", None),
            P("mp"),
            P("mp"),
            P("mp"),
            P("mp"),
            P("mp", None),
            P("dp", None),
            P("dp"),
        ),
        out_specs=(P("dp", None, None, "mp"), P("dp", None)),
        check_vma=False,
    )
```

profile of v0, /device:TPU:1, one launch (start us, length us, event | category | flops | bytes accessed | tf_op | source)
XLA Modules:
  0.0 688.2 jit_solution(14038501027492908805)
XLA Ops:
  8.2 1.0 fusion.226
  11.1 2.5 convert_reduce_fusion
  15.4 35.7 %all-reduce.5 = (f32[256]{0:T(256)S(1)}, f32[256]{0:T(256)S(1)}) all-reduce(f32[256]{0:T(256)S(1)} %reduce_sum.152, f32[256]{0:T(256)S(1)} %reduce_sum.150), channel_id=1, replica_groups=mesh['dp'=16,'mp'=16] {'mp'}, use_global_device_ids=true, to_apply=%region_4.5 | all-reduce | flops 512 | bytes 4096 | tf_op jit(solution)/shard_map/psum | solution.py:75
  52.0 53.4 %all-gather.3.cloned.1.call-done = bf16[256,3072]{0,1:T(8,128)(2,1)} async-done(((bf16[256,192]{0,1:T(8,128)(2,1)}), bf16[256,3072]{0,1:T(8,128)(2,1)}) %all-gather.3.cloned.1.call-update) | async-done | bytes 1572880 | tf_op jit(solution)/shard_map/all_gather | solution.py:84
  105.4 4.3 convolution_add_fusion
  109.8 5.5 convolution_convert_fusion.1
  115.7 73.0 %reduce-scatter.3.cloned.1.call-done = bf16[256,192]{0,1:T(8,128)(2,1)} async-done(((bf16[256,3072]{0,1:T(8,128)(2,1)}), bf16[256,192]{0,1:T(8,128)(2,1)}) %reduce-scatter.3.cloned.1.call-update) | async-done | bytes 98320 | tf_op jit(solution)/shard_map/reduce_scatter | solution.py:91
  189.9 35.0 %all-reduce.4 = (f32[4]{0:T(128)S(1)}, f32[4]{0:T(128)S(1)}) all-reduce(f32[4]{0:T(128)S(1)} %get-tuple-element.315, f32[4]{0:T(128)S(1)} %get-tuple-element.314), channel_id=1, replica_groups=mesh['dp'=16,'mp'=16] {'mp'}, use_global_device_ids=true, to_apply=%region_10.11 | all-reduce | flops 8 | bytes 64 | tf_op jit(solution)/shard_map/psum | solution.py:100
  225.2 59.8 %psum.67 = f32[4,1024]{1,0:T(4,128)S(1)} all-reduce(f32[4,1024]{1,0:T(4,128)S(1)} %fusion.215), channel_id=1, replica_groups=mesh['dp'=16,'mp'=16] {'mp'}, use_global_device_ids=true, to_apply=%region_12.13 | all-reduce | flops 4096 | bytes 32768 | tf_op jit(solution)/shard_map/psum | solution.py:107
  285.2 80.4 %while.37 = (s32[]{:T(128)}, f32[4,1024]{1,0:T(4,128)S(1)}, f32[4]{0:T(128)S(1)}, f32[4]{0:T(128)S(1)}, f32[4,1024]{1,0:T(4,128)S(1)}, /*index=5*/s32[]{:T(128)}, s32[]{:T(128)}) while((s32[]{:T(128)}, f32[4,1024]{1,0:T(4,128)S(1)}, f32[4]{0:T(128)S(1)}, f32[4]{0:T(128)S(1)}, f32[4,1024]{1,0:T(4,128)S(1)}, ...), condition=%wide.region_17.18_spmd.clone, body=%wide.region_14.17_spmd.clone.sunk | while | flops 196663 | bytes 131431 | solution.py:136
  285.2 1.4 collective-permute-start
  286.8 1.3 collective-permute-start.1
  288.2 3.2 collective-permute-done.1
  291.7 1.3 collective-permute-start.1
  293.0 3.6 collective-permute-done.1
  297.7 3.8 collective-permute-done.1
  302.2 4.2 collective-permute-done.1
  306.9 4.5 collective-permute-done.1
  311.8 4.7 collective-permute-done.1
  317.0 4.5 collective-permute-done.1
  321.9 4.5 collective-permute-done.1
  326.8 4.5 collective-permute-done.1
  331.7 4.5 collective-permute-done.1
  336.6 4.5 collective-permute-done.1
  341.5 4.5 collective-permute-done.1
  346.4 4.5 collective-permute-done.1
  351.3 4.5 collective-permute-done.1
  356.2 4.5 collective-permute-done.1
  361.1 4.5 collective-permute-done.1
  365.6 94.1 %while.38 = (s32[]{:T(128)}, f32[4,1024]{1,0:T(4,128)S(1)}, f32[4]{0:T(128)S(1)}, f32[4,1024]{1,0:T(4,128)S(1)}, f32[4,1024]{1,0:T(4,128)S(1)}, /*index=5*/f32[4...) while((s32[]{:T(128)}, f32[4,1024]{1,0:T(4,128)S(1)}, ...), condition=%wide.region_19.20_spmd.clone, body=%wide.region_18.19_spmd.clone.sunk | while | flops 610468 | bytes 295680 | solution.py:156
  366.5 3.9 collective-permute-done.3
  372.0 3.9 collective-permute-done.3
  378.6 2.7 collective-permute-done.3
  382.3 1.7 collective-permute-start.3
  384.7 2.3 collective-permute-done.3
  387.0 2.3 collective-permute-done.4
  390.3 3.8 collective-permute-done.3
  395.6 3.9 collective-permute-done.3
  400.7 1.3 collective-permute-start.4
  402.2 2.7 collective-permute-done.3
  405.9 1.7 collective-permute-start.3
  408.4 2.0 collective-permute-done.3
  410.4 2.4 collective-permute-done.4
  414.0 3.5 collective-permute-done.3
  419.3 3.9 collective-permute-done.3
  425.5 3.1 collective-permute-done.3
  429.6 1.3 collective-permute-start.3
  431.7 2.7 collective-permute-done.3
  434.3 1.8 collective-permute-done.4
  437.2 4.0 collective-permute-done.3
  442.6 3.8 collective-permute-done.3
  447.8 1.1 collective-permute-start.4
  449.1 2.9 collective-permute-done.3
  452.7 1.7 collective-permute-start.3
  455.2 2.2 collective-permute-done.3
  457.4 2.3 collective-permute-done.4
  460.2 83.4 %all-reduce.3 = (f32[4]{0:T(128)S(1)}, f32[4]{0:T(128)S(1)}) all-reduce(f32[4]{0:T(128)S(1)} %get-tuple-element.313, f32[4]{0:T(128)S(1)} %get-tuple-element.312), channel_id=1, replica_groups=mesh['dp'=16,'mp'=16] {'mp'}, use_global_device_ids=true, to_apply=%region_24.25 | all-reduce | flops 8 | bytes 64 | tf_op jit(solution)/shard_map/psum | solution.py:176
  543.7 19.7 %all-gather = bf16[16,192,4]{1,2,0:T(4,128)(2,1)S(1)} all-gather(bf16[1,192,4]{1,2,0:T(4,128)(2,1)S(1)} %fusion.216), channel_id=1, replica_groups=mesh['dp'=16,'mp'=16] {'mp'}, dimensions={0}, use_global_device_ids=true | all-gather | bytes 26112 | tf_op jit(solution)/shard_map/all_gather | solution.py:186
  563.5 3.6 fusion.228
  567.5 4.9 convolution_convert_fusion
  573.3 68.8 %reduce-scatter.5.cloned.1.call-done = bf16[256,192]{0,1:T(8,128)(2,1)} async-done(((bf16[256,3072]{0,1:T(8,128)(2,1)}), bf16[256,192]{0,1:T(8,128)(2,1)}) %reduce-scatter.5.cloned.1.call-update) | async-done | bytes 98320 | tf_op jit(solution)/shard_map/reduce_scatter | solution.py:193
  642.2 1.0 fusion.210
  643.2 35.1 %all-reduce.2 = (f32[256]{0:T(256)S(1)}, f32[256]{0:T(256)S(1)}) all-reduce(f32[256]{0:T(256)S(1)} %get-tuple-element.311, f32[256]{0:T(256)S(1)} %get-tuple-element.310), channel_id=1, replica_groups=mesh['dp'=16,'mp'=16] {'mp'}, use_global_device_ids=true, to_apply=%region_29.30 | all-reduce | flops 512 | bytes 4096 | tf_op jit(solution)/shard_map/psum | solution.py:197
  679.4 2.3 fusion.201
  (337 shorter events, 42.3 us)
Async XLA Ops:
  7.2 98.3 %all-gather.3.cloned.1.call-start = ((), (), s32[]{:S(2)}) async-start(), calls=%async_computation.2 | async-start | bytes 1671168 | tf_op jit(solution)/shard_map/all_gather | solution.py:84
  52.0 136.7 %reduce-scatter.3.cloned.1.call-start = ((), (), s32[]{:S(2)}) async-start(), calls=%async_computation.3 | async-start | bytes 1671168 | tf_op jit(solution)/shard_map/reduce_scatter | solution.py:91
  115.3 526.8 %reduce-scatter.5.cloned.1.call-start = ((), (), s32[]{:S(2)}) async-start(), calls=%async_computation.4 | async-start | bytes 1671168 | tf_op jit(solution)/shard_map/reduce_scatter | solution.py:193
  285.2 6.2 collective-permute-start
  291.4 5.2 collective-permute-start
  291.7 4.9 collective-permute-start.1
  296.6 4.9 collective-permute-start
  301.5 4.9 collective-permute-start
  306.4 4.9 collective-permute-start
  311.3 5.2 collective-permute-start
  311.7 4.8 collective-permute-start.1
  316.5 4.9 collective-permute-start
  321.4 4.9 collective-permute-start
  326.3 4.9 collective-permute-start
  331.2 4.9 collective-permute-start
  336.1 4.9 collective-permute-start
  341.0 4.9 collective-permute-start
  345.9 4.9 collective-permute-start
  350.9 4.9 collective-permute-start
  355.8 4.9 collective-permute-start
  360.7 4.9 collective-permute-start
  365.6 5.6 collective-permute-start.2
  366.3 4.9 collective-permute-start.4
  371.2 5.4 collective-permute-start.2
  371.2 4.7 collective-permute-start.3
  371.7 4.8 collective-permute-start.4
  376.5 5.8 collective-permute-start.2
  376.5 4.7 collective-permute-start.3
  377.5 4.8 collective-permute-start.4
  382.3 7.1 %collective-permute-start.2 = (f32[4,1024]{1,0:T(4,128)S(1)}, f32[4,1024]{1,0:T(4,128)S(1)}, u32[]{:S(2)}, u32[]{:S(2)}) collective-permute-start(f32[4,1024]{1,0:T(4,128)S(1)} %copy.46), channel_id=1, source_target_pairs={{0,16},{16,32},{32,48},{48,64},{64,80},{80,96},{96,112},{112,128},... | collective-permute-start | bytes 49160 | tf_op jit(solution)/shard_map/while/body/eval_jaxpr/ppermute | solution.py:15
  382.3 4.7 collective-permute-start.3
  384.4 4.9 collective-permute-start.4
  389.3 5.4 collective-permute-start.2
  389.4 4.7 collective-permute-start.3
  389.9 4.8 collective-permute-start.4
  394.7 5.4 collective-permute-start.2
  394.7 4.7 collective-permute-start.3
  395.3 4.8 collective-permute-start.4
  400.1 5.4 collective-permute-start.2
  400.1 4.7 collective-permute-start.3
  400.7 4.8 collective-permute-start.4
  405.5 7.3 %collective-permute-start.2 = (f32[4,1024]{1,0:T(4,128)S(1)}, f32[4,1024]{1,0:T(4,128)S(1)}, u32[]{:S(2)}, u32[]{:S(2)}) collective-permute-start(f32[4,1024]{1,0:T(4,128)S(1)} %copy.46), channel_id=1, source_target_pairs={{0,16},{16,32},{32,48},{48,64},{64,80},{80,96},{96,112},{112,128},... | collective-permute-start | bytes 49160 | tf_op jit(solution)/shard_map/while/body/eval_jaxpr/ppermute | solution.py:15
  408.0 4.8 collective-permute-start.4
  412.8 5.7 collective-permute-start.2
  412.8 4.7 collective-permute-start.3
  413.7 4.8 collective-permute-start.4
  418.5 5.4 collective-permute-start.2
  419.1 4.8 collective-permute-start.4
  423.8 5.7 collective-permute-start.2
  423.9 4.7 collective-permute-start.3
  424.8 4.8 collective-permute-start.4
  429.6 6.5 collective-permute-start.2
  429.6 4.7 collective-permute-start.3
  431.3 4.8 collective-permute-start.4
  436.1 5.5 collective-permute-start.2
  436.1 5.0 collective-permute-start.3
  436.8 4.8 collective-permute-start.4
  441.6 5.6 collective-permute-start.2
  441.6 4.8 collective-permute-start.3
  442.2 5.1 collective-permute-start.4
  447.2 5.4 collective-permute-start.2
  447.8 4.8 collective-permute-start.4
  452.6 7.0 %collective-permute-start.2 = (f32[4,1024]{1,0:T(4,128)S(1)}, f32[4,1024]{1,0:T(4,128)S(1)}, u32[]{:S(2)}, u32[]{:S(2)}) collective-permute-start(f32[4,1024]{1,0:T(4,128)S(1)} %copy.46), channel_id=1, source_target_pairs={{0,16},{16,32},{32,48},{48,64},{64,80},{80,96},{96,112},{112,128},... | collective-permute-start | bytes 49160 | tf_op jit(solution)/shard_map/while/body/eval_jaxpr/ppermute | solution.py:15
  454.9 4.8 collective-permute-start.4
  (27 other events, 888.8 us)
Sparse Core Ops, SparseCore 0:
  52.1 53.2 all-gather.2
  115.5 73.1 reduce-scatter.2
  572.6 69.5 reduce-scatter.4
where the time goes:
time: 689 us; the launch traced here: 688 us
  waiting for transfers between devices  332 us (48%)
  blocking collectives  269 us (39%)
  matrix products  33 us (5%)
  starting transfers between devices  21.4 us (3%)
  between operations  14 us (2%)
  other arithmetic  11 us (2%)
    ppermute x80, waiting for transfers between devices, from_behind(): lax.ppermute(array, axis, [(i, (i + by) % length) for i in range(length)])  137 us
    psum x1, blocking collectives, body(): lax.psum((jnp.sum(head_scaled, axis=1), jnp.sum(head_scaled * head_centre...  83.4 us
    reduce_scatter x1, waiting for transfers between devices, body(): lax.psum_scatter(jnp.dot(activation, w_out, preferred_element_type=jnp.fl...  73 us
    reduce_scatter x1, waiting for transfers between devices, body(): lax.psum_scatter(grad_part.astype(jnp.bfloat16), 'mp', scatter_dimension=...  68.8 us
    psum x1, blocking collectives, body(): lax.psum(jnp.dot(head_normed, projection, preferred_element_type=jnp.floa...  59.8 us
    all_gather x1, waiting for transfers between devices, body(): lax.all_gather(normed, 'mp', axis=1, tiled=True)  53.4 us
    psum x1, blocking collectives, body(): lax.psum((jnp.sum(conv_float, axis=1), jnp.sum(conv_float * conv_float, a...  35.7 us
    psum x1, blocking collectives, body(): lax.psum((jnp.sum(normed_scaled, axis=1), jnp.sum(normed_scaled * centred...  35.1 us
  transfers between devices with their start and end apart: 83, of which 51 were waited for; matrix products, arithmetic and copies ran while one was open for 2% of the time, Pallas kernels for 0%

commit v1 on v0

v1 whole, which is shorter than its diff:
```python
import jax
import jax.numpy as jnp
from jax import lax
from jax.sharding import PartitionSpec as P

eps = 1e-06
logit_scale = 20.0
loss_scale = 512.0
root_half = 0.7071067811865476
inv_root_two_pi = 0.3989422804014327
f32 = jnp.float32
bf16 = jnp.bfloat16
highest = lax.Precision.HIGHEST


def core_swap(array):
    length = lax.axis_size("mp")
    return lax.ppermute(array, "mp", [(i, i ^ 1) for i in range(length)])


def chip_exchange(array):
    length = lax.axis_size("mp")
    groups = [[i for i in range(core, length, 2)] for core in range(2)]
    return lax.all_to_all(array, "mp", 0, 0, axis_index_groups=groups)


def chip_gather(array):
    count = lax.axis_size("mp") // 2
    return chip_exchange(jnp.broadcast_to(array, (count,) + array.shape))


def dp_gather(array):
    count = lax.axis_size("dp")
    return lax.all_to_all(jnp.broadcast_to(array, (count,) + array.shape), "dp", 0, 0)


def own_first(array, core):
    first, second = array[..., 0, :], array[..., 1, :]
    return jnp.where(core == 0, jnp.stack([first, second]), jnp.stack([second, first]))


def split_two(array):
    high = lax.reduce_precision(array, 8, 7)
    return high, array - high


def depthwise(source, kernel):
    extent = source.shape[1]
    reach = kernel.shape[0] // 2
    padded = jnp.pad(source, ((0, 0), (reach, reach), (reach, reach), (0, 0)))
    summed = jnp.zeros(source.shape, f32)
    for offset_row in range(kernel.shape[0]):
        for offset_col in range(kernel.shape[1]):
            summed = (
                summed
                + padded[:, offset_row : offset_row + extent, offset_col : offset_col + extent, :]
                * kernel[offset_row, offset_col]
            )
    return summed


def gelu_value(pre_act):
    return 0.5 * pre_act * (1.0 + lax.erf(pre_act * root_half))


def gelu_slope(pre_act):
    return (
        0.5 * (1.0 + lax.erf(pre_act * root_half))
        + pre_act * jnp.exp(-0.5 * pre_act * pre_act) * inv_root_two_pi
    )


def body(
    x_in,
    dw_weight,
    dw_bias,
    ln_gain,
    ln_bias,
    w_in,
    b_in,
    w_out,
    b_out,
    layer_scale,
    head_gain,
    head_bias,
    projection,
    text_emb,
    labels,
):
    images, side = x_in.shape[0], x_in.shape[1]
    shard = x_in.shape[3]
    channels, hidden = w_in.shape
    positions = side * side
    rows = images * positions
    index = lax.axis_index("mp")
    core = index % 2
    chips = lax.axis_size("mp") // 2
    width = text_emb.shape[1]
    pairs = text_emb.shape[0]
    batch = pairs * lax.axis_size("dp")
    home = lax.axis_index("dp")

    text_block = jnp.concatenate(
        [text_emb, jnp.pad(labels.astype(f32)[None, :], ((0, 3), (0, width - pairs)))]
    )
    text_all = dp_gather(text_block)

    source = x_in.astype(f32)
    conv = (depthwise(source, dw_weight) + dw_bias).astype(bf16).reshape(rows, shard)
    conv_mine = chip_gather(conv.T)
    conv_other = core_swap(conv_mine)
    whole = jnp.stack([conv_mine, conv_other]).reshape(channels, rows).astype(f32)
    average = jnp.sum(whole, axis=0) / channels
    inverse = lax.rsqrt(jnp.sum(whole * whole, axis=0) / channels - average * average + eps)
    gain_own = own_first(ln_gain.reshape(chips, 2, shard), core).reshape(channels)
    bias_own = own_first(ln_bias.reshape(chips, 2, shard), core).reshape(channels)
    weight_pairs = w_in.reshape(chips, 2, shard, hidden)
    weight_own = jnp.where(
        core == 0,
        jnp.swapaxes(weight_pairs, 0, 1),
        jnp.swapaxes(weight_pairs[:, ::-1], 0, 1),
    ).reshape(channels, hidden)
    normed = (
        ((whole - average) * inverse) * gain_own[:, None] + bias_own[:, None]
    ).astype(bf16)
    hidden_pre = (
        lax.dot_general(normed, weight_own, (((0,), (0,)), ((), ())), preferred_element_type=f32)
        + b_in
    )
    activation = gelu_value(hidden_pre).reshape(images, positions, hidden)
    act_mean = jnp.mean(activation, axis=1)

    high, low = split_two(act_mean)
    mixed = jnp.dot(
        jnp.concatenate([high, low]).astype(bf16), w_out, preferred_element_type=f32
    )
    mixed = own_first((mixed[:images] + mixed[images:]).reshape(images, chips, 2, shard), core)
    mixed = mixed[0] + core_swap(mixed[1])
    mixed_mean = jnp.sum(chip_exchange(jnp.swapaxes(mixed, 0, 1)), axis=0)

    input_mean = jnp.mean(source.reshape(images, positions, shard), axis=1)
    pooled = input_mean + layer_scale * (mixed_mean + b_out)

    stats = jnp.concatenate([jnp.sum(pooled, axis=1), jnp.sum(pooled * pooled, axis=1)])
    stacked = jnp.concatenate([pooled * head_gain, head_gain[None], head_bias[None]])
    sums = jnp.concatenate(
        [
            jnp.dot(stacked, projection.astype(f32), precision=highest),
            jnp.pad(stats[None, :], ((0, 1), (0, width - 2 * images))),
        ]
    )
    sums = jnp.sum(chip_gather(sums + core_swap(sums)), axis=0)
    head_mean = sums[images + 2, :images] / channels
    head_inverse = lax.rsqrt(
        sums[images + 2, images : 2 * images] / channels - head_mean * head_mean + eps
    )
    head_centred = (pooled - head_mean[:, None]) * head_inverse[:, None]
    emb = (
        head_inverse[:, None] * (sums[:images] - head_mean[:, None] * sums[images])
        + sums[images + 1]
    )

    emb_all = dp_gather(emb).reshape(batch, width)
    text_raw = text_all[:, :pairs].reshape(batch, width)
    labels_all = text_all[:, pairs, :pairs].reshape(batch)
    image_len = jnp.sqrt(jnp.sum(emb_all * emb_all, axis=1, keepdims=True) + eps)
    image_unit = emb_all / image_len
    text_len = jnp.sqrt(jnp.sum(text_raw * text_raw, axis=1, keepdims=True) + eps)
    text_unit = text_raw / text_len
    logits = logit_scale * jnp.dot(image_unit, text_unit.T, precision=highest)
    weights = jnp.exp(logits)
    matched = (labels_all[:, None] == jnp.arange(batch, dtype=f32)[None, :]).astype(f32)
    grad_logits = loss_scale * (
        0.5
        * (
            weights / jnp.sum(weights, axis=1, keepdims=True)
            + weights / jnp.sum(weights, axis=0, keepdims=True)
        )
        - matched
    )

    def own(array, axis):
        return lax.dynamic_slice_in_dim(array, home * pairs, pairs, axis)

    grad_image_unit = logit_scale * jnp.dot(own(grad_logits, 0), text_unit, precision=highest)
    grad_text_unit = logit_scale * jnp.dot(own(grad_logits, 1).T, image_unit, precision=highest)
    own_text, own_image = own(text_unit, 0), own(image_unit, 0)
    grad_text = (
        grad_text_unit - own_text * jnp.sum(own_text * grad_text_unit, axis=1, keepdims=True)
    ) / own(text_len, 0)
    grad_image = (
        (
            grad_image_unit
            - own_image * jnp.sum(own_image * grad_image_unit, axis=1, keepdims=True)
        )
        / own(image_len, 0)
    ).astype(bf16)

    grad_head = jnp.dot(grad_image, projection.T, preferred_element_type=f32)
    block = jnp.concatenate([grad_head * head_gain, head_centred, layer_scale[None]])
    block_mine = chip_gather(block)
    block_all = jnp.stack([block_mine, core_swap(block_mine)])
    scaled_all = block_all[:, :, :images]
    centred_all = block_all[:, :, images : 2 * images]
    scale_all = block_all[:, :, 2 * images :]
    mean_scaled = jnp.sum(scaled_all, axis=(0, 1, 3)) / channels
    mean_product = jnp.sum(scaled_all * centred_all, axis=(0, 1, 3)) / channels

    def to_pooled(scaled, centred):
        return (head_inverse[:, None] / positions) * (
            scaled - mean_scaled[:, None] - centred * mean_product[:, None]
        )

    grad_block = to_pooled(block[:images], head_centred)
    grad_mixed = (to_pooled(scaled_all, centred_all) * scale_all).astype(bf16)
    grad_mixed = jnp.where(core == 0, grad_mixed, grad_mixed[::-1])
    grad_mixed = grad_mixed.transpose(2, 1, 0, 3).reshape(images, channels)
    grad_act = lax.dot_general(
        grad_mixed, w_out, (((1,), (1,)), ((), ())), preferred_element_type=f32
    )
    grad_pre = (
        (grad_act[:, None, :] * gelu_slope(hidden_pre).reshape(images, positions, hidden))
        .reshape(rows, hidden)
        .astype(bf16)
    )
    gain_high, gain_low = split_two(gain_own)
    bias_high, bias_low = split_two(bias_own)
    through = jnp.dot(
        jnp.stack([gain_high, gain_low, bias_high, bias_low]).astype(bf16),
        weight_own,
        preferred_element_type=f32,
    )
    through_gain = through[0] + through[1]
    through_bias = through[2] + through[3] + b_in
    grad_float = grad_pre.astype(f32)
    row_sums = jnp.stack(
        [
            jnp.sum(grad_float * through_gain, axis=1),
            jnp.sum(grad_float * (hidden_pre - through_bias), axis=1),
        ]
    )
    grad_part = lax.dot_general(
        weight_own, grad_pre, (((1,), (1,)), ((), ())), preferred_element_type=f32
    ).astype(bf16)
    half = channels // 2

    def as_rows(sums):
        return jnp.pad(jnp.concatenate(split_two(sums)), ((0, 12), (0, 0))).astype(bf16)

    passed = core_swap(jnp.concatenate([grad_part[half:], as_rows(row_sums)]))
    passed_float = passed.astype(f32)
    pair = (grad_part[:half].astype(f32) + passed_float[:half]).astype(bf16)
    pair_sums = row_sums + passed_float[half : half + 2] + passed_float[half + 2 : half + 4]
    blocks = jnp.concatenate(
        [
            pair.reshape(chips, shard, rows),
            jnp.broadcast_to(as_rows(pair_sums), (chips, 16, rows)),
        ],
        axis=1,
    )
    total = jnp.sum(chip_exchange(blocks).astype(f32), axis=0)
    sum_first = total[shard] + total[shard + 2]
    sum_second = total[shard + 1] + total[shard + 3]
    gain_local = lax.dynamic_slice_in_dim(ln_gain, index * shard, shard, 0)
    normed_scaled = total[:shard].T * gain_local
    centred = (conv.astype(f32) - average[:, None]) * inverse[:, None]
    grad_conv = inverse[:, None] * (
        normed_scaled - sum_first[:, None] / channels - centred * sum_second[:, None] / channels
    )
    grad_field = grad_conv.reshape(images, side, side, shard)
    grad_input = grad_block[:, None, None, :] + depthwise(grad_field, dw_weight[::-1, ::-1])
    return (grad_input, grad_text)


def solution(mesh):
    return jax.shard_map(
        body,
        mesh=mesh,
        in_specs=(
            P("dp", None, None, "mp"),
            P(None, None, "mp"),
            P("mp"),
            P(),
            P(),
            P(None, "mp"),
            P("mp"),
            P("mp", None),
            P("mp"),
            P("mp"),
            P("mp"),
            P("mp"),
            P("mp", None),
            P("dp", None),
            P("dp"),
        ),
        out_specs=(P("dp", None, None, "mp"), P("dp", None)),
        check_vma=False,
    )
```

time: 689 us -> 158 us (0.23)
  waiting for transfers between devices: 332 us -> 42.7 us
  blocking collectives: 269 us -> 0 us
  starting transfers between devices: 21.4 us -> 49.2 us
  matrix products: 33 us -> 18.4 us
  local copies, waits for them, and re-layouts: 6.15 us -> 19.4 us
  other arithmetic: 11 us -> 24.1 us
  between operations: 14 us -> 2.7 us
    psum x5 -> x0, blocking collectives: 249 us -> none  [the longest x1 83.4 us: body(): lax.psum((jnp.sum(head_scaled, axis=1), jnp.sum(head_scaled * head_centre...]
    reduce_scatter x2 -> x0, waiting for transfers between devices: 142 us -> none  [the longest x1 73 us: body(): lax.psum_scatter(jnp.dot(activation, w_out, preferred_element_type=jnp.fl...]
    ppermute x80 -> x5, waiting for transfers between devices: 137 us -> 2.84 us  [core_swap(): return lax.ppermute(array, 'mp', [(i, i ^ 1) for i in range(length)])]
    all_gather x1 -> x0, waiting for transfers between devices: 53.4 us -> none  [body(): lax.all_gather(normed, 'mp', axis=1, tiled=True)]
    all_to_all x0 -> x7, waiting for transfers between devices: none -> 39.9 us  [the longest x5 32.9 us: chip_exchange(): return lax.all_to_all(array, 'mp', 0, 0, axis_index_groups=groups)]
    all_to_all x0 -> x7, starting transfers between devices: none -> 39.9 us  [the longest x5 24.2 us: chip_exchange(): return lax.all_to_all(array, 'mp', 0, 0, axis_index_groups=groups)]
    all_gather x1 -> x0, blocking collectives: 19.7 us -> none  [body(): mixed_whole = lax.all_gather(grad_mixed, 'mp', axis=1, tiled=True)]
    dot_general x70 -> x10, matrix products: 33 us -> 18.4 us  [the longest x1 5.42 us: body(): lax.dot_general(normed, weight_own, (((0,), (0,)), ((), ())), preferred_e...]
  transfers between devices with their start and end apart: 83 -> 12, of which waited for: 51 -> 10; matrix products, arithmetic and copies ran while one was open for 2% -> 18% of each run, Pallas kernels for 0% -> 0%
where the time goes in v1:
time: 158 us; the launch traced here: 157 us
  starting transfers between devices  49.2 us (31%)
  waiting for transfers between devices  42.7 us (27%)
  other arithmetic  24.1 us (15%)
  local copies, waits for them, and re-layouts  19.4 us (12%)
  matrix products  18.4 us (12%)
  between operations  2.7 us (2%)
    all_to_all x5, waiting for transfers between devices, chip_exchange(): return lax.all_to_all(array, 'mp', 0, 0, axis_index_groups=groups)  32.9 us
    all_to_all x5, starting transfers between devices, chip_exchange(): return lax.all_to_all(array, 'mp', 0, 0, axis_index_groups=groups)  24.2 us
    all_to_all x2, starting transfers between devices, dp_gather(): lax.all_to_all(jnp.broadcast_to(array, (count,) + array.shape), 'dp', 0, 0)  15.7 us
    ppermute x5, starting transfers between devices, core_swap(): return lax.ppermute(array, 'mp', [(i, i ^ 1) for i in range(length)])  9.31 us
    select_n x1, other arithmetic, body(): jnp.where(core == 0, jnp.swapaxes(weight_pairs, 0, 1), jnp.swapaxes(weigh...  7.43 us
    all_to_all x2, waiting for transfers between devices, dp_gather(): lax.all_to_all(jnp.broadcast_to(array, (count,) + array.shape), 'dp', 0, 0)  6.99 us
    dot_general x1, matrix products, body(): lax.dot_general(normed, weight_own, (((0,), (0,)), ((), ())), preferred_e...  5.42 us
    reshape x1, local copies, waits for them, and re-layouts, body(): weight_pairs = w_in.reshape(chips, 2, shard, hidden)  4.97 us
  transfers between devices with their start and end apart: 12, of which 10 were waited for; matrix products, arithmetic and copies ran while one was open for 18% of the time, Pallas kernels for 0%

profile of v1, /device:TPU:1, one launch (start us, length us, event | category | flops | bytes accessed | tf_op | source)
XLA Modules:
  0.0 156.6 jit_solution(16377834672781426358)
XLA Ops:
  0.7 0.9 fusion.293
  1.7 1.0 fusion.291
  2.9 1.6 %fusion.292 = (f32[1,1,192]{2,1,0:T(1,128)S(1)}, f32[1,1,192]{2,1,0:T(1,128)S(1)}, f32[1,1,192]{2,1,0:T(1,128)S(1)}, f32[1,1,192]{2,1,0:T(1,128)S(1)}, f32[1,1,1...) fusion(f32[7,7,192]{2,1,0:T(8,128)} %param.16), kind=kLoop, calls=%fused_computation.474 | loop fusion | bytes 29184 | tf_op jit(solution)/shard_map/slice | solution.py:57
  4.6 0.9 convert_element_type.67
  5.5 2.3 %fusion.226 = bf16[4,8,8,192]{3,2,1,0:T(8,128)(2,1)S(1)} fusion(f32[4,8,8,192]{3,2,1,0:T(8,128)S(1)} %convert_element_type.67, f32[192]{0:T(256)} %param.17, f32[192]{0:T(256)S(1)} %bitcast.197, f32[192]{0:T(256)S(1)} %bitcast.199, f32[192]{0:T(256)S(1)} %bitcast.203, f32[192]{0:T(256)S(1)} %bitcast.205, f32[192]{0:T(256)S(1)} %bitcast.207, ...), kind=kLoop, calls=%fused_computation.335 | loop fusion | flops 4866048 | bytes 333312 | tf_op jit(solution)/shard_map/convert_element_type | solution.py:109
  7.9 1.0 broadcast_in_dim.22
  8.9 7.5 %all-to-all-start = ((bf16[8,192,256]{2,1,0:T(8,128)(2,1)}), bf16[8,192,256]{2,1,0:T(8,128)(2,1)S(1)}, u32[]{:S(2)}, u32[]{:S(2)}) async-start(bf16[8,192,256]{2,1,0:T(8,128)(2,1)} %broadcast_in_dim.22), calls=%async_computation | async-start | bytes 1572864 | tf_op jit(solution)/shard_map/all_to_all | solution.py:24
  16.7 5.0 %copy.116 = bf16[8,2,192,768]{3,2,0,1:T(8,128)(2,1)} copy(bf16[8,2,192,768]{3,2,1,0:T(8,128)(2,1)} %bitcast.161) | data formatting | bytes 9437184 | tf_op jit(solution)/shard_map/reshape | solution.py:117
  22.1 5.6 %all-to-all-done = bf16[8,192,256]{2,1,0:T(8,128)(2,1)S(1)} async-done(((bf16[8,192,256]{2,1,0:T(8,128)(2,1)}), bf16[8,192,256]{2,1,0:T(8,128)(2,1)S(1)}, u32[]{:S(2)}, u32[]{:S(2)}) %all-to-all-start) | async-done | bytes 786464 | tf_op jit(solution)/shard_map/all_to_all | solution.py:24
  27.7 0.8 broadcast_in_dim.29
  28.6 8.3 %all-to-all-start.4 = ((f32[16,8,1024]{2,1,0:T(8,128)}), f32[16,8,1024]{2,1,0:T(8,128)S(1)}, u32[]{:S(2)}, u32[]{:S(2)}) async-start(f32[16,8,1024]{2,1,0:T(8,128)} %broadcast_in_dim.29), calls=%async_computation.4 | async-start | bytes 1048576 | tf_op jit(solution)/shard_map/all_to_all | solution.py:34
  36.9 3.3 %collective-permute-start = (bf16[8,192,256]{2,1,0:T(8,128)(2,1)S(1)}, bf16[8,192,256]{2,1,0:T(8,128)(2,1)S(1)}, u32[]{:S(2)}, u32[]{:S(2)}) collective-permute-start(bf16[8,192,256]{2,1,0:T(8,128)(2,1)S(1)} %all-to-all-done), channel_id=1, source_target_pairs={{0,1},{1,0},{2,3},{3,2},{4,5},{5,4},{6,7},{7,6},{8,9},{9,8},{10,11... | collective-permute-start | bytes 2359304 | tf_op jit(solution)/shard_map/ppermute | solution.py:18
  40.2 7.4 %reverse_select_fusion = bf16[8,2,192,768]{3,2,0,1:T(8,128)(2,1)} fusion(bf16[8,2,192,768]{3,2,0,1:T(8,128)(2,1)} %copy.116, pred[]{:T(512)S(6)} %eq.12), kind=kLoop, calls=%fused_computation.96 | loop fusion | flops 2359296 | bytes 9437185 | tf_op jit(solution)/shard_map/jit(_where)/select_n | solution.py:118
  47.8 0.5 convert_reduce_fusion
  48.3 0.4 copy-done.1
  48.7 5.4 %bitcast_reduce_fusion = (f32[4,768]{1,0:T(4,128)S(1)}, f32[256,768]{1,0:T(8,128)S(1)}) fusion(f32[768]{0:T(1024)S(1)} %copy-done.96, bf16[8,2,192,768]{3,2,0,1:T(8,128)(2,1)} %reverse_select_fusion, f32[2,8,192]{2,1,0:T(8,128)S(1)} %copy.114, f32[2,8,192]{2,1,0:T(8,128)S(1)} %copy.113, f32[256]{0:T(256)S(1)} %get-tuple-element.91, ...), kind=kOutput, calls=%fused_computation.136 | convolution fusion | flops 1214641152 | bytes 7119872 | tf_op jit(solution)/shard_map/dot_general | solution.py:127
  54.2 0.7 fusion.253
  55.5 1.1 collective-permute-done.1
  56.6 0.6 fusion.233
  57.2 4.1 %all-to-all-start.1 = ((f32[8,4,192]{2,1,0:T(4,128)}), f32[8,4,192]{2,1,0:T(4,128)S(1)}, u32[]{:S(2)}, u32[]{:S(2)}) async-start(f32[8,4,192]{2,1,0:T(4,128)} %fusion.233), calls=%async_computation.1 | async-start | bytes 65536 | tf_op jit(solution)/shard_map/all_to_all | solution.py:24
  61.2 0.2 multiply_reduce_fusion
  61.5 6.3 %all-to-all-done.1 = f32[8,4,192]{2,1,0:T(4,128)S(1)} async-done(((f32[8,4,192]{2,1,0:T(4,128)}), f32[8,4,192]{2,1,0:T(4,128)S(1)}, u32[]{:S(2)}, u32[]{:S(2)}) %all-to-all-start.1) | async-done | bytes 24608 | tf_op jit(solution)/shard_map/all_to_all | solution.py:24
  68.2 0.3 fusion.260
  68.5 1.7 %collective-permute-start.2 = (f32[8,1024]{1,0:T(8,128)S(1)}, f32[8,1024]{1,0:T(8,128)S(1)}, u32[]{:S(2)}, u32[]{:S(2)}) collective-permute-start(f32[8,1024]{1,0:T(8,128)S(1)} %select_maximum_fusion.1), channel_id=1, source_target_pairs={{0,1},{1,0},{2,3},{3,2},{4,5},{5,4},{6,7},{7,6},{8,9},{9,8},{10,11... | collective-permute-start | bytes 98312 | tf_op jit(solution)/shard_map/ppermute | solution.py:18
  70.2 0.8 collective-permute-done.2
  71.0 0.7 broadcast_in_dim.26
  71.7 3.4 %all-to-all-start.2 = ((f32[8,8,1024]{2,1,0:T(8,128)}), f32[8,8,1024]{2,1,0:T(8,128)S(1)}, u32[]{:S(2)}, u32[]{:S(2)}) async-start(f32[8,8,1024]{2,1,0:T(8,128)} %broadcast_in_dim.26), calls=%async_computation.2 | async-start | bytes 524288 | tf_op jit(solution)/shard_map/all_to_all | solution.py:24
  75.3 7.3 %all-to-all-done.2 = f32[8,8,1024]{2,1,0:T(8,128)S(1)} async-done(((f32[8,8,1024]{2,1,0:T(8,128)}), f32[8,8,1024]{2,1,0:T(8,128)S(1)}, u32[]{:S(2)}, u32[]{:S(2)}) %all-to-all-start.2) | async-done | bytes 262176 | tf_op jit(solution)/shard_map/all_to_all | solution.py:24
  82.7 0.6 broadcast_multiply_fusion.4
  83.4 0.8 broadcast_in_dim.27
  84.2 7.4 %all-to-all-start.3 = ((f32[16,4,1024]{2,1,0:T(4,128)}), f32[16,4,1024]{2,1,0:T(4,128)S(1)}, u32[]{:S(2)}, u32[]{:S(2)}) async-start(f32[16,4,1024]{2,1,0:T(4,128)} %broadcast_in_dim.27), calls=%async_computation.3 | async-start | bytes 524288 | tf_op jit(solution)/shard_map/all_to_all | solution.py:34
  91.8 0.2 copy.122
  92.3 7.0 %all-to-all-done.3 = f32[16,4,1024]{2,1,0:T(4,128)S(1)} async-done(((f32[16,4,1024]{2,1,0:T(4,128)}), f32[16,4,1024]{2,1,0:T(4,128)S(1)}, u32[]{:S(2)}, u32[]{:S(2)}) %all-to-all-start.3) | async-done | bytes 262176 | tf_op jit(solution)/shard_map/all_to_all | solution.py:34
  100.0 0.5 fusion.287
  100.7 0.4 multiply_reduce_fusion.4
  101.1 0.2 convolution_multiply_fusion.3
  101.4 0.7 reshape.451
  102.1 5.7 %all-to-all-start.5 = ((f32[8,1,1728]{2,1,0:T(1,128)}), f32[8,1,1728]{2,1,0:T(1,128)S(1)}, u32[]{:S(2)}, u32[]{:S(2)}) async-start(f32[8,1,1728]{2,1,0:T(1,128)} %reshape.451), calls=%async_computation.5 | async-start | bytes 114688 | tf_op jit(solution)/shard_map/all_to_all | solution.py:24
  107.8 3.1 %fusion.235 = f32[4,768]{1,0:T(4,128)S(1)} fusion(bf16[3072,768]{1,0:T(8,128)(2,1)} %bitcast.157, bf16[1,3072]{1,0:T(2,128)(2,1)S(1)} %get-tuple-element.87, bf16[1,3072]{1,0:T(2,128)(2,1)S(1)} %get-tuple-element.86, bf16[1,3072]{1,0:T(2,128)(2,1)S(1)} %get-tuple-element.85, bf16[1,3072]{1,0:T(2,128)(2,1)S(1)} %get-tuple-element.84), kind=kOutput, calls=%fused_computation.367 | convolution fusion | flops 18972672 | bytes 4755456 | tf_op jit(solution)/shard_map/dot_general | solution.py:228
  110.8 3.6 %all-to-all-done.5 = f32[8,1,1728]{2,1,0:T(1,128)S(1)} async-done(((f32[8,1,1728]{2,1,0:T(1,128)}), f32[8,1,1728]{2,1,0:T(1,128)S(1)}, u32[]{:S(2)}, u32[]{:S(2)}) %all-to-all-start.5) | async-done | bytes 55328 | tf_op jit(solution)/shard_map/all_to_all | solution.py:24
  114.4 0.5 broadcast.325
  115.0 0.8 reduce.13
  115.8 3.8 %collective-permute-start.3 = (f32[8,9,192]{2,1,0:T(8,128)S(1)}, f32[8,9,192]{2,1,0:T(8,128)S(1)}, u32[]{:S(2)}, u32[]{:S(2)}) collective-permute-start(f32[8,9,192]{2,1,0:T(8,128)S(1)} %reshape.452), channel_id=1, source_target_pairs={{0,1},{1,0},{2,3},{3,2},{4,5},{5,4},{6,7},{7,6},{8,9},{9,8},{10,11... | collective-permute-start | bytes 165896 | tf_op jit(solution)/shard_map/ppermute | solution.py:18
  119.6 0.9 collective-permute-done.3
  120.6 0.2 fusion.286
  120.8 0.5 copy-done.100
  121.7 3.6 %fusion.295 = f32[4,768]{1,0:T(4,128)S(1)} fusion(bf16[4,3072]{1,0:T(4,128)(2,1)S(1)} %reshape.438, bf16[768,3072]{1,0:T(8,128)(2,1)} %param.22), kind=kOutput, calls=%fused_computation.477 | convolution fusion | flops 18874368 | bytes 4755456 | tf_op jit(solution)/shard_map/dot_general | solution.py:218
  125.3 0.5 fusion.24
  125.9 3.8 %convolution_convert_fusion = bf16[3072,256]{1,0:T(8,128)(2,1)S(1)} fusion(bf16[3072,768]{1,0:T(8,128)(2,1)} %bitcast.158, bf16[256,768]{1,0:T(8,128)(2,1)S(1)} %get-tuple-element.16), kind=kOutput, calls=%fused_computation.102 | convolution fusion | flops 1208745984 | bytes 6684672 | tf_op jit(solution)/shard_map/dot_general | solution.py:242
  129.8 0.4 collective-permute-start.4
  130.4 1.3 dynamic_slice.24
  131.7 0.6 sqrt.43
  132.4 1.2 convert_element_type.79
  133.6 0.7 reduce-precision_convert_fusion.3
  134.3 0.3 fusion.8
  135.0 1.0 pad_maximum_fusion.1
  136.0 3.5 %all-to-all-start.6 = ((bf16[8,208,256]{2,1,0:T(8,128)(2,1)}), bf16[8,208,256]{2,1,0:T(8,128)(2,1)S(1)}, u32[]{:S(2)}, u32[]{:S(2)}) async-start(bf16[8,208,256]{2,1,0:T(8,128)(2,1)} %pad_maximum_fusion.1), calls=%async_computation.6 | async-start | bytes 1703936 | tf_op jit(solution)/shard_map/all_to_all | solution.py:24
  139.6 0.7 fusion.278
  140.3 0.5 multiply_reduce_fusion.3
  140.7 0.7 subtract_divide_fusion
  141.4 0.8 subtract_multiply_fusion.1
  142.2 10.0 %all-to-all-done.6 = bf16[8,208,256]{2,1,0:T(8,128)(2,1)S(1)} async-done(((bf16[8,208,256]{2,1,0:T(8,128)(2,1)}), bf16[8,208,256]{2,1,0:T(8,128)(2,1)S(1)}, u32[]{:S(2)}, u32[]{:S(2)}) %all-to-all-start.6) | async-done | bytes 852000 | tf_op jit(solution)/shard_map/all_to_all | solution.py:24
  152.4 0.8 fusion.230
  153.7 2.9 %fusion.218 = f32[4,8,8,192]{3,2,1,0:T(8,128)} fusion(f32[4,8,8,192]{3,2,1,0:T(8,128)S(1)} %bitcast.169, f32[4,192]{1,0:T(4,128)S(1)} %subtract_multiply_fusion.1, f32[192]{0:T(256)S(1)} %bitcast.198, f32[192]{0:T(256)S(1)} %bitcast.200, f32[192]{0:T(256)S(1)} %bitcast.204, f32[192]{0:T(256)S(1)} %bitcast.206, f32[192]{0:T(256)S(1)} %bitcast.208, ...), kind=kLoop, calls=%fused_computation.325 | loop fusion | flops 4816896 | bytes 433920 | tf_op jit(solution)/shard_map/add | solution.py:271
  (297 shorter events, 4.7 us)
Async XLA Ops:
  0.6 67.5 %copy-start = (bf16[192,1024]{1,0:T(8,128)(2,1)S(1)}, bf16[192,1024]{1,0:T(8,128)(2,1)}, u32[]{:S(2)}) copy-start(bf16[192,1024]{1,0:T(8,128)(2,1)} %param.27) | copy-start | bytes 1179652
  1.6 20.1 %copy-start.12 = (f32[1,1,192]{2,1,0:T(1,128)}, f32[1,1,192]{2,1,0:T(1,128)S(1)}, u32[]{:S(2)}) copy-start(f32[1,1,192]{2,1,0:T(1,128)S(1)} %get-tuple-element.66) | copy-start | bytes 2308
  1.6 20.1 %copy-start.14 = (f32[1,1,192]{2,1,0:T(1,128)}, f32[1,1,192]{2,1,0:T(1,128)S(1)}, u32[]{:S(2)}) copy-start(f32[1,1,192]{2,1,0:T(1,128)S(1)} %get-tuple-element.67) | copy-start | bytes 2308
  1.6 20.0 %copy-start.16 = (f32[1,1,192]{2,1,0:T(1,128)}, f32[1,1,192]{2,1,0:T(1,128)S(1)}, u32[]{:S(2)}) copy-start(f32[1,1,192]{2,1,0:T(1,128)S(1)} %get-tuple-element.68) | copy-start | bytes 2308
  1.6 20.0 %copy-start.18 = (f32[1,1,192]{2,1,0:T(1,128)}, f32[1,1,192]{2,1,0:T(1,128)S(1)}, u32[]{:S(2)}) copy-start(f32[1,1,192]{2,1,0:T(1,128)S(1)} %get-tuple-element.69) | copy-start | bytes 2308
  1.6 20.0 %copy-start.20 = (f32[1,1,192]{2,1,0:T(1,128)}, f32[1,1,192]{2,1,0:T(1,128)S(1)}, u32[]{:S(2)}) copy-start(f32[1,1,192]{2,1,0:T(1,128)S(1)} %get-tuple-element.70) | copy-start | bytes 2308
  1.7 20.0 %copy-start.22 = (f32[1,1,192]{2,1,0:T(1,128)}, f32[1,1,192]{2,1,0:T(1,128)S(1)}, u32[]{:S(2)}) copy-start(f32[1,1,192]{2,1,0:T(1,128)S(1)} %get-tuple-element.71) | copy-start | bytes 2308
  1.7 20.0 %copy-start.24 = (f32[1,1,192]{2,1,0:T(1,128)}, f32[1,1,192]{2,1,0:T(1,128)S(1)}, u32[]{:S(2)}) copy-start(f32[1,1,192]{2,1,0:T(1,128)S(1)} %get-tuple-element.72) | copy-start | bytes 2308
  1.7 20.0 %copy-start.26 = (f32[1,1,192]{2,1,0:T(1,128)}, f32[1,1,192]{2,1,0:T(1,128)S(1)}, u32[]{:S(2)}) copy-start(f32[1,1,192]{2,1,0:T(1,128)S(1)} %get-tuple-element.73) | copy-start | bytes 2308
  1.7 20.0 %copy-start.28 = (f32[1,1,192]{2,1,0:T(1,128)}, f32[1,1,192]{2,1,0:T(1,128)S(1)}, u32[]{:S(2)}) copy-start(f32[1,1,192]{2,1,0:T(1,128)S(1)} %get-tuple-element.74) | copy-start | bytes 2308
  1.7 20.0 %copy-start.30 = (f32[1,1,192]{2,1,0:T(1,128)}, f32[1,1,192]{2,1,0:T(1,128)S(1)}, u32[]{:S(2)}) copy-start(f32[1,1,192]{2,1,0:T(1,128)S(1)} %get-tuple-element.75) | copy-start | bytes 2308
  2.7 19.0 %copy-start.32 = (f32[1,1,192]{2,1,0:T(1,128)}, f32[1,1,192]{2,1,0:T(1,128)S(1)}, u32[]{:S(2)}) copy-start(f32[1,1,192]{2,1,0:T(1,128)S(1)} %get-tuple-element.27) | copy-start | bytes 2308
  2.7 19.0 %copy-start.34 = (f32[1,1,192]{2,1,0:T(1,128)}, f32[1,1,192]{2,1,0:T(1,128)S(1)}, u32[]{:S(2)}) copy-start(f32[1,1,192]{2,1,0:T(1,128)S(1)} %get-tuple-element.28) | copy-start | bytes 2308
  2.7 19.0 %copy-start.36 = (f32[1,1,192]{2,1,0:T(1,128)}, f32[1,1,192]{2,1,0:T(1,128)S(1)}, u32[]{:S(2)}) copy-start(f32[1,1,192]{2,1,0:T(1,128)S(1)} %get-tuple-element.29) | copy-start | bytes 2308
  2.7 19.0 %copy-start.38 = (f32[1,1,192]{2,1,0:T(1,128)}, f32[1,1,192]{2,1,0:T(1,128)S(1)}, u32[]{:S(2)}) copy-start(f32[1,1,192]{2,1,0:T(1,128)S(1)} %get-tuple-element.30) | copy-start | bytes 2308
  2.7 19.0 %copy-start.40 = (f32[1,1,192]{2,1,0:T(1,128)}, f32[1,1,192]{2,1,0:T(1,128)S(1)}, u32[]{:S(2)}) copy-start(f32[1,1,192]{2,1,0:T(1,128)S(1)} %get-tuple-element.31) | copy-start | bytes 2308
  2.7 19.0 %copy-start.42 = (f32[1,1,192]{2,1,0:T(1,128)}, f32[1,1,192]{2,1,0:T(1,128)S(1)}, u32[]{:S(2)}) copy-start(f32[1,1,192]{2,1,0:T(1,128)S(1)} %get-tuple-element.32) | copy-start | bytes 2308
  2.8 19.0 %copy-start.44 = (f32[1,1,192]{2,1,0:T(1,128)}, f32[1,1,192]{2,1,0:T(1,128)S(1)}, u32[]{:S(2)}) copy-start(f32[1,1,192]{2,1,0:T(1,128)S(1)} %get-tuple-element.33) | copy-start | bytes 2308
  2.8 19.0 %copy-start.46 = (f32[1,1,192]{2,1,0:T(1,128)}, f32[1,1,192]{2,1,0:T(1,128)S(1)}, u32[]{:S(2)}) copy-start(f32[1,1,192]{2,1,0:T(1,128)S(1)} %get-tuple-element.34) | copy-start | bytes 2308
  2.8 19.0 %copy-start.48 = (f32[1,1,192]{2,1,0:T(1,128)}, f32[1,1,192]{2,1,0:T(1,128)S(1)}, u32[]{:S(2)}) copy-start(f32[1,1,192]{2,1,0:T(1,128)S(1)} %get-tuple-element.35) | copy-start | bytes 2308
  2.8 19.0 %copy-start.50 = (f32[1,1,192]{2,1,0:T(1,128)}, f32[1,1,192]{2,1,0:T(1,128)S(1)}, u32[]{:S(2)}) copy-start(f32[1,1,192]{2,1,0:T(1,128)S(1)} %get-tuple-element.36) | copy-start | bytes 2308
  2.8 19.0 %copy-start.52 = (f32[1,1,192]{2,1,0:T(1,128)}, f32[1,1,192]{2,1,0:T(1,128)S(1)}, u32[]{:S(2)}) copy-start(f32[1,1,192]{2,1,0:T(1,128)S(1)} %get-tuple-element.37) | copy-start | bytes 2308
  2.8 19.0 %copy-start.54 = (f32[1,1,192]{2,1,0:T(1,128)}, f32[1,1,192]{2,1,0:T(1,128)S(1)}, u32[]{:S(2)}) copy-start(f32[1,1,192]{2,1,0:T(1,128)S(1)} %get-tuple-element.38) | copy-start | bytes 2308
  2.8 19.0 %copy-start.56 = (f32[1,1,192]{2,1,0:T(1,128)}, f32[1,1,192]{2,1,0:T(1,128)S(1)}, u32[]{:S(2)}) copy-start(f32[1,1,192]{2,1,0:T(1,128)S(1)} %get-tuple-element.39) | copy-start | bytes 2308
  2.8 19.0 %copy-start.58 = (f32[1,1,192]{2,1,0:T(1,128)}, f32[1,1,192]{2,1,0:T(1,128)S(1)}, u32[]{:S(2)}) copy-start(f32[1,1,192]{2,1,0:T(1,128)S(1)} %get-tuple-element.40) | copy-start | bytes 2308
  2.8 19.0 %copy-start.60 = (f32[1,1,192]{2,1,0:T(1,128)}, f32[1,1,192]{2,1,0:T(1,128)S(1)}, u32[]{:S(2)}) copy-start(f32[1,1,192]{2,1,0:T(1,128)S(1)} %get-tuple-element.41) | copy-start | bytes 2308
  2.8 19.0 %copy-start.62 = (f32[1,1,192]{2,1,0:T(1,128)}, f32[1,1,192]{2,1,0:T(1,128)S(1)}, u32[]{:S(2)}) copy-start(f32[1,1,192]{2,1,0:T(1,128)S(1)} %get-tuple-element.42) | copy-start | bytes 2308
  2.9 19.0 %copy-start.64 = (f32[1,1,192]{2,1,0:T(1,128)}, f32[1,1,192]{2,1,0:T(1,128)S(1)}, u32[]{:S(2)}) copy-start(f32[1,1,192]{2,1,0:T(1,128)S(1)} %get-tuple-element.43) | copy-start | bytes 2308
  2.9 19.0 %copy-start.66 = (f32[1,1,192]{2,1,0:T(1,128)}, f32[1,1,192]{2,1,0:T(1,128)S(1)}, u32[]{:S(2)}) copy-start(f32[1,1,192]{2,1,0:T(1,128)S(1)} %get-tuple-element.44) | copy-start | bytes 2308
  2.9 19.0 %copy-start.68 = (f32[1,1,192]{2,1,0:T(1,128)}, f32[1,1,192]{2,1,0:T(1,128)S(1)}, u32[]{:S(2)}) copy-start(f32[1,1,192]{2,1,0:T(1,128)S(1)} %get-tuple-element.45) | copy-start | bytes 2308
  8.9 18.9 %all-to-all-start = ((bf16[8,192,256]{2,1,0:T(8,128)(2,1)}), bf16[8,192,256]{2,1,0:T(8,128)(2,1)S(1)}, u32[]{:S(2)}, u32[]{:S(2)}) async-start(bf16[8,192,256]{2,1,0:T(8,128)(2,1)} %broadcast_in_dim.22), calls=%async_computation | async-start | bytes 1572864 | tf_op jit(solution)/shard_map/all_to_all | solution.py:24
  28.6 26.8 %all-to-all-start.4 = ((f32[16,8,1024]{2,1,0:T(8,128)}), f32[16,8,1024]{2,1,0:T(8,128)S(1)}, u32[]{:S(2)}, u32[]{:S(2)}) async-start(f32[16,8,1024]{2,1,0:T(8,128)} %broadcast_in_dim.29), calls=%async_computation.4 | async-start | bytes 1048576 | tf_op jit(solution)/shard_map/all_to_all | solution.py:34
  36.9 10.9 %collective-permute-start = (bf16[8,192,256]{2,1,0:T(8,128)(2,1)S(1)}, bf16[8,192,256]{2,1,0:T(8,128)(2,1)S(1)}, u32[]{:S(2)}, u32[]{:S(2)}) collective-permute-start(bf16[8,192,256]{2,1,0:T(8,128)(2,1)S(1)} %all-to-all-done), channel_id=1, source_target_pairs={{0,1},{1,0},{2,3},{3,2},{4,5},{5,4},{6,7},{7,6},{8,9},{9,8},{10,11... | collective-permute-start | bytes 2359304 | tf_op jit(solution)/shard_map/ppermute | solution.py:18
  55.3 1.3 collective-permute-start.1
  57.2 10.7 %all-to-all-start.1 = ((f32[8,4,192]{2,1,0:T(4,128)}), f32[8,4,192]{2,1,0:T(4,128)S(1)}, u32[]{:S(2)}, u32[]{:S(2)}) async-start(f32[8,4,192]{2,1,0:T(4,128)} %fusion.233), calls=%async_computation.1 | async-start | bytes 65536 | tf_op jit(solution)/shard_map/all_to_all | solution.py:24
  67.9 31.9 %copy-start.3 = (f32[4,192]{1,0:T(4,128)}, f32[4,192]{1,0:T(4,128)S(1)}, u32[]{:S(2)}) copy-start(f32[4,192]{1,0:T(4,128)S(1)} %get-tuple-element.22) | copy-start | bytes 9220
  68.5 2.5 %collective-permute-start.2 = (f32[8,1024]{1,0:T(8,128)S(1)}, f32[8,1024]{1,0:T(8,128)S(1)}, u32[]{:S(2)}, u32[]{:S(2)}) collective-permute-start(f32[8,1024]{1,0:T(8,128)S(1)} %select_maximum_fusion.1), channel_id=1, source_target_pairs={{0,1},{1,0},{2,3},{3,2},{4,5},{5,4},{6,7},{7,6},{8,9},{9,8},{10,11... | collective-permute-start | bytes 98312 | tf_op jit(solution)/shard_map/ppermute | solution.py:18
  71.7 10.9 %all-to-all-start.2 = ((f32[8,8,1024]{2,1,0:T(8,128)}), f32[8,8,1024]{2,1,0:T(8,128)S(1)}, u32[]{:S(2)}, u32[]{:S(2)}) async-start(f32[8,8,1024]{2,1,0:T(8,128)} %broadcast_in_dim.26), calls=%async_computation.2 | async-start | bytes 524288 | tf_op jit(solution)/shard_map/all_to_all | solution.py:24
  84.2 15.1 %all-to-all-start.3 = ((f32[16,4,1024]{2,1,0:T(4,128)}), f32[16,4,1024]{2,1,0:T(4,128)S(1)}, u32[]{:S(2)}, u32[]{:S(2)}) async-start(f32[16,4,1024]{2,1,0:T(4,128)} %broadcast_in_dim.27), calls=%async_computation.3 | async-start | bytes 524288 | tf_op jit(solution)/shard_map/all_to_all | solution.py:34
  100.7 18.9 %copy-start.97 = (f32[768]{0:T(1024)S(1)}, f32[768]{0:T(1024)}, u32[]{:S(2)}) copy-start(f32[768]{0:T(1024)} %param.21) | copy-start | bytes 9220
  101.3 19.5 %copy-start.6 = (f32[4,192]{1,0:T(4,128)}, f32[4,192]{1,0:T(4,128)S(1)}, u32[]{:S(2)}) copy-start(f32[4,192]{1,0:T(4,128)S(1)} %convolution_multiply_fusion.3) | copy-start | bytes 9220
  101.3 20.1 %copy-start.91 = (f32[4]{0:T(128)S(1)}, f32[4]{0:T(128)}, u32[]{:S(2)}) copy-start(f32[4]{0:T(128)} %get-tuple-element.17) | copy-start | bytes 52
  102.1 12.4 %all-to-all-start.5 = ((f32[8,1,1728]{2,1,0:T(1,128)}), f32[8,1,1728]{2,1,0:T(1,128)S(1)}, u32[]{:S(2)}, u32[]{:S(2)}) async-start(f32[8,1,1728]{2,1,0:T(1,128)} %reshape.451), calls=%async_computation.5 | async-start | bytes 114688 | tf_op jit(solution)/shard_map/all_to_all | solution.py:24
  115.8 4.7 %collective-permute-start.3 = (f32[8,9,192]{2,1,0:T(8,128)S(1)}, f32[8,9,192]{2,1,0:T(8,128)S(1)}, u32[]{:S(2)}, u32[]{:S(2)}) collective-permute-start(f32[8,9,192]{2,1,0:T(8,128)S(1)} %reshape.452), channel_id=1, source_target_pairs={{0,1},{1,0},{2,3},{3,2},{4,5},{5,4},{6,7},{7,6},{8,9},{9,8},{10,11... | collective-permute-start | bytes 165896 | tf_op jit(solution)/shard_map/ppermute | solution.py:18
  129.8 2.5 %collective-permute-start.4 = (bf16[1552,256]{1,0:T(8,128)(2,1)S(1)}, bf16[1552,256]{1,0:T(8,128)(2,1)}, u32[]{:S(2)}, u32[]{:S(2)}) collective-permute-start(bf16[1552,256]{1,0:T(8,128)(2,1)S(1)} %pad_maximum_fusion.2), channel_id=1, source_target_pairs={{0,1},{1,0},{2,3},{3,2},{4,5},{5,4},{6,7},{7,6},{8,9},{9,8},{10,11... | collective-permute-start | bytes 2383880 | tf_op jit(solution)/shard_map/ppermute | solution.py:18
  134.6 18.7 %copy-start.11 = (f32[1,1,192]{2,1,0:T(1,128)S(1)}, f32[1,1,192]{2,1,0:T(1,128)}, u32[]{:S(2)}) copy-start(f32[1,1,192]{2,1,0:T(1,128)} %copy-done.10) | copy-start | bytes 2308
  134.6 18.7 %copy-start.13 = (f32[1,1,192]{2,1,0:T(1,128)S(1)}, f32[1,1,192]{2,1,0:T(1,128)}, u32[]{:S(2)}) copy-start(f32[1,1,192]{2,1,0:T(1,128)} %copy-done.12) | copy-start | bytes 2308
  134.6 18.7 %copy-start.15 = (f32[1,1,192]{2,1,0:T(1,128)S(1)}, f32[1,1,192]{2,1,0:T(1,128)}, u32[]{:S(2)}) copy-start(f32[1,1,192]{2,1,0:T(1,128)} %copy-done.14) | copy-start | bytes 2308
  134.6 18.7 %copy-start.17 = (f32[1,1,192]{2,1,0:T(1,128)S(1)}, f32[1,1,192]{2,1,0:T(1,128)}, u32[]{:S(2)}) copy-start(f32[1,1,192]{2,1,0:T(1,128)} %copy-done.16) | copy-start | bytes 2308
  134.6 18.7 %copy-start.19 = (f32[1,1,192]{2,1,0:T(1,128)S(1)}, f32[1,1,192]{2,1,0:T(1,128)}, u32[]{:S(2)}) copy-start(f32[1,1,192]{2,1,0:T(1,128)} %copy-done.18) | copy-start | bytes 2308
  134.6 18.7 %copy-start.21 = (f32[1,1,192]{2,1,0:T(1,128)S(1)}, f32[1,1,192]{2,1,0:T(1,128)}, u32[]{:S(2)}) copy-start(f32[1,1,192]{2,1,0:T(1,128)} %copy-done.20) | copy-start | bytes 2308
  134.7 18.7 %copy-start.23 = (f32[1,1,192]{2,1,0:T(1,128)S(1)}, f32[1,1,192]{2,1,0:T(1,128)}, u32[]{:S(2)}) copy-start(f32[1,1,192]{2,1,0:T(1,128)} %copy-done.22) | copy-start | bytes 2308
  134.7 18.7 %copy-start.25 = (f32[1,1,192]{2,1,0:T(1,128)S(1)}, f32[1,1,192]{2,1,0:T(1,128)}, u32[]{:S(2)}) copy-start(f32[1,1,192]{2,1,0:T(1,128)} %copy-done.24) | copy-start | bytes 2308
  134.7 18.7 %copy-start.27 = (f32[1,1,192]{2,1,0:T(1,128)S(1)}, f32[1,1,192]{2,1,0:T(1,128)}, u32[]{:S(2)}) copy-start(f32[1,1,192]{2,1,0:T(1,128)} %copy-done.26) | copy-start | bytes 2308
  134.7 18.7 %copy-start.29 = (f32[1,1,192]{2,1,0:T(1,128)S(1)}, f32[1,1,192]{2,1,0:T(1,128)}, u32[]{:S(2)}) copy-start(f32[1,1,192]{2,1,0:T(1,128)} %copy-done.28) | copy-start | bytes 2308
  134.7 18.7 %copy-start.31 = (f32[1,1,192]{2,1,0:T(1,128)S(1)}, f32[1,1,192]{2,1,0:T(1,128)}, u32[]{:S(2)}) copy-start(f32[1,1,192]{2,1,0:T(1,128)} %copy-done.30) | copy-start | bytes 2308
  134.7 18.7 %copy-start.33 = (f32[1,1,192]{2,1,0:T(1,128)S(1)}, f32[1,1,192]{2,1,0:T(1,128)}, u32[]{:S(2)}) copy-start(f32[1,1,192]{2,1,0:T(1,128)} %copy-done.32) | copy-start | bytes 2308
  134.7 18.7 %copy-start.35 = (f32[1,1,192]{2,1,0:T(1,128)S(1)}, f32[1,1,192]{2,1,0:T(1,128)}, u32[]{:S(2)}) copy-start(f32[1,1,192]{2,1,0:T(1,128)} %copy-done.34) | copy-start | bytes 2308
  134.7 18.7 %copy-start.37 = (f32[1,1,192]{2,1,0:T(1,128)S(1)}, f32[1,1,192]{2,1,0:T(1,128)}, u32[]{:S(2)}) copy-start(f32[1,1,192]{2,1,0:T(1,128)} %copy-done.36) | copy-start | bytes 2308
  134.7 18.7 %copy-start.39 = (f32[1,1,192]{2,1,0:T(1,128)S(1)}, f32[1,1,192]{2,1,0:T(1,128)}, u32[]{:S(2)}) copy-start(f32[1,1,192]{2,1,0:T(1,128)} %copy-done.38) | copy-start | bytes 2308
  134.7 18.7 %copy-start.41 = (f32[1,1,192]{2,1,0:T(1,128)S(1)}, f32[1,1,192]{2,1,0:T(1,128)}, u32[]{:S(2)}) copy-start(f32[1,1,192]{2,1,0:T(1,128)} %copy-done.40) | copy-start | bytes 2308
  134.8 18.7 %copy-start.43 = (f32[1,1,192]{2,1,0:T(1,128)S(1)}, f32[1,1,192]{2,1,0:T(1,128)}, u32[]{:S(2)}) copy-start(f32[1,1,192]{2,1,0:T(1,128)} %copy-done.42) | copy-start | bytes 2308
  134.8 18.7 %copy-start.45 = (f32[1,1,192]{2,1,0:T(1,128)S(1)}, f32[1,1,192]{2,1,0:T(1,128)}, u32[]{:S(2)}) copy-start(f32[1,1,192]{2,1,0:T(1,128)} %copy-done.44) | copy-start | bytes 2308
  136.0 16.2 %all-to-all-start.6 = ((bf16[8,208,256]{2,1,0:T(8,128)(2,1)}), bf16[8,208,256]{2,1,0:T(8,128)(2,1)S(1)}, u32[]{:S(2)}, u32[]{:S(2)}) async-start(bf16[8,208,256]{2,1,0:T(8,128)(2,1)} %pad_maximum_fusion.1), calls=%async_computation.6 | async-start | bytes 1703936 | tf_op jit(solution)/shard_map/all_to_all | solution.py:24
  (55 other events, 792.5 us)

commit v2 on v1

--- a/solution.py
+++ b/solution.py
@@ -16,6 +16,24 @@
 def core_swap(array):
     length = lax.axis_size("mp")
     return lax.ppermute(array, "mp", [(i, i ^ 1) for i in range(length)])
+
+
+def x_swap(array):
+    dp_len, mp_len = lax.axis_size("dp"), lax.axis_size("mp")
+    pairs = []
+    for d in range(dp_len):
+        for m in range(mp_len):
+            there = (d + dp_len // 2) % dp_len * mp_len + (m + mp_len // 2) % mp_len
+            pairs.append((d * mp_len + m, there))
+    return lax.ppermute(array, ("dp", "mp"), pairs)
+
+
+def y_shift(array, by):
+    length = lax.axis_size("mp")
+    half = length // 2
+    return lax.ppermute(
+        array, "mp", [(i, i // half * half + (i % half + 2 * by) % half) for i in range(length)]
+    )
 
 
 def chip_exchange(array):
@@ -100,10 +118,19 @@
     batch = pairs * lax.axis_size("dp")
     home = lax.axis_index("dp")
 
-    text_block = jnp.concatenate(
-        [text_emb, jnp.pad(labels.astype(f32)[None, :], ((0, 3), (0, width - pairs)))]
-    )
-    text_all = dp_gather(text_block)
+    near = jnp.stack([projection, x_swap(projection)])
+    below, above = y_shift(near, 1), y_shift(near, -1)
+    far_first, far_second = y_shift(above[0], -1), y_shift(below[1], 1)
+    project = jnp.concatenate([near, below, above, far_first[None], far_second[None]])
+    project = project.reshape(channels // 2, width)
+    chip = index // 2
+    x_half, y_place = chip // 4, chip % 4
+    order = [(x_half ^ dx) * 4 + (y_place + dy) % 4 for dy in (0, 3, 1, 2) for dx in (0, 1)]
+
+    def place_of(c):
+        away = (c % 4 - y_place) % 4
+        slot = jnp.where(away == 0, 0, jnp.where(away == 3, 1, jnp.where(away == 1, 2, 3)))
+        return slot * 2 + ((c // 4) ^ x_half)
 
     source = x_in.astype(f32)
     conv = (depthwise(source, dw_weight) + dw_bias).astype(bf16).reshape(rows, shard)
@@ -136,33 +163,54 @@
     )
     mixed = own_first((mixed[:images] + mixed[images:]).reshape(images, chips, 2, shard), core)
     mixed = mixed[0] + core_swap(mixed[1])
-    mixed_mean = jnp.sum(chip_exchange(jnp.swapaxes(mixed, 0, 1)), axis=0)
-
     input_mean = jnp.mean(source.reshape(images, positions, shard), axis=1)
-    pooled = input_mean + layer_scale * (mixed_mean + b_out)
+    vectors = jnp.stack([layer_scale, b_out, head_gain, head_bias])
+    got = chip_gather(
+        jnp.concatenate([mixed.reshape(images * chips, shard), input_mean, vectors])
+    )
+    mixed_mean = jnp.sum(got[:, : images * chips], axis=0).reshape(images, chips, shard)
+    vectors = got[:, images * chips :]
+    head_rows = jnp.concatenate([jnp.swapaxes(mixed_mean, 0, 1), vectors], axis=1)
+    head_rows = jnp.stack([lax.dynamic_index_in_dim(head_rows, c, 0, False) for c in order])
+    head_rows = jnp.swapaxes(head_rows, 0, 1).reshape(3 * images, channels // 2)
+    mixed_mean, input_mean = head_rows[:images], head_rows[images : 2 * images]
+    scale_half, bout_half, gain_half, hbias_half = (
+        head_rows[2 * images + i][None] for i in range(4)
+    )
+    pooled = input_mean + scale_half * (mixed_mean + bout_half)
 
     stats = jnp.concatenate([jnp.sum(pooled, axis=1), jnp.sum(pooled * pooled, axis=1)])
-    stacked = jnp.concatenate([pooled * head_gain, head_gain[None], head_bias[None]])
+    stacked = jnp.concatenate([pooled * gain_half, gain_half, hbias_half])
+    terms = stacked.shape[0]
+    high, rest = split_two(stacked)
+    middle, low = split_two(rest)
+    product = jnp.dot(
+        jnp.concatenate([high, middle, low]).astype(bf16), project, preferred_element_type=f32
+    )
     sums = jnp.concatenate(
         [
-            jnp.dot(stacked, projection.astype(f32), precision=highest),
+            product[:terms] + (product[terms : 2 * terms] + product[2 * terms :]),
             jnp.pad(stats[None, :], ((0, 1), (0, width - 2 * images))),
         ]
     )
-    sums = jnp.sum(chip_gather(sums + core_swap(sums)), axis=0)
+    sums = sums + core_swap(sums)
     head_mean = sums[images + 2, :images] / channels
     head_inverse = lax.rsqrt(
         sums[images + 2, images : 2 * images] / channels - head_mean * head_mean + eps
     )
-    head_centred = (pooled - head_mean[:, None]) * head_inverse[:, None]
     emb = (
         head_inverse[:, None] * (sums[:images] - head_mean[:, None] * sums[images])
         + sums[images + 1]
     )
-
-    emb_all = dp_gather(emb).reshape(batch, width)
-    text_raw = text_all[:, :pairs].reshape(batch, width)
-    labels_all = text_all[:, pairs, :pairs].reshape(batch)
+    head_own = jnp.concatenate([pooled, gain_half, scale_half])
+    head_both = jnp.stack([head_own, core_swap(head_own)])
+    centred_both = (head_both[:, :images] - head_mean[:, None]) * head_inverse[:, None]
+
+    tail = jnp.pad(labels.astype(f32)[:, None], ((images, 0), (0, 127)))
+    pair_all = dp_gather(jnp.concatenate([jnp.concatenate([emb, text_emb]), tail], axis=1))
+    emb_all = pair_all[:, :images, :width].reshape(batch, width)
+    text_raw = pair_all[:, images:, :width].reshape(batch, width)
+    labels_all = pair_all[:, images:, width].reshape(batch)
     image_len = jnp.sqrt(jnp.sum(emb_all * emb_all, axis=1, keepdims=True) + eps)
     image_unit = emb_all / image_len
     text_len = jnp.sqrt(jnp.sum(text_raw * text_raw, axis=1, keepdims=True) + eps)
@@ -196,25 +244,22 @@
         / own(image_len, 0)
     ).astype(bf16)
 
-    grad_head = jnp.dot(grad_image, projection.T, preferred_element_type=f32)
-    block = jnp.concatenate([grad_head * head_gain, head_centred, layer_scale[None]])
-    block_mine = chip_gather(block)
-    block_all = jnp.stack([block_mine, core_swap(block_mine)])
-    scaled_all = block_all[:, :, :images]
-    centred_all = block_all[:, :, images : 2 * images]
-    scale_all = block_all[:, :, 2 * images :]
-    mean_scaled = jnp.sum(scaled_all, axis=(0, 1, 3)) / channels
-    mean_product = jnp.sum(scaled_all * centred_all, axis=(0, 1, 3)) / channels
-
-    def to_pooled(scaled, centred):
-        return (head_inverse[:, None] / positions) * (
-            scaled - mean_scaled[:, None] - centred * mean_product[:, None]
-        )
-
-    grad_block = to_pooled(block[:images], head_centred)
-    grad_mixed = (to_pooled(scaled_all, centred_all) * scale_all).astype(bf16)
+    grad_head = lax.dot_general(
+        grad_image, project, (((1,), (1,)), ((), ())), preferred_element_type=f32
+    )
+    scaled_both = jnp.stack([grad_head, core_swap(grad_head)]) * head_both[:, images : images + 1]
+    mean_scaled = jnp.sum(scaled_both, axis=(0, 2)) / channels
+    mean_product = jnp.sum(scaled_both * centred_both, axis=(0, 2)) / channels
+    grad_blocks = (head_inverse[:, None] / positions) * (
+        scaled_both - mean_scaled[:, None] - centred_both * mean_product[:, None]
+    )
+    grad_block = grad_blocks[0, :, :shard]
+    grad_mixed = (grad_blocks * head_both[:, images + 1 :]).astype(bf16)
     grad_mixed = jnp.where(core == 0, grad_mixed, grad_mixed[::-1])
-    grad_mixed = grad_mixed.transpose(2, 1, 0, 3).reshape(images, channels)
+    grad_mixed = grad_mixed.reshape(2, images, chips, shard).transpose(2, 1, 0, 3)
+    grad_mixed = jnp.stack(
+        [lax.dynamic_index_in_dim(grad_mixed, place_of(c), 0, False) for c in range(chips)], axis=1
+    ).reshape(images, channels)
     grad_act = lax.dot_general(
         grad_mixed, w_out, (((1,), (1,)), ((), ())), preferred_element_type=f32
     )

time: 158 us -> 179 us (1.13)
  local copies, waits for them, and re-layouts: 19.4 us -> 33 us
  other arithmetic: 24.1 us -> 32.8 us
  starting transfers between devices: 49.2 us -> 41.1 us
  waiting for transfers between devices: 42.7 us -> 46.4 us
    all_to_all x5 -> x3, waiting for transfers between devices: 32.9 us -> 16 us  [chip_exchange(): return lax.all_to_all(array, 'mp', 0, 0, axis_index_groups=groups)]
    ppermute x0 -> x5, waiting for transfers between devices: none -> 16.4 us  [the longest x4 12.6 us: y_shift(): lax.ppermute(array, 'mp', [(i, i // half * half + (i % half + 2 * by) % h...]
    ppermute x0 -> x5, starting transfers between devices: none -> 9.02 us  [the longest x4 6.32 us: y_shift(): lax.ppermute(array, 'mp', [(i, i // half * half + (i % half + 2 * by) % h...]
    all_to_all x5 -> x3, starting transfers between devices: 24.2 us -> 15.7 us  [chip_exchange(): return lax.all_to_all(array, 'mp', 0, 0, axis_index_groups=groups)]
    all_to_all x2 -> x1, starting transfers between devices: 15.7 us -> 8.37 us  [dp_gather(): lax.all_to_all(jnp.broadcast_to(array, (count,) + array.shape), 'dp', 0, 0)]
    all_to_all x2 -> x1, waiting for transfers between devices: 6.99 us -> 11.9 us  [dp_gather(): lax.all_to_all(jnp.broadcast_to(array, (count,) + array.shape), 'dp', 0, 0)]
    squeeze x1 -> x2, local copies, waits for them, and re-layouts: 0.01 us -> 3.59 us  [body(): far_first, far_second = (y_shift(above[0], -1), y_shift(below[1], 1))]
    reshape x3 -> x4, local copies, waits for them, and re-layouts: 0.29 us -> 3.68 us  [the longest x1 1.74 us: body(): text_raw = pair_all[:, images:, :width].reshape(batch, width)]
  transfers between devices with their start and end apart: 12 -> 15, of which waited for: 10 -> 8; matrix products, arithmetic and copies ran while one was open for 18% -> 33% of each run, Pallas kernels for 0% -> 0%
where the time goes in v2:
time: 179 us; the launch traced here: 176 us
  waiting for transfers between devices  46.4 us (26%)
  starting transfers between devices  41.1 us (23%)
  local copies, waits for them, and re-layouts  33 us (18%)
  other arithmetic  32.8 us (18%)
  matrix products  20.1 us (11%)
  between operations  2.94 us (2%)
    all_to_all x3, waiting for transfers between devices, chip_exchange(): return lax.all_to_all(array, 'mp', 0, 0, axis_index_groups=groups)  16 us
    all_to_all x3, starting transfers between devices, chip_exchange(): return lax.all_to_all(array, 'mp', 0, 0, axis_index_groups=groups)  15.7 us
    ppermute x4, waiting for transfers between devices, y_shift(): lax.ppermute(array, 'mp', [(i, i // half * half + (i % half + 2 * by) % h...  12.6 us
    all_to_all x1, waiting for transfers between devices, dp_gather(): lax.all_to_all(jnp.broadcast_to(array, (count,) + array.shape), 'dp', 0, 0)  11.9 us
    all_to_all x1, starting transfers between devices, dp_gather(): lax.all_to_all(jnp.broadcast_to(array, (count,) + array.shape), 'dp', 0, 0)  8.37 us
    ppermute x6, starting transfers between devices, core_swap(): return lax.ppermute(array, 'mp', [(i, i ^ 1) for i in range(length)])  7.98 us
    select_n x1, other arithmetic, body(): jnp.where(core == 0, jnp.swapaxes(weight_pairs, 0, 1), jnp.swapaxes(weigh...  7.46 us
    ppermute x4, starting transfers between devices, y_shift(): lax.ppermute(array, 'mp', [(i, i // half * half + (i % half + 2 * by) % h...  6.32 us
  transfers between devices with their start and end apart: 15, of which 8 were waited for; matrix products, arithmetic and copies ran while one was open for 33% of the time, Pallas kernels for 0%

profile of v2, /device:TPU:1, one launch (start us, length us, event | category | flops | bytes accessed | tf_op | source)
XLA Modules:
  0.0 176.3 jit_solution(17280442906401421611)
XLA Ops:
  0.6 0.9 fusion.309
  1.7 1.0 fusion.307
  2.8 1.6 fusion.308
  4.6 0.9 convert_element_type.67
  5.5 2.2 %fusion.226 = bf16[4,8,8,192]{3,2,1,0:T(8,128)(2,1)S(1)} fusion(f32[4,8,8,192]{3,2,1,0:T(8,128)S(1)} %convert_element_type.67, f32[192]{0:T(256)} %param.17, f32[192]{0:T(256)S(1)} %bitcast.284, f32[192]{0:T(256)S(1)} %bitcast.286, f32[192]{0:T(256)S(1)} %bitcast.290, f32[192]{0:T(256)S(1)} %bitcast.292, f32[192]{0:T(256)S(1)} %bitcast.294, ...), kind=kLoop, calls=%fused_computation.356 | loop fusion | flops 4866048 | bytes 333312 | tf_op jit(solution)/shard_map/convert_element_type | solution.py:136
  7.8 0.9 broadcast_in_dim.16
  8.8 7.5 %all-to-all-start = ((bf16[8,192,256]{2,1,0:T(8,128)(2,1)}), bf16[8,192,256]{2,1,0:T(8,128)(2,1)}, u32[]{:S(2)}, u32[]{:S(2)}) async-start(bf16[8,192,256]{2,1,0:T(8,128)(2,1)} %broadcast_in_dim.16), calls=%async_computation | async-start | bytes 1572864 | tf_op jit(solution)/shard_map/all_to_all | solution.py:42
  16.3 2.7 %collective-permute-start.2 = (bf16[192,1024]{1,0:T(8,128)(2,1)S(1)}, bf16[192,1024]{1,0:T(8,128)(2,1)S(1)}, u32[]{:S(2)}, u32[]{:S(2)}) collective-permute-start(bf16[192,1024]{1,0:T(8,128)(2,1)S(1)} %copy-done.1), channel_id=1, source_target_pairs={{0,136},{1,137},{2,138},{3,139},{4,140},{5,141},{6,142},{7,143},{8... | collective-permute-start | bytes 1179656 | tf_op jit(solution)/shard_map/ppermute | solution.py:28
  19.0 5.0 %copy.106 = bf16[8,2,192,768]{3,2,0,1:T(8,128)(2,1)} copy(bf16[8,2,192,768]{3,2,1,0:T(8,128)(2,1)} %bitcast.240) | data formatting | bytes 9437184 | tf_op jit(solution)/shard_map/reshape | solution.py:144
  25.3 7.5 %reverse_select_fusion = bf16[8,2,192,768]{3,2,0,1:T(8,128)(2,1)} fusion(bf16[8,2,192,768]{3,2,0,1:T(8,128)(2,1)} %copy.106, pred[]{:T(512)S(6)} %eq.89), kind=kLoop, calls=%fused_computation.96 | loop fusion | flops 2359296 | bytes 9437185 | tf_op jit(solution)/shard_map/jit(_where)/select_n | solution.py:145
  32.8 3.8 %collective-permute-done.2 = bf16[192,1024]{1,0:T(8,128)(2,1)S(1)} collective-permute-done((bf16[192,1024]{1,0:T(8,128)(2,1)S(1)}, bf16[192,1024]{1,0:T(8,128)(2,1)S(1)}, u32[]{:S(2)}, u32[]{:S(2)}) %collective-permute-start.2) | collective-permute-done | bytes 393248 | tf_op jit(solution)/shard_map/ppermute | solution.py:28
  36.6 1.1 pad_maximum_fusion.3
  37.7 2.8 %collective-permute-start.4 = (bf16[2,192,1024]{2,1,0:T(8,128)(2,1)}, bf16[2,192,1024]{2,1,0:T(8,128)(2,1)}, u32[]{:S(2)}, u32[]{:S(2)}) collective-permute-start(bf16[2,192,1024]{2,1,0:T(8,128)(2,1)} %pad_maximum_fusion.3), channel_id=1, source_target_pairs={{0,6},{1,7},{2,0},{3,1},{4,2},{5,3},{6,4},{7,5},{8,14},{9,15},{10,... | collective-permute-start | bytes 2359304 | tf_op jit(solution)/shard_map/ppermute | solution.py:34
  41.9 1.1 collective-permute-start
  43.0 1.4 constant_dynamic-update-slice_fusion.10
  44.4 12.6 %collective-permute-done.4 = bf16[2,192,1024]{2,1,0:T(8,128)(2,1)} collective-permute-done((bf16[2,192,1024]{2,1,0:T(8,128)(2,1)}, bf16[2,192,1024]{2,1,0:T(8,128)(2,1)}, u32[]{:S(2)}, u32[]{:S(2)}) %collective-permute-start.4) | collective-permute-done | bytes 786464 | tf_op jit(solution)/shard_map/ppermute | solution.py:34
  57.0 1.8 %slice_bitcast_fusion.1 = bf16[192,1024]{1,0:T(8,128)(2,1)} fusion(bf16[2,192,1024]{2,1,0:T(8,128)(2,1)} %collective-permute-done.4), kind=kLoop, calls=%fused_computation.148 | loop fusion | bytes 786432 | tf_op jit(solution)/shard_map/squeeze | solution.py:123
  58.8 3.4 %collective-permute-start.5 = (bf16[192,1024]{1,0:T(8,128)(2,1)}, bf16[192,1024]{1,0:T(8,128)(2,1)}, u32[]{:S(2)}, u32[]{:S(2)}) collective-permute-start(bf16[192,1024]{1,0:T(8,128)(2,1)} %slice_bitcast_fusion.1), channel_id=1, source_target_pairs={{0,6},{1,7},{2,0},{3,1},{4,2},{5,3},{6,4},{7,5},{8,14},{9,15},{10,... | collective-permute-start | bytes 1179656 | tf_op jit(solution)/shard_map/ppermute | solution.py:34
  62.2 1.8 %slice_bitcast_fusion = bf16[192,1024]{1,0:T(8,128)(2,1)} fusion(bf16[2,192,1024]{2,1,0:T(8,128)(2,1)} %collective-permute-done.3), kind=kLoop, calls=%fused_computation.147 | loop fusion | bytes 786432 | tf_op jit(solution)/shard_map/squeeze | solution.py:123
  64.0 1.2 constant_dynamic-update-slice_fusion.9
  65.2 1.8 convert_reduce_fusion
  67.0 4.3 %bitcast_reduce_fusion = (f32[4,768]{1,0:T(4,128)S(1)}, f32[256,768]{1,0:T(8,128)}) fusion(f32[768]{0:T(1024)S(1)} %copy-done.96, bf16[8,2,192,768]{3,2,0,1:T(8,128)(2,1)S(1)} %copy-done, f32[2,8,192]{2,1,0:T(8,128)S(1)} %copy.104, f32[2,8,192]{2,1,0:T(8,128)S(1)} %copy-done.8, f32[256]{0:T(256)S(1)} %get-tuple-element.125, ...), kind=kOutput, calls=%fused_computation.136 | convolution fusion | flops 1214641152 | bytes 7119872 | tf_op jit(solution)/shard_map/dot_general | solution.py:154
  71.4 0.7 fusion.273
  72.6 2.0 %collective-permute-start.1 = (f32[4,8,192]{2,1,0:T(8,128)S(1)}, f32[4,8,192]{2,1,0:T(8,128)S(1)}, u32[]{:S(2)}, u32[]{:S(2)}) collective-permute-start(f32[4,8,192]{2,1,0:T(8,128)S(1)} %bitcast.263), channel_id=1, source_target_pairs={{0,1},{1,0},{2,3},{3,2},{4,5},{5,4},{6,7},{7,6},{8,9},{9,8},{10,11... | collective-permute-start | bytes 73736 | tf_op jit(solution)/shard_map/ppermute | solution.py:18
  74.5 1.2 constant_dynamic-update-slice_fusion.8
  75.8 0.8 broadcast_in_dim.17
  76.6 4.7 %all-to-all-start.1 = ((f32[8,40,192]{2,1,0:T(8,128)}), f32[8,40,192]{2,1,0:T(8,128)S(1)}, u32[]{:S(2)}, u32[]{:S(2)}) async-start(f32[8,40,192]{2,1,0:T(8,128)} %broadcast_in_dim.17), calls=%async_computation.1 | async-start | bytes 655360 | tf_op jit(solution)/shard_map/all_to_all | solution.py:42
  81.2 1.0 bitcast_dynamic-update-slice_fusion.1
  82.3 1.0 bitcast_dynamic-update-slice_fusion
  83.3 6.3 %all-to-all-done.1 = f32[8,40,192]{2,1,0:T(8,128)S(1)} async-done(((f32[8,40,192]{2,1,0:T(8,128)}), f32[8,40,192]{2,1,0:T(8,128)S(1)}, u32[]{:S(2)}, u32[]{:S(2)}) %all-to-all-start.1) | async-done | bytes 245792 | tf_op jit(solution)/shard_map/all_to_all | solution.py:42
  92.2 1.6 collective-permute-start.7
  95.4 0.8 broadcast_in_dim.22
  96.3 8.4 %all-to-all-start.2 = ((f32[16,8,1152]{2,1,0:T(8,128)}), f32[16,8,1152]{2,1,0:T(8,128)}, u32[]{:S(2)}, u32[]{:S(2)}) async-start(f32[16,8,1152]{2,1,0:T(8,128)} %broadcast_in_dim.22), calls=%async_computation.2 | async-start | bytes 1179648 | tf_op jit(solution)/shard_map/all_to_all | solution.py:52
  104.7 3.1 %fusion.247 = f32[4,768]{1,0:T(4,128)S(1)} fusion(bf16[3072,768]{1,0:T(8,128)(2,1)} %bitcast.234, bf16[1,3072]{1,0:T(2,128)(2,1)S(1)} %copy-done.10, bf16[1,3072]{1,0:T(2,128)(2,1)S(1)} %copy-done.9, bf16[1,3072]{1,0:T(2,128)(2,1)S(1)} %get-tuple-element.117, bf16[1,3072]{1,0:T(2,128)(2,1)S(1)} %get-tuple-element.116), kind=kOutput, calls=%fused_computation.432 | convolution fusion | flops 18972672 | bytes 4755456 | tf_op jit(solution)/shard_map/dot_general | solution.py:273
  107.9 0.7 collective-permute-start.9
  108.6 11.9 %all-to-all-done.2 = f32[16,8,1152]{2,1,0:T(8,128)} async-done(((f32[16,8,1152]{2,1,0:T(8,128)}), f32[16,8,1152]{2,1,0:T(8,128)}, u32[]{:S(2)}, u32[]{:S(2)}) %all-to-all-start.2) | async-done | bytes 589856 | tf_op jit(solution)/shard_map/all_to_all | solution.py:52
  120.4 1.5 multiply_reduce_fusion.1
  122.2 2.2 %fusion.305 = (f32[16,4,1024]{2,1,0:T(4,128)}, f32[16,4,1024]{2,1,0:T(4,128)}, f32[16,4,1024]{2,1,0:T(4,128)S(1)}, f32[16,4,1024]{2,1,0:T(4,128)}) fusion(f32[16,8,1152]{2,1,0:T(8,128)} %all-to-all-done.2, f32[16,4]{1,0:T(8,128)S(1)} %add_sqrt_fusion.1, f32[16,4]{1,0:T(8,128)S(1)} %add_sqrt_fusion), kind=kLoop, calls=%fused_computation.561 | loop fusion | flops 131072 | bytes 1573376 | tf_op jit(solution)/shard_map/slice | solution.py:211
  124.4 1.7 reshape.484
  126.1 1.7 reshape.483
  127.9 1.7 div.149
  129.6 0.8 div.152
  130.4 0.9 slice_reduce_fusion.1
  131.3 0.7 eq.90
  132.0 1.0 broadcast_divide_fusion
  133.1 1.0 broadcast_divide_fusion.1
  134.1 1.6 fusion.302
  135.8 0.8 subtract_multiply_fusion.1
  137.0 0.9 fusion.277
  137.9 2.2 %collective-permute-start.8 = (f32[4,1536]{1,0:T(4,128)S(1)}, f32[4,1536]{1,0:T(4,128)S(1)}, u32[]{:S(2)}, u32[]{:S(2)}) collective-permute-start(f32[4,1536]{1,0:T(4,128)S(1)} %fusion.277), channel_id=1, source_target_pairs={{0,1},{1,0},{2,3},{3,2},{4,5},{5,4},{6,7},{7,6},{8,9},{9,8},{10,11... | collective-permute-start | bytes 73736 | tf_op jit(solution)/shard_map/ppermute | solution.py:18
  140.1 0.8 collective-permute-done.8
  140.9 0.9 fusion.301
  141.8 0.8 multiply_convert_fusion
  143.1 3.6 %fusion.311 = f32[4,768]{1,0:T(4,128)S(1)} fusion(bf16[4,3072]{1,0:T(4,128)(2,1)S(1)} %reshape.487, bf16[768,3072]{1,0:T(8,128)(2,1)} %param.22), kind=kOutput, calls=%fused_computation.567 | convolution fusion | flops 18874368 | bytes 4755456 | tf_op jit(solution)/shard_map/dot_general | solution.py:263
  147.2 3.8 %convolution_convert_fusion = bf16[3072,256]{1,0:T(8,128)(2,1)S(1)} fusion(bf16[3072,768]{1,0:T(8,128)(2,1)} %bitcast.235, bf16[256,768]{1,0:T(8,128)(2,1)S(1)} %get-tuple-element.22), kind=kOutput, calls=%fused_computation.102 | convolution fusion | flops 1208745984 | bytes 6684672 | tf_op jit(solution)/shard_map/dot_general | solution.py:287
  152.0 0.8 dynamic_slice.90
  152.9 0.8 collective-permute-done.10
  153.7 1.2 convert_element_type.79
  155.7 1.0 pad_maximum_fusion.1
  156.7 3.5 %all-to-all-start.3 = ((bf16[8,208,256]{2,1,0:T(8,128)(2,1)}), bf16[8,208,256]{2,1,0:T(8,128)(2,1)S(1)}, u32[]{:S(2)}, u32[]{:S(2)}) async-start(bf16[8,208,256]{2,1,0:T(8,128)(2,1)} %pad_maximum_fusion.1), calls=%async_computation.3 | async-start | bytes 1703936 | tf_op jit(solution)/shard_map/all_to_all | solution.py:42
  160.3 1.2 multiply_reduce_fusion.4
  161.5 1.4 subtract_divide_fusion
  163.0 9.7 %all-to-all-done.3 = bf16[8,208,256]{2,1,0:T(8,128)(2,1)S(1)} async-done(((bf16[8,208,256]{2,1,0:T(8,128)(2,1)}), bf16[8,208,256]{2,1,0:T(8,128)(2,1)S(1)}, u32[]{:S(2)}, u32[]{:S(2)}) %all-to-all-start.3) | async-done | bytes 852000 | tf_op jit(solution)/shard_map/all_to_all | solution.py:42
  173.4 2.9 %fusion.218 = f32[4,8,8,192]{3,2,1,0:T(8,128)} fusion(f32[4,8,8,192]{3,2,1,0:T(8,128)S(1)} %bitcast.246, f32[4,192]{1,0:T(4,128)S(1)} %slice_bitcast_fusion.8, f32[192]{0:T(256)S(1)} %bitcast.285, f32[192]{0:T(256)S(1)} %bitcast.287, f32[192]{0:T(256)S(1)} %bitcast.291, f32[192]{0:T(256)S(1)} %bitcast.293, f32[192]{0:T(256)S(1)} %bitcast.295, ...), kind=kLoop, calls=%fused_computation.345 | loop fusion | flops 4816896 | bytes 433920 | tf_op jit(solution)/shard_map/add | solution.py:316
  (331 shorter events, 10.7 us)
Async XLA Ops:
  1.6 22.4 %copy-start.15 = (f32[1,1,192]{2,1,0:T(1,128)}, f32[1,1,192]{2,1,0:T(1,128)S(1)}, u32[]{:S(2)}) copy-start(f32[1,1,192]{2,1,0:T(1,128)S(1)} %get-tuple-element.84) | copy-start | bytes 2308
  1.6 22.4 %copy-start.17 = (f32[1,1,192]{2,1,0:T(1,128)}, f32[1,1,192]{2,1,0:T(1,128)S(1)}, u32[]{:S(2)}) copy-start(f32[1,1,192]{2,1,0:T(1,128)S(1)} %get-tuple-element.85) | copy-start | bytes 2308
  1.6 22.4 %copy-start.19 = (f32[1,1,192]{2,1,0:T(1,128)}, f32[1,1,192]{2,1,0:T(1,128)S(1)}, u32[]{:S(2)}) copy-start(f32[1,1,192]{2,1,0:T(1,128)S(1)} %get-tuple-element.86) | copy-start | bytes 2308
  1.6 22.4 %copy-start.21 = (f32[1,1,192]{2,1,0:T(1,128)}, f32[1,1,192]{2,1,0:T(1,128)S(1)}, u32[]{:S(2)}) copy-start(f32[1,1,192]{2,1,0:T(1,128)S(1)} %get-tuple-element.87) | copy-start | bytes 2308
  1.6 22.4 %copy-start.29 = (f32[1,1,192]{2,1,0:T(1,128)}, f32[1,1,192]{2,1,0:T(1,128)S(1)}, u32[]{:S(2)}) copy-start(f32[1,1,192]{2,1,0:T(1,128)S(1)} %get-tuple-element.91) | copy-start | bytes 2308
  2.7 21.4 %copy-start.37 = (f32[1,1,192]{2,1,0:T(1,128)}, f32[1,1,192]{2,1,0:T(1,128)S(1)}, u32[]{:S(2)}) copy-start(f32[1,1,192]{2,1,0:T(1,128)S(1)} %get-tuple-element.46) | copy-start | bytes 2308
  2.7 21.4 %copy-start.39 = (f32[1,1,192]{2,1,0:T(1,128)}, f32[1,1,192]{2,1,0:T(1,128)S(1)}, u32[]{:S(2)}) copy-start(f32[1,1,192]{2,1,0:T(1,128)S(1)} %get-tuple-element.47) | copy-start | bytes 2308
  2.7 21.4 %copy-start.41 = (f32[1,1,192]{2,1,0:T(1,128)}, f32[1,1,192]{2,1,0:T(1,128)S(1)}, u32[]{:S(2)}) copy-start(f32[1,1,192]{2,1,0:T(1,128)S(1)} %get-tuple-element.48) | copy-start | bytes 2308
  2.7 21.4 %copy-start.43 = (f32[1,1,192]{2,1,0:T(1,128)}, f32[1,1,192]{2,1,0:T(1,128)S(1)}, u32[]{:S(2)}) copy-start(f32[1,1,192]{2,1,0:T(1,128)S(1)} %get-tuple-element.49) | copy-start | bytes 2308
  2.7 21.4 %copy-start.45 = (f32[1,1,192]{2,1,0:T(1,128)}, f32[1,1,192]{2,1,0:T(1,128)S(1)}, u32[]{:S(2)}) copy-start(f32[1,1,192]{2,1,0:T(1,128)S(1)} %get-tuple-element.50) | copy-start | bytes 2308
  2.7 21.4 %copy-start.47 = (f32[1,1,192]{2,1,0:T(1,128)}, f32[1,1,192]{2,1,0:T(1,128)S(1)}, u32[]{:S(2)}) copy-start(f32[1,1,192]{2,1,0:T(1,128)S(1)} %get-tuple-element.51) | copy-start | bytes 2308
  2.7 21.4 %copy-start.49 = (f32[1,1,192]{2,1,0:T(1,128)}, f32[1,1,192]{2,1,0:T(1,128)S(1)}, u32[]{:S(2)}) copy-start(f32[1,1,192]{2,1,0:T(1,128)S(1)} %get-tuple-element.52) | copy-start | bytes 2308
  2.7 21.4 %copy-start.51 = (f32[1,1,192]{2,1,0:T(1,128)}, f32[1,1,192]{2,1,0:T(1,128)S(1)}, u32[]{:S(2)}) copy-start(f32[1,1,192]{2,1,0:T(1,128)S(1)} %get-tuple-element.53) | copy-start | bytes 2308
  2.7 21.4 %copy-start.53 = (f32[1,1,192]{2,1,0:T(1,128)}, f32[1,1,192]{2,1,0:T(1,128)S(1)}, u32[]{:S(2)}) copy-start(f32[1,1,192]{2,1,0:T(1,128)S(1)} %get-tuple-element.54) | copy-start | bytes 2308
  2.7 21.4 %copy-start.55 = (f32[1,1,192]{2,1,0:T(1,128)}, f32[1,1,192]{2,1,0:T(1,128)S(1)}, u32[]{:S(2)}) copy-start(f32[1,1,192]{2,1,0:T(1,128)S(1)} %get-tuple-element.55) | copy-start | bytes 2308
  2.8 21.4 %copy-start.57 = (f32[1,1,192]{2,1,0:T(1,128)}, f32[1,1,192]{2,1,0:T(1,128)S(1)}, u32[]{:S(2)}) copy-start(f32[1,1,192]{2,1,0:T(1,128)S(1)} %get-tuple-element.56) | copy-start | bytes 2308
  2.8 21.4 %copy-start.59 = (f32[1,1,192]{2,1,0:T(1,128)}, f32[1,1,192]{2,1,0:T(1,128)S(1)}, u32[]{:S(2)}) copy-start(f32[1,1,192]{2,1,0:T(1,128)S(1)} %get-tuple-element.57) | copy-start | bytes 2308
  2.8 21.4 %copy-start.61 = (f32[1,1,192]{2,1,0:T(1,128)}, f32[1,1,192]{2,1,0:T(1,128)S(1)}, u32[]{:S(2)}) copy-start(f32[1,1,192]{2,1,0:T(1,128)S(1)} %get-tuple-element.58) | copy-start | bytes 2308
  2.8 21.4 %copy-start.63 = (f32[1,1,192]{2,1,0:T(1,128)}, f32[1,1,192]{2,1,0:T(1,128)S(1)}, u32[]{:S(2)}) copy-start(f32[1,1,192]{2,1,0:T(1,128)S(1)} %get-tuple-element.59) | copy-start | bytes 2308
  2.8 21.4 %copy-start.65 = (f32[1,1,192]{2,1,0:T(1,128)}, f32[1,1,192]{2,1,0:T(1,128)S(1)}, u32[]{:S(2)}) copy-start(f32[1,1,192]{2,1,0:T(1,128)S(1)} %get-tuple-element.60) | copy-start | bytes 2308
  2.8 21.4 %copy-start.67 = (f32[1,1,192]{2,1,0:T(1,128)}, f32[1,1,192]{2,1,0:T(1,128)S(1)}, u32[]{:S(2)}) copy-start(f32[1,1,192]{2,1,0:T(1,128)S(1)} %get-tuple-element.61) | copy-start | bytes 2308
  2.8 21.4 %copy-start.69 = (f32[1,1,192]{2,1,0:T(1,128)}, f32[1,1,192]{2,1,0:T(1,128)S(1)}, u32[]{:S(2)}) copy-start(f32[1,1,192]{2,1,0:T(1,128)S(1)} %get-tuple-element.62) | copy-start | bytes 2308
  2.8 21.4 %copy-start.71 = (f32[1,1,192]{2,1,0:T(1,128)}, f32[1,1,192]{2,1,0:T(1,128)S(1)}, u32[]{:S(2)}) copy-start(f32[1,1,192]{2,1,0:T(1,128)S(1)} %get-tuple-element.63) | copy-start | bytes 2308
  2.8 21.4 %copy-start.73 = (f32[1,1,192]{2,1,0:T(1,128)}, f32[1,1,192]{2,1,0:T(1,128)S(1)}, u32[]{:S(2)}) copy-start(f32[1,1,192]{2,1,0:T(1,128)S(1)} %get-tuple-element.64) | copy-start | bytes 2308
  4.5 19.7 %copy-start.75 = (f32[1,1,192]{2,1,0:T(1,128)}, f32[1,1,192]{2,1,0:T(1,128)S(1)}, u32[]{:S(2)}) copy-start(f32[1,1,192]{2,1,0:T(1,128)S(1)} %get-tuple-element.65) | copy-start | bytes 2308
  4.5 19.7 %copy-start.77 = (f32[1,1,192]{2,1,0:T(1,128)}, f32[1,1,192]{2,1,0:T(1,128)S(1)}, u32[]{:S(2)}) copy-start(f32[1,1,192]{2,1,0:T(1,128)S(1)} %get-tuple-element.66) | copy-start | bytes 2308
  4.5 19.7 %copy-start.79 = (f32[1,1,192]{2,1,0:T(1,128)}, f32[1,1,192]{2,1,0:T(1,128)S(1)}, u32[]{:S(2)}) copy-start(f32[1,1,192]{2,1,0:T(1,128)S(1)} %get-tuple-element.67) | copy-start | bytes 2308
  4.5 19.7 %copy-start.81 = (f32[1,1,192]{2,1,0:T(1,128)}, f32[1,1,192]{2,1,0:T(1,128)S(1)}, u32[]{:S(2)}) copy-start(f32[1,1,192]{2,1,0:T(1,128)S(1)} %get-tuple-element.68) | copy-start | bytes 2308
  4.5 19.7 %copy-start.83 = (f32[1,1,192]{2,1,0:T(1,128)}, f32[1,1,192]{2,1,0:T(1,128)S(1)}, u32[]{:S(2)}) copy-start(f32[1,1,192]{2,1,0:T(1,128)S(1)} %get-tuple-element.69) | copy-start | bytes 2308
  4.5 19.7 %copy-start.85 = (f32[1,1,192]{2,1,0:T(1,128)}, f32[1,1,192]{2,1,0:T(1,128)S(1)}, u32[]{:S(2)}) copy-start(f32[1,1,192]{2,1,0:T(1,128)S(1)} %get-tuple-element.70) | copy-start | bytes 2308
  4.5 19.7 %copy-start.87 = (f32[1,1,192]{2,1,0:T(1,128)}, f32[1,1,192]{2,1,0:T(1,128)S(1)}, u32[]{:S(2)}) copy-start(f32[1,1,192]{2,1,0:T(1,128)S(1)} %get-tuple-element.71) | copy-start | bytes 2308
  4.6 19.7 %copy-start.89 = (f32[1,1,192]{2,1,0:T(1,128)}, f32[1,1,192]{2,1,0:T(1,128)S(1)}, u32[]{:S(2)}) copy-start(f32[1,1,192]{2,1,0:T(1,128)S(1)} %get-tuple-element.72) | copy-start | bytes 2308
  8.8 33.1 %all-to-all-start = ((bf16[8,192,256]{2,1,0:T(8,128)(2,1)}), bf16[8,192,256]{2,1,0:T(8,128)(2,1)}, u32[]{:S(2)}, u32[]{:S(2)}) async-start(bf16[8,192,256]{2,1,0:T(8,128)(2,1)} %broadcast_in_dim.16), calls=%async_computation | async-start | bytes 1572864 | tf_op jit(solution)/shard_map/all_to_all | solution.py:42
  16.3 20.3 %collective-permute-start.2 = (bf16[192,1024]{1,0:T(8,128)(2,1)S(1)}, bf16[192,1024]{1,0:T(8,128)(2,1)S(1)}, u32[]{:S(2)}, u32[]{:S(2)}) collective-permute-start(bf16[192,1024]{1,0:T(8,128)(2,1)S(1)} %copy-done.1), channel_id=1, source_target_pairs={{0,136},{1,137},{2,138},{3,139},{4,140},{5,141},{6,142},{7,143},{8... | collective-permute-start | bytes 1179656 | tf_op jit(solution)/shard_map/ppermute | solution.py:28
  37.7 19.3 %collective-permute-start.4 = (bf16[2,192,1024]{2,1,0:T(8,128)(2,1)}, bf16[2,192,1024]{2,1,0:T(8,128)(2,1)}, u32[]{:S(2)}, u32[]{:S(2)}) collective-permute-start(bf16[2,192,1024]{2,1,0:T(8,128)(2,1)} %pad_maximum_fusion.3), channel_id=1, source_target_pairs={{0,6},{1,7},{2,0},{3,1},{4,2},{5,3},{6,4},{7,5},{8,14},{9,15},{10,... | collective-permute-start | bytes 2359304 | tf_op jit(solution)/shard_map/ppermute | solution.py:34
  40.5 21.7 %collective-permute-start.3 = (bf16[2,192,1024]{2,1,0:T(8,128)(2,1)}, bf16[2,192,1024]{2,1,0:T(8,128)(2,1)}, u32[]{:S(2)}, u32[]{:S(2)}) collective-permute-start(bf16[2,192,1024]{2,1,0:T(8,128)(2,1)} %pad_maximum_fusion.3), channel_id=1, source_target_pairs={{0,2},{1,3},{2,4},{3,5},{4,6},{5,7},{6,0},{7,1},{8,10},{9,11},{10,... | collective-permute-start | bytes 2359304 | tf_op jit(solution)/shard_map/ppermute | solution.py:34
  41.9 25.1 %copy-start.8 = (f32[2,8,192]{2,1,0:T(8,128)S(1)}, f32[2,8,192]{2,1,0:T(8,128)}, u32[]{:S(2)}) copy-start(f32[2,8,192]{2,1,0:T(8,128)} %copy.103) | copy-start | bytes 36868
  41.9 25.1 %copy-start.96 = (f32[768]{0:T(1024)S(1)}, f32[768]{0:T(1024)}, u32[]{:S(2)}) copy-start(f32[768]{0:T(1024)} %param.21) | copy-start | bytes 9220
  41.9 25.1 %copy-start = (bf16[8,2,192,768]{3,2,0,1:T(8,128)(2,1)S(1)}, bf16[8,2,192,768]{3,2,0,1:T(8,128)(2,1)}, u32[]{:S(2)}) copy-start(bf16[8,2,192,768]{3,2,0,1:T(8,128)(2,1)} %reverse_select_fusion) | copy-start | bytes 14155780
  41.9 23.3 %collective-permute-start = (bf16[8,192,256]{2,1,0:T(8,128)(2,1)}, bf16[8,192,256]{2,1,0:T(8,128)(2,1)S(1)}, u32[]{:S(2)}, u32[]{:S(2)}) collective-permute-start(bf16[8,192,256]{2,1,0:T(8,128)(2,1)} %all-to-all-done), channel_id=1, source_target_pairs={{0,1},{1,0},{2,3},{3,2},{4,5},{5,4},{6,7},{7,6},{8,9},{9,8},{10,11... | collective-permute-start | bytes 2359304 | tf_op jit(solution)/shard_map/ppermute | solution.py:18
  58.8 22.4 %collective-permute-start.5 = (bf16[192,1024]{1,0:T(8,128)(2,1)}, bf16[192,1024]{1,0:T(8,128)(2,1)}, u32[]{:S(2)}, u32[]{:S(2)}) collective-permute-start(bf16[192,1024]{1,0:T(8,128)(2,1)} %slice_bitcast_fusion.1), channel_id=1, source_target_pairs={{0,6},{1,7},{2,0},{3,1},{4,2},{5,3},{6,4},{7,5},{8,14},{9,15},{10,... | collective-permute-start | bytes 1179656 | tf_op jit(solution)/shard_map/ppermute | solution.py:34
  64.0 18.3 %collective-permute-start.6 = (bf16[192,1024]{1,0:T(8,128)(2,1)}, bf16[192,1024]{1,0:T(8,128)(2,1)}, u32[]{:S(2)}, u32[]{:S(2)}) collective-permute-start(bf16[192,1024]{1,0:T(8,128)(2,1)} %slice_bitcast_fusion), channel_id=1, source_target_pairs={{0,2},{1,3},{2,4},{3,5},{4,6},{5,7},{6,0},{7,1},{8,10},{9,11},{10,... | collective-permute-start | bytes 1179656 | tf_op jit(solution)/shard_map/ppermute | solution.py:34
  72.6 3.1 %collective-permute-start.1 = (f32[4,8,192]{2,1,0:T(8,128)S(1)}, f32[4,8,192]{2,1,0:T(8,128)S(1)}, u32[]{:S(2)}, u32[]{:S(2)}) collective-permute-start(f32[4,8,192]{2,1,0:T(8,128)S(1)} %bitcast.263), channel_id=1, source_target_pairs={{0,1},{1,0},{2,3},{3,2},{4,5},{5,4},{6,7},{7,6},{8,9},{9,8},{10,11... | collective-permute-start | bytes 73736 | tf_op jit(solution)/shard_map/ppermute | solution.py:18
  76.6 13.1 %all-to-all-start.1 = ((f32[8,40,192]{2,1,0:T(8,128)}), f32[8,40,192]{2,1,0:T(8,128)S(1)}, u32[]{:S(2)}, u32[]{:S(2)}) async-start(f32[8,40,192]{2,1,0:T(8,128)} %broadcast_in_dim.17), calls=%async_computation.1 | async-start | bytes 655360 | tf_op jit(solution)/shard_map/all_to_all | solution.py:42
  92.2 2.5 %collective-permute-start.7 = (f32[8,1024]{1,0:T(8,128)S(1)}, f32[8,1024]{1,0:T(8,128)S(1)}, u32[]{:S(2)}, u32[]{:S(2)}) collective-permute-start(f32[8,1024]{1,0:T(8,128)S(1)} %select_maximum_fusion.1), channel_id=1, source_target_pairs={{0,1},{1,0},{2,3},{3,2},{4,5},{5,4},{6,7},{7,6},{8,9},{9,8},{10,11... | collective-permute-start | bytes 98312 | tf_op jit(solution)/shard_map/ppermute | solution.py:18
  96.3 24.2 %all-to-all-start.2 = ((f32[16,8,1152]{2,1,0:T(8,128)}), f32[16,8,1152]{2,1,0:T(8,128)}, u32[]{:S(2)}, u32[]{:S(2)}) async-start(f32[16,8,1152]{2,1,0:T(8,128)} %broadcast_in_dim.22), calls=%async_computation.2 | async-start | bytes 1179648 | tf_op jit(solution)/shard_map/all_to_all | solution.py:52
  107.9 32.2 %collective-permute-start.9 = (f32[6,1536]{1,0:T(8,128)}, f32[6,1536]{1,0:T(8,128)S(1)}, u32[]{:S(2)}, u32[]{:S(2)}) collective-permute-start(f32[6,1536]{1,0:T(8,128)} %get-tuple-element.120), channel_id=1, source_target_pairs={{0,1},{1,0},{2,3},{3,2},{4,5},{5,4},{6,7},{7,6},{8,9},{9,8},{10,11... | collective-permute-start | bytes 110600 | tf_op jit(solution)/shard_map/ppermute | solution.py:18
  137.9 3.0 %collective-permute-start.8 = (f32[4,1536]{1,0:T(4,128)S(1)}, f32[4,1536]{1,0:T(4,128)S(1)}, u32[]{:S(2)}, u32[]{:S(2)}) collective-permute-start(f32[4,1536]{1,0:T(4,128)S(1)} %fusion.277), channel_id=1, source_target_pairs={{0,1},{1,0},{2,3},{3,2},{4,5},{5,4},{6,7},{7,6},{8,9},{9,8},{10,11... | collective-permute-start | bytes 73736 | tf_op jit(solution)/shard_map/ppermute | solution.py:18
  151.2 2.5 %collective-permute-start.10 = (bf16[1552,256]{1,0:T(8,128)(2,1)S(1)}, bf16[1552,256]{1,0:T(8,128)(2,1)}, u32[]{:S(2)}, u32[]{:S(2)}) collective-permute-start(bf16[1552,256]{1,0:T(8,128)(2,1)S(1)} %pad_maximum_fusion.2), channel_id=1, source_target_pairs={{0,1},{1,0},{2,3},{3,2},{4,5},{5,4},{6,7},{7,6},{8,9},{9,8},{10,11... | collective-permute-start | bytes 2383880 | tf_op jit(solution)/shard_map/ppermute | solution.py:18
  155.3 17.8 %copy-start.16 = (f32[1,1,192]{2,1,0:T(1,128)S(1)}, f32[1,1,192]{2,1,0:T(1,128)}, u32[]{:S(2)}) copy-start(f32[1,1,192]{2,1,0:T(1,128)} %copy-done.15) | copy-start | bytes 2308
  155.3 17.8 %copy-start.18 = (f32[1,1,192]{2,1,0:T(1,128)S(1)}, f32[1,1,192]{2,1,0:T(1,128)}, u32[]{:S(2)}) copy-start(f32[1,1,192]{2,1,0:T(1,128)} %copy-done.17) | copy-start | bytes 2308
  155.3 17.8 %copy-start.20 = (f32[1,1,192]{2,1,0:T(1,128)S(1)}, f32[1,1,192]{2,1,0:T(1,128)}, u32[]{:S(2)}) copy-start(f32[1,1,192]{2,1,0:T(1,128)} %copy-done.19) | copy-start | bytes 2308
  155.3 17.8 %copy-start.22 = (f32[1,1,192]{2,1,0:T(1,128)S(1)}, f32[1,1,192]{2,1,0:T(1,128)}, u32[]{:S(2)}) copy-start(f32[1,1,192]{2,1,0:T(1,128)} %copy-done.21) | copy-start | bytes 2308
  155.3 17.8 %copy-start.24 = (f32[1,1,192]{2,1,0:T(1,128)S(1)}, f32[1,1,192]{2,1,0:T(1,128)}, u32[]{:S(2)}) copy-start(f32[1,1,192]{2,1,0:T(1,128)} %copy-done.23) | copy-start | bytes 2308
  155.3 17.8 %copy-start.26 = (f32[1,1,192]{2,1,0:T(1,128)S(1)}, f32[1,1,192]{2,1,0:T(1,128)}, u32[]{:S(2)}) copy-start(f32[1,1,192]{2,1,0:T(1,128)} %copy-done.25) | copy-start | bytes 2308
  155.3 17.8 %copy-start.28 = (f32[1,1,192]{2,1,0:T(1,128)S(1)}, f32[1,1,192]{2,1,0:T(1,128)}, u32[]{:S(2)}) copy-start(f32[1,1,192]{2,1,0:T(1,128)} %copy-done.27) | copy-start | bytes 2308
  155.3 17.8 %copy-start.30 = (f32[1,1,192]{2,1,0:T(1,128)S(1)}, f32[1,1,192]{2,1,0:T(1,128)}, u32[]{:S(2)}) copy-start(f32[1,1,192]{2,1,0:T(1,128)} %copy-done.29) | copy-start | bytes 2308
  155.3 17.8 %copy-start.32 = (f32[1,1,192]{2,1,0:T(1,128)S(1)}, f32[1,1,192]{2,1,0:T(1,128)}, u32[]{:S(2)}) copy-start(f32[1,1,192]{2,1,0:T(1,128)} %copy-done.31) | copy-start | bytes 2308
  155.3 17.8 %copy-start.34 = (f32[1,1,192]{2,1,0:T(1,128)S(1)}, f32[1,1,192]{2,1,0:T(1,128)}, u32[]{:S(2)}) copy-start(f32[1,1,192]{2,1,0:T(1,128)} %copy-done.33) | copy-start | bytes 2308
  155.4 17.8 %copy-start.36 = (f32[1,1,192]{2,1,0:T(1,128)S(1)}, f32[1,1,192]{2,1,0:T(1,128)}, u32[]{:S(2)}) copy-start(f32[1,1,192]{2,1,0:T(1,128)} %copy-done.35) | copy-start | bytes 2308
  155.4 17.8 %copy-start.38 = (f32[1,1,192]{2,1,0:T(1,128)S(1)}, f32[1,1,192]{2,1,0:T(1,128)}, u32[]{:S(2)}) copy-start(f32[1,1,192]{2,1,0:T(1,128)} %copy-done.37) | copy-start | bytes 2308
  155.4 17.8 %copy-start.40 = (f32[1,1,192]{2,1,0:T(1,128)S(1)}, f32[1,1,192]{2,1,0:T(1,128)}, u32[]{:S(2)}) copy-start(f32[1,1,192]{2,1,0:T(1,128)} %copy-done.39) | copy-start | bytes 2308
  155.4 17.8 %copy-start.42 = (f32[1,1,192]{2,1,0:T(1,128)S(1)}, f32[1,1,192]{2,1,0:T(1,128)}, u32[]{:S(2)}) copy-start(f32[1,1,192]{2,1,0:T(1,128)} %copy-done.41) | copy-start | bytes 2308
  156.7 16.0 %all-to-all-start.3 = ((bf16[8,208,256]{2,1,0:T(8,128)(2,1)}), bf16[8,208,256]{2,1,0:T(8,128)(2,1)S(1)}, u32[]{:S(2)}, u32[]{:S(2)}) async-start(bf16[8,208,256]{2,1,0:T(8,128)(2,1)} %pad_maximum_fusion.1), calls=%async_computation.3 | async-start | bytes 1703936 | tf_op jit(solution)/shard_map/all_to_all | solution.py:42
  (56 other events, 731.2 us)

commit v3 on v0

v3 whole, which is shorter than its diff:
```python
import functools
import jax
import jax.numpy as jnp
from jax import lax
from jax.experimental import pallas as pl
from jax.experimental.pallas import tpu as pltpu
from jax.sharding import PartitionSpec as P

eps = 1e-06
logit_scale = 20.0
loss_scale = 512.0
root_half = 0.7071067811865476
inv_root_two_pi = 0.3989422804014327
f32 = jnp.float32
bf16 = jnp.bfloat16
highest = lax.Precision.HIGHEST
MIB = 1 << 20
CHIPS = 8
HALVES = 2
BLOCKS = 16


def core_swap(array):
    return lax.ppermute(array, "mp", [(i, i ^ 1) for i in range(BLOCKS)])


def x_swap(array):
    return lax.ppermute(array, "mp", [(i, i ^ CHIPS) for i in range(BLOCKS)])


def chip_exchange(array):
    groups = [[i for i in range(core, BLOCKS, 2)] for core in range(2)]
    return lax.all_to_all(array, "mp", 0, 0, axis_index_groups=groups)


def half_gather(array):
    groups = [[half * CHIPS + i for i in range(CHIPS)] for half in range(HALVES)]
    return lax.all_gather(array, "mp", axis_index_groups=groups, tiled=True)


def run(kernel, outs, *operands, scratch=(), limit=24, flops=0):
    specs = [
        pl.BlockSpec(memory_space=pltpu.SMEM if a.dtype == jnp.int32 else pltpu.VMEM)
        for a in operands
    ]
    size = sum(a.size * a.dtype.itemsize for a in operands)
    return pl.pallas_call(
        kernel,
        out_shape=outs,
        in_specs=specs,
        out_specs=[pl.BlockSpec(memory_space=pltpu.VMEM) for _ in outs],
        scratch_shapes=list(scratch),
        compiler_params=pltpu.CompilerParams(vmem_limit_bytes=limit * MIB),
        cost_estimate=pl.CostEstimate(flops=flops, bytes_accessed=size, transcendentals=0),
    )(*operands)


def shape(*dims, dtype=f32):
    return jax.ShapeDtypeStruct(dims, dtype)


def iota(dims, axis):
    return lax.broadcasted_iota(jnp.int32, dims, axis)


def to_terms(array):
    high = array.astype(bf16).astype(f32)
    return high, array - high


def taps(x, w_ref, flip):
    side, _, shard = x.shape
    size = w_ref.shape[0]
    reach = size // 2
    column = iota((side, side, shard), 1)
    acc = [jnp.zeros((side, shard), f32) for _ in range(side)]
    for b in range(size):
        by = b - reach
        if by:
            moved = jnp.where(
                (column + by >= 0) & (column + by < side), pltpu.roll(x, (-by) % side, 1), 0.0
            )
        else:
            moved = x
        for a in range(size):
            wa, wb = (size - 1 - a, size - 1 - b) if flip else (a, b)
            weight = w_ref[wa, wb : wb + 1, :]
            for p in range(side):
                if 0 <= p + a - reach < side:
                    acc[p] = acc[p] + moved[p + a - reach] * weight
    return acc


def conv_kernel(x_ref, w_ref, b_ref, copies_ref, conv_ref, mean_ref, rows_ref):
    images, side = x_ref.shape[:2]
    positions = side * side

    def image(n, carry):
        x = x_ref[n].astype(f32)
        total = jnp.sum(jnp.sum(x, axis=0), axis=0, keepdims=True)
        mean_ref[pl.ds(n, 1), :] = total / positions
        for p, row in enumerate(taps(x, w_ref, False)):
            rows_ref[pl.ds(pl.multiple_of(n * positions + p * side, side), side), :] = row
        return carry

    lax.fori_loop(0, images, image, 0)
    turned = (rows_ref[...] + b_ref[...]).T.astype(bf16)
    conv_ref[...] = turned
    for j in range(CHIPS):
        copies_ref[j] = turned


def forward_kernel(
    place_ref,
    mine_ref,
    other_ref,
    own_ref,
    vec_ref,
    w_ref,
    b_ref,
    wout_ref,
    slope_ref,
    hidden_ref,
    through_ref,
    stat_ref,
    mixed_ref,
    turned_ref,
    normed_ref,
):
    shard, rows = mine_ref.shape[1:]
    channels, hidden = w_ref.shape
    images = mixed_ref.shape[1]
    positions = rows // images
    core = place_ref[0]
    first = jnp.zeros((1, rows), f32)
    second = jnp.zeros((1, rows), f32)
    for ref in (mine_ref, other_ref):
        for j in range(CHIPS):
            value = ref[j].astype(f32)
            first = first + jnp.sum(value, axis=0, keepdims=True)
            second = second + jnp.sum(value * value, axis=0, keepdims=True)
    average = first / channels
    inverse = lax.rsqrt(second / channels - average * average + eps)
    stat_ref[0:1, :] = average
    stat_ref[1:2, :] = inverse
    own = own_ref[...].T
    for h, ref in enumerate((mine_ref, other_ref)):
        for j in range(CHIPS):
            k = h * CHIPS + j
            value = (ref[j].astype(f32) - average) * inverse
            value = value * own[:, k : k + 1] + own[:, BLOCKS + k : BLOCKS + k + 1]
            start = (2 * j + (core if h == 0 else 1 - core)) * shard
            turned_ref[pl.ds(pl.multiple_of(start, 64), shard), :] = value.astype(bf16)
    step = 256
    for c in range(channels // step):
        normed_ref[0:rows, c * step : (c + 1) * step] = turned_ref[c * step : (c + 1) * step, :].T
    normed_ref[rows : rows + 16, :] = vec_ref[...].astype(bf16)
    total = [None] * images
    for t in range(hidden // step):
        at = slice(t * step, (t + 1) * step)
        product = jnp.dot(normed_ref[...], w_ref[:, at], preferred_element_type=f32)
        through_ref[:, at] = product[rows:]
        pre = product[:rows] + b_ref[:, at]
        hidden_ref[:, at] = pre
        gate = 0.5 + 0.5 * lax.erf(pre * root_half)
        slope_ref[:, at] = gate + pre * jnp.exp(-0.5 * pre * pre) * inv_root_two_pi
        active = pre * gate
        sums = [
            jnp.sum(active[n * positions : (n + 1) * positions], axis=0, keepdims=True) / positions
            for n in range(images)
        ]
        sums = jnp.concatenate(sums + [jnp.zeros((8 - images, step), f32)], axis=0)
        high, low = to_terms(sums)
        part = jnp.dot(
            jnp.concatenate([high, low], axis=0).astype(bf16),
            wout_ref[at, :],
            preferred_element_type=f32,
        )
        part = part[:8] + part[8:]
        mixed = part if t == 0 else mixed + part
    for k in range(BLOCKS):
        mixed_ref[k] = mixed[:images, k * shard : (k + 1) * shard]


def payload_kernel(place_ref, mine_ref, other_ref, out_ref):
    core = place_ref[0]
    for half in range(HALVES):
        for b in range(CHIPS):
            value = mine_ref[half * CHIPS + b] + other_ref[half * CHIPS + b]
            for j in range(4):
                out_ref[half * 4 + j, b] = value
    for i in range(2):
        for j in range(CHIPS):
            out_ref[j, CHIPS + 2 * core + i] = mine_ref[BLOCKS + i]
            out_ref[j, CHIPS + 2 * (1 - core) + i] = other_ref[BLOCKS + i]


def head_kernel(place_ref, got_ref, project_ref, out_ref, head_ref):
    images, shard = got_ref.shape[2:]
    width = project_ref.shape[1]
    half = place_ref[1]
    product = jnp.zeros((24, width), f32)
    first = jnp.zeros((8, 1), f32)
    second = jnp.zeros((8, 1), f32)
    row = iota((8, shard), 0)
    for k in range(CHIPS):
        source = half * 4 + k // 2
        mixed = got_ref[0, k]
        for j in range(1, CHIPS):
            mixed = mixed + got_ref[j, k]
        vectors = got_ref[source, CHIPS + 2 * (k % 2) + 1]
        pooled = got_ref[source, CHIPS + 2 * (k % 2)] + vectors[0:1] * (mixed + vectors[1:2])
        head_ref[k, 0:images, :] = pooled
        head_ref[k, images:, :] = vectors
        value = head_ref[k]
        first = first + jnp.sum(value, axis=1, keepdims=True)
        second = second + jnp.sum(value * value, axis=1, keepdims=True)
        value = jnp.where(row < images, value * vectors[2:3], value)
        high, rest = to_terms(value)
        middle, low = to_terms(rest)
        product = product + jnp.dot(
            jnp.concatenate([high, middle, low], axis=0).astype(bf16),
            project_ref[k * shard : (k + 1) * shard, :],
            preferred_element_type=f32,
        )
    out_ref[:, :width] = product[:8] + (product[8:16] + product[16:])
    lane = iota((8, 128), 1)
    out_ref[:, width:] = jnp.where(lane == 0, first, jnp.where(lane == 1, second, 0.0))


def embed_kernel(channels, mine_ref, other_ref, text_ref, tail_ref, out_ref, stat_ref):
    width = text_ref.shape[1]
    sums = mine_ref[...] + other_ref[...]
    mean = sums[:, width : width + 1] / channels
    inverse = lax.rsqrt(sums[:, width + 1 : width + 2] / channels - mean * mean + eps)
    emb = inverse * (sums[:, :width] - mean * sums[6:7, :width]) + sums[7:8, :width]
    both = jnp.where(iota((8, width), 0) < 4, emb, text_ref[...])
    for d in range(out_ref.shape[0]):
        out_ref[d, :, :width] = both
        out_ref[d, :, width:] = tail_ref[...]
    stat_ref[0] = jnp.broadcast_to(mean, (8, 128))
    stat_ref[1] = jnp.broadcast_to(inverse, (8, 128))


def loss_kernel(place_ref, got_ref, project_ref, text_ref, back_ref, unit_ref, len_ref, both_ref):
    width = project_ref.shape[1]
    count = got_ref.shape[0] * 8
    shard = back_ref.shape[2]
    home = pl.ds(pl.multiple_of(place_ref[3] * 8, 8), 8)
    raw = got_ref[:, :, :width].reshape(count, width)
    length = jnp.sqrt(jnp.sum(raw * raw, axis=1, keepdims=True) + eps)
    unit = raw / length
    unit_ref[...] = unit
    len_ref[...] = jnp.broadcast_to(length, (count, 128))
    logits = logit_scale * lax.dot_general(
        unit, unit, (((1,), (1,)), ((), ())), precision=highest, preferred_element_type=f32
    )
    column = iota((count, count), 1)
    valid = (iota((count, count), 0) % 8 < 4) & (column % 8 >= 4)
    weights = jnp.where(valid, jnp.exp(jnp.where(valid, logits, 0.0)), 0.0)
    row_total = jnp.sum(weights, axis=1, keepdims=True)
    col_total = jnp.sum(weights, axis=0, keepdims=True)
    target = got_ref[:, :, width:].reshape(count, 128)[:, 0:1]
    matched = jnp.where(target == column.astype(f32), 1.0, 0.0)
    grads = loss_scale * (0.5 * (weights / row_total + weights / col_total) - matched)
    grads = jnp.where(valid, grads, 0.0)
    both_ref[...] = grads + grads.T
    grad_unit = logit_scale * jnp.dot(
        both_ref[home, :], unit, precision=highest, preferred_element_type=f32
    )
    own = unit_ref[home, :]
    grad = (grad_unit - own * jnp.sum(own * grad_unit, axis=1, keepdims=True)) / len_ref[home, 0:1]
    text_ref[...] = grad[4:]
    back = lax.dot_general(
        grad.astype(bf16),
        project_ref[...],
        (((1,), (1,)), ((), ())),
        preferred_element_type=f32,
    )
    for k in range(CHIPS):
        back_ref[k] = back[:4, k * shard : (k + 1) * shard]


def backward_kernel(
    place_ref,
    gh_mine_ref,
    gh_other_ref,
    head_mine_ref,
    head_other_ref,
    head_stat_ref,
    wout_ref,
    slope_ref,
    hidden_ref,
    w_ref,
    through_ref,
    b_ref,
    other_ref,
    turned_ref,
    sums_ref,
    block_ref,
    mixed_ref,
    pre_ref,
):
    images, shard = gh_mine_ref.shape[1:]
    rows, hidden = slope_ref.shape
    channels = w_ref.shape[0]
    positions = rows // images
    core, half, spot = place_ref[0], place_ref[1], place_ref[2]
    mean = head_stat_ref[0][:images, 0:1]
    inverse = head_stat_ref[1][:images, 0:1]
    first = jnp.zeros((images, 1), f32)
    second = jnp.zeros((images, 1), f32)

    def parts(gh_ref, head_ref, k):
        head = head_ref[k]
        return gh_ref[k] * head[6:7], (head[:images] - mean) * inverse, head[4:5]

    for refs in ((gh_mine_ref, head_mine_ref), (gh_other_ref, head_other_ref)):
        for k in range(CHIPS):
            scaled, centred, _ = parts(*refs, k)
            first = first + jnp.sum(scaled, axis=1, keepdims=True)
            second = second + jnp.sum(scaled * centred, axis=1, keepdims=True)
    first = first / channels
    second = second / channels

    def block(gh_ref, head_ref, k):
        scaled, centred, scale = parts(gh_ref, head_ref, k)
        grad = (inverse / positions) * (scaled - first - centred * second)
        return grad, grad * scale

    block_ref[...] = block(gh_mine_ref, head_mine_ref, spot)[0]
    mixed_ref[...] = jnp.zeros_like(mixed_ref)
    for k in range(CHIPS):
        mine = block(gh_mine_ref, head_mine_ref, k)[1]
        other = block(gh_other_ref, head_other_ref, k)[1]
        low, high = jnp.where(half == 0, mine, other), jnp.where(half == 0, other, mine)
        mixed_ref[0:images, k * shard : (k + 1) * shard] = low
        mixed_ref[0:images, (CHIPS + k) * shard : (CHIPS + k + 1) * shard] = high
    act = lax.dot_general(
        mixed_ref[...].astype(bf16),
        wout_ref[...],
        (((1,), (1,)), ((), ())),
        preferred_element_type=f32,
    )
    step = 256
    one = jnp.zeros((rows, 1), f32)
    two = jnp.zeros((rows, 1), f32)
    for t in range(hidden // step):
        at = slice(t * step, (t + 1) * step)
        for n in range(images):
            span = slice(n * positions, (n + 1) * positions)
            pre_ref[span, :] = (act[n : n + 1, at] * slope_ref[span, at]).astype(bf16).astype(f32)
        value = pre_ref[...]
        gain = through_ref[0:1, at] + through_ref[1:2, at]
        bias = through_ref[2:3, at] + through_ref[3:4, at] + b_ref[:, at]
        one = one + jnp.sum(value * gain, axis=1, keepdims=True)
        two = two + jnp.sum(value * (hidden_ref[:, at] - bias), axis=1, keepdims=True)
        turned_ref[at, :] = value.T.astype(bf16)
    lane = iota((rows, 128), 1)
    sums = jnp.where(lane == 0, one, jnp.where(lane == 1, two, 0.0)).T[:8]
    sums_ref[...] = sums
    high, low = to_terms(sums)
    other_ref[channels // 2 :, :] = jnp.concatenate([high, low], axis=0).astype(bf16)
    for j in range(CHIPS):
        start = pl.multiple_of((2 * j + 1 - core) * shard, 64)
        other_ref[j * shard : (j + 1) * shard, :] = jnp.dot(
            w_ref[pl.ds(start, shard), :], turned_ref[...], preferred_element_type=f32
        ).astype(bf16)


def mine_kernel(place_ref, w_ref, turned_ref, mine_ref):
    shard = w_ref.shape[0] // BLOCKS
    for j in range(CHIPS):
        start = pl.multiple_of((2 * j + place_ref[0]) * shard, 64)
        mine_ref[j * shard : (j + 1) * shard, :] = jnp.dot(
            w_ref[pl.ds(start, shard), :], turned_ref[...], preferred_element_type=f32
        ).astype(bf16)


def pair_kernel(mine_ref, got_ref, sums_ref, out_ref):
    half = mine_ref.shape[0]
    shard = half // CHIPS
    for j in range(CHIPS):
        span = slice(j * shard, (j + 1) * shard)
        out_ref[j, :shard, :] = (mine_ref[span, :].astype(f32) + got_ref[span, :].astype(f32)).astype(
            bf16
        )
    tail = got_ref[half:, :].astype(f32)
    high, low = to_terms(sums_ref[...] + (tail[:8] + tail[8:]))
    tail = jnp.concatenate([high, low], axis=0).astype(bf16)
    for j in range(CHIPS):
        out_ref[j, shard:, :] = tail


def final_kernel(
    channels, got_ref, conv_ref, stat_ref, gain_ref, w_ref, block_ref, out_ref, rows_ref
):
    shard = conv_ref.shape[0]
    images, side = out_ref.shape[:2]
    positions = side * side
    total = got_ref[0].astype(f32)
    for j in range(1, CHIPS):
        total = total + got_ref[j].astype(f32)
    first = (total[shard : shard + 1] + total[shard + 8 : shard + 9]) / channels
    second = (total[shard + 1 : shard + 2] + total[shard + 9 : shard + 10]) / channels
    average, inverse = stat_ref[0:1, :], stat_ref[1:2, :]
    centred = (conv_ref[...].astype(f32) - average) * inverse
    grad = inverse * (total[:shard] * gain_ref[...].T[:, 0:1] - first - centred * second)
    rows_ref[...] = grad.T

    def image(n, carry):
        span = pl.ds(pl.multiple_of(n * positions, positions), positions)
        x = rows_ref[span, :].reshape(side, side, shard)
        base = block_ref[pl.ds(n, 1), :]
        for p, row in enumerate(taps(x, w_ref, True)):
            out_ref[n, p] = row + base
        return carry

    lax.fori_loop(0, images, image, 0)


def body(
    x_in,
    dw_weight,
    dw_bias,
    ln_gain,
    ln_bias,
    w_in,
    b_in,
    w_out,
    b_out,
    layer_scale,
    head_gain,
    head_bias,
    projection,
    text_emb,
    labels,
):
    images, side, _, shard = x_in.shape
    channels, hidden = w_in.shape
    rows = images * side * side
    pairs, width = text_emb.shape
    shards = lax.axis_size("dp")
    index = lax.axis_index("mp")
    core = index % 2
    place = jnp.stack(
        [core, index // CHIPS, index % CHIPS, lax.axis_index("dp")]
    ).astype(jnp.int32)
    project = half_gather(projection)

    def own_first(vector):
        pair = vector.reshape(CHIPS, 2, shard)
        mine = jnp.where(core == 0, pair[:, 0], pair[:, 1])
        other = jnp.where(core == 0, pair[:, 1], pair[:, 0])
        return jnp.concatenate([mine, other])

    own = jnp.concatenate([own_first(ln_gain), own_first(ln_bias)])
    terms = []
    for vector in (ln_gain, ln_bias):
        high = lax.reduce_precision(vector, 8, 7)
        terms += [high, vector - high]
    vec = jnp.pad(jnp.stack(terms), ((0, 12), (0, 0)))
    gain_local = lax.dynamic_slice_in_dim(ln_gain, index * shard, shard, 0)
    gain_local = jnp.broadcast_to(gain_local[None, :], (8, shard))
    b_row = b_in[None, :]
    target = (labels // pairs) * 8 + 4 + labels % pairs
    tail = jnp.pad(target.astype(f32)[:, None], ((0, 8 - pairs), (0, 127)))
    text_low = jnp.pad(text_emb, ((8 - pairs, 0), (0, 0)))

    copies, conv, input_mean = run(
        conv_kernel,
        [
            shape(CHIPS, shard, rows, dtype=bf16),
            shape(shard, rows, dtype=bf16),
            shape(images, shard),
        ],
        x_in,
        dw_weight,
        dw_bias[None, :],
        scratch=[pltpu.VMEM((rows, shard), f32)],
        flops=2 * 49 * rows * shard,
    )
    conv_mine = chip_exchange(copies)
    conv_other = core_swap(conv_mine)
    slope, hidden_pre, through, row_stat, mixed = run(
        forward_kernel,
        [
            shape(rows, hidden),
            shape(rows, hidden),
            shape(16, hidden),
            shape(8, rows),
            shape(BLOCKS, images, shard),
        ],
        place,
        conv_mine,
        conv_other,
        own,
        vec,
        w_in,
        b_row,
        w_out,
        scratch=[pltpu.VMEM((channels, rows), bf16), pltpu.VMEM((rows + 16, channels), bf16)],
        limit=32,
        flops=2 * rows * channels * hidden,
    )
    vectors = jnp.stack([layer_scale, b_out, head_gain, head_bias])
    partial = jnp.concatenate([mixed, input_mean[None], vectors[None]])
    (payload,) = run(
        payload_kernel,
        [shape(CHIPS, CHIPS + 4, images, shard)],
        place,
        partial,
        core_swap(partial),
    )
    sums, head = run(
        head_kernel,
        [shape(8, width + 128), shape(CHIPS, 8, shard)],
        place,
        chip_exchange(payload),
        project,
    )
    pair_block, head_stat = run(
        functools.partial(embed_kernel, channels),
        [shape(shards, 8, width + 128), shape(2, 8, 128)],
        sums,
        x_swap(sums),
        text_low,
        tail,
    )
    head_other = x_swap(head)
    grad_text, back = run(
        loss_kernel,
        [shape(pairs, width), shape(CHIPS, images, shard)],
        place,
        lax.all_to_all(pair_block, "dp", 0, 0),
        project,
        scratch=[
            pltpu.VMEM((shards * 8, width), f32),
            pltpu.VMEM((shards * 8, 128), f32),
            pltpu.VMEM((shards * 8, shards * 8), f32),
        ],
    )
    other, turned, row_sums, grad_block = run(
        backward_kernel,
        [
            shape(channels // 2 + 16, rows, dtype=bf16),
            shape(hidden, rows, dtype=bf16),
            shape(8, rows),
            shape(images, shard),
        ],
        place,
        back,
        x_swap(back),
        head,
        head_other,
        head_stat,
        w_out,
        slope,
        hidden_pre,
        w_in,
        through,
        b_row,
        scratch=[pltpu.VMEM((8, channels), f32), pltpu.VMEM((rows, 256), f32)],
        limit=32,
        flops=rows * channels * hidden,
    )
    passed = core_swap(other)
    (mine,) = run(
        mine_kernel,
        [shape(channels // 2, rows, dtype=bf16)],
        place,
        w_in,
        turned,
        flops=rows * channels * hidden,
    )
    (blocks,) = run(
        pair_kernel, [shape(CHIPS, shard + 16, rows, dtype=bf16)], mine, passed, row_sums
    )
    (grad_input,) = run(
        functools.partial(final_kernel, channels),
        [shape(images, side, side, shard)],
        chip_exchange(blocks),
        conv,
        row_stat,
        gain_local,
        dw_weight,
        grad_block,
        scratch=[pltpu.VMEM((rows, shard), f32)],
        flops=2 * 49 * rows * shard,
    )
    return (grad_input, grad_text)


def solution(mesh):
    return jax.shard_map(
        body,
        mesh=mesh,
        in_specs=(
            P("dp", None, None, "mp"),
            P(None, None, "mp"),
            P("mp"),
            P(),
            P(),
            P(None, "mp"),
            P("mp"),
            P("mp", None),
            P("mp"),
            P("mp"),
            P("mp"),
            P("mp"),
            P("mp", None),
            P("dp", None),
            P("dp"),
        ),
        out_specs=(P("dp", None, None, "mp"), P("dp", None)),
        check_vma=False,
    )
```

time: 689 us -> 155 us (0.22)
  waiting for transfers between devices: 332 us -> 41 us
  blocking collectives: 269 us -> 15.2 us
  matrix products: 33 us -> 0 us
  Pallas kernels: 0 us -> 23.8 us
  local copies, waits for them, and re-layouts: 6.15 us -> 23.9 us
  starting transfers between devices: 21.4 us -> 31.6 us
  other arithmetic: 11 us -> 3 us
    psum x5 -> x0, blocking collectives: 249 us -> none  [the longest x1 83.4 us: body(): lax.psum((jnp.sum(head_scaled, axis=1), jnp.sum(head_scaled * head_centre...]
    reduce_scatter x2 -> x0, waiting for transfers between devices: 142 us -> none  [the longest x1 73 us: body(): lax.psum_scatter(jnp.dot(activation, w_out, preferred_element_type=jnp.fl...]
    ppermute x80 -> x6, waiting for transfers between devices: 137 us -> 7.93 us  [the longest x3 5.99 us: x_swap(): return lax.ppermute(array, 'mp', [(i, i ^ CHIPS) for i in range(BLOCKS)])]
    all_gather x1, waiting for transfers between devices: 53.4 us -> 0.01 us  [half_gather(): return lax.all_gather(array, 'mp', axis_index_groups=groups, tiled=True)]
    dot_general x70 -> x0, matrix products: 33 us -> none  [the longest x32 7.35 us: block_logits(): return logit_scale * jnp.dot(image_unit, other_unit.T, precision=highest)]
    all_to_all x0 -> x3, waiting for transfers between devices: none -> 32.4 us  [the longest x2 19.9 us: chip_exchange(): return lax.all_to_all(array, 'mp', 0, 0, axis_index_groups=groups)]
    pallas_call x0 -> x10, Pallas kernels: none -> 23.8 us  [run(): pl.pallas_call(kernel, out_shape=outs, in_specs=specs, out_specs=[pl.Bloc...]
    all_to_all x0 -> x3, starting transfers between devices: none -> 20.2 us  [the longest x2 11 us: chip_exchange(): return lax.all_to_all(array, 'mp', 0, 0, axis_index_groups=groups)]
  transfers between devices with their start and end apart: 83 -> 10, of which waited for: 51 -> 8; matrix products, arithmetic and copies ran while one was open for 2% -> 5% of each run, Pallas kernels for 0% -> 9%
where the time goes in v3:
time: 155 us; the launch traced here: 153 us
  waiting for transfers between devices  41 us (26%)
  starting transfers between devices  31.6 us (20%)
  local copies, waits for them, and re-layouts  23.9 us (15%)
  Pallas kernels  23.8 us (15%)
  blocking collectives  15.2 us (10%)
  between operations  14.2 us (9%)
  other arithmetic  3 us (2%)
    pallas_call x10, Pallas kernels, run(): pl.pallas_call(kernel, out_shape=outs, in_specs=specs, out_specs=[pl.Bloc...  23.8 us
    unnamed x42, local copies, waits for them, and re-layouts  20 us
    all_to_all x2, waiting for transfers between devices, chip_exchange(): return lax.all_to_all(array, 'mp', 0, 0, axis_index_groups=groups)  19.9 us
    all_to_all x1, blocking collectives, chip_exchange(): return lax.all_to_all(array, 'mp', 0, 0, axis_index_groups=groups)  15.2 us
    all_to_all x1, waiting for transfers between devices, body(): lax.all_to_all(pair_block, 'dp', 0, 0)  12.4 us
    all_to_all x2, starting transfers between devices, chip_exchange(): return lax.all_to_all(array, 'mp', 0, 0, axis_index_groups=groups)  11 us
    all_to_all x1, starting transfers between devices, body(): lax.all_to_all(pair_block, 'dp', 0, 0)  9.16 us
    ppermute x3, starting transfers between devices, core_swap(): return lax.ppermute(array, 'mp', [(i, i ^ 1) for i in range(BLOCKS)])  9.09 us
  transfers between devices with their start and end apart: 10, of which 8 were waited for; matrix products, arithmetic and copies ran while one was open for 5% of the time, Pallas kernels for 9%

profile of v3, /device:TPU:1, one launch (start us, length us, event | category | flops | bytes accessed | tf_op | source)
XLA Modules:
  0.0 152.8 jit_solution(7801212501263791785)
XLA Ops:
  7.2 0.0 all-gather.2.cloned.1.call-start
  7.2 0.7 all-gather.2.cloned.1.call-update
  7.9 0.0 copy-start.11
  7.9 0.8 copy-done.11
  8.7 0.9 copy-done.13
  9.6 0.7 copy-done.20
  10.3 1.8 %shard_map.158 = (bf16[8,192,256]{2,1,0:T(8,128)(2,1)}, bf16[192,256]{1,0:T(8,128)(2,1)S(1)}, f32[4,192]{1,0:T(4,128)S(1)}) custom-call(bf16[4,8,8,192]{3,2,1,0:T(8,128)(2,1)S(1)} %copy-done.13, f32[7,7,192]{2,1,0:T(8,128)S(1)} %copy-done.11, f32[1,192]{1,0:T(1,128)S(1)} %bitcast.27), custom_call_target="tpu_custom_call" | custom-call | flops 4816896 | bytes 136704 | tf_op jit(solution)/shard_map/pallas_call | solution.py:47
  12.1 0.6 copy-done.14
  12.8 7.5 %all-to-all-start = ((bf16[8,192,256]{2,1,0:T(8,128)(2,1)}), bf16[8,192,256]{2,1,0:T(8,128)(2,1)S(1)}, u32[]{:S(2)}, u32[]{:S(2)}) async-start(bf16[8,192,256]{2,1,0:T(8,128)(2,1)} %get-tuple-element.20), calls=%async_computation | async-start | bytes 1572864 | tf_op jit(solution)/shard_map/all_to_all | solution.py:33
  20.3 0.8 reshape.19
  21.1 0.1 pad_add_fusion.place_ref
  21.2 0.8 reshape.20
  22.0 0.7 broadcast_in_dim.22.b_ref
  22.7 0.7 maximum_bitcast_fusion
  23.5 8.2 %all-to-all-done.mine_ref = bf16[8,192,256]{2,1,0:T(8,128)(2,1)S(1)} async-done(((bf16[8,192,256]{2,1,0:T(8,128)(2,1)}), bf16[8,192,256]{2,1,0:T(8,128)(2,1)S(1)}, u32[]{:S(2)}, u32[]{:S(2)}) %all-to-all-start) | async-done | bytes 786464 | tf_op jit(solution)/shard_map/all_to_all | solution.py:33
  31.6 3.0 %collective-permute-start = (bf16[8,192,256]{2,1,0:T(8,128)(2,1)S(1)}, bf16[8,192,256]{2,1,0:T(8,128)(2,1)S(1)}, u32[]{:S(2)}, u32[]{:S(2)}) collective-permute-start(bf16[8,192,256]{2,1,0:T(8,128)(2,1)S(1)} %all-to-all-done.mine_ref), channel_id=1, source_target_pairs={{0,1},{1,0},{2,3},{3,2},{4,5},{5,4},{6,7},{7,6},{8,9},{9,8},{10,11... | collective-permute-start | bytes 2359304 | tf_op jit(solution)/shard_map/ppermute | solution.py:24
  34.7 0.7 fusion.3
  35.4 0.7 fusion.4
  36.1 0.1 select_maximum_fusion.vec_ref
  36.1 0.4 collective-permute-done.other_ref
  36.6 2.4 %copy-done = bf16[3072,768]{1,0:T(8,128)(2,1)S(1)} copy-done((bf16[3072,768]{1,0:T(8,128)(2,1)S(1)}, bf16[3072,768]{1,0:T(8,128)(2,1)}, u32[]{:S(2)}) %copy-start) | copy-done | bytes 4718616
  39.0 2.4 %copy-done.2 = bf16[768,3072]{1,0:T(8,128)(2,1)S(1)} copy-done((bf16[768,3072]{1,0:T(8,128)(2,1)S(1)}, bf16[768,3072]{1,0:T(8,128)(2,1)}, u32[]{:S(2)}) %copy-start.2) | copy-done | bytes 4718616
  41.4 6.1 %shard_map.159 = (f32[256,768]{1,0:T(8,128)S(1)}, f32[256,768]{1,0:T(8,128)S(1)}, f32[16,768]{1,0:T(8,128)S(1)}, f32[8,256]{1,0:T(8,128)S(1)}, f32[16,4,192]{2,1,0:T(4,128)S(1)}) custom-call(s32[4]{0:T(128)S(1)} %pad_add_fusion.place_ref, bf16[8,192,256]{2,1,0:T(8,128)(2,1)S(1)} %all-to-all-done.mine_ref, ...), custom_call_target="tpu_custom_call" | custom-call | flops 1207959552 | bytes 11234320 | tf_op jit(solution)/shard_map/pallas_call | solution.py:47
  47.5 0.9 copy-done.6
  48.4 0.9 copy-done.8
  49.3 0.5 collective-permute-start.1
  49.8 0.9 collective-permute-done.1.other_ref
  50.7 0.6 shard_map.160
  51.3 0.0 copy-done.18
  51.3 15.2 %all_to_all.20.got_ref = f32[8,12,4,192]{3,2,1,0:T(4,128)S(1)} all-to-all(f32[8,12,4,192]{3,2,1,0:T(4,128)S(1)} %shard_map.160), channel_id=1, replica_groups={{0,2,4,6,8,10,12,14},{1,3,5,7,9,11,13,15},{16,18,20,22,24,26,28,30},{17..., dimensions={0} | all-to-all | bytes 589824 | tf_op jit(solution)/shard_map/all_to_all | solution.py:33
  66.5 1.9 %copy-done.4 = bf16[1536,1024]{1,0:T(8,128)(2,1)S(1)} copy-done((bf16[1536,1024]{1,0:T(8,128)(2,1)S(1)}, bf16[1536,1024]{1,0:T(8,128)(2,1)}, u32[]{:S(2)}) %copy-start.4) | copy-done | bytes 3145752
  68.4 1.9 %shard_map.161 = (f32[8,1152]{1,0:T(8,128)}, f32[8,8,192]{2,1,0:T(8,128)S(1)}) custom-call(s32[4]{0:T(128)S(1)} %pad_add_fusion.place_ref, f32[8,12,4,192]{3,2,1,0:T(4,128)S(1)} %all_to_all.20.got_ref, bf16[1536,1024]{1,0:T(8,128)(2,1)S(1)} %copy-done.4), custom_call_target="tpu_custom_call" | custom-call | bytes 3440656 | tf_op jit(solution)/shard_map/pallas_call | solution.py:47
  70.3 0.6 copy-done.16
  70.9 0.3 collective-permute-start.2
  71.2 0.7 convert_bitcast_fusion
  71.9 0.1 copy.22
  72.0 0.7 pad.13.text_ref
  72.7 2.7 %collective-permute-done.2.other_ref = f32[8,1152]{1,0:T(8,128)S(1)} collective-permute-done((f32[8,1152]{1,0:T(8,128)}, f32[8,1152]{1,0:T(8,128)S(1)}, u32[]{:S(2)}, u32[]{:S(2)}) %collective-permute-start.2) | collective-permute-done | bytes 36896 | tf_op jit(solution)/shard_map/ppermute | solution.py:28
  75.4 0.9 shard_map.162
  76.4 0.0 copy-start.10
  76.4 0.8 copy-done.10
  77.2 9.2 %all-to-all-start.2 = ((f32[16,8,1152]{2,1,0:T(8,128)}), f32[16,8,1152]{2,1,0:T(8,128)}, u32[]{:S(2)}, u32[]{:S(2)}) async-start(f32[16,8,1152]{2,1,0:T(8,128)} %copy-done.10), calls=%async_computation.2 | async-start | bytes 1179648 | tf_op jit(solution)/shard_map/all_to_all | solution.py:535
  86.4 1.0 collective-permute-start.4
  87.4 12.4 %all-to-all-done.2.got_ref = f32[16,8,1152]{2,1,0:T(8,128)} async-done(((f32[16,8,1152]{2,1,0:T(8,128)}), f32[16,8,1152]{2,1,0:T(8,128)}, u32[]{:S(2)}, u32[]{:S(2)}) %all-to-all-start.2) | async-done | bytes 589856 | tf_op jit(solution)/shard_map/all_to_all | solution.py:535
  99.8 0.0 copy-done.5
  99.9 4.4 %shard_map.163 = (f32[4,1024]{1,0:T(4,128)}, f32[8,4,192]{2,1,0:T(4,128)S(1)}) custom-call(s32[4]{0:T(128)S(1)} %pad_add_fusion.place_ref, f32[16,8,1152]{2,1,0:T(8,128)} %all-to-all-done.2.got_ref, bf16[1536,1024]{1,0:T(8,128)(2,1)S(1)} %copy-done.5), custom_call_target="tpu_custom_call" | custom-call | bytes 3735568 | tf_op jit(solution)/shard_map/pallas_call | solution.py:47
  104.2 1.0 collective-permute-start.3
  105.2 0.0 collective-permute-done.4.head_other_ref
  105.2 3.3 %collective-permute-done.3.gh_other_ref = f32[8,4,192]{2,1,0:T(4,128)S(1)} collective-permute-done((f32[8,4,192]{2,1,0:T(4,128)S(1)}, f32[8,4,192]{2,1,0:T(4,128)S(1)}, u32[]{:S(2)}, u32[]{:S(2)}) %collective-permute-start.3) | collective-permute-done | bytes 24608 | tf_op jit(solution)/shard_map/ppermute | solution.py:28
  108.5 0.0 copy-done.19
  108.5 0.0 copy-done.17
  108.5 2.3 %copy-done.1 = bf16[3072,768]{1,0:T(8,128)(2,1)S(1)} copy-done((bf16[3072,768]{1,0:T(8,128)(2,1)S(1)}, bf16[3072,768]{1,0:T(8,128)(2,1)}, u32[]{:S(2)}) %copy-start.1) | copy-done | bytes 4718616
  110.9 2.3 %copy-done.3 = bf16[768,3072]{1,0:T(8,128)(2,1)S(1)} copy-done((bf16[768,3072]{1,0:T(8,128)(2,1)S(1)}, bf16[768,3072]{1,0:T(8,128)(2,1)}, u32[]{:S(2)}) %copy-start.3) | copy-done | bytes 4718616
  113.2 1.1 copy-done.7
  114.3 1.1 copy-done.9
  115.5 3.8 %shard_map.164 = (bf16[1552,256]{1,0:T(8,128)(2,1)S(1)}, bf16[768,256]{1,0:T(8,128)(2,1)S(1)}, f32[8,256]{1,0:T(8,128)S(1)}, f32[4,192]{1,0:T(4,128)S(1)}) custom-call(s32[4]{0:T(128)S(1)} %pad_add_fusion.place_ref, f32[8,4,192]{2,1,0:T(4,128)S(1)} %get-tuple-element.25.gh_mine_ref, f32[8,4,192]{2,1,0:T(4,128)S(1)} %collective-permute-done.3.gh_other_ref, ...), custom_call_target="tpu_custom_call" | custom-call | flops 603979776 | bytes 11217936 | tf_op jit(solution)/shard_map/pallas_call | solution.py:47
  119.2 5.6 %collective-permute-start.5 = (bf16[1552,256]{1,0:T(8,128)(2,1)S(1)}, bf16[1552,256]{1,0:T(8,128)(2,1)S(1)}, u32[]{:S(2)}, u32[]{:S(2)}) collective-permute-start(bf16[1552,256]{1,0:T(8,128)(2,1)S(1)} %get-tuple-element.32), channel_id=1, source_target_pairs={{0,1},{1,0},{2,3},{3,2},{4,5},{5,4},{6,7},{7,6},{8,9},{9,8},{10,11... | collective-permute-start | bytes 2383880 | tf_op jit(solution)/shard_map/ppermute | solution.py:24
  124.8 1.3 shard_map.165.mine_ref
  126.1 0.6 collective-permute-done.5.got_ref
  126.7 1.1 shard_map.166
  127.8 3.5 %all-to-all-start.3 = ((bf16[8,208,256]{2,1,0:T(8,128)(2,1)}), bf16[8,208,256]{2,1,0:T(8,128)(2,1)S(1)}, u32[]{:S(2)}, u32[]{:S(2)}) async-start(bf16[8,208,256]{2,1,0:T(8,128)(2,1)} %shard_map.166), calls=%async_computation.3 | async-start | bytes 1703936 | tf_op jit(solution)/shard_map/all_to_all | solution.py:33
  131.4 0.8 dynamic_slice.3
  132.2 11.8 %all-to-all-done.3.got_ref = bf16[8,208,256]{2,1,0:T(8,128)(2,1)S(1)} async-done(((bf16[8,208,256]{2,1,0:T(8,128)(2,1)}), bf16[8,208,256]{2,1,0:T(8,128)(2,1)S(1)}, u32[]{:S(2)}, u32[]{:S(2)}) %all-to-all-start.3) | async-done | bytes 852000 | tf_op jit(solution)/shard_map/all_to_all | solution.py:33
  143.9 2.0 %shard_map.167 = f32[4,8,8,192]{3,2,1,0:T(8,128)} custom-call(bf16[8,208,256]{2,1,0:T(8,128)(2,1)S(1)} %all-to-all-done.3.got_ref, bf16[192,256]{1,0:T(8,128)(2,1)S(1)} %copy-done.15, f32[8,256]{1,0:T(8,128)S(1)} %get-tuple-element.35.stat_ref, f32[8,192]{1,0:T(8,128)S(1)} %broadcast_in_dim.26.gain_ref, f32[7,7,192]{2,1,0:T(8,128)S(1)} %copy-done.12, ...), custom_call_target="tpu_custom_call" | custom-call | flops 4816896 | bytes 1005312 | tf_op jit(solution)/shard_map/pallas_call | solution.py:47
  (29 shorter events, 0.1 us)
Async XLA Ops:
  7.2 59.4 %all-gather.2.cloned.1.call-start = ((), (), s32[]{:S(2)}) async-start(), calls=%async_computation.4 | async-start | bytes 3538944 | tf_op jit(solution)/shard_map/all_gather | solution.py:38
  7.9 0.8 copy-start.11
  8.7 0.9 copy-start.13
  9.6 0.7 copy-start.20
  12.1 0.6 copy-start.14
  12.8 18.9 %all-to-all-start = ((bf16[8,192,256]{2,1,0:T(8,128)(2,1)}), bf16[8,192,256]{2,1,0:T(8,128)(2,1)S(1)}, u32[]{:S(2)}, u32[]{:S(2)}) async-start(bf16[8,192,256]{2,1,0:T(8,128)(2,1)} %get-tuple-element.20), calls=%async_computation | async-start | bytes 1572864 | tf_op jit(solution)/shard_map/all_to_all | solution.py:33
  31.6 4.9 %collective-permute-start = (bf16[8,192,256]{2,1,0:T(8,128)(2,1)S(1)}, bf16[8,192,256]{2,1,0:T(8,128)(2,1)S(1)}, u32[]{:S(2)}, u32[]{:S(2)}) collective-permute-start(bf16[8,192,256]{2,1,0:T(8,128)(2,1)S(1)} %all-to-all-done.mine_ref), channel_id=1, source_target_pairs={{0,1},{1,0},{2,3},{3,2},{4,5},{5,4},{6,7},{7,6},{8,9},{9,8},{10,11... | collective-permute-start | bytes 2359304 | tf_op jit(solution)/shard_map/ppermute | solution.py:24
  36.6 2.4 %copy-start = (bf16[3072,768]{1,0:T(8,128)(2,1)S(1)}, bf16[3072,768]{1,0:T(8,128)(2,1)}, u32[]{:S(2)}) copy-start(bf16[3072,768]{1,0:T(8,128)(2,1)} %w_ref.8) | copy-start | bytes 14155780
  39.0 2.4 %copy-start.2 = (bf16[768,3072]{1,0:T(8,128)(2,1)S(1)}, bf16[768,3072]{1,0:T(8,128)(2,1)}, u32[]{:S(2)}) copy-start(bf16[768,3072]{1,0:T(8,128)(2,1)} %wout_ref.3) | copy-start | bytes 14155780
  47.5 0.9 copy-start.6
  48.4 0.9 copy-start.8
  49.3 2.0 %copy-start.18 = (f32[16,768]{1,0:T(8,128)}, f32[16,768]{1,0:T(8,128)S(1)}, u32[]{:S(2)}) copy-start(f32[16,768]{1,0:T(8,128)S(1)} %get-tuple-element.30.through_ref) | copy-start | bytes 147460
  49.3 1.4 collective-permute-start.1
  66.5 1.9 %copy-start.4 = (bf16[1536,1024]{1,0:T(8,128)(2,1)S(1)}, bf16[1536,1024]{1,0:T(8,128)(2,1)}, u32[]{:S(2)}) copy-start(bf16[1536,1024]{1,0:T(8,128)(2,1)} %all-gather.2.cloned.1.call-done.project_ref) | copy-start | bytes 9437188
  68.4 31.4 %copy-start.5 = (bf16[1536,1024]{1,0:T(8,128)(2,1)S(1)}, bf16[1536,1024]{1,0:T(8,128)(2,1)}, u32[]{:S(2)}) copy-start(bf16[1536,1024]{1,0:T(8,128)(2,1)} %all-gather.2.cloned.1.call-done.project_ref) | copy-start | bytes 9437188
  70.3 0.6 copy-start.16
  70.9 37.6 %copy-start.19 = (f32[16,768]{1,0:T(8,128)S(1)}, f32[16,768]{1,0:T(8,128)}, u32[]{:S(2)}) copy-start(f32[16,768]{1,0:T(8,128)} %copy-done.18) | copy-start | bytes 147460
  70.9 37.6 %copy-start.17 = (f32[8,8,192]{2,1,0:T(8,128)S(1)}, f32[8,8,192]{2,1,0:T(8,128)}, u32[]{:S(2)}) copy-start(f32[8,8,192]{2,1,0:T(8,128)} %copy-done.16) | copy-start | bytes 147460
  70.9 4.5 %collective-permute-start.2 = (f32[8,1152]{1,0:T(8,128)}, f32[8,1152]{1,0:T(8,128)S(1)}, u32[]{:S(2)}, u32[]{:S(2)}) collective-permute-start(f32[8,1152]{1,0:T(8,128)} %get-tuple-element.23.mine_ref), channel_id=1, source_target_pairs={{0,8},{1,9},{2,10},{3,11},{4,12},{5,13},{6,14},{7,15},{8,0},{9,1},... | collective-permute-start | bytes 110600 | tf_op jit(solution)/shard_map/ppermute | solution.py:28
  76.4 0.8 copy-start.10
  77.2 22.6 %all-to-all-start.2 = ((f32[16,8,1152]{2,1,0:T(8,128)}), f32[16,8,1152]{2,1,0:T(8,128)}, u32[]{:S(2)}, u32[]{:S(2)}) async-start(f32[16,8,1152]{2,1,0:T(8,128)} %copy-done.10), calls=%async_computation.2 | async-start | bytes 1179648 | tf_op jit(solution)/shard_map/all_to_all | solution.py:535
  86.4 18.8 %collective-permute-start.4 = (f32[8,8,192]{2,1,0:T(8,128)}, f32[8,8,192]{2,1,0:T(8,128)S(1)}, u32[]{:S(2)}, u32[]{:S(2)}) collective-permute-start(f32[8,8,192]{2,1,0:T(8,128)} %copy-done.16), channel_id=1, source_target_pairs={{0,8},{1,9},{2,10},{3,11},{4,12},{5,13},{6,14},{7,15},{8,0},{9,1},... | collective-permute-start | bytes 147464 | tf_op jit(solution)/shard_map/ppermute | solution.py:28
  104.2 4.3 %collective-permute-start.3 = (f32[8,4,192]{2,1,0:T(4,128)S(1)}, f32[8,4,192]{2,1,0:T(4,128)S(1)}, u32[]{:S(2)}, u32[]{:S(2)}) collective-permute-start(f32[8,4,192]{2,1,0:T(4,128)S(1)} %get-tuple-element.25.gh_mine_ref), channel_id=1, source_target_pairs={{0,8},{1,9},{2,10},{3,11},{4,12},{5,13},{6,14},{7,15},{8,0},{9,1},... | collective-permute-start | bytes 73736 | tf_op jit(solution)/shard_map/ppermute | solution.py:28
  108.5 2.3 %copy-start.1 = (bf16[3072,768]{1,0:T(8,128)(2,1)S(1)}, bf16[3072,768]{1,0:T(8,128)(2,1)}, u32[]{:S(2)}) copy-start(bf16[3072,768]{1,0:T(8,128)(2,1)} %w_ref.8) | copy-start | bytes 14155780
  110.9 2.3 %copy-start.3 = (bf16[768,3072]{1,0:T(8,128)(2,1)S(1)}, bf16[768,3072]{1,0:T(8,128)(2,1)}, u32[]{:S(2)}) copy-start(bf16[768,3072]{1,0:T(8,128)(2,1)} %wout_ref.3) | copy-start | bytes 14155780
  113.2 1.1 copy-start.7
  114.3 1.1 copy-start.9
  119.2 7.5 %collective-permute-start.5 = (bf16[1552,256]{1,0:T(8,128)(2,1)S(1)}, bf16[1552,256]{1,0:T(8,128)(2,1)S(1)}, u32[]{:S(2)}, u32[]{:S(2)}) collective-permute-start(bf16[1552,256]{1,0:T(8,128)(2,1)S(1)} %get-tuple-element.32), channel_id=1, source_target_pairs={{0,1},{1,0},{2,3},{3,2},{4,5},{5,4},{6,7},{7,6},{8,9},{9,8},{10,11... | collective-permute-start | bytes 2383880 | tf_op jit(solution)/shard_map/ppermute | solution.py:24
  124.8 19.1 %copy-start.12 = (f32[7,7,192]{2,1,0:T(8,128)S(1)}, f32[7,7,192]{2,1,0:T(8,128)}, u32[]{:S(2)}) copy-start(f32[7,7,192]{2,1,0:T(8,128)} %w_ref.9) | copy-start | bytes 112900
  124.8 19.1 %copy-start.15 = (bf16[192,256]{1,0:T(8,128)(2,1)S(1)}, bf16[192,256]{1,0:T(8,128)(2,1)}, u32[]{:S(2)}) copy-start(bf16[192,256]{1,0:T(8,128)(2,1)} %copy-done.14) | copy-start | bytes 294916
  127.8 16.1 %all-to-all-start.3 = ((bf16[8,208,256]{2,1,0:T(8,128)(2,1)}), bf16[8,208,256]{2,1,0:T(8,128)(2,1)S(1)}, u32[]{:S(2)}, u32[]{:S(2)}) async-start(bf16[8,208,256]{2,1,0:T(8,128)(2,1)} %shard_map.166), calls=%async_computation.3 | async-start | bytes 1703936 | tf_op jit(solution)/shard_map/all_to_all | solution.py:33
Sparse Core Ops, SparseCore 0:
  9.8 37.4 all-gather.1

commit v4 on v3

--- a/solution.py
+++ b/solution.py
@@ -1,4 +1,3 @@
-import functools
 import jax
 import jax.numpy as jnp
 from jax import lax
@@ -16,16 +15,12 @@
 highest = lax.Precision.HIGHEST
 MIB = 1 << 20
 CHIPS = 8
-HALVES = 2
 BLOCKS = 16
+SHARD = 192
 
 
 def core_swap(array):
     return lax.ppermute(array, "mp", [(i, i ^ 1) for i in range(BLOCKS)])
-
-
-def x_swap(array):
-    return lax.ppermute(array, "mp", [(i, i ^ CHIPS) for i in range(BLOCKS)])
 
 
 def chip_exchange(array):
@@ -33,9 +28,8 @@
     return lax.all_to_all(array, "mp", 0, 0, axis_index_groups=groups)
 
 
-def half_gather(array):
-    groups = [[half * CHIPS + i for i in range(CHIPS)] for half in range(HALVES)]
-    return lax.all_gather(array, "mp", axis_index_groups=groups, tiled=True)
+def shard_exchange(array):
+    return lax.all_to_all(array, "mp", 0, 0)
 
 
 def run(kernel, outs, *operands, scratch=(), limit=24, flops=0):
@@ -111,11 +105,10 @@
 
 
 def forward_kernel(
-    place_ref,
     mine_ref,
     other_ref,
-    own_ref,
-    vec_ref,
+    gain_ref,
+    bias_ref,
     w_ref,
     b_ref,
     wout_ref,
@@ -126,12 +119,23 @@
     mixed_ref,
     turned_ref,
     normed_ref,
+    own_ref,
+    vec_ref,
 ):
     shard, rows = mine_ref.shape[1:]
     channels, hidden = w_ref.shape
     images = mixed_ref.shape[1]
     positions = rows // images
-    core = place_ref[0]
+    core = lax.axis_index("mp") % 2
+    vec_ref[...] = jnp.zeros_like(vec_ref)
+    for i, ref in enumerate((gain_ref, bias_ref)):
+        vec_ref[i : i + 1, :] = ref[...]
+        for j in range(CHIPS):
+            low = ref[:, 2 * j * shard : (2 * j + 1) * shard]
+            high = ref[:, (2 * j + 1) * shard : (2 * j + 2) * shard]
+            at = i * BLOCKS + j
+            own_ref[at : at + 1, :] = jnp.where(core == 0, low, high)
+            own_ref[at + CHIPS : at + CHIPS + 1, :] = jnp.where(core == 0, high, low)
     first = jnp.zeros((1, rows), f32)
     second = jnp.zeros((1, rows), f32)
     for ref in (mine_ref, other_ref):
@@ -154,13 +158,13 @@
     step = 256
     for c in range(channels // step):
         normed_ref[0:rows, c * step : (c + 1) * step] = turned_ref[c * step : (c + 1) * step, :].T
-    normed_ref[rows : rows + 16, :] = vec_ref[...].astype(bf16)
-    total = [None] * images
+    normed_ref[rows : rows + 16, :] = jnp.concatenate(to_terms(vec_ref[...]), axis=0).astype(bf16)
+    b_row = b_ref[...][None, :]
     for t in range(hidden // step):
         at = slice(t * step, (t + 1) * step)
         product = jnp.dot(normed_ref[...], w_ref[:, at], preferred_element_type=f32)
         through_ref[:, at] = product[rows:]
-        pre = product[:rows] + b_ref[:, at]
+        pre = product[:rows] + b_row[:, at]
         hidden_ref[:, at] = pre
         gate = 0.5 + 0.5 * lax.erf(pre * root_half)
         slope_ref[:, at] = gate + pre * jnp.exp(-0.5 * pre * pre) * inv_root_two_pi
@@ -182,71 +186,83 @@
         mixed_ref[k] = mixed[:images, k * shard : (k + 1) * shard]
 
 
-def payload_kernel(place_ref, mine_ref, other_ref, out_ref):
-    core = place_ref[0]
-    for half in range(HALVES):
-        for b in range(CHIPS):
-            value = mine_ref[half * CHIPS + b] + other_ref[half * CHIPS + b]
-            for j in range(4):
-                out_ref[half * 4 + j, b] = value
-    for i in range(2):
-        for j in range(CHIPS):
-            out_ref[j, CHIPS + 2 * core + i] = mine_ref[BLOCKS + i]
-            out_ref[j, CHIPS + 2 * (1 - core) + i] = other_ref[BLOCKS + i]
-
-
-def head_kernel(place_ref, got_ref, project_ref, out_ref, head_ref):
-    images, shard = got_ref.shape[2:]
+def head_kernel(
+    got_ref, mean_ref, scale_ref, bout_ref, gain_ref, bias_ref, project_ref, out_ref
+):
+    images, shard = got_ref.shape[1:]
     width = project_ref.shape[1]
-    half = place_ref[1]
-    product = jnp.zeros((24, width), f32)
-    first = jnp.zeros((8, 1), f32)
-    second = jnp.zeros((8, 1), f32)
-    row = iota((8, shard), 0)
-    for k in range(CHIPS):
-        source = half * 4 + k // 2
-        mixed = got_ref[0, k]
-        for j in range(1, CHIPS):
-            mixed = mixed + got_ref[j, k]
-        vectors = got_ref[source, CHIPS + 2 * (k % 2) + 1]
-        pooled = got_ref[source, CHIPS + 2 * (k % 2)] + vectors[0:1] * (mixed + vectors[1:2])
-        head_ref[k, 0:images, :] = pooled
-        head_ref[k, images:, :] = vectors
-        value = head_ref[k]
-        first = first + jnp.sum(value, axis=1, keepdims=True)
-        second = second + jnp.sum(value * value, axis=1, keepdims=True)
-        value = jnp.where(row < images, value * vectors[2:3], value)
-        high, rest = to_terms(value)
-        middle, low = to_terms(rest)
-        product = product + jnp.dot(
-            jnp.concatenate([high, middle, low], axis=0).astype(bf16),
-            project_ref[k * shard : (k + 1) * shard, :],
-            preferred_element_type=f32,
-        )
+    mixed = got_ref[0]
+    for j in range(1, BLOCKS):
+        mixed = mixed + got_ref[j]
+    scale, bias_out = scale_ref[...], bout_ref[...]
+    gain, bias = gain_ref[...], bias_ref[...]
+    head = jnp.concatenate(
+        [mean_ref[...] + scale * (mixed + bias_out), scale, bias_out, gain, bias], axis=0
+    )
+    first = jnp.sum(head, axis=1, keepdims=True)
+    second = jnp.sum(head * head, axis=1, keepdims=True)
+    value = jnp.where(iota((8, shard), 0) < images, head * gain, head)
+    high, rest = to_terms(value)
+    middle, low = to_terms(rest)
+    product = jnp.dot(
+        jnp.concatenate([high, middle, low], axis=0).astype(bf16),
+        project_ref[...],
+        preferred_element_type=f32,
+    )
     out_ref[:, :width] = product[:8] + (product[8:16] + product[16:])
     lane = iota((8, 128), 1)
-    out_ref[:, width:] = jnp.where(lane == 0, first, jnp.where(lane == 1, second, 0.0))
-
-
-def embed_kernel(channels, mine_ref, other_ref, text_ref, tail_ref, out_ref, stat_ref):
-    width = text_ref.shape[1]
-    sums = mine_ref[...] + other_ref[...]
+    out_ref[:, width : width + 128] = jnp.where(
+        lane == 0, first, jnp.where(lane == 1, second, 0.0)
+    )
+    out_ref[:, width + 128 : width + 128 + shard] = head
+
+
+def pair_sum_kernel(mine_ref, other_ref, out_ref):
+    cut = out_ref.shape[2] - 2 * SHARD
+    block = jnp.concatenate(
+        [
+            mine_ref[:, :cut] + other_ref[:, :cut],
+            mine_ref[:, cut : cut + SHARD],
+            other_ref[:, cut : cut + SHARD],
+        ],
+        axis=1,
+    )
+    for j in range(CHIPS):
+        out_ref[j] = block
+
+
+def embed_kernel(got_ref, text_ref, labels_ref, out_ref, head_ref, stat_ref):
+    pairs, width = text_ref.shape
+    cut = width + 128
+    core = lax.axis_index("mp") % 2
+    channels = BLOCKS * SHARD
+    for j in range(CHIPS):
+        head_ref[2 * j + core] = got_ref[j, :, cut : cut + SHARD]
+        head_ref[2 * j + 1 - core] = got_ref[j, :, cut + SHARD :]
+    sums = got_ref[0, :, :cut]
+    for j in range(1, CHIPS):
+        sums = sums + got_ref[j, :, :cut]
     mean = sums[:, width : width + 1] / channels
     inverse = lax.rsqrt(sums[:, width + 1 : width + 2] / channels - mean * mean + eps)
     emb = inverse * (sums[:, :width] - mean * sums[6:7, :width]) + sums[7:8, :width]
-    both = jnp.where(iota((8, width), 0) < 4, emb, text_ref[...])
+    row = iota((8, 128), 0)
+    tail = jnp.zeros((8, 128), f32)
+    for r in range(pairs):
+        label = labels_ref[r]
+        target = (label // pairs) * 8 + 4 + label % pairs
+        tail = jnp.where(row == r, target.astype(f32), tail)
+    block = jnp.concatenate([emb[:4], text_ref[...]], axis=0)
     for d in range(out_ref.shape[0]):
-        out_ref[d, :, :width] = both
-        out_ref[d, :, width:] = tail_ref[...]
+        out_ref[d, :, :width] = block
+        out_ref[d, :, width:] = tail
     stat_ref[0] = jnp.broadcast_to(mean, (8, 128))
     stat_ref[1] = jnp.broadcast_to(inverse, (8, 128))
 
 
-def loss_kernel(place_ref, got_ref, project_ref, text_ref, back_ref, unit_ref, len_ref, both_ref):
+def loss_kernel(got_ref, project_ref, text_ref, back_ref, unit_ref, len_ref, both_ref):
     width = project_ref.shape[1]
     count = got_ref.shape[0] * 8
-    shard = back_ref.shape[2]
-    home = pl.ds(pl.multiple_of(place_ref[3] * 8, 8), 8)
+    home = pl.ds(pl.multiple_of(lax.axis_index("dp") * 8, 8), 8)
     raw = got_ref[:, :, :width].reshape(count, width)
     length = jnp.sqrt(jnp.sum(raw * raw, axis=1, keepdims=True) + eps)
     unit = raw / length
@@ -277,16 +293,13 @@
         (((1,), (1,)), ((), ())),
         preferred_element_type=f32,
     )
-    for k in range(CHIPS):
-        back_ref[k] = back[:4, k * shard : (k + 1) * shard]
+    for k in range(BLOCKS):
+        back_ref[k] = back[:4]
 
 
 def backward_kernel(
-    place_ref,
-    gh_mine_ref,
-    gh_other_ref,
-    head_mine_ref,
-    head_other_ref,
+    back_ref,
+    head_ref,
     head_stat_ref,
     wout_ref,
     slope_ref,
@@ -301,47 +314,44 @@
     mixed_ref,
     pre_ref,
 ):
-    images, shard = gh_mine_ref.shape[1:]
+    images, shard = back_ref.shape[1:]
     rows, hidden = slope_ref.shape
     channels = w_ref.shape[0]
     positions = rows // images
-    core, half, spot = place_ref[0], place_ref[1], place_ref[2]
+    index = lax.axis_index("mp")
+    core = index % 2
     mean = head_stat_ref[0][:images, 0:1]
     inverse = head_stat_ref[1][:images, 0:1]
     first = jnp.zeros((images, 1), f32)
     second = jnp.zeros((images, 1), f32)
 
-    def parts(gh_ref, head_ref, k):
+    def parts(k):
         head = head_ref[k]
-        return gh_ref[k] * head[6:7], (head[:images] - mean) * inverse, head[4:5]
-
-    for refs in ((gh_mine_ref, head_mine_ref), (gh_other_ref, head_other_ref)):
-        for k in range(CHIPS):
-            scaled, centred, _ = parts(*refs, k)
-            first = first + jnp.sum(scaled, axis=1, keepdims=True)
-            second = second + jnp.sum(scaled * centred, axis=1, keepdims=True)
+        return back_ref[k] * head[6:7], (head[:images] - mean) * inverse, head[4:5]
+
+    for k in range(BLOCKS):
+        scaled, centred, _ = parts(k)
+        first = first + jnp.sum(scaled, axis=1, keepdims=True)
+        second = second + jnp.sum(scaled * centred, axis=1, keepdims=True)
     first = first / channels
     second = second / channels
 
-    def block(gh_ref, head_ref, k):
-        scaled, centred, scale = parts(gh_ref, head_ref, k)
+    def block(k):
+        scaled, centred, scale = parts(k)
         grad = (inverse / positions) * (scaled - first - centred * second)
         return grad, grad * scale
 
-    block_ref[...] = block(gh_mine_ref, head_mine_ref, spot)[0]
+    block_ref[...] = block(index)[0]
     mixed_ref[...] = jnp.zeros_like(mixed_ref)
-    for k in range(CHIPS):
-        mine = block(gh_mine_ref, head_mine_ref, k)[1]
-        other = block(gh_other_ref, head_other_ref, k)[1]
-        low, high = jnp.where(half == 0, mine, other), jnp.where(half == 0, other, mine)
-        mixed_ref[0:images, k * shard : (k + 1) * shard] = low
-        mixed_ref[0:images, (CHIPS + k) * shard : (CHIPS + k + 1) * shard] = high
+    for k in range(BLOCKS):
+        mixed_ref[0:images, k * shard : (k + 1) * shard] = block(k)[1]
     act = lax.dot_general(
         mixed_ref[...].astype(bf16),
         wout_ref[...],
         (((1,), (1,)), ((), ())),
         preferred_element_type=f32,
     )
+    b_row = b_ref[...][None, :]
     step = 256
     one = jnp.zeros((rows, 1), f32)
     two = jnp.zeros((rows, 1), f32)
@@ -351,8 +361,8 @@
             span = slice(n * positions, (n + 1) * positions)
             pre_ref[span, :] = (act[n : n + 1, at] * slope_ref[span, at]).astype(bf16).astype(f32)
         value = pre_ref[...]
-        gain = through_ref[0:1, at] + through_ref[1:2, at]
-        bias = through_ref[2:3, at] + through_ref[3:4, at] + b_ref[:, at]
+        gain = through_ref[0:1, at] + through_ref[8:9, at]
+        bias = through_ref[1:2, at] + through_ref[9:10, at] + b_row[:, at]
         one = one + jnp.sum(value * gain, axis=1, keepdims=True)
         two = two + jnp.sum(value * (hidden_ref[:, at] - bias), axis=1, keepdims=True)
         turned_ref[at, :] = value.T.astype(bf16)
@@ -368,10 +378,11 @@
         ).astype(bf16)
 
 
-def mine_kernel(place_ref, w_ref, turned_ref, mine_ref):
+def mine_kernel(w_ref, turned_ref, mine_ref):
     shard = w_ref.shape[0] // BLOCKS
-    for j in range(CHIPS):
-        start = pl.multiple_of((2 * j + place_ref[0]) * shard, 64)
+    core = lax.axis_index("mp") % 2
+    for j in range(CHIPS):
+        start = pl.multiple_of((2 * j + core) * shard, 64)
         mine_ref[j * shard : (j + 1) * shard, :] = jnp.dot(
             w_ref[pl.ds(start, shard), :], turned_ref[...], preferred_element_type=f32
         ).astype(bf16)
@@ -392,10 +403,14 @@
         out_ref[j, shard:, :] = tail
 
 
-def final_kernel(
-    channels, got_ref, conv_ref, stat_ref, gain_ref, w_ref, block_ref, out_ref, rows_ref
-):
+def final_kernel(got_ref, conv_ref, stat_ref, gain_ref, w_ref, block_ref, out_ref, rows_ref):
     shard = conv_ref.shape[0]
+    channels = shard * BLOCKS
+    index = lax.axis_index("mp")
+    gain = jnp.zeros((1, shard), f32)
+    for k in range(BLOCKS):
+        gain = jnp.where(index == k, gain_ref[:, k * shard : (k + 1) * shard], gain)
+    gain = jnp.broadcast_to(gain, (8, shard)).T[:, 0:1]
     images, side = out_ref.shape[:2]
     positions = side * side
     total = got_ref[0].astype(f32)
@@ -405,7 +420,7 @@
     second = (total[shard + 1 : shard + 2] + total[shard + 9 : shard + 10]) / channels
     average, inverse = stat_ref[0:1, :], stat_ref[1:2, :]
     centred = (conv_ref[...].astype(f32) - average) * inverse
-    grad = inverse * (total[:shard] * gain_ref[...].T[:, 0:1] - first - centred * second)
+    grad = inverse * (total[:shard] * gain - first - centred * second)
     rows_ref[...] = grad.T
 
     def image(n, carry):
@@ -441,32 +456,6 @@
     rows = images * side * side
     pairs, width = text_emb.shape
     shards = lax.axis_size("dp")
-    index = lax.axis_index("mp")
-    core = index % 2
-    place = jnp.stack(
-        [core, index // CHIPS, index % CHIPS, lax.axis_index("dp")]
-    ).astype(jnp.int32)
-    project = half_gather(projection)
-
-    def own_first(vector):
-        pair = vector.reshape(CHIPS, 2, shard)
-        mine = jnp.where(core == 0, pair[:, 0], pair[:, 1])
-        other = jnp.where(core == 0, pair[:, 1], pair[:, 0])
-        return jnp.concatenate([mine, other])
-
-    own = jnp.concatenate([own_first(ln_gain), own_first(ln_bias)])
-    terms = []
-    for vector in (ln_gain, ln_bias):
-        high = lax.reduce_precision(vector, 8, 7)
-        terms += [high, vector - high]
-    vec = jnp.pad(jnp.stack(terms), ((0, 12), (0, 0)))
-    gain_local = lax.dynamic_slice_in_dim(ln_gain, index * shard, shard, 0)
-    gain_local = jnp.broadcast_to(gain_local[None, :], (8, shard))
-    b_row = b_in[None, :]
-    target = (labels // pairs) * 8 + 4 + labels % pairs
-    tail = jnp.pad(target.astype(f32)[:, None], ((0, 8 - pairs), (0, 127)))
-    text_low = jnp.pad(text_emb, ((8 - pairs, 0), (0, 0)))
-
     copies, conv, input_mean = run(
         conv_kernel,
         [
@@ -491,49 +480,47 @@
             shape(8, rows),
             shape(BLOCKS, images, shard),
         ],
-        place,
         conv_mine,
         conv_other,
-        own,
-        vec,
+        ln_gain[None, :],
+        ln_bias[None, :],
         w_in,
-        b_row,
+        b_in,
         w_out,
-        scratch=[pltpu.VMEM((channels, rows), bf16), pltpu.VMEM((rows + 16, channels), bf16)],
-        limit=32,
+        scratch=[
+            pltpu.VMEM((channels, rows), bf16),
+            pltpu.VMEM((rows + 16, channels), bf16),
+            pltpu.VMEM((2 * BLOCKS, shard), f32),
+            pltpu.VMEM((8, channels), f32),
+        ],
         flops=2 * rows * channels * hidden,
     )
-    vectors = jnp.stack([layer_scale, b_out, head_gain, head_bias])
-    partial = jnp.concatenate([mixed, input_mean[None], vectors[None]])
-    (payload,) = run(
-        payload_kernel,
-        [shape(CHIPS, CHIPS + 4, images, shard)],
-        place,
-        partial,
-        core_swap(partial),
-    )
-    sums, head = run(
+    (sums,) = run(
         head_kernel,
-        [shape(8, width + 128), shape(CHIPS, 8, shard)],
-        place,
-        chip_exchange(payload),
-        project,
-    )
-    pair_block, head_stat = run(
-        functools.partial(embed_kernel, channels),
-        [shape(shards, 8, width + 128), shape(2, 8, 128)],
-        sums,
-        x_swap(sums),
-        text_low,
-        tail,
-    )
-    head_other = x_swap(head)
+        [shape(8, width + 128 + 256)],
+        shard_exchange(mixed),
+        input_mean,
+        layer_scale[None, :],
+        b_out[None, :],
+        head_gain[None, :],
+        head_bias[None, :],
+        projection,
+    )
+    (blocks,) = run(
+        pair_sum_kernel, [shape(CHIPS, 8, width + 128 + 2 * shard)], sums, core_swap(sums)
+    )
+    pair_block, head, head_stat = run(
+        embed_kernel,
+        [shape(shards, 8, width + 128), shape(BLOCKS, 8, shard), shape(2, 8, 128)],
+        chip_exchange(blocks),
+        text_emb,
+        labels,
+    )
     grad_text, back = run(
         loss_kernel,
-        [shape(pairs, width), shape(CHIPS, images, shard)],
-        place,
+        [shape(pairs, width), shape(BLOCKS, images, shard)],
         lax.all_to_all(pair_block, "dp", 0, 0),
-        project,
+        projection,
         scratch=[
             pltpu.VMEM((shards * 8, width), f32),
             pltpu.VMEM((shards * 8, 128), f32),
@@ -548,27 +535,22 @@
             shape(8, rows),
             shape(images, shard),
         ],
-        place,
-        back,
-        x_swap(back),
+        shard_exchange(back),
         head,
-        head_other,
         head_stat,
         w_out,
         slope,
         hidden_pre,
         w_in,
         through,
-        b_row,
+        b_in,
         scratch=[pltpu.VMEM((8, channels), f32), pltpu.VMEM((rows, 256), f32)],
-        limit=32,
         flops=rows * channels * hidden,
     )
     passed = core_swap(other)
     (mine,) = run(
         mine_kernel,
         [shape(channels // 2, rows, dtype=bf16)],
-        place,
         w_in,
         turned,
         flops=rows * channels * hidden,
@@ -577,12 +559,12 @@
         pair_kernel, [shape(CHIPS, shard + 16, rows, dtype=bf16)], mine, passed, row_sums
     )
     (grad_input,) = run(
-        functools.partial(final_kernel, channels),
+        final_kernel,
         [shape(images, side, side, shard)],
         chip_exchange(blocks),
         conv,
         row_stat,
-        gain_local,
+        ln_gain[None, :],
         dw_weight,
         grad_block,
         scratch=[pltpu.VMEM((rows, shard), f32)],

time: 155 us -> 135 us (0.87)
  blocking collectives: 15.2 us -> 99.1 us
  waiting for transfers between devices: 41 us -> 3.92 us
  starting transfers between devices: 31.6 us -> 3.56 us
  local copies, waits for them, and re-layouts: 23.9 us -> 9.22 us
  between operations: 14.2 us -> 0.76 us
  Pallas kernels: 23.8 us -> 17.7 us
  other arithmetic: 3 us -> 0 us
    all_to_all x0 -> x3, blocking collectives: none -> 50.2 us  [the longest x2 26.4 us: shard_exchange(): return lax.all_to_all(array, 'mp', 0, 0)]
    all_to_all x1 -> x3, blocking collectives: 15.2 us -> 48.9 us  [chip_exchange(): return lax.all_to_all(array, 'mp', 0, 0, axis_index_groups=groups)]
    all_to_all x3 -> x0, waiting for transfers between devices: 32.4 us -> none  [the longest x2 19.9 us: chip_exchange(): return lax.all_to_all(array, 'mp', 0, 0, axis_index_groups=groups)]
    all_to_all x3 -> x0, starting transfers between devices: 20.2 us -> none  [the longest x2 11 us: chip_exchange(): return lax.all_to_all(array, 'mp', 0, 0, axis_index_groups=groups)]
    unnamed x42 -> x38, local copies, waits for them, and re-layouts: 20 us -> 9.22 us
    pallas_call x10, Pallas kernels: 23.8 us -> 17.7 us  [run(): pl.pallas_call(kernel, out_shape=outs, in_specs=specs, out_specs=[pl.Bloc...]
    ppermute x3 -> x0, waiting for transfers between devices: 5.99 us -> none  [x_swap(): return lax.ppermute(array, 'mp', [(i, i ^ CHIPS) for i in range(BLOCKS)])]
    ppermute x3, starting transfers between devices: 9.09 us -> 3.56 us  [core_swap(): return lax.ppermute(array, 'mp', [(i, i ^ 1) for i in range(BLOCKS)])]
  transfers between devices with their start and end apart: 10 -> 3, of which waited for: 8 -> 3; matrix products, arithmetic and copies ran while one was open for 5% -> 0% of each run, Pallas kernels for 9% -> 1%
where the time goes in v4:
time: 135 us; the launch traced here: 134 us
  blocking collectives  99.1 us (73%)
  Pallas kernels  17.7 us (13%)
  local copies, waits for them, and re-layouts  9.22 us (7%)
  waiting for transfers between devices  3.92 us (3%)
  starting transfers between devices  3.56 us (3%)
    all_to_all x3, blocking collectives, chip_exchange(): return lax.all_to_all(array, 'mp', 0, 0, axis_index_groups=groups)  48.9 us
    all_to_all x2, blocking collectives, shard_exchange(): return lax.all_to_all(array, 'mp', 0, 0)  26.4 us
    all_to_all x1, blocking collectives, body(): lax.all_to_all(pair_block, 'dp', 0, 0)  23.7 us
    pallas_call x10, Pallas kernels, run(): pl.pallas_call(kernel, out_shape=outs, in_specs=specs, out_specs=[pl.Bloc...  17.7 us
    unnamed x38, local copies, waits for them, and re-layouts  9.22 us
    ppermute x3, waiting for transfers between devices, core_swap(): return lax.ppermute(array, 'mp', [(i, i ^ 1) for i in range(BLOCKS)])  3.92 us
    ppermute x3, starting transfers between devices, core_swap(): return lax.ppermute(array, 'mp', [(i, i ^ 1) for i in range(BLOCKS)])  3.56 us
  transfers between devices with their start and end apart: 3, of which 3 were waited for; matrix products, arithmetic and copies ran while one was open for 0% of the time, Pallas kernels for 1%

profile of v4, /device:TPU:1, one launch (start us, length us, event | category | flops | bytes accessed | tf_op | source)
XLA Modules:
  0.0 134.3 jit_solution(15763193260082399742)
XLA Ops:
  0.6 0.0 copy-start.5
  0.6 0.8 copy-done.5
  1.5 0.0 copy-start.7
  1.5 0.9 copy-done.7
  2.4 0.0 copy-start.13
  2.4 0.7 copy-done.13
  3.0 1.0 shard_map.158
  4.0 20.1 %all_to_all.30.mine_ref = bf16[8,192,256]{2,1,0:T(8,128)(2,1)S(1)} all-to-all(bf16[8,192,256]{2,1,0:T(8,128)(2,1)S(1)} %get-tuple-element.19), channel_id=1, replica_groups={{0,2,4,6,8,10,12,14},{1,3,5,7,9,11,13,15},{16,18,20,22,24,26,28,30},{17..., dimensions={0} | all-to-all | bytes 1572864 | tf_op jit(solution)/shard_map/all_to_all | solution.py:28
  24.1 2.5 %collective-permute-start = (bf16[8,192,256]{2,1,0:T(8,128)(2,1)S(1)}, bf16[8,192,256]{2,1,0:T(8,128)(2,1)S(1)}, u32[]{:S(2)}, u32[]{:S(2)}) collective-permute-start(bf16[8,192,256]{2,1,0:T(8,128)(2,1)S(1)} %all_to_all.30.mine_ref), channel_id=1, source_target_pairs={{0,1},{1,0},{2,3},{3,2},{4,5},{5,4},{6,7},{7,6},{8,9},{9,8},{10,11... | collective-permute-start | bytes 2359304 | tf_op jit(solution)/shard_map/ppermute | solution.py:23
  26.6 1.9 %collective-permute-done.other_ref = bf16[8,192,256]{2,1,0:T(8,128)(2,1)S(1)} collective-permute-done((bf16[8,192,256]{2,1,0:T(8,128)(2,1)S(1)}, bf16[8,192,256]{2,1,0:T(8,128)(2,1)S(1)}, u32[]{:S(2)}, u32[]{:S(2)}) %collective-permute-start) | collective-permute-done | bytes 786464 | tf_op jit(solution)/shard_map/ppermute | solution.py:23
  28.5 0.0 copy-start
  28.5 2.3 %copy-done = bf16[3072,768]{1,0:T(8,128)(2,1)S(1)} copy-done((bf16[3072,768]{1,0:T(8,128)(2,1)S(1)}, bf16[3072,768]{1,0:T(8,128)(2,1)}, u32[]{:S(2)}) %copy-start) | copy-done | bytes 4718616
  30.8 0.0 copy-start.2
  30.8 2.3 %copy-done.2 = bf16[768,3072]{1,0:T(8,128)(2,1)S(1)} copy-done((bf16[768,3072]{1,0:T(8,128)(2,1)S(1)}, bf16[768,3072]{1,0:T(8,128)(2,1)}, u32[]{:S(2)}) %copy-start.2) | copy-done | bytes 4718616
  33.2 0.0 copy-start.8
  33.2 0.7 copy-done.8
  33.9 0.0 copy-start.10
  33.9 0.7 copy-done.10
  34.6 0.0 copy-start.12
  34.6 0.7 copy-done.12
  35.3 0.0 copy-start.4
  35.3 0.0 copy-start.14
  35.3 0.0 copy-start.15
  35.3 0.0 copy-start.16
  35.3 0.0 copy-start.17
  35.3 0.0 copy-start.11
  35.3 0.0 copy-start.18
  35.3 0.0 copy-start.1
  35.3 0.0 copy-start.3
  35.3 6.1 %shard_map.159 = (f32[256,768]{1,0:T(8,128)S(1)}, f32[256,768]{1,0:T(8,128)S(1)}, f32[16,768]{1,0:T(8,128)S(1)}, f32[8,256]{1,0:T(8,128)S(1)}, f32[16,4,192]{2,1,0:T(4,128)S(1)}) custom-call(bf16[8,192,256]{2,1,0:T(8,128)(2,1)S(1)} %all_to_all.30.mine_ref, bf16[8,192,256]{2,1,0:T(8,128)(2,1)S(1)} %collective-permute-done.other_ref, f32[1,3072]{1,0:T(1,128)S(1)} %bitcast.7, ...), custom_call_target="tpu_custom_call" | custom-call | flops 1207959552 | bytes 11037696 | tf_op jit(solution)/shard_map/pallas_call | solution.py:41
  41.5 10.3 %all_to_all.31.got_ref = f32[16,4,192]{2,1,0:T(4,128)S(1)} all-to-all(f32[16,4,192]{2,1,0:T(4,128)S(1)} %get-tuple-element.20), channel_id=1, replica_groups=mesh['dp'=16,'mp'=16] {'mp'}, dimensions={0} | all-to-all | bytes 98304 | tf_op jit(solution)/shard_map/all_to_all | solution.py:32
  51.8 0.0 copy-done.4
  51.8 0.0 copy-done.14
  51.8 0.0 copy-done.15
  51.8 0.0 copy-done.16
  51.8 0.0 copy-done.17
  51.8 0.2 shard_map.160.mine_ref
  52.0 0.5 collective-permute-start.1
  52.5 0.9 collective-permute-done.1.other_ref
  53.4 0.1 shard_map.161
  53.4 11.8 %all_to_all.32.got_ref = f32[8,8,1536]{2,1,0:T(8,128)S(1)} all-to-all(f32[8,8,1536]{2,1,0:T(8,128)S(1)} %shard_map.161), channel_id=1, replica_groups={{0,2,4,6,8,10,12,14},{1,3,5,7,9,11,13,15},{16,18,20,22,24,26,28,30},{17..., dimensions={0} | all-to-all | bytes 786432 | tf_op jit(solution)/shard_map/all_to_all | solution.py:28
  65.2 0.0 copy-done.11
  65.2 0.0 copy-done.18
  65.2 0.7 shard_map.162
  66.0 23.7 %all_to_all.33.got_ref = f32[16,8,1152]{2,1,0:T(8,128)S(1)} all-to-all(f32[16,8,1152]{2,1,0:T(8,128)S(1)} %get-tuple-element.22), channel_id=1, replica_groups=mesh['dp'=16,'mp'=16] {'dp'}, dimensions={0} | all-to-all | bytes 1179648 | tf_op jit(solution)/shard_map/all_to_all | solution.py:522
  89.7 2.4 %shard_map.163 = (f32[4,1024]{1,0:T(4,128)}, f32[16,4,192]{2,1,0:T(4,128)S(1)}) custom-call(f32[16,8,1152]{2,1,0:T(8,128)S(1)} %all_to_all.33.got_ref, bf16[192,1024]{1,0:T(8,128)(2,1)S(1)} %copy-done.4), custom_call_target="tpu_custom_call" | custom-call | bytes 983040 | tf_op jit(solution)/shard_map/pallas_call | solution.py:41
  92.1 16.1 %all_to_all.34.back_ref = f32[16,4,192]{2,1,0:T(4,128)S(1)} all-to-all(f32[16,4,192]{2,1,0:T(4,128)S(1)} %get-tuple-element.23), channel_id=1, replica_groups=mesh['dp'=16,'mp'=16] {'mp'}, dimensions={0} | all-to-all | bytes 98304 | tf_op jit(solution)/shard_map/all_to_all | solution.py:32
  108.2 0.0 copy-done.1
  108.2 0.0 copy-done.3
  108.2 3.2 %shard_map.164 = (bf16[1552,256]{1,0:T(8,128)(2,1)S(1)}, bf16[768,256]{1,0:T(8,128)(2,1)S(1)}, f32[8,256]{1,0:T(8,128)S(1)}, f32[4,192]{1,0:T(4,128)S(1)}) custom-call(f32[16,4,192]{2,1,0:T(4,128)S(1)} %all_to_all.34.back_ref, f32[16,8,192]{2,1,0:T(8,128)S(1)} %get-tuple-element.24.head_ref, f32[2,8,128]{2,1,0:T(8,128)S(1)} %get-tuple-element.25.head_stat_ref, ...), custom_call_target="tpu_custom_call" | custom-call | flops 603979776 | bytes 11217920 | tf_op jit(solution)/shard_map/pallas_call | solution.py:41
  111.4 0.5 collective-permute-start.2
  112.0 0.0 copy-start.6
  112.0 0.0 copy-start.9
  112.0 0.8 shard_map.165.mine_ref
  112.7 1.1 collective-permute-done.2.got_ref
  113.9 0.2 shard_map.166
  114.1 17.1 %all_to_all.35.got_ref = bf16[8,208,256]{2,1,0:T(8,128)(2,1)S(1)} all-to-all(bf16[8,208,256]{2,1,0:T(8,128)(2,1)S(1)} %shard_map.166), channel_id=1, replica_groups={{0,2,4,6,8,10,12,14},{1,3,5,7,9,11,13,15},{16,18,20,22,24,26,28,30},{17..., dimensions={0} | all-to-all | bytes 1703936 | tf_op jit(solution)/shard_map/all_to_all | solution.py:28
  131.1 0.0 copy-done.6
  131.1 0.0 copy-done.9
  131.1 3.2 %shard_map.167 = f32[4,8,8,192]{3,2,1,0:T(8,128)} custom-call(bf16[8,208,256]{2,1,0:T(8,128)(2,1)S(1)} %all_to_all.35.got_ref, bf16[192,256]{1,0:T(8,128)(2,1)S(1)} %get-tuple-element.32.conv_ref, f32[8,256]{1,0:T(8,128)S(1)} %get-tuple-element.33.stat_ref, f32[1,3072]{1,0:T(1,128)S(1)} %bitcast.8, f32[7,7,192]{2,1,0:T(8,128)S(1)} %copy-done.6, ...), custom_call_target="tpu_custom_call" | custom-call | flops 4816896 | bytes 1011456 | tf_op jit(solution)/shard_map/pallas_call | solution.py:41
Async XLA Ops:
  0.6 0.8 copy-start.5
  1.5 0.9 copy-start.7
  2.4 0.7 copy-start.13
  24.1 4.4 %collective-permute-start = (bf16[8,192,256]{2,1,0:T(8,128)(2,1)S(1)}, bf16[8,192,256]{2,1,0:T(8,128)(2,1)S(1)}, u32[]{:S(2)}, u32[]{:S(2)}) collective-permute-start(bf16[8,192,256]{2,1,0:T(8,128)(2,1)S(1)} %all_to_all.30.mine_ref), channel_id=1, source_target_pairs={{0,1},{1,0},{2,3},{3,2},{4,5},{5,4},{6,7},{7,6},{8,9},{9,8},{10,11... | collective-permute-start | bytes 2359304 | tf_op jit(solution)/shard_map/ppermute | solution.py:23
  28.5 2.3 %copy-start = (bf16[3072,768]{1,0:T(8,128)(2,1)S(1)}, bf16[3072,768]{1,0:T(8,128)(2,1)}, u32[]{:S(2)}) copy-start(bf16[3072,768]{1,0:T(8,128)(2,1)} %w_ref.8) | copy-start | bytes 14155780
  30.8 2.3 %copy-start.2 = (bf16[768,3072]{1,0:T(8,128)(2,1)S(1)}, bf16[768,3072]{1,0:T(8,128)(2,1)}, u32[]{:S(2)}) copy-start(bf16[768,3072]{1,0:T(8,128)(2,1)} %wout_ref.3) | copy-start | bytes 14155780
  33.2 0.7 copy-start.8
  33.9 0.7 copy-start.10
  34.6 0.7 copy-start.12
  35.3 16.5 %copy-start.4 = (bf16[192,1024]{1,0:T(8,128)(2,1)S(1)}, bf16[192,1024]{1,0:T(8,128)(2,1)}, u32[]{:S(2)}) copy-start(bf16[192,1024]{1,0:T(8,128)(2,1)} %project_ref.3) | copy-start | bytes 1179652
  35.3 16.5 %copy-start.14 = (f32[192]{0:T(256)S(1)}, f32[192]{0:T(256)}, u32[]{:S(2)}) copy-start(f32[192]{0:T(256)} %param.24) | copy-start | bytes 2308
  35.3 16.5 %copy-start.15 = (f32[192]{0:T(256)S(1)}, f32[192]{0:T(256)}, u32[]{:S(2)}) copy-start(f32[192]{0:T(256)} %param.23) | copy-start | bytes 2308
  35.3 16.5 %copy-start.16 = (f32[192]{0:T(256)S(1)}, f32[192]{0:T(256)}, u32[]{:S(2)}) copy-start(f32[192]{0:T(256)} %param.25) | copy-start | bytes 2308
  35.3 16.5 %copy-start.17 = (f32[192]{0:T(256)S(1)}, f32[192]{0:T(256)}, u32[]{:S(2)}) copy-start(f32[192]{0:T(256)} %param.26) | copy-start | bytes 2308
  35.3 30.0 %copy-start.11 = (f32[4,1024]{1,0:T(4,128)S(1)}, f32[4,1024]{1,0:T(4,128)}, u32[]{:S(2)}) copy-start(f32[4,1024]{1,0:T(4,128)} %text_ref.1) | copy-start | bytes 49156
  35.3 29.9 %copy-start.18 = (s32[4]{0:T(128)S(1)}, s32[4]{0:T(128)}, u32[]{:S(2)}) copy-start(s32[4]{0:T(128)} %labels_ref.1) | copy-start | bytes 52
  35.3 72.9 %copy-start.1 = (bf16[3072,768]{1,0:T(8,128)(2,1)S(1)}, bf16[3072,768]{1,0:T(8,128)(2,1)}, u32[]{:S(2)}) copy-start(bf16[3072,768]{1,0:T(8,128)(2,1)} %w_ref.8) | copy-start | bytes 14155780
  35.3 72.9 %copy-start.3 = (bf16[768,3072]{1,0:T(8,128)(2,1)S(1)}, bf16[768,3072]{1,0:T(8,128)(2,1)}, u32[]{:S(2)}) copy-start(bf16[768,3072]{1,0:T(8,128)(2,1)} %wout_ref.3) | copy-start | bytes 14155780
  52.0 1.4 %collective-permute-start.1 = (f32[8,1408]{1,0:T(8,128)S(1)}, f32[8,1408]{1,0:T(8,128)S(1)}, u32[]{:S(2)}, u32[]{:S(2)}) collective-permute-start(f32[8,1408]{1,0:T(8,128)S(1)} %shard_map.160.mine_ref), channel_id=1, source_target_pairs={{0,1},{1,0},{2,3},{3,2},{4,5},{5,4},{6,7},{7,6},{8,9},{9,8},{10,11... | collective-permute-start | bytes 135176 | tf_op jit(solution)/shard_map/ppermute | solution.py:23
  111.4 2.5 %collective-permute-start.2 = (bf16[1552,256]{1,0:T(8,128)(2,1)S(1)}, bf16[1552,256]{1,0:T(8,128)(2,1)S(1)}, u32[]{:S(2)}, u32[]{:S(2)}) collective-permute-start(bf16[1552,256]{1,0:T(8,128)(2,1)S(1)} %get-tuple-element.30), channel_id=1, source_target_pairs={{0,1},{1,0},{2,3},{3,2},{4,5},{5,4},{6,7},{7,6},{8,9},{9,8},{10,11... | collective-permute-start | bytes 2383880 | tf_op jit(solution)/shard_map/ppermute | solution.py:23
  112.0 19.2 %copy-start.6 = (f32[7,7,192]{2,1,0:T(8,128)S(1)}, f32[7,7,192]{2,1,0:T(8,128)}, u32[]{:S(2)}) copy-start(f32[7,7,192]{2,1,0:T(8,128)} %w_ref.9) | copy-start | bytes 112900
  112.0 19.2 %copy-start.9 = (f32[3072]{0:T(1024)S(1)}, f32[3072]{0:T(1024)}, u32[]{:S(2)}) copy-start(f32[3072]{0:T(1024)} %param.18) | copy-start | bytes 36868

commit v5 on v4

--- a/solution.py
+++ b/solution.py
@@ -14,6 +14,8 @@
 bf16 = jnp.bfloat16
 highest = lax.Precision.HIGHEST
 MIB = 1 << 20
+CONV_LIMIT = 50 * MIB
+CONV_FLOPS = 16 * 10**9
 CHIPS = 8
 BLOCKS = 16
 SHARD = 192
@@ -32,21 +34,31 @@
     return lax.all_to_all(array, "mp", 0, 0)
 
 
-def run(kernel, outs, *operands, scratch=(), limit=24, flops=0):
-    specs = [
-        pl.BlockSpec(memory_space=pltpu.SMEM if a.dtype == jnp.int32 else pltpu.VMEM)
-        for a in operands
-    ]
-    size = sum(a.size * a.dtype.itemsize for a in operands)
+class Far:
+    def __init__(self, array):
+        self.array = array
+
+
+def run(kernel, outs, *operands, scratch=(), limit=24 * MIB, flops=0):
+    def spec(a):
+        if isinstance(a, Far):
+            return pl.BlockSpec(memory_space=pltpu.HBM)
+        return pl.BlockSpec(memory_space=pltpu.SMEM if a.dtype == jnp.int32 else pltpu.VMEM)
+
+    arrays = [a.array if isinstance(a, Far) else a for a in operands]
     return pl.pallas_call(
         kernel,
         out_shape=outs,
-        in_specs=specs,
+        in_specs=[spec(a) for a in operands],
         out_specs=[pl.BlockSpec(memory_space=pltpu.VMEM) for _ in outs],
         scratch_shapes=list(scratch),
-        compiler_params=pltpu.CompilerParams(vmem_limit_bytes=limit * MIB),
-        cost_estimate=pl.CostEstimate(flops=flops, bytes_accessed=size, transcendentals=0),
-    )(*operands)
+        compiler_params=pltpu.CompilerParams(vmem_limit_bytes=limit),
+        cost_estimate=pl.CostEstimate(
+            flops=flops,
+            bytes_accessed=sum(a.size * a.dtype.itemsize for a in arrays),
+            transcendentals=0,
+        ),
+    )(*arrays)
 
 
 def shape(*dims, dtype=f32):
@@ -85,20 +97,28 @@
     return acc
 
 
-def conv_kernel(x_ref, w_ref, b_ref, copies_ref, conv_ref, mean_ref, rows_ref):
+def conv_kernel(
+    x_far, dw_far, bias_far, copies_ref, conv_ref, mean_ref, x_ref, dw_ref, bias_ref, rows_ref, sems
+):
     images, side = x_ref.shape[:2]
     positions = side * side
+    loads = ((x_far, x_ref), (dw_far, dw_ref), (bias_far, bias_ref))
+    loads = [pltpu.make_async_copy(far, near, sems.at[i]) for i, (far, near) in enumerate(loads)]
+    for copy in loads:
+        copy.start()
+    for copy in loads:
+        copy.wait()
 
     def image(n, carry):
         x = x_ref[n].astype(f32)
         total = jnp.sum(jnp.sum(x, axis=0), axis=0, keepdims=True)
         mean_ref[pl.ds(n, 1), :] = total / positions
-        for p, row in enumerate(taps(x, w_ref, False)):
+        for p, row in enumerate(taps(x, dw_ref, False)):
             rows_ref[pl.ds(pl.multiple_of(n * positions + p * side, side), side), :] = row
         return carry
 
     lax.fori_loop(0, images, image, 0)
-    turned = (rows_ref[...] + b_ref[...]).T.astype(bf16)
+    turned = (rows_ref[...] + bias_ref[...]).T.astype(bf16)
     conv_ref[...] = turned
     for j in range(CHIPS):
         copies_ref[j] = turned
@@ -231,7 +251,7 @@
         out_ref[j] = block
 
 
-def embed_kernel(got_ref, text_ref, labels_ref, out_ref, head_ref, stat_ref):
+def embed_kernel(got_ref, text_ref, labels_ref, out_ref, own_ref, head_ref, stat_ref):
     pairs, width = text_ref.shape
     cut = width + 128
     core = lax.axis_index("mp") % 2
@@ -252,22 +272,27 @@
         target = (label // pairs) * 8 + 4 + label % pairs
         tail = jnp.where(row == r, target.astype(f32), tail)
     block = jnp.concatenate([emb[:4], text_ref[...]], axis=0)
+    own_ref[...] = block
+    half = width // 2
+    block = jnp.concatenate([block[:, :half], block[:, half:]], axis=0).astype(bf16)
+    tail = jnp.concatenate([tail, tail], axis=0).astype(bf16)
     for d in range(out_ref.shape[0]):
-        out_ref[d, :, :width] = block
-        out_ref[d, :, width:] = tail
+        out_ref[d, :, :half] = block
+        out_ref[d, :, half:] = tail
     stat_ref[0] = jnp.broadcast_to(mean, (8, 128))
     stat_ref[1] = jnp.broadcast_to(inverse, (8, 128))
 
 
-def loss_kernel(got_ref, project_ref, text_ref, back_ref, unit_ref, len_ref, both_ref):
+def loss_kernel(got_ref, own_ref, project_ref, text_ref, back_ref, both_ref):
     width = project_ref.shape[1]
     count = got_ref.shape[0] * 8
     home = pl.ds(pl.multiple_of(lax.axis_index("dp") * 8, 8), 8)
-    raw = got_ref[:, :, :width].reshape(count, width)
-    length = jnp.sqrt(jnp.sum(raw * raw, axis=1, keepdims=True) + eps)
-    unit = raw / length
-    unit_ref[...] = unit
-    len_ref[...] = jnp.broadcast_to(length, (count, 128))
+    half = width // 2
+    got = got_ref[...].astype(f32)
+    raw = jnp.concatenate(
+        [got[:, :8, :half].reshape(count, half), got[:, 8:, :half].reshape(count, half)], axis=1
+    )
+    unit = raw / jnp.sqrt(jnp.sum(raw * raw, axis=1, keepdims=True) + eps)
     logits = logit_scale * lax.dot_general(
         unit, unit, (((1,), (1,)), ((), ())), precision=highest, preferred_element_type=f32
     )
@@ -276,7 +301,7 @@
     weights = jnp.where(valid, jnp.exp(jnp.where(valid, logits, 0.0)), 0.0)
     row_total = jnp.sum(weights, axis=1, keepdims=True)
     col_total = jnp.sum(weights, axis=0, keepdims=True)
-    target = got_ref[:, :, width:].reshape(count, 128)[:, 0:1]
+    target = got[:, :8, half:].reshape(count, 128)[:, 0:1]
     matched = jnp.where(target == column.astype(f32), 1.0, 0.0)
     grads = loss_scale * (0.5 * (weights / row_total + weights / col_total) - matched)
     grads = jnp.where(valid, grads, 0.0)
@@ -284,8 +309,10 @@
     grad_unit = logit_scale * jnp.dot(
         both_ref[home, :], unit, precision=highest, preferred_element_type=f32
     )
-    own = unit_ref[home, :]
-    grad = (grad_unit - own * jnp.sum(own * grad_unit, axis=1, keepdims=True)) / len_ref[home, 0:1]
+    own = own_ref[...]
+    length = jnp.sqrt(jnp.sum(own * own, axis=1, keepdims=True) + eps)
+    own = own / length
+    grad = (grad_unit - own * jnp.sum(own * grad_unit, axis=1, keepdims=True)) / length
     text_ref[...] = grad[4:]
     back = lax.dot_general(
         grad.astype(bf16),
@@ -407,9 +434,8 @@
     shard = conv_ref.shape[0]
     channels = shard * BLOCKS
     index = lax.axis_index("mp")
-    gain = jnp.zeros((1, shard), f32)
-    for k in range(BLOCKS):
-        gain = jnp.where(index == k, gain_ref[:, k * shard : (k + 1) * shard], gain)
+    pair = gain_ref[:, pl.ds(pl.multiple_of(index // 2 * 2 * shard, 128), 2 * shard)]
+    gain = jnp.where(index % 2 == 0, pair[:, :shard], pair[:, shard:])
     gain = jnp.broadcast_to(gain, (8, shard)).T[:, 0:1]
     images, side = out_ref.shape[:2]
     positions = side * side
@@ -463,11 +489,18 @@
             shape(shard, rows, dtype=bf16),
             shape(images, shard),
         ],
-        x_in,
-        dw_weight,
-        dw_bias[None, :],
-        scratch=[pltpu.VMEM((rows, shard), f32)],
-        flops=2 * 49 * rows * shard,
+        Far(x_in),
+        Far(dw_weight),
+        Far(dw_bias[None, :]),
+        scratch=[
+            pltpu.VMEM(x_in.shape, bf16),
+            pltpu.VMEM(dw_weight.shape, f32),
+            pltpu.VMEM((1, shard), f32),
+            pltpu.VMEM((rows, shard), f32),
+            pltpu.SemaphoreType.DMA((3,)),
+        ],
+        limit=CONV_LIMIT,
+        flops=CONV_FLOPS,
     )
     conv_mine = chip_exchange(copies)
     conv_other = core_swap(conv_mine)
@@ -509,9 +542,14 @@
     (blocks,) = run(
         pair_sum_kernel, [shape(CHIPS, 8, width + 128 + 2 * shard)], sums, core_swap(sums)
     )
-    pair_block, head, head_stat = run(
+    pair_block, own_block, head, head_stat = run(
         embed_kernel,
-        [shape(shards, 8, width + 128), shape(BLOCKS, 8, shard), shape(2, 8, 128)],
+        [
+            shape(shards, 16, width // 2 + 128, dtype=bf16),
+            shape(8, width),
+            shape(BLOCKS, 8, shard),
+            shape(2, 8, 128),
+        ],
         chip_exchange(blocks),
         text_emb,
         labels,
@@ -520,12 +558,9 @@
         loss_kernel,
         [shape(pairs, width), shape(BLOCKS, images, shard)],
         lax.all_to_all(pair_block, "dp", 0, 0),
+        own_block,
         projection,
-        scratch=[
-            pltpu.VMEM((shards * 8, width), f32),
-            pltpu.VMEM((shards * 8, 128), f32),
-            pltpu.VMEM((shards * 8, shards * 8), f32),
-        ],
+        scratch=[pltpu.VMEM((shards * 8, shards * 8), f32)],
     )
     other, turned, row_sums, grad_block = run(
         backward_kernel,

time: 135 us -> 120 us (0.89)
  blocking collectives: 99.1 us -> 91.6 us
  local copies, waits for them, and re-layouts: 9.22 us -> 2.46 us
    all_to_all x1, blocking collectives: 23.7 us -> 16.2 us  [body(): lax.all_to_all(pair_block, 'dp', 0, 0)]
    unnamed x38 -> x30, local copies, waits for them, and re-layouts: 9.22 us -> 2.46 us
where the time goes in v5:
time: 120 us; the launch traced here: 119 us
  blocking collectives  91.6 us (76%)
  Pallas kernels  16.8 us (14%)
  waiting for transfers between devices  3.94 us (3%)
  starting transfers between devices  3.56 us (3%)
  local copies, waits for them, and re-layouts  2.46 us (2%)
    all_to_all x3, blocking collectives, chip_exchange(): return lax.all_to_all(array, 'mp', 0, 0, axis_index_groups=groups)  49.2 us
    all_to_all x2, blocking collectives, shard_exchange(): return lax.all_to_all(array, 'mp', 0, 0)  26.3 us
    pallas_call x10, Pallas kernels, run(): pl.pallas_call(kernel, out_shape=outs, in_specs=[spec(a) for a in operand...  16.8 us
    all_to_all x1, blocking collectives, body(): lax.all_to_all(pair_block, 'dp', 0, 0)  16.2 us
    ppermute x3, waiting for transfers between devices, core_swap(): return lax.ppermute(array, 'mp', [(i, i ^ 1) for i in range(BLOCKS)])  3.94 us
    ppermute x3, starting transfers between devices, core_swap(): return lax.ppermute(array, 'mp', [(i, i ^ 1) for i in range(BLOCKS)])  3.56 us
    unnamed x30, local copies, waits for them, and re-layouts  2.46 us
  transfers between devices with their start and end apart: 3, of which 3 were waited for; matrix products, arithmetic and copies ran while one was open for 0% of the time, Pallas kernels for 1%

profile of v5, /device:TPU:1, one launch (start us, length us, event | category | flops | bytes accessed | tf_op | source)
XLA Modules:
  0.0 119.2 jit_solution(14492366299425136771)
XLA Ops:
  0.6 0.0 copy-start.3
  0.6 0.8 copy-done.3
  1.5 0.0 copy-start.13
  1.5 0.9 copy-done.13
  2.4 0.0 copy-start.14
  2.4 0.7 copy-done.14
  3.0 0.0 copy-start
  3.0 0.0 copy-start.1
  3.0 0.0 copy-start.4
  3.0 0.0 copy-start.5
  3.0 0.0 copy-start.7
  3.1 1.2 %shard_map.158 = (bf16[8,192,256]{2,1,0:T(8,128)(2,1)S(1)}, bf16[192,256]{1,0:T(8,128)(2,1)S(1)}, f32[4,192]{1,0:T(4,128)S(1)}) custom-call(bf16[4,8,8,192]{3,2,1,0:T(8,128)(2,1)S(1)} %copy-done.13, f32[7,7,192]{2,1,0:T(8,128)S(1)} %copy-done.3, f32[1,192]{1,0:T(1,128)S(1)} %bitcast.14), custom_call_target="tpu_custom_call" | custom-call | flops 16000000000 | bytes 136704 | tf_op jit(solution)/shard_map/pallas_call | solution.py:49
  4.3 20.3 %all_to_all.30.mine_ref = bf16[8,192,256]{2,1,0:T(8,128)(2,1)S(1)} all-to-all(bf16[8,192,256]{2,1,0:T(8,128)(2,1)S(1)} %get-tuple-element.20), channel_id=1, replica_groups={{0,2,4,6,8,10,12,14},{1,3,5,7,9,11,13,15},{16,18,20,22,24,26,28,30},{17..., dimensions={0} | all-to-all | bytes 1572864 | tf_op jit(solution)/shard_map/all_to_all | solution.py:30
  24.6 2.5 %collective-permute-start = (bf16[8,192,256]{2,1,0:T(8,128)(2,1)S(1)}, bf16[8,192,256]{2,1,0:T(8,128)(2,1)S(1)}, u32[]{:S(2)}, u32[]{:S(2)}) collective-permute-start(bf16[8,192,256]{2,1,0:T(8,128)(2,1)S(1)} %all_to_all.30.mine_ref), channel_id=1, source_target_pairs={{0,1},{1,0},{2,3},{3,2},{4,5},{5,4},{6,7},{7,6},{8,9},{9,8},{10,11... | collective-permute-start | bytes 2359304 | tf_op jit(solution)/shard_map/ppermute | solution.py:25
  27.1 1.9 %collective-permute-done.other_ref = bf16[8,192,256]{2,1,0:T(8,128)(2,1)S(1)} collective-permute-done((bf16[8,192,256]{2,1,0:T(8,128)(2,1)S(1)}, bf16[8,192,256]{2,1,0:T(8,128)(2,1)S(1)}, u32[]{:S(2)}, u32[]{:S(2)}) %collective-permute-start) | collective-permute-done | bytes 786464 | tf_op jit(solution)/shard_map/ppermute | solution.py:25
  29.1 0.0 copy-done
  29.1 0.0 copy-done.1
  29.1 0.0 copy-done.4
  29.1 0.0 copy-done.5
  29.1 0.0 copy-done.7
  29.1 0.0 copy-start.2
  29.1 0.0 copy-start.8
  29.1 0.0 copy-start.9
  29.1 0.0 copy-start.10
  29.1 0.0 copy-start.11
  29.1 0.0 copy-start.6
  29.2 0.0 copy-start.12
  29.2 6.1 %shard_map.159 = (f32[256,768]{1,0:T(8,128)S(1)}, f32[256,768]{1,0:T(8,128)S(1)}, f32[16,768]{1,0:T(8,128)S(1)}, f32[8,256]{1,0:T(8,128)S(1)}, f32[16,4,192]{2,1,0:T(4,128)S(1)}) custom-call(bf16[8,192,256]{2,1,0:T(8,128)(2,1)S(1)} %all_to_all.30.mine_ref, bf16[8,192,256]{2,1,0:T(8,128)(2,1)S(1)} %collective-permute-done.other_ref, f32[1,3072]{1,0:T(1,128)S(1)} %bitcast.7, ...), custom_call_target="tpu_custom_call" | custom-call | flops 1207959552 | bytes 11037696 | tf_op jit(solution)/shard_map/pallas_call | solution.py:49
  35.3 10.3 %all_to_all.31.got_ref = f32[16,4,192]{2,1,0:T(4,128)S(1)} all-to-all(f32[16,4,192]{2,1,0:T(4,128)S(1)} %get-tuple-element.21), channel_id=1, replica_groups=mesh['dp'=16,'mp'=16] {'mp'}, dimensions={0} | all-to-all | bytes 98304 | tf_op jit(solution)/shard_map/all_to_all | solution.py:34
  45.6 0.0 copy-done.2
  45.6 0.0 copy-done.8
  45.6 0.0 copy-done.9
  45.6 0.0 copy-done.10
  45.6 0.0 copy-done.11
  45.6 0.2 shard_map.160.mine_ref
  45.8 0.5 collective-permute-start.1
  46.3 0.9 collective-permute-done.1.other_ref
  47.2 0.1 shard_map.161
  47.3 11.8 %all_to_all.32.got_ref = f32[8,8,1536]{2,1,0:T(8,128)S(1)} all-to-all(f32[8,8,1536]{2,1,0:T(8,128)S(1)} %shard_map.161), channel_id=1, replica_groups={{0,2,4,6,8,10,12,14},{1,3,5,7,9,11,13,15},{16,18,20,22,24,26,28,30},{17..., dimensions={0} | all-to-all | bytes 786432 | tf_op jit(solution)/shard_map/all_to_all | solution.py:30
  59.1 0.0 copy-done.6
  59.1 0.0 copy-done.12
  59.1 0.7 shard_map.162
  59.8 16.2 %all_to_all.33.got_ref = bf16[16,16,640]{2,1,0:T(8,128)(2,1)S(1)} all-to-all(bf16[16,16,640]{2,1,0:T(8,128)(2,1)S(1)} %get-tuple-element.23), channel_id=1, replica_groups=mesh['dp'=16,'mp'=16] {'dp'}, dimensions={0} | all-to-all | bytes 655360 | tf_op jit(solution)/shard_map/all_to_all | solution.py:560
  76.0 2.4 %shard_map.163 = (f32[4,1024]{1,0:T(4,128)}, f32[16,4,192]{2,1,0:T(4,128)S(1)}) custom-call(bf16[16,16,640]{2,1,0:T(8,128)(2,1)S(1)} %all_to_all.33.got_ref, f32[8,1024]{1,0:T(8,128)S(1)} %get-tuple-element.24.own_ref, bf16[192,1024]{1,0:T(8,128)(2,1)S(1)} %copy-done.2), custom_call_target="tpu_custom_call" | custom-call | bytes 753664 | tf_op jit(solution)/shard_map/pallas_call | solution.py:49
  78.4 15.9 %all_to_all.34.back_ref = f32[16,4,192]{2,1,0:T(4,128)S(1)} all-to-all(f32[16,4,192]{2,1,0:T(4,128)S(1)} %get-tuple-element.25), channel_id=1, replica_groups=mesh['dp'=16,'mp'=16] {'mp'}, dimensions={0} | all-to-all | bytes 98304 | tf_op jit(solution)/shard_map/all_to_all | solution.py:34
  94.3 3.2 %shard_map.164 = (bf16[1552,256]{1,0:T(8,128)(2,1)S(1)}, bf16[768,256]{1,0:T(8,128)(2,1)S(1)}, f32[8,256]{1,0:T(8,128)S(1)}, f32[4,192]{1,0:T(4,128)S(1)}) custom-call(f32[16,4,192]{2,1,0:T(4,128)S(1)} %all_to_all.34.back_ref, f32[16,8,192]{2,1,0:T(8,128)S(1)} %get-tuple-element.26.head_ref, f32[2,8,128]{2,1,0:T(8,128)S(1)} %get-tuple-element.27.head_stat_ref, ...), custom_call_target="tpu_custom_call" | custom-call | flops 603979776 | bytes 11217920 | tf_op jit(solution)/shard_map/pallas_call | solution.py:49
  97.5 0.5 collective-permute-start.2
  98.0 0.8 shard_map.165.mine_ref
  98.8 1.2 collective-permute-done.2.got_ref
  100.0 0.2 shard_map.166
  100.2 17.1 %all_to_all.35.got_ref = bf16[8,208,256]{2,1,0:T(8,128)(2,1)S(1)} all-to-all(bf16[8,208,256]{2,1,0:T(8,128)(2,1)S(1)} %shard_map.166), channel_id=1, replica_groups={{0,2,4,6,8,10,12,14},{1,3,5,7,9,11,13,15},{16,18,20,22,24,26,28,30},{17..., dimensions={0} | all-to-all | bytes 1703936 | tf_op jit(solution)/shard_map/all_to_all | solution.py:30
  117.2 2.0 %shard_map.167 = f32[4,8,8,192]{3,2,1,0:T(8,128)} custom-call(bf16[8,208,256]{2,1,0:T(8,128)(2,1)S(1)} %all_to_all.35.got_ref, bf16[192,256]{1,0:T(8,128)(2,1)S(1)} %get-tuple-element.34.conv_ref, f32[8,256]{1,0:T(8,128)S(1)} %get-tuple-element.35.stat_ref, f32[1,3072]{1,0:T(1,128)S(1)} %bitcast.8, f32[7,7,192]{2,1,0:T(8,128)S(1)} %copy-done.3, ...), custom_call_target="tpu_custom_call" | custom-call | flops 4816896 | bytes 1011456 | tf_op jit(solution)/shard_map/pallas_call | solution.py:49
Async XLA Ops:
  0.6 0.8 copy-start.3
  1.5 0.9 copy-start.13
  2.4 0.7 copy-start.14
  3.0 26.0 %copy-start = (bf16[3072,768]{1,0:T(8,128)(2,1)S(1)}, bf16[3072,768]{1,0:T(8,128)(2,1)}, u32[]{:S(2)}) copy-start(bf16[3072,768]{1,0:T(8,128)(2,1)} %w_ref.6) | copy-start | bytes 14155780
  3.0 26.0 %copy-start.1 = (bf16[768,3072]{1,0:T(8,128)(2,1)S(1)}, bf16[768,3072]{1,0:T(8,128)(2,1)}, u32[]{:S(2)}) copy-start(bf16[768,3072]{1,0:T(8,128)(2,1)} %wout_ref.3) | copy-start | bytes 14155780
  3.0 26.0 %copy-start.4 = (f32[3072]{0:T(1024)S(1)}, f32[3072]{0:T(1024)}, u32[]{:S(2)}) copy-start(f32[3072]{0:T(1024)} %param.18) | copy-start | bytes 36868
  3.0 26.0 %copy-start.5 = (f32[768]{0:T(1024)S(1)}, f32[768]{0:T(1024)}, u32[]{:S(2)}) copy-start(f32[768]{0:T(1024)} %b_ref.3) | copy-start | bytes 9220
  3.0 26.0 %copy-start.7 = (f32[3072]{0:T(1024)S(1)}, f32[3072]{0:T(1024)}, u32[]{:S(2)}) copy-start(f32[3072]{0:T(1024)} %param.19) | copy-start | bytes 36868
  24.6 4.4 %collective-permute-start = (bf16[8,192,256]{2,1,0:T(8,128)(2,1)S(1)}, bf16[8,192,256]{2,1,0:T(8,128)(2,1)S(1)}, u32[]{:S(2)}, u32[]{:S(2)}) collective-permute-start(bf16[8,192,256]{2,1,0:T(8,128)(2,1)S(1)} %all_to_all.30.mine_ref), channel_id=1, source_target_pairs={{0,1},{1,0},{2,3},{3,2},{4,5},{5,4},{6,7},{7,6},{8,9},{9,8},{10,11... | collective-permute-start | bytes 2359304 | tf_op jit(solution)/shard_map/ppermute | solution.py:25
  29.1 16.5 %copy-start.2 = (bf16[192,1024]{1,0:T(8,128)(2,1)S(1)}, bf16[192,1024]{1,0:T(8,128)(2,1)}, u32[]{:S(2)}) copy-start(bf16[192,1024]{1,0:T(8,128)(2,1)} %project_ref.3) | copy-start | bytes 1179652
  29.1 16.5 %copy-start.8 = (f32[192]{0:T(256)S(1)}, f32[192]{0:T(256)}, u32[]{:S(2)}) copy-start(f32[192]{0:T(256)} %param.24) | copy-start | bytes 2308
  29.1 16.5 %copy-start.9 = (f32[192]{0:T(256)S(1)}, f32[192]{0:T(256)}, u32[]{:S(2)}) copy-start(f32[192]{0:T(256)} %param.23) | copy-start | bytes 2308
  29.1 16.5 %copy-start.10 = (f32[192]{0:T(256)S(1)}, f32[192]{0:T(256)}, u32[]{:S(2)}) copy-start(f32[192]{0:T(256)} %param.25) | copy-start | bytes 2308
  29.1 16.5 %copy-start.11 = (f32[192]{0:T(256)S(1)}, f32[192]{0:T(256)}, u32[]{:S(2)}) copy-start(f32[192]{0:T(256)} %param.26) | copy-start | bytes 2308
  29.1 29.9 %copy-start.6 = (f32[4,1024]{1,0:T(4,128)S(1)}, f32[4,1024]{1,0:T(4,128)}, u32[]{:S(2)}) copy-start(f32[4,1024]{1,0:T(4,128)} %text_ref.1) | copy-start | bytes 49156
  29.2 29.9 %copy-start.12 = (s32[4]{0:T(128)S(1)}, s32[4]{0:T(128)}, u32[]{:S(2)}) copy-start(s32[4]{0:T(128)} %labels_ref.1) | copy-start | bytes 52
  45.8 1.4 %collective-permute-start.1 = (f32[8,1408]{1,0:T(8,128)S(1)}, f32[8,1408]{1,0:T(8,128)S(1)}, u32[]{:S(2)}, u32[]{:S(2)}) collective-permute-start(f32[8,1408]{1,0:T(8,128)S(1)} %shard_map.160.mine_ref), channel_id=1, source_target_pairs={{0,1},{1,0},{2,3},{3,2},{4,5},{5,4},{6,7},{7,6},{8,9},{9,8},{10,11... | collective-permute-start | bytes 135176 | tf_op jit(solution)/shard_map/ppermute | solution.py:25
  97.5 2.5 %collective-permute-start.2 = (bf16[1552,256]{1,0:T(8,128)(2,1)S(1)}, bf16[1552,256]{1,0:T(8,128)(2,1)S(1)}, u32[]{:S(2)}, u32[]{:S(2)}) collective-permute-start(bf16[1552,256]{1,0:T(8,128)(2,1)S(1)} %get-tuple-element.32), channel_id=1, source_target_pairs={{0,1},{1,0},{2,3},{3,2},{4,5},{5,4},{6,7},{7,6},{8,9},{9,8},{10,11... | collective-permute-start | bytes 2383880 | tf_op jit(solution)/shard_map/ppermute | solution.py:25

commit v6 on v5

--- a/solution.py
+++ b/solution.py
@@ -16,9 +16,11 @@
 MIB = 1 << 20
 CONV_LIMIT = 50 * MIB
 CONV_FLOPS = 16 * 10**9
+START_FLOPS = 4 * 10**9
 CHIPS = 8
 BLOCKS = 16
 SHARD = 192
+POSITIONS = 64
 
 
 def core_swap(array):
@@ -97,8 +99,19 @@
     return acc
 
 
+def start_kernel(labels_ref, tail_ref):
+    pairs = labels_ref.shape[0]
+    row = iota((8, 128), 0)
+    tail = jnp.zeros((8, 128), f32)
+    for r in range(pairs):
+        label = labels_ref[r]
+        target = (label // pairs) * 8 + 4 + label % pairs
+        tail = jnp.where(row == r, target.astype(f32), tail)
+    tail_ref[...] = tail
+
+
 def conv_kernel(
-    x_far, dw_far, bias_far, copies_ref, conv_ref, mean_ref, x_ref, dw_ref, bias_ref, rows_ref, sems
+    _, x_far, dw_far, bias_far, copies_ref, conv_ref, mean_ref, x_ref, dw_ref, bias_ref, rows_ref, sems
 ):
     images, side = x_ref.shape[:2]
     positions = side * side
@@ -124,11 +137,52 @@
         copies_ref[j] = turned
 
 
+def ready_kernel(
+    mine_ref, gain_ref, bias_ref, w_ref, rows_ref, part_ref, vec_ref, own_ref, sems
+):
+    shard = w_ref.shape[0] // BLOCKS
+    core = lax.axis_index("mp") % 2
+    moves = []
+    for k in range(BLOCKS):
+        place = 2 * (k % CHIPS) + (core if k < CHIPS else 1 - core)
+        source = pl.ds(pl.multiple_of(place * shard, 64), shard)
+        moves.append(
+            pltpu.make_async_copy(
+                w_ref.at[source], own_ref.at[k * shard : (k + 1) * shard], sems.at[k]
+            )
+        )
+    for copy in moves:
+        copy.start()
+    half, rows = mine_ref.shape
+    step = 256
+    first = jnp.zeros((1, rows), f32)
+    second = jnp.zeros((1, rows), f32)
+    for c in range(half // step):
+        at = slice(c * step, (c + 1) * step)
+        rows_ref[:, at] = mine_ref[at, :].T
+        value = mine_ref[at, :].astype(f32)
+        first = first + jnp.sum(value, axis=0, keepdims=True)
+        second = second + jnp.sum(value * value, axis=0, keepdims=True)
+    part_ref[0:1, :] = first
+    part_ref[1:2, :] = second
+    vec_ref[...] = jnp.zeros_like(vec_ref)
+    for i, ref in enumerate((gain_ref, bias_ref)):
+        for j in range(CHIPS):
+            low = ref[:, 2 * j * shard : (2 * j + 1) * shard]
+            high = ref[:, (2 * j + 1) * shard : (2 * j + 2) * shard]
+            vec_ref[i : i + 1, j * shard : (j + 1) * shard] = jnp.where(core == 0, low, high)
+            vec_ref[i : i + 1, half + j * shard : half + (j + 1) * shard] = jnp.where(
+                core == 0, high, low
+            )
+    for copy in moves:
+        copy.wait()
+
+
 def forward_kernel(
-    mine_ref,
+    rows_ref,
     other_ref,
-    gain_ref,
-    bias_ref,
+    part_ref,
+    vec_ref,
     w_ref,
     b_ref,
     wout_ref,
@@ -137,47 +191,33 @@
     through_ref,
     stat_ref,
     mixed_ref,
-    turned_ref,
     normed_ref,
-    own_ref,
-    vec_ref,
 ):
-    shard, rows = mine_ref.shape[1:]
+    half, rows = other_ref.shape
     channels, hidden = w_ref.shape
-    images = mixed_ref.shape[1]
+    images, shard = mixed_ref.shape[1:]
     positions = rows // images
-    core = lax.axis_index("mp") % 2
-    vec_ref[...] = jnp.zeros_like(vec_ref)
-    for i, ref in enumerate((gain_ref, bias_ref)):
-        vec_ref[i : i + 1, :] = ref[...]
-        for j in range(CHIPS):
-            low = ref[:, 2 * j * shard : (2 * j + 1) * shard]
-            high = ref[:, (2 * j + 1) * shard : (2 * j + 2) * shard]
-            at = i * BLOCKS + j
-            own_ref[at : at + 1, :] = jnp.where(core == 0, low, high)
-            own_ref[at + CHIPS : at + CHIPS + 1, :] = jnp.where(core == 0, high, low)
-    first = jnp.zeros((1, rows), f32)
-    second = jnp.zeros((1, rows), f32)
-    for ref in (mine_ref, other_ref):
-        for j in range(CHIPS):
-            value = ref[j].astype(f32)
-            first = first + jnp.sum(value, axis=0, keepdims=True)
-            second = second + jnp.sum(value * value, axis=0, keepdims=True)
+    step = 256
+    first, second = part_ref[0:1, :], part_ref[1:2, :]
+    for c in range(half // step):
+        value = other_ref[c * step : (c + 1) * step, :].astype(f32)
+        first = first + jnp.sum(value, axis=0, keepdims=True)
+        second = second + jnp.sum(value * value, axis=0, keepdims=True)
     average = first / channels
     inverse = lax.rsqrt(second / channels - average * average + eps)
-    stat_ref[0:1, :] = average
-    stat_ref[1:2, :] = inverse
-    own = own_ref[...].T
-    for h, ref in enumerate((mine_ref, other_ref)):
-        for j in range(CHIPS):
-            k = h * CHIPS + j
-            value = (ref[j].astype(f32) - average) * inverse
-            value = value * own[:, k : k + 1] + own[:, BLOCKS + k : BLOCKS + k + 1]
-            start = (2 * j + (core if h == 0 else 1 - core)) * shard
-            turned_ref[pl.ds(pl.multiple_of(start, 64), shard), :] = value.astype(bf16)
-    step = 256
+    lane = iota((8, rows), 0)
+    stat_ref[...] = jnp.where(lane == 0, average, jnp.where(lane == 1, inverse, 0.0))
+    turned = stat_ref[...].T
+    average = jnp.broadcast_to(turned[:, 0:1], (rows, step))
+    inverse = jnp.broadcast_to(turned[:, 1:2], (rows, step))
     for c in range(channels // step):
-        normed_ref[0:rows, c * step : (c + 1) * step] = turned_ref[c * step : (c + 1) * step, :].T
+        at = slice(c * step, (c + 1) * step)
+        if c * step < half:
+            value = rows_ref[:, at]
+        else:
+            value = other_ref[c * step - half : (c + 1) * step - half, :].T
+        value = (value.astype(f32) - average) * inverse
+        normed_ref[0:rows, at] = (value * vec_ref[0:1, at] + vec_ref[1:2, at]).astype(bf16)
     normed_ref[rows : rows + 16, :] = jnp.concatenate(to_terms(vec_ref[...]), axis=0).astype(bf16)
     b_row = b_ref[...][None, :]
     for t in range(hidden // step):
@@ -207,7 +247,7 @@
 
 
 def head_kernel(
-    got_ref, mean_ref, scale_ref, bout_ref, gain_ref, bias_ref, project_ref, out_ref
+    got_ref, mean_ref, scale_ref, bout_ref, gain_ref, bias_ref, project_ref, out_ref, pooled_ref
 ):
     images, shard = got_ref.shape[1:]
     width = project_ref.shape[1]
@@ -216,9 +256,9 @@
         mixed = mixed + got_ref[j]
     scale, bias_out = scale_ref[...], bout_ref[...]
     gain, bias = gain_ref[...], bias_ref[...]
-    head = jnp.concatenate(
-        [mean_ref[...] + scale * (mixed + bias_out), scale, bias_out, gain, bias], axis=0
-    )
+    pooled = mean_ref[...] + scale * (mixed + bias_out)
+    pooled_ref[...] = pooled
+    head = jnp.concatenate([pooled, scale, bias_out, gain, bias], axis=0)
     first = jnp.sum(head, axis=1, keepdims=True)
     second = jnp.sum(head * head, axis=1, keepdims=True)
     value = jnp.where(iota((8, shard), 0) < images, head * gain, head)
@@ -234,43 +274,26 @@
     out_ref[:, width : width + 128] = jnp.where(
         lane == 0, first, jnp.where(lane == 1, second, 0.0)
     )
-    out_ref[:, width + 128 : width + 128 + shard] = head
 
 
 def pair_sum_kernel(mine_ref, other_ref, out_ref):
-    cut = out_ref.shape[2] - 2 * SHARD
-    block = jnp.concatenate(
-        [
-            mine_ref[:, :cut] + other_ref[:, :cut],
-            mine_ref[:, cut : cut + SHARD],
-            other_ref[:, cut : cut + SHARD],
-        ],
-        axis=1,
-    )
+    block = mine_ref[...] + other_ref[...]
     for j in range(CHIPS):
         out_ref[j] = block
 
 
-def embed_kernel(got_ref, text_ref, labels_ref, out_ref, own_ref, head_ref, stat_ref):
-    pairs, width = text_ref.shape
-    cut = width + 128
-    core = lax.axis_index("mp") % 2
+def embed_kernel(got_ref, text_ref, tail_ref, out_ref, own_ref, back_ref, stat_ref):
+    width = text_ref.shape[1]
     channels = BLOCKS * SHARD
-    for j in range(CHIPS):
-        head_ref[2 * j + core] = got_ref[j, :, cut : cut + SHARD]
-        head_ref[2 * j + 1 - core] = got_ref[j, :, cut + SHARD :]
-    sums = got_ref[0, :, :cut]
+    sums = got_ref[0]
     for j in range(1, CHIPS):
-        sums = sums + got_ref[j, :, :cut]
+        sums = sums + got_ref[j]
     mean = sums[:, width : width + 1] / channels
     inverse = lax.rsqrt(sums[:, width + 1 : width + 2] / channels - mean * mean + eps)
-    emb = inverse * (sums[:, :width] - mean * sums[6:7, :width]) + sums[7:8, :width]
-    row = iota((8, 128), 0)
-    tail = jnp.zeros((8, 128), f32)
-    for r in range(pairs):
-        label = labels_ref[r]
-        target = (label // pairs) * 8 + 4 + label % pairs
-        tail = jnp.where(row == r, target.astype(f32), tail)
+    centred = inverse * (sums[:, :width] - mean * sums[6:7, :width])
+    emb = centred + sums[7:8, :width]
+    back_ref[...] = jnp.concatenate([centred[:4], sums[4:, :width]], axis=0)
+    tail = tail_ref[...]
     block = jnp.concatenate([emb[:4], text_ref[...]], axis=0)
     own_ref[...] = block
     half = width // 2
@@ -283,7 +306,20 @@
     stat_ref[1] = jnp.broadcast_to(inverse, (8, 128))
 
 
-def loss_kernel(got_ref, own_ref, project_ref, text_ref, back_ref, both_ref):
+def loss_kernel(
+    got_ref,
+    own_ref,
+    rows_ref,
+    stat_ref,
+    pooled_ref,
+    scale_ref,
+    gain_ref,
+    project_ref,
+    text_ref,
+    block_ref,
+    mixed_ref,
+    both_ref,
+):
     width = project_ref.shape[1]
     count = got_ref.shape[0] * 8
     home = pl.ds(pl.multiple_of(lax.axis_index("dp") * 8, 8), 8)
@@ -314,20 +350,27 @@
     own = own / length
     grad = (grad_unit - own * jnp.sum(own * grad_unit, axis=1, keepdims=True)) / length
     text_ref[...] = grad[4:]
+    grad = grad[:4].astype(bf16)
     back = lax.dot_general(
-        grad.astype(bf16),
+        jnp.concatenate([grad, jnp.zeros_like(grad)], axis=0),
         project_ref[...],
         (((1,), (1,)), ((), ())),
         preferred_element_type=f32,
-    )
+    )[:4]
+    channels = BLOCKS * SHARD
+    grad = grad.astype(f32)
+    first = jnp.sum(grad * rows_ref[6:7, :], axis=1, keepdims=True) / channels
+    second = jnp.sum(grad * rows_ref[:4, :], axis=1, keepdims=True) / channels
+    mean, inverse = stat_ref[0][:4, 0:1], stat_ref[1][:4, 0:1]
+    centred = (pooled_ref[...] - mean) * inverse
+    block = (inverse / POSITIONS) * (back * gain_ref[...] - first - centred * second)
+    block_ref[...] = block
     for k in range(BLOCKS):
-        back_ref[k] = back[:4]
+        mixed_ref[k] = block * scale_ref[...]
 
 
 def backward_kernel(
-    back_ref,
-    head_ref,
-    head_stat_ref,
+    got_ref,
     wout_ref,
     slope_ref,
     hidden_ref,
@@ -337,41 +380,16 @@
     other_ref,
     turned_ref,
     sums_ref,
-    block_ref,
     mixed_ref,
     pre_ref,
 ):
-    images, shard = back_ref.shape[1:]
+    images, shard = got_ref.shape[1:]
     rows, hidden = slope_ref.shape
     channels = w_ref.shape[0]
     positions = rows // images
-    index = lax.axis_index("mp")
-    core = index % 2
-    mean = head_stat_ref[0][:images, 0:1]
-    inverse = head_stat_ref[1][:images, 0:1]
-    first = jnp.zeros((images, 1), f32)
-    second = jnp.zeros((images, 1), f32)
-
-    def parts(k):
-        head = head_ref[k]
-        return back_ref[k] * head[6:7], (head[:images] - mean) * inverse, head[4:5]
-
-    for k in range(BLOCKS):
-        scaled, centred, _ = parts(k)
-        first = first + jnp.sum(scaled, axis=1, keepdims=True)
-        second = second + jnp.sum(scaled * centred, axis=1, keepdims=True)
-    first = first / channels
-    second = second / channels
-
-    def block(k):
-        scaled, centred, scale = parts(k)
-        grad = (inverse / positions) * (scaled - first - centred * second)
-        return grad, grad * scale
-
-    block_ref[...] = block(index)[0]
     mixed_ref[...] = jnp.zeros_like(mixed_ref)
     for k in range(BLOCKS):
-        mixed_ref[0:images, k * shard : (k + 1) * shard] = block(k)[1]
+        mixed_ref[0:images, k * shard : (k + 1) * shard] = got_ref[k]
     act = lax.dot_general(
         mixed_ref[...].astype(bf16),
         wout_ref[...],
@@ -398,20 +416,21 @@
     sums_ref[...] = sums
     high, low = to_terms(sums)
     other_ref[channels // 2 :, :] = jnp.concatenate([high, low], axis=0).astype(bf16)
-    for j in range(CHIPS):
-        start = pl.multiple_of((2 * j + 1 - core) * shard, 64)
-        other_ref[j * shard : (j + 1) * shard, :] = jnp.dot(
-            w_ref[pl.ds(start, shard), :], turned_ref[...], preferred_element_type=f32
+    half = channels // 2
+    for c in range(half // step):
+        other_ref[c * step : (c + 1) * step, :] = jnp.dot(
+            w_ref[half + c * step : half + (c + 1) * step, :],
+            turned_ref[...],
+            preferred_element_type=f32,
         ).astype(bf16)
 
 
 def mine_kernel(w_ref, turned_ref, mine_ref):
-    shard = w_ref.shape[0] // BLOCKS
-    core = lax.axis_index("mp") % 2
-    for j in range(CHIPS):
-        start = pl.multiple_of((2 * j + core) * shard, 64)
-        mine_ref[j * shard : (j + 1) * shard, :] = jnp.dot(
-            w_ref[pl.ds(start, shard), :], turned_ref[...], preferred_element_type=f32
+    step = 256
+    for c in range(mine_ref.shape[0] // step):
+        at = slice(c * step, (c + 1) * step)
+        mine_ref[at, :] = jnp.dot(
+            w_ref[at, :], turned_ref[...], preferred_element_type=f32
         ).astype(bf16)
 
 
@@ -482,6 +501,7 @@
     rows = images * side * side
     pairs, width = text_emb.shape
     shards = lax.axis_size("dp")
+    (tail,) = run(start_kernel, [shape(8, 128)], labels, flops=START_FLOPS)
     copies, conv, input_mean = run(
         conv_kernel,
         [
@@ -489,6 +509,7 @@
             shape(shard, rows, dtype=bf16),
             shape(images, shard),
         ],
+        Far(tail),
         Far(x_in),
         Far(dw_weight),
         Far(dw_bias[None, :]),
@@ -504,6 +525,22 @@
     )
     conv_mine = chip_exchange(copies)
     conv_other = core_swap(conv_mine)
+    conv_mine = conv_mine.reshape(channels // 2, rows)
+    conv_other = conv_other.reshape(channels // 2, rows)
+    own_rows, part, vec, w_own = run(
+        ready_kernel,
+        [
+            shape(rows, channels // 2, dtype=bf16),
+            shape(8, rows),
+            shape(8, channels),
+            shape(channels, hidden, dtype=bf16),
+        ],
+        conv_mine,
+        ln_gain[None, :],
+        ln_bias[None, :],
+        w_in,
+        scratch=[pltpu.SemaphoreType.DMA((BLOCKS,))],
+    )
     slope, hidden_pre, through, row_stat, mixed = run(
         forward_kernel,
         [
@@ -513,24 +550,19 @@
             shape(8, rows),
             shape(BLOCKS, images, shard),
         ],
-        conv_mine,
+        own_rows,
         conv_other,
-        ln_gain[None, :],
-        ln_bias[None, :],
-        w_in,
+        part,
+        vec,
+        w_own,
         b_in,
         w_out,
-        scratch=[
-            pltpu.VMEM((channels, rows), bf16),
-            pltpu.VMEM((rows + 16, channels), bf16),
-            pltpu.VMEM((2 * BLOCKS, shard), f32),
-            pltpu.VMEM((8, channels), f32),
-        ],
+        scratch=[pltpu.VMEM((rows + 16, channels), bf16)],
         flops=2 * rows * channels * hidden,
     )
-    (sums,) = run(
+    sums, pooled = run(
         head_kernel,
-        [shape(8, width + 128 + 256)],
+        [shape(8, width + 128), shape(images, shard)],
         shard_exchange(mixed),
         input_mean,
         layer_scale[None, :],
@@ -540,43 +572,45 @@
         projection,
     )
     (blocks,) = run(
-        pair_sum_kernel, [shape(CHIPS, 8, width + 128 + 2 * shard)], sums, core_swap(sums)
-    )
-    pair_block, own_block, head, head_stat = run(
+        pair_sum_kernel, [shape(CHIPS, 8, width + 128)], sums, core_swap(sums)
+    )
+    pair_block, own_block, back_rows, head_stat = run(
         embed_kernel,
         [
             shape(shards, 16, width // 2 + 128, dtype=bf16),
             shape(8, width),
-            shape(BLOCKS, 8, shard),
+            shape(8, width),
             shape(2, 8, 128),
         ],
         chip_exchange(blocks),
         text_emb,
-        labels,
-    )
-    grad_text, back = run(
+        tail,
+    )
+    grad_text, grad_block, mixed_block = run(
         loss_kernel,
-        [shape(pairs, width), shape(BLOCKS, images, shard)],
+        [shape(pairs, width), shape(images, shard), shape(BLOCKS, images, shard)],
         lax.all_to_all(pair_block, "dp", 0, 0),
         own_block,
+        back_rows,
+        head_stat,
+        pooled,
+        layer_scale[None, :],
+        head_gain[None, :],
         projection,
         scratch=[pltpu.VMEM((shards * 8, shards * 8), f32)],
     )
-    other, turned, row_sums, grad_block = run(
+    other, turned, row_sums = run(
         backward_kernel,
         [
             shape(channels // 2 + 16, rows, dtype=bf16),
             shape(hidden, rows, dtype=bf16),
             shape(8, rows),
-            shape(images, shard),
         ],
-        shard_exchange(back),
-        head,
-        head_stat,
+        shard_exchange(mixed_block),
         w_out,
         slope,
         hidden_pre,
-        w_in,
+        w_own,
         through,
         b_in,
         scratch=[pltpu.VMEM((8, channels), f32), pltpu.VMEM((rows, 256), f32)],
@@ -586,7 +620,7 @@
     (mine,) = run(
         mine_kernel,
         [shape(channels // 2, rows, dtype=bf16)],
-        w_in,
+        w_own,
         turned,
         flops=rows * channels * hidden,
     )

time: 120 us -> 115 us (0.958)
  local copies, waits for them, and re-layouts: 2.46 us -> 0.78 us
  waiting for transfers between devices: 3.94 us -> 2.28 us
    unnamed x30 -> x34, local copies, waits for them, and re-layouts: 2.46 us -> 0.78 us
    ppermute x3, waiting for transfers between devices: 3.94 us -> 2.28 us  [core_swap(): return lax.ppermute(array, 'mp', [(i, i ^ 1) for i in range(BLOCKS)])]
    all_to_all x2, blocking collectives: 26.3 us -> 24.6 us  [shard_exchange(): return lax.all_to_all(array, 'mp', 0, 0)]
    pallas_call x10 -> x12, Pallas kernels: 16.8 us -> 17.1 us  [run(): pl.pallas_call(kernel, out_shape=outs, in_specs=[spec(a) for a in operand...]
  transfers between devices with their start and end apart: 3 -> 3, of which waited for: 3 -> 3; matrix products, arithmetic and copies ran while one was open for 0% -> 0% of each run, Pallas kernels for 1% -> 2%
where the time goes in v6:
time: 115 us
  blocking collectives  90.5 us (79%)
  Pallas kernels  17.1 us (15%)
  starting transfers between devices  3.56 us (3%)
  waiting for transfers between devices  2.28 us (2%)
    all_to_all x3, blocking collectives, chip_exchange(): return lax.all_to_all(array, 'mp', 0, 0, axis_index_groups=groups)  48.8 us
    all_to_all x2, blocking collectives, shard_exchange(): return lax.all_to_all(array, 'mp', 0, 0)  24.6 us
    all_to_all x1, blocking collectives, body(): lax.all_to_all(pair_block, 'dp', 0, 0)  17.1 us
    pallas_call x12, Pallas kernels, run(): pl.pallas_call(kernel, out_shape=outs, in_specs=[spec(a) for a in operand...  17.1 us
    ppermute x3, starting transfers between devices, core_swap(): return lax.ppermute(array, 'mp', [(i, i ^ 1) for i in range(BLOCKS)])  3.56 us
  transfers between devices with their start and end apart: 3, of which 3 were waited for; matrix products, arithmetic and copies ran while one was open for 0% of the time, Pallas kernels for 2%

profile of v6, /device:TPU:1, one launch (start us, length us, event | category | flops | bytes accessed | tf_op | source)
XLA Modules:
  0.0 115.1 jit_solution(3804819575282328786)
XLA Ops:
  0.6 0.0 copy-start.1
  0.6 0.0 copy-start.11
  0.7 0.0 copy-start.10
  0.7 0.0 copy-start.12
  0.7 0.7 copy-done.12
  1.4 0.0 slice-start.2
  1.4 0.6 shard_map.158._.tail_ref
  1.9 0.0 slice-start
  1.9 0.0 copy-done.1
  2.0 0.0 copy-done.11
  2.0 0.0 copy-done.10
  2.0 0.0 slice-start.3
  2.0 0.0 copy-start.2
  2.0 0.0 copy-start.5
  2.0 0.0 slice-start.1
  2.0 1.2 %shard_map.159 = (bf16[8,192,256]{2,1,0:T(8,128)(2,1)S(1)}, bf16[192,256]{1,0:T(8,128)(2,1)S(1)}, f32[4,192]{1,0:T(4,128)S(1)}) custom-call(f32[8,128]{1,0:T(8,128)S(1)} %shard_map.158._.tail_ref, bf16[4,8,8,192]{3,2,1,0:T(8,128)(2,1)S(1)} %copy-done.10, f32[7,7,192]{2,1,0:T(8,128)S(1)} %copy-done.1, f32[1,192]{1,0:T(1,128)S(1)} %bitcast.24), custom_call_target="tpu_custom_call" | custom-call | flops 16000000000 | bytes 140800 | tf_op jit(solution)/shard_map/pallas_call | solution.py:51
  3.3 0.0 copy-start.3
  3.3 20.3 %all_to_all.30 = bf16[8,192,256]{2,1,0:T(8,128)(2,1)S(1)} all-to-all(bf16[8,192,256]{2,1,0:T(8,128)(2,1)S(1)} %get-tuple-element.26), channel_id=1, replica_groups={{0,2,4,6,8,10,12,14},{1,3,5,7,9,11,13,15},{16,18,20,22,24,26,28,30},{17..., dimensions={0} | all-to-all | bytes 1572864 | tf_op jit(solution)/shard_map/all_to_all | solution.py:32
  23.6 2.5 %collective-permute-start = (bf16[8,192,256]{2,1,0:T(8,128)(2,1)S(1)}, bf16[8,192,256]{2,1,0:T(8,128)(2,1)S(1)}, u32[]{:S(2)}, u32[]{:S(2)}) collective-permute-start(bf16[8,192,256]{2,1,0:T(8,128)(2,1)S(1)} %all_to_all.30), channel_id=1, source_target_pairs={{0,1},{1,0},{2,3},{3,2},{4,5},{5,4},{6,7},{7,6},{8,9},{9,8},{10,11... | collective-permute-start | bytes 2359304 | tf_op jit(solution)/shard_map/ppermute | solution.py:27
  26.1 0.0 slice-done.2
  26.1 0.0 slice-done.3
  26.1 0.0 copy-done.2
  26.1 0.0 copy-done.5
  26.1 1.6 %shard_map.160 = (bf16[256,1536]{1,0:T(8,128)(2,1)S(1)}, f32[8,256]{1,0:T(8,128)S(1)}, f32[8,3072]{1,0:T(8,128)S(1)}, bf16[3072,768]{1,0:T(8,128)(2,1)S(1)}) custom-call(bf16[1536,256]{1,0:T(8,128)(2,1)S(1)} %bitcast.13, f32[1,3072]{1,0:T(1,128)S(1)} %bitcast.15, f32[1,3072]{1,0:T(1,128)S(1)} %bitcast.17, bf16[3072,768]{1,0:T(8,128)(2,1)S(1)} %bitcast.12), custom_call_target="tpu_custom_call" | custom-call | bytes 5529600 | tf_op jit(solution)/shard_map/pallas_call | solution.py:51
  27.8 0.3 collective-permute-done
  28.0 0.0 slice-done
  28.0 0.0 slice-done.1
  28.0 0.0 copy-done.3
  28.0 0.0 copy-start
  28.1 0.0 copy-start.6
  28.1 0.0 copy-start.7
  28.1 0.0 copy-start.8
  28.1 0.0 copy-start.9
  28.1 0.0 copy-start.4
  28.1 4.9 %shard_map.161 = (f32[256,768]{1,0:T(8,128)S(1)}, f32[256,768]{1,0:T(8,128)S(1)}, f32[16,768]{1,0:T(8,128)S(1)}, f32[8,256]{1,0:T(8,128)S(1)}, f32[16,4,192]{2,1,0:T(4,128)S(1)}) custom-call(bf16[256,1536]{1,0:T(8,128)(2,1)S(1)} %get-tuple-element.28.rows_ref, bf16[1536,256]{1,0:T(8,128)(2,1)S(1)} %bitcast.14, f32[8,256]{1,0:T(8,128)S(1)} %get-tuple-element.29.part_ref, ...), custom_call_target="tpu_custom_call" | custom-call | flops 1207959552 | bytes 11119616 | tf_op jit(solution)/shard_map/pallas_call | solution.py:51
  33.1 10.3 %all_to_all.31.got_ref = f32[16,4,192]{2,1,0:T(4,128)S(1)} all-to-all(f32[16,4,192]{2,1,0:T(4,128)S(1)} %get-tuple-element.31), channel_id=1, replica_groups=mesh['dp'=16,'mp'=16] {'mp'}, dimensions={0} | all-to-all | bytes 98304 | tf_op jit(solution)/shard_map/all_to_all | solution.py:36
  43.4 0.0 copy-done
  43.4 0.0 copy-done.6
  43.4 0.0 copy-done.7
  43.4 0.0 copy-done.8
  43.4 0.0 copy-done.9
  43.4 0.2 shard_map.162
  43.6 0.5 collective-permute-start.1
  44.1 0.9 collective-permute-done.1.other_ref
  45.0 11.4 %all_to_all.32.got_ref = f32[8,8,1152]{2,1,0:T(8,128)S(1)} all-to-all(f32[8,8,1152]{2,1,0:T(8,128)S(1)} %shard_map.163), channel_id=1, replica_groups={{0,2,4,6,8,10,12,14},{1,3,5,7,9,11,13,15},{16,18,20,22,24,26,28,30},{17..., dimensions={0} | all-to-all | bytes 589824 | tf_op jit(solution)/shard_map/all_to_all | solution.py:32
  56.4 0.0 copy-done.4
  56.4 0.2 shard_map.164
  56.6 17.1 %all_to_all.33.got_ref = bf16[16,16,640]{2,1,0:T(8,128)(2,1)S(1)} all-to-all(bf16[16,16,640]{2,1,0:T(8,128)(2,1)S(1)} %get-tuple-element.34), channel_id=1, replica_groups=mesh['dp'=16,'mp'=16] {'dp'}, dimensions={0} | all-to-all | bytes 655360 | tf_op jit(solution)/shard_map/all_to_all | solution.py:592
  73.6 2.4 %shard_map.165 = (f32[4,1024]{1,0:T(4,128)}, f32[4,192]{1,0:T(4,128)S(1)}, f32[16,4,192]{2,1,0:T(4,128)S(1)}) custom-call(bf16[16,16,640]{2,1,0:T(8,128)(2,1)S(1)} %all_to_all.33.got_ref, f32[8,1024]{1,0:T(8,128)S(1)} %get-tuple-element.35.own_ref, f32[8,1024]{1,0:T(8,128)S(1)} %get-tuple-element.36.rows_ref, f32[2,8,128]{2,1,0:T(8,128)S(1)} %get-tuple-element.37.stat_ref, ...), custom_call_target="tpu_custom_call" | custom-call | bytes 799232 | tf_op jit(solution)/shard_map/pallas_call | solution.py:51
  76.0 14.3 %all_to_all.34.got_ref = f32[16,4,192]{2,1,0:T(4,128)S(1)} all-to-all(f32[16,4,192]{2,1,0:T(4,128)S(1)} %get-tuple-element.39), channel_id=1, replica_groups=mesh['dp'=16,'mp'=16] {'mp'}, dimensions={0} | all-to-all | bytes 98304 | tf_op jit(solution)/shard_map/all_to_all | solution.py:36
  90.3 2.9 %shard_map.166 = (bf16[1552,256]{1,0:T(8,128)(2,1)S(1)}, bf16[768,256]{1,0:T(8,128)(2,1)S(1)}, f32[8,256]{1,0:T(8,128)S(1)}) custom-call(f32[16,4,192]{2,1,0:T(4,128)S(1)} %all_to_all.34.got_ref, bf16[768,3072]{1,0:T(8,128)(2,1)S(1)} %bitcast.10, f32[256,768]{1,0:T(8,128)S(1)} %get-tuple-element.40.slope_ref, f32[256,768]{1,0:T(8,128)S(1)} %get-tuple-element.41.hidden_ref, ...), custom_call_target="tpu_custom_call" | custom-call | flops 603979776 | bytes 11111424 | tf_op jit(solution)/shard_map/pallas_call | solution.py:51
  93.3 0.5 collective-permute-start.2
  93.8 0.8 shard_map.167.mine_ref
  94.6 1.1 collective-permute-done.2.got_ref
  95.7 0.2 shard_map.168
  95.9 17.1 %all_to_all.35.got_ref = bf16[8,208,256]{2,1,0:T(8,128)(2,1)S(1)} all-to-all(bf16[8,208,256]{2,1,0:T(8,128)(2,1)S(1)} %shard_map.168), channel_id=1, replica_groups={{0,2,4,6,8,10,12,14},{1,3,5,7,9,11,13,15},{16,18,20,22,24,26,28,30},{17..., dimensions={0} | all-to-all | bytes 1703936 | tf_op jit(solution)/shard_map/all_to_all | solution.py:32
  113.0 2.1 %shard_map.169 = f32[4,8,8,192]{3,2,1,0:T(8,128)} custom-call(bf16[8,208,256]{2,1,0:T(8,128)(2,1)S(1)} %all_to_all.35.got_ref, bf16[192,256]{1,0:T(8,128)(2,1)S(1)} %get-tuple-element.46.conv_ref, f32[8,256]{1,0:T(8,128)S(1)} %get-tuple-element.47.stat_ref, f32[1,3072]{1,0:T(1,128)S(1)} %bitcast.16, f32[7,7,192]{2,1,0:T(8,128)S(1)} %copy-done.1, ...), custom_call_target="tpu_custom_call" | custom-call | flops 4816896 | bytes 1011456 | tf_op jit(solution)/shard_map/pallas_call | solution.py:51
  (3 shorter events, 0.0 us)
Async XLA Ops:
  0.6 1.3 %copy-start.1 = (f32[7,7,192]{2,1,0:T(8,128)S(1)}, f32[7,7,192]{2,1,0:T(8,128)}, u32[]{:S(2)}) copy-start(f32[7,7,192]{2,1,0:T(8,128)} %w_ref.3) | copy-start | bytes 112900
  0.6 1.3 %copy-start.11 = (f32[192]{0:T(256)S(1)}, f32[192]{0:T(256)}, u32[]{:S(2)}) copy-start(f32[192]{0:T(256)} %param.17) | copy-start | bytes 2308
  0.7 1.3 %copy-start.10 = (bf16[4,8,8,192]{3,2,1,0:T(8,128)(2,1)S(1)}, bf16[4,8,8,192]{3,2,1,0:T(8,128)(2,1)}, u32[]{:S(2)}) copy-start(bf16[4,8,8,192]{3,2,1,0:T(8,128)(2,1)} %x_far.1) | copy-start | bytes 294916
  0.7 0.7 copy-start.12
  1.4 24.8 %slice-start.2 = ((s8[4718592]{0:T(1024)(128)(4,1)}), s8[4194304]{0:T(1024)(128)(4,1)S(1)}, s32[]{:S(2)}) async-start(s8[4718592]{0:T(1024)(128)(4,1)} %bitcast.11), calls=%async_computation.8 | async-start | bytes 8388608
  1.9 26.1 %slice-start = ((s8[4718592]{0:T(1024)(128)(4,1)}), s8[4194304]{0:T(1024)(128)(4,1)S(1)}, s32[]{:S(2)}) async-start(s8[4718592]{0:T(1024)(128)(4,1)} %bitcast.9), calls=%async_computation.6 | async-start | bytes 8388608
  2.0 24.2 %slice-start.3 = ((s8[4718592]{0:T(1024)(128)(4,1)}), s8[524288]{0:T(1024)(128)(4,1)S(1)}, s32[]{:S(2)}) async-start(s8[4718592]{0:T(1024)(128)(4,1)} %bitcast.11), calls=%async_computation.9 | async-start | bytes 1048576
  2.0 24.1 %copy-start.2 = (f32[3072]{0:T(1024)S(1)}, f32[3072]{0:T(1024)}, u32[]{:S(2)}) copy-start(f32[3072]{0:T(1024)} %param.18) | copy-start | bytes 36868
  2.0 24.1 %copy-start.5 = (f32[3072]{0:T(1024)S(1)}, f32[3072]{0:T(1024)}, u32[]{:S(2)}) copy-start(f32[3072]{0:T(1024)} %param.19) | copy-start | bytes 36868
  2.0 26.0 %slice-start.1 = ((s8[4718592]{0:T(1024)(128)(4,1)}), s8[524288]{0:T(1024)(128)(4,1)S(1)}, s32[]{:S(2)}) async-start(s8[4718592]{0:T(1024)(128)(4,1)} %bitcast.9), calls=%async_computation.7 | async-start | bytes 1048576
  3.3 24.8 %copy-start.3 = (f32[768]{0:T(1024)S(1)}, f32[768]{0:T(1024)}, u32[]{:S(2)}) copy-start(f32[768]{0:T(1024)} %b_ref.3) | copy-start | bytes 9220
  23.6 4.4 %collective-permute-start = (bf16[8,192,256]{2,1,0:T(8,128)(2,1)S(1)}, bf16[8,192,256]{2,1,0:T(8,128)(2,1)S(1)}, u32[]{:S(2)}, u32[]{:S(2)}) collective-permute-start(bf16[8,192,256]{2,1,0:T(8,128)(2,1)S(1)} %all_to_all.30), channel_id=1, source_target_pairs={{0,1},{1,0},{2,3},{3,2},{4,5},{5,4},{6,7},{7,6},{8,9},{9,8},{10,11... | collective-permute-start | bytes 2359304 | tf_op jit(solution)/shard_map/ppermute | solution.py:27
  28.0 15.3 %copy-start = (bf16[192,1024]{1,0:T(8,128)(2,1)S(1)}, bf16[192,1024]{1,0:T(8,128)(2,1)}, u32[]{:S(2)}) copy-start(bf16[192,1024]{1,0:T(8,128)(2,1)} %project_ref.3) | copy-start | bytes 1179652
  28.1 15.3 %copy-start.6 = (f32[192]{0:T(256)S(1)}, f32[192]{0:T(256)}, u32[]{:S(2)}) copy-start(f32[192]{0:T(256)} %param.24) | copy-start | bytes 2308
  28.1 15.3 %copy-start.7 = (f32[192]{0:T(256)S(1)}, f32[192]{0:T(256)}, u32[]{:S(2)}) copy-start(f32[192]{0:T(256)} %param.25) | copy-start | bytes 2308
  28.1 15.3 %copy-start.8 = (f32[192]{0:T(256)S(1)}, f32[192]{0:T(256)}, u32[]{:S(2)}) copy-start(f32[192]{0:T(256)} %param.23) | copy-start | bytes 2308
  28.1 15.3 %copy-start.9 = (f32[192]{0:T(256)S(1)}, f32[192]{0:T(256)}, u32[]{:S(2)}) copy-start(f32[192]{0:T(256)} %param.26) | copy-start | bytes 2308
  28.1 28.3 %copy-start.4 = (f32[4,1024]{1,0:T(4,128)S(1)}, f32[4,1024]{1,0:T(4,128)}, u32[]{:S(2)}) copy-start(f32[4,1024]{1,0:T(4,128)} %text_ref.1) | copy-start | bytes 49156
  43.6 1.4 %collective-permute-start.1 = (f32[8,1152]{1,0:T(8,128)S(1)}, f32[8,1152]{1,0:T(8,128)S(1)}, u32[]{:S(2)}, u32[]{:S(2)}) collective-permute-start(f32[8,1152]{1,0:T(8,128)S(1)} %get-tuple-element.33.mine_ref), channel_id=1, source_target_pairs={{0,1},{1,0},{2,3},{3,2},{4,5},{5,4},{6,7},{7,6},{8,9},{9,8},{10,11... | collective-permute-start | bytes 110600 | tf_op jit(solution)/shard_map/ppermute | solution.py:27
  93.3 2.4 %collective-permute-start.2 = (bf16[1552,256]{1,0:T(8,128)(2,1)S(1)}, bf16[1552,256]{1,0:T(8,128)(2,1)S(1)}, u32[]{:S(2)}, u32[]{:S(2)}) collective-permute-start(bf16[1552,256]{1,0:T(8,128)(2,1)S(1)} %get-tuple-element.44), channel_id=1, source_target_pairs={{0,1},{1,0},{2,3},{3,2},{4,5},{5,4},{6,7},{7,6},{8,9},{9,8},{10,11... | collective-permute-start | bytes 2383880 | tf_op jit(solution)/shard_map/ppermute | solution.py:27

commit v7 on v6

--- a/solution.py
+++ b/solution.py
@@ -12,7 +12,6 @@
 inv_root_two_pi = 0.3989422804014327
 f32 = jnp.float32
 bf16 = jnp.bfloat16
-highest = lax.Precision.HIGHEST
 MIB = 1 << 20
 CONV_LIMIT = 50 * MIB
 CONV_FLOPS = 16 * 10**9
@@ -50,9 +49,12 @@
     arrays = [a.array if isinstance(a, Far) else a for a in operands]
     return pl.pallas_call(
         kernel,
-        out_shape=outs,
+        out_shape=[a.array if isinstance(a, Far) else a for a in outs],
         in_specs=[spec(a) for a in operands],
-        out_specs=[pl.BlockSpec(memory_space=pltpu.VMEM) for _ in outs],
+        out_specs=[
+            pl.BlockSpec(memory_space=pltpu.HBM if isinstance(a, Far) else pltpu.VMEM)
+            for a in outs
+        ],
         scratch_shapes=list(scratch),
         compiler_params=pltpu.CompilerParams(vmem_limit_bytes=limit),
         cost_estimate=pl.CostEstimate(
@@ -99,15 +101,8 @@
     return acc
 
 
-def start_kernel(labels_ref, tail_ref):
-    pairs = labels_ref.shape[0]
-    row = iota((8, 128), 0)
-    tail = jnp.zeros((8, 128), f32)
-    for r in range(pairs):
-        label = labels_ref[r]
-        target = (label // pairs) * 8 + 4 + label % pairs
-        tail = jnp.where(row == r, target.astype(f32), tail)
-    tail_ref[...] = tail
+def start_kernel(out_ref):
+    out_ref[...] = jnp.zeros_like(out_ref)
 
 
 def conv_kernel(
@@ -138,7 +133,7 @@
 
 
 def ready_kernel(
-    mine_ref, gain_ref, bias_ref, w_ref, rows_ref, part_ref, vec_ref, own_ref, sems
+    mine_ref, gain_ref, bias_ref, w_ref, labels_ref, rows_ref, part_ref, vec_ref, own_ref, tail_ref, sems
 ):
     shard = w_ref.shape[0] // BLOCKS
     core = lax.axis_index("mp") % 2
@@ -174,6 +169,14 @@
             vec_ref[i : i + 1, half + j * shard : half + (j + 1) * shard] = jnp.where(
                 core == 0, high, low
             )
+    pairs = labels_ref.shape[0]
+    row = iota((8, 128), 0)
+    tail = jnp.zeros((8, 128), f32)
+    for r in range(pairs):
+        label = labels_ref[r]
+        target = (label // pairs) * 8 + 4 + label % pairs
+        tail = jnp.where(row == r, target.astype(f32), tail)
+    tail_ref[...] = tail
     for copy in moves:
         copy.wait()
 
@@ -220,9 +223,10 @@
         normed_ref[0:rows, at] = (value * vec_ref[0:1, at] + vec_ref[1:2, at]).astype(bf16)
     normed_ref[rows : rows + 16, :] = jnp.concatenate(to_terms(vec_ref[...]), axis=0).astype(bf16)
     b_row = b_ref[...][None, :]
+    whole = jnp.dot(normed_ref[...], w_ref[...], preferred_element_type=f32)
     for t in range(hidden // step):
         at = slice(t * step, (t + 1) * step)
-        product = jnp.dot(normed_ref[...], w_ref[:, at], preferred_element_type=f32)
+        product = whole[:, at]
         through_ref[:, at] = product[rows:]
         pre = product[:rows] + b_row[:, at]
         hidden_ref[:, at] = pre
@@ -315,10 +319,12 @@
     scale_ref,
     gain_ref,
     project_ref,
-    text_ref,
+    text_far,
     block_ref,
     mixed_ref,
     both_ref,
+    text_ref,
+    sem,
 ):
     width = project_ref.shape[1]
     count = got_ref.shape[0] * 8
@@ -327,11 +333,13 @@
     got = got_ref[...].astype(f32)
     raw = jnp.concatenate(
         [got[:, :8, :half].reshape(count, half), got[:, 8:, :half].reshape(count, half)], axis=1
-    )
-    unit = raw / jnp.sqrt(jnp.sum(raw * raw, axis=1, keepdims=True) + eps)
-    logits = logit_scale * lax.dot_general(
-        unit, unit, (((1,), (1,)), ((), ())), precision=highest, preferred_element_type=f32
-    )
+    ).astype(bf16)
+    product = lax.dot_general(raw, raw, (((1,), (1,)), ((), ())), preferred_element_type=f32)
+    same = iota((count, count), 0) == iota((count, count), 1)
+    square = jnp.where(same, product, 0.0)
+    row_len = jnp.sqrt(jnp.sum(square, axis=1, keepdims=True) + eps)
+    col_len = jnp.sqrt(jnp.sum(square, axis=0, keepdims=True) + eps)
+    logits = logit_scale * (product / (row_len * col_len))
     column = iota((count, count), 1)
     valid = (iota((count, count), 0) % 8 < 4) & (column % 8 >= 4)
     weights = jnp.where(valid, jnp.exp(jnp.where(valid, logits, 0.0)), 0.0)
@@ -341,15 +349,20 @@
     matched = jnp.where(target == column.astype(f32), 1.0, 0.0)
     grads = loss_scale * (0.5 * (weights / row_total + weights / col_total) - matched)
     grads = jnp.where(valid, grads, 0.0)
-    both_ref[...] = grads + grads.T
-    grad_unit = logit_scale * jnp.dot(
-        both_ref[home, :], unit, precision=highest, preferred_element_type=f32
-    )
+    both_ref[...] = (grads + grads.T) / col_len
+    high, rest = to_terms(both_ref[home, :])
+    middle, low = to_terms(rest)
+    grad_unit = jnp.dot(
+        jnp.concatenate([high, middle, low], axis=0).astype(bf16), raw, preferred_element_type=f32
+    )
+    grad_unit = logit_scale * (grad_unit[:8] + (grad_unit[8:16] + grad_unit[16:]))
     own = own_ref[...]
     length = jnp.sqrt(jnp.sum(own * own, axis=1, keepdims=True) + eps)
     own = own / length
     grad = (grad_unit - own * jnp.sum(own * grad_unit, axis=1, keepdims=True)) / length
     text_ref[...] = grad[4:]
+    send = pltpu.make_async_copy(text_ref, text_far, sem)
+    send.start()
     grad = grad[:4].astype(bf16)
     back = lax.dot_general(
         jnp.concatenate([grad, jnp.zeros_like(grad)], axis=0),
@@ -367,6 +380,7 @@
     block_ref[...] = block
     for k in range(BLOCKS):
         mixed_ref[k] = block * scale_ref[...]
+    send.wait()
 
 
 def backward_kernel(
@@ -417,21 +431,15 @@
     high, low = to_terms(sums)
     other_ref[channels // 2 :, :] = jnp.concatenate([high, low], axis=0).astype(bf16)
     half = channels // 2
-    for c in range(half // step):
-        other_ref[c * step : (c + 1) * step, :] = jnp.dot(
-            w_ref[half + c * step : half + (c + 1) * step, :],
-            turned_ref[...],
-            preferred_element_type=f32,
-        ).astype(bf16)
+    other_ref[:half, :] = jnp.dot(
+        w_ref[half:, :], turned_ref[...], preferred_element_type=f32
+    ).astype(bf16)
 
 
 def mine_kernel(w_ref, turned_ref, mine_ref):
-    step = 256
-    for c in range(mine_ref.shape[0] // step):
-        at = slice(c * step, (c + 1) * step)
-        mine_ref[at, :] = jnp.dot(
-            w_ref[at, :], turned_ref[...], preferred_element_type=f32
-        ).astype(bf16)
+    mine_ref[...] = jnp.dot(
+        w_ref[: mine_ref.shape[0], :], turned_ref[...], preferred_element_type=f32
+    ).astype(bf16)
 
 
 def pair_kernel(mine_ref, got_ref, sums_ref, out_ref):
@@ -449,7 +457,9 @@
         out_ref[j, shard:, :] = tail
 
 
-def final_kernel(got_ref, conv_ref, stat_ref, gain_ref, w_ref, block_ref, out_ref, rows_ref):
+def final_kernel(
+    got_ref, conv_ref, stat_ref, gain_ref, w_ref, block_ref, out_far, rows_ref, out_ref, sems
+):
     shard = conv_ref.shape[0]
     channels = shard * BLOCKS
     index = lax.axis_index("mp")
@@ -474,9 +484,12 @@
         base = block_ref[pl.ds(n, 1), :]
         for p, row in enumerate(taps(x, w_ref, True)):
             out_ref[n, p] = row + base
+        pltpu.make_async_copy(out_ref.at[n], out_far.at[n], sems.at[n]).start()
         return carry
 
     lax.fori_loop(0, images, image, 0)
+    for n in range(images):
+        pltpu.make_async_copy(out_ref.at[n], out_far.at[n], sems.at[n]).wait()
 
 
 def body(
@@ -501,7 +514,7 @@
     rows = images * side * side
     pairs, width = text_emb.shape
     shards = lax.axis_size("dp")
-    (tail,) = run(start_kernel, [shape(8, 128)], labels, flops=START_FLOPS)
+    (begun,) = run(start_kernel, [shape(8, 128)], flops=START_FLOPS)
     copies, conv, input_mean = run(
         conv_kernel,
         [
@@ -509,7 +522,7 @@
             shape(shard, rows, dtype=bf16),
             shape(images, shard),
         ],
-        Far(tail),
+        Far(begun),
         Far(x_in),
         Far(dw_weight),
         Far(dw_bias[None, :]),
@@ -527,18 +540,20 @@
     conv_other = core_swap(conv_mine)
     conv_mine = conv_mine.reshape(channels // 2, rows)
     conv_other = conv_other.reshape(channels // 2, rows)
-    own_rows, part, vec, w_own = run(
+    own_rows, part, vec, w_own, tail = run(
         ready_kernel,
         [
             shape(rows, channels // 2, dtype=bf16),
             shape(8, rows),
             shape(8, channels),
             shape(channels, hidden, dtype=bf16),
+            shape(8, 128),
         ],
         conv_mine,
         ln_gain[None, :],
         ln_bias[None, :],
         w_in,
+        labels,
         scratch=[pltpu.SemaphoreType.DMA((BLOCKS,))],
     )
     slope, hidden_pre, through, row_stat, mixed = run(
@@ -588,7 +603,7 @@
     )
     grad_text, grad_block, mixed_block = run(
         loss_kernel,
-        [shape(pairs, width), shape(images, shard), shape(BLOCKS, images, shard)],
+        [Far(shape(pairs, width)), shape(images, shard), shape(BLOCKS, images, shard)],
         lax.all_to_all(pair_block, "dp", 0, 0),
         own_block,
         back_rows,
@@ -597,7 +612,11 @@
         layer_scale[None, :],
         head_gain[None, :],
         projection,
-        scratch=[pltpu.VMEM((shards * 8, shards * 8), f32)],
+        scratch=[
+            pltpu.VMEM((shards * 8, shards * 8), f32),
+            pltpu.VMEM((pairs, width), f32),
+            pltpu.SemaphoreType.DMA,
+        ],
     )
     other, turned, row_sums = run(
         backward_kernel,
@@ -629,14 +648,18 @@
     )
     (grad_input,) = run(
         final_kernel,
-        [shape(images, side, side, shard)],
+        [Far(shape(images, side, side, shard))],
         chip_exchange(blocks),
         conv,
         row_stat,
         ln_gain[None, :],
         dw_weight,
         grad_block,
-        scratch=[pltpu.VMEM((rows, shard), f32)],
+        scratch=[
+            pltpu.VMEM((rows, shard), f32),
+            pltpu.VMEM((images, side, side, shard), f32),
+            pltpu.SemaphoreType.DMA((images,)),
+        ],
         flops=2 * 49 * rows * shard,
     )
     return (grad_input, grad_text)

time: 115 us -> 112 us (0.974)
  Pallas kernels: 17.1 us -> 13.8 us
    pallas_call x12, Pallas kernels: 17.1 us -> 13.8 us  [run(): pl.pallas_call(kernel, out_shape=[a.array if isinstance(a, Far) else a fo...]
  transfers between devices with their start and end apart: 3 -> 3, of which waited for: 3 -> 2; matrix products, arithmetic and copies ran while one was open for 0% -> 0% of each run, Pallas kernels for 2% -> 3%
where the time goes in v7:
time: 112 us; the launch traced here: 111 us
  blocking collectives  90.1 us (80%)
  Pallas kernels  13.8 us (12%)
  starting transfers between devices  3.56 us (3%)
  waiting for transfers between devices  2 us (2%)
    all_to_all x3, blocking collectives, chip_exchange(): return lax.all_to_all(array, 'mp', 0, 0, axis_index_groups=groups)  48.6 us
    all_to_all x2, blocking collectives, shard_exchange(): return lax.all_to_all(array, 'mp', 0, 0)  24.4 us
    all_to_all x1, blocking collectives, body(): lax.all_to_all(pair_block, 'dp', 0, 0)  17.1 us
    pallas_call x12, Pallas kernels, run(): pl.pallas_call(kernel, out_shape=[a.array if isinstance(a, Far) else a fo...  13.8 us
    ppermute x3, starting transfers between devices, core_swap(): return lax.ppermute(array, 'mp', [(i, i ^ 1) for i in range(BLOCKS)])  3.56 us
  transfers between devices with their start and end apart: 3, of which 2 were waited for; matrix products, arithmetic and copies ran while one was open for 0% of the time, Pallas kernels for 3%

profile of v7, /device:TPU:1, one launch (start us, length us, event | category | flops | bytes accessed | tf_op | source)
XLA Modules:
  0.0 111.3 jit_solution(5925716093590060245)
XLA Ops:
  0.6 0.0 copy-start.1
  0.6 0.0 copy-start.12
  0.6 0.0 copy-start.11
  0.7 0.0 slice-start.2
  0.7 0.0 slice-start
  0.7 0.8 copy-done.1
  1.4 0.0 copy-done.12
  1.5 0.1 copy-done.11
  1.6 0.0 slice-start.3
  1.6 0.0 copy-start.2
  1.6 0.0 copy-start.5
  1.6 0.0 copy-start.10
  1.6 0.0 slice-start.1
  1.6 1.2 %shard_map.159 = (bf16[8,192,256]{2,1,0:T(8,128)(2,1)S(1)}, bf16[192,256]{1,0:T(8,128)(2,1)S(1)}, f32[4,192]{1,0:T(4,128)S(1)}) custom-call(f32[8,128]{1,0:T(8,128)S(1)} %shard_map.158._, bf16[4,8,8,192]{3,2,1,0:T(8,128)(2,1)S(1)} %copy-done.11, f32[7,7,192]{2,1,0:T(8,128)S(1)} %copy-done.1, f32[1,192]{1,0:T(1,128)S(1)} %bitcast.24), custom_call_target="tpu_custom_call" | custom-call | flops 16000000000 | bytes 140800 | tf_op jit(solution)/shard_map/pallas_call | solution.py:50
  2.9 0.0 copy-start.3
  2.9 20.2 %all_to_all.30 = bf16[8,192,256]{2,1,0:T(8,128)(2,1)S(1)} all-to-all(bf16[8,192,256]{2,1,0:T(8,128)(2,1)S(1)} %get-tuple-element.27), channel_id=1, replica_groups={{0,2,4,6,8,10,12,14},{1,3,5,7,9,11,13,15},{16,18,20,22,24,26,28,30},{17..., dimensions={0} | all-to-all | bytes 1572864 | tf_op jit(solution)/shard_map/all_to_all | solution.py:31
  23.1 2.5 %collective-permute-start = (bf16[8,192,256]{2,1,0:T(8,128)(2,1)S(1)}, bf16[8,192,256]{2,1,0:T(8,128)(2,1)S(1)}, u32[]{:S(2)}, u32[]{:S(2)}) collective-permute-start(bf16[8,192,256]{2,1,0:T(8,128)(2,1)S(1)} %all_to_all.30), channel_id=1, source_target_pairs={{0,1},{1,0},{2,3},{3,2},{4,5},{5,4},{6,7},{7,6},{8,9},{9,8},{10,11... | collective-permute-start | bytes 2359304 | tf_op jit(solution)/shard_map/ppermute | solution.py:26
  25.6 0.0 slice-done.2
  25.6 0.0 slice-done.3
  25.6 0.0 copy-done.2
  25.6 0.0 copy-done.5
  25.6 0.0 copy-done.10
  25.6 2.2 %shard_map.160 = (bf16[256,1536]{1,0:T(8,128)(2,1)S(1)}, f32[8,256]{1,0:T(8,128)S(1)}, f32[8,3072]{1,0:T(8,128)S(1)}, bf16[3072,768]{1,0:T(8,128)(2,1)S(1)}, f32[8,128]{1,0:T(8,128)S(1)}) custom-call(bf16[1536,256]{1,0:T(8,128)(2,1)S(1)} %bitcast.13, f32[1,3072]{1,0:T(1,128)S(1)} %bitcast.15, f32[1,3072]{1,0:T(1,128)S(1)} %bitcast.17, ...), custom_call_target="tpu_custom_call" | custom-call | bytes 5529616 | tf_op jit(solution)/shard_map/pallas_call | solution.py:50
  27.8 0.0 collective-permute-done
  27.8 0.0 slice-done
  27.8 0.0 slice-done.1
  27.8 0.0 copy-done.3
  27.8 0.0 copy-start
  27.8 0.0 copy-start.6
  27.8 0.0 copy-start.7
  27.9 0.0 copy-start.8
  27.9 0.0 copy-start.9
  27.9 0.0 copy-start.4
  27.9 3.1 %shard_map.161 = (f32[256,768]{1,0:T(8,128)S(1)}, f32[256,768]{1,0:T(8,128)S(1)}, f32[16,768]{1,0:T(8,128)S(1)}, f32[8,256]{1,0:T(8,128)S(1)}, f32[16,4,192]{2,1,0:T(4,128)S(1)}) custom-call(bf16[256,1536]{1,0:T(8,128)(2,1)S(1)} %get-tuple-element.29.rows_ref, bf16[1536,256]{1,0:T(8,128)(2,1)S(1)} %bitcast.14, f32[8,256]{1,0:T(8,128)S(1)} %get-tuple-element.30.part_ref, ...), custom_call_target="tpu_custom_call" | custom-call | flops 1207959552 | bytes 11119616 | tf_op jit(solution)/shard_map/pallas_call | solution.py:50
  31.0 10.1 %all_to_all.31.got_ref = f32[16,4,192]{2,1,0:T(4,128)S(1)} all-to-all(f32[16,4,192]{2,1,0:T(4,128)S(1)} %get-tuple-element.32), channel_id=1, replica_groups=mesh['dp'=16,'mp'=16] {'mp'}, dimensions={0} | all-to-all | bytes 98304 | tf_op jit(solution)/shard_map/all_to_all | solution.py:35
  41.0 0.0 copy-done
  41.0 0.0 copy-done.6
  41.0 0.0 copy-done.7
  41.0 0.0 copy-done.8
  41.0 0.0 copy-done.9
  41.0 0.2 shard_map.162
  41.2 0.5 collective-permute-start.1
  41.7 0.9 collective-permute-done.1.other_ref
  42.6 11.4 %all_to_all.32.got_ref = f32[8,8,1152]{2,1,0:T(8,128)S(1)} all-to-all(f32[8,8,1152]{2,1,0:T(8,128)S(1)} %shard_map.163), channel_id=1, replica_groups={{0,2,4,6,8,10,12,14},{1,3,5,7,9,11,13,15},{16,18,20,22,24,26,28,30},{17..., dimensions={0} | all-to-all | bytes 589824 | tf_op jit(solution)/shard_map/all_to_all | solution.py:31
  54.0 0.0 copy-done.4
  54.0 0.2 shard_map.164
  54.2 17.1 %all_to_all.33.got_ref = bf16[16,16,640]{2,1,0:T(8,128)(2,1)S(1)} all-to-all(bf16[16,16,640]{2,1,0:T(8,128)(2,1)S(1)} %get-tuple-element.36), channel_id=1, replica_groups=mesh['dp'=16,'mp'=16] {'dp'}, dimensions={0} | all-to-all | bytes 655360 | tf_op jit(solution)/shard_map/all_to_all | solution.py:607
  71.3 1.4 %shard_map.165 = (f32[4,1024]{1,0:T(4,128)}, f32[4,192]{1,0:T(4,128)S(1)}, f32[16,4,192]{2,1,0:T(4,128)S(1)}) custom-call(bf16[16,16,640]{2,1,0:T(8,128)(2,1)S(1)} %all_to_all.33.got_ref, f32[8,1024]{1,0:T(8,128)S(1)} %get-tuple-element.37.own_ref, f32[8,1024]{1,0:T(8,128)S(1)} %get-tuple-element.38.rows_ref, f32[2,8,128]{2,1,0:T(8,128)S(1)} %get-tuple-element.39.stat_ref, ...), custom_call_target="tpu_custom_call" | custom-call | bytes 799232 | tf_op jit(solution)/shard_map/pallas_call | solution.py:50
  72.7 14.3 %all_to_all.34.got_ref = f32[16,4,192]{2,1,0:T(4,128)S(1)} all-to-all(f32[16,4,192]{2,1,0:T(4,128)S(1)} %get-tuple-element.41), channel_id=1, replica_groups=mesh['dp'=16,'mp'=16] {'mp'}, dimensions={0} | all-to-all | bytes 98304 | tf_op jit(solution)/shard_map/all_to_all | solution.py:35
  87.1 2.5 %shard_map.166 = (bf16[1552,256]{1,0:T(8,128)(2,1)S(1)}, bf16[768,256]{1,0:T(8,128)(2,1)S(1)}, f32[8,256]{1,0:T(8,128)S(1)}) custom-call(f32[16,4,192]{2,1,0:T(4,128)S(1)} %all_to_all.34.got_ref, bf16[768,3072]{1,0:T(8,128)(2,1)S(1)} %bitcast.10, f32[256,768]{1,0:T(8,128)S(1)} %get-tuple-element.42.slope_ref, f32[256,768]{1,0:T(8,128)S(1)} %get-tuple-element.43.hidden_ref, ...), custom_call_target="tpu_custom_call" | custom-call | flops 603979776 | bytes 11111424 | tf_op jit(solution)/shard_map/pallas_call | solution.py:50
  89.5 0.5 collective-permute-start.2
  90.0 0.8 shard_map.167.mine_ref
  90.8 1.1 %collective-permute-done.2.got_ref = bf16[1552,256]{1,0:T(8,128)(2,1)S(1)} collective-permute-done((bf16[1552,256]{1,0:T(8,128)(2,1)S(1)}, bf16[1552,256]{1,0:T(8,128)(2,1)S(1)}, u32[]{:S(2)}, u32[]{:S(2)}) %collective-permute-start.2) | collective-permute-done | bytes 794656 | tf_op jit(solution)/shard_map/ppermute | solution.py:26
  92.0 0.2 shard_map.168
  92.2 17.1 %all_to_all.35.got_ref = bf16[8,208,256]{2,1,0:T(8,128)(2,1)S(1)} all-to-all(bf16[8,208,256]{2,1,0:T(8,128)(2,1)S(1)} %shard_map.168), channel_id=1, replica_groups={{0,2,4,6,8,10,12,14},{1,3,5,7,9,11,13,15},{16,18,20,22,24,26,28,30},{17..., dimensions={0} | all-to-all | bytes 1703936 | tf_op jit(solution)/shard_map/all_to_all | solution.py:31
  109.2 2.1 %shard_map.169 = f32[4,8,8,192]{3,2,1,0:T(8,128)} custom-call(bf16[8,208,256]{2,1,0:T(8,128)(2,1)S(1)} %all_to_all.35.got_ref, bf16[192,256]{1,0:T(8,128)(2,1)S(1)} %get-tuple-element.48.conv_ref, f32[8,256]{1,0:T(8,128)S(1)} %get-tuple-element.49.stat_ref, f32[1,3072]{1,0:T(1,128)S(1)} %bitcast.16, f32[7,7,192]{2,1,0:T(8,128)S(1)} %copy-done.1, ...), custom_call_target="tpu_custom_call" | custom-call | flops 4816896 | bytes 1011456 | tf_op jit(solution)/shard_map/pallas_call | solution.py:50
  (4 shorter events, 0.0 us)
Async XLA Ops:
  0.6 0.8 copy-start.1
  0.6 0.8 copy-start.12
  0.6 0.9 copy-start.11
  0.7 24.9 %slice-start.2 = ((s8[4718592]{0:T(1024)(128)(4,1)}), s8[4194304]{0:T(1024)(128)(4,1)S(1)}, s32[]{:S(2)}) async-start(s8[4718592]{0:T(1024)(128)(4,1)} %bitcast.11), calls=%async_computation.8 | async-start | bytes 8388608
  0.7 27.1 %slice-start = ((s8[4718592]{0:T(1024)(128)(4,1)}), s8[4194304]{0:T(1024)(128)(4,1)S(1)}, s32[]{:S(2)}) async-start(s8[4718592]{0:T(1024)(128)(4,1)} %bitcast.9), calls=%async_computation.6 | async-start | bytes 8388608
  1.6 24.0 %slice-start.3 = ((s8[4718592]{0:T(1024)(128)(4,1)}), s8[524288]{0:T(1024)(128)(4,1)S(1)}, s32[]{:S(2)}) async-start(s8[4718592]{0:T(1024)(128)(4,1)} %bitcast.11), calls=%async_computation.9 | async-start | bytes 1048576
  1.6 24.0 %copy-start.2 = (f32[3072]{0:T(1024)S(1)}, f32[3072]{0:T(1024)}, u32[]{:S(2)}) copy-start(f32[3072]{0:T(1024)} %param.18) | copy-start | bytes 36868
  1.6 24.0 %copy-start.5 = (f32[3072]{0:T(1024)S(1)}, f32[3072]{0:T(1024)}, u32[]{:S(2)}) copy-start(f32[3072]{0:T(1024)} %param.19) | copy-start | bytes 36868
  1.6 24.0 %copy-start.10 = (s32[4]{0:T(128)S(1)}, s32[4]{0:T(128)}, u32[]{:S(2)}) copy-start(s32[4]{0:T(128)} %labels_ref.1) | copy-start | bytes 52
  1.6 26.2 %slice-start.1 = ((s8[4718592]{0:T(1024)(128)(4,1)}), s8[524288]{0:T(1024)(128)(4,1)S(1)}, s32[]{:S(2)}) async-start(s8[4718592]{0:T(1024)(128)(4,1)} %bitcast.9), calls=%async_computation.7 | async-start | bytes 1048576
  2.9 24.9 %copy-start.3 = (f32[768]{0:T(1024)S(1)}, f32[768]{0:T(1024)}, u32[]{:S(2)}) copy-start(f32[768]{0:T(1024)} %b_ref.3) | copy-start | bytes 9220
  23.1 4.7 %collective-permute-start = (bf16[8,192,256]{2,1,0:T(8,128)(2,1)S(1)}, bf16[8,192,256]{2,1,0:T(8,128)(2,1)S(1)}, u32[]{:S(2)}, u32[]{:S(2)}) collective-permute-start(bf16[8,192,256]{2,1,0:T(8,128)(2,1)S(1)} %all_to_all.30), channel_id=1, source_target_pairs={{0,1},{1,0},{2,3},{3,2},{4,5},{5,4},{6,7},{7,6},{8,9},{9,8},{10,11... | collective-permute-start | bytes 2359304 | tf_op jit(solution)/shard_map/ppermute | solution.py:26
  27.8 13.2 %copy-start = (bf16[192,1024]{1,0:T(8,128)(2,1)S(1)}, bf16[192,1024]{1,0:T(8,128)(2,1)}, u32[]{:S(2)}) copy-start(bf16[192,1024]{1,0:T(8,128)(2,1)} %project_ref.3) | copy-start | bytes 1179652
  27.8 13.2 %copy-start.6 = (f32[192]{0:T(256)S(1)}, f32[192]{0:T(256)}, u32[]{:S(2)}) copy-start(f32[192]{0:T(256)} %param.24) | copy-start | bytes 2308
  27.8 13.2 %copy-start.7 = (f32[192]{0:T(256)S(1)}, f32[192]{0:T(256)}, u32[]{:S(2)}) copy-start(f32[192]{0:T(256)} %param.25) | copy-start | bytes 2308
  27.9 13.2 %copy-start.8 = (f32[192]{0:T(256)S(1)}, f32[192]{0:T(256)}, u32[]{:S(2)}) copy-start(f32[192]{0:T(256)} %param.23) | copy-start | bytes 2308
  27.9 13.2 %copy-start.9 = (f32[192]{0:T(256)S(1)}, f32[192]{0:T(256)}, u32[]{:S(2)}) copy-start(f32[192]{0:T(256)} %param.26) | copy-start | bytes 2308
  27.9 26.1 %copy-start.4 = (f32[4,1024]{1,0:T(4,128)S(1)}, f32[4,1024]{1,0:T(4,128)}, u32[]{:S(2)}) copy-start(f32[4,1024]{1,0:T(4,128)} %text_ref.1) | copy-start | bytes 49156
  41.2 1.4 %collective-permute-start.1 = (f32[8,1152]{1,0:T(8,128)S(1)}, f32[8,1152]{1,0:T(8,128)S(1)}, u32[]{:S(2)}, u32[]{:S(2)}) collective-permute-start(f32[8,1152]{1,0:T(8,128)S(1)} %get-tuple-element.34.mine_ref), channel_id=1, source_target_pairs={{0,1},{1,0},{2,3},{3,2},{4,5},{5,4},{6,7},{7,6},{8,9},{9,8},{10,11... | collective-permute-start | bytes 110600 | tf_op jit(solution)/shard_map/ppermute | solution.py:26
  89.5 2.4 %collective-permute-start.2 = (bf16[1552,256]{1,0:T(8,128)(2,1)S(1)}, bf16[1552,256]{1,0:T(8,128)(2,1)S(1)}, u32[]{:S(2)}, u32[]{:S(2)}) collective-permute-start(bf16[1552,256]{1,0:T(8,128)(2,1)S(1)} %get-tuple-element.46), channel_id=1, source_target_pairs={{0,1},{1,0},{2,3},{3,2},{4,5},{5,4},{6,7},{7,6},{8,9},{9,8},{10,11... | collective-permute-start | bytes 2383880 | tf_op jit(solution)/shard_map/ppermute | solution.py:26

commit v8 on v7

--- a/solution.py
+++ b/solution.py
@@ -16,6 +16,7 @@
 CONV_LIMIT = 50 * MIB
 CONV_FLOPS = 16 * 10**9
 START_FLOPS = 4 * 10**9
+READY_FLOPS = 12 * 10**9
 CHIPS = 8
 BLOCKS = 16
 SHARD = 192
@@ -106,7 +107,22 @@
 
 
 def conv_kernel(
-    _, x_far, dw_far, bias_far, copies_ref, conv_ref, mean_ref, x_ref, dw_ref, bias_ref, rows_ref, sems
+    _,
+    scale_ref,
+    bout_ref,
+    gain_ref,
+    shift_ref,
+    x_far,
+    dw_far,
+    bias_far,
+    copies_ref,
+    conv_ref,
+    head_ref,
+    x_ref,
+    dw_ref,
+    bias_ref,
+    rows_ref,
+    sems,
 ):
     images, side = x_ref.shape[:2]
     positions = side * side
@@ -120,12 +136,14 @@
     def image(n, carry):
         x = x_ref[n].astype(f32)
         total = jnp.sum(jnp.sum(x, axis=0), axis=0, keepdims=True)
-        mean_ref[pl.ds(n, 1), :] = total / positions
+        head_ref[pl.ds(n, 1), :] = total / positions
         for p, row in enumerate(taps(x, dw_ref, False)):
             rows_ref[pl.ds(pl.multiple_of(n * positions + p * side, side), side), :] = row
         return carry
 
     lax.fori_loop(0, images, image, 0)
+    for i, ref in enumerate((scale_ref, bout_ref, gain_ref, shift_ref)):
+        head_ref[images + i : images + i + 1, :] = ref[...]
     turned = (rows_ref[...] + bias_ref[...]).T.astype(bf16)
     conv_ref[...] = turned
     for j in range(CHIPS):
@@ -133,7 +151,21 @@
 
 
 def ready_kernel(
-    mine_ref, gain_ref, bias_ref, w_ref, labels_ref, rows_ref, part_ref, vec_ref, own_ref, tail_ref, sems
+    mine_ref,
+    gain_ref,
+    bias_ref,
+    w_ref,
+    labels_ref,
+    head_ref,
+    project_far,
+    rows_ref,
+    part_ref,
+    vec_ref,
+    own_ref,
+    tail_ref,
+    head_out_ref,
+    project_ref,
+    sems,
 ):
     shard = w_ref.shape[0] // BLOCKS
     core = lax.axis_index("mp") % 2
@@ -146,8 +178,10 @@
                 w_ref.at[source], own_ref.at[k * shard : (k + 1) * shard], sems.at[k]
             )
         )
+    moves.append(pltpu.make_async_copy(project_far, project_ref, sems.at[BLOCKS]))
     for copy in moves:
         copy.start()
+    head_out_ref[...] = head_ref[...]
     half, rows = mine_ref.shape
     step = 256
     first = jnp.zeros((1, rows), f32)
@@ -198,8 +232,8 @@
 ):
     half, rows = other_ref.shape
     channels, hidden = w_ref.shape
-    images, shard = mixed_ref.shape[1:]
-    positions = rows // images
+    images = rows // POSITIONS
+    positions = POSITIONS
     step = 256
     first, second = part_ref[0:1, :], part_ref[1:2, :]
     for c in range(half // step):
@@ -246,44 +280,52 @@
         )
         part = part[:8] + part[8:]
         mixed = part if t == 0 else mixed + part
+    mixed_ref[...] = mixed
+
+
+def block_kernel(mixed_ref, _head, _project, out_ref):
+    shard = out_ref.shape[2]
+    images = out_ref.shape[1] // 2
     for k in range(BLOCKS):
-        mixed_ref[k] = mixed[:images, k * shard : (k + 1) * shard]
+        block = mixed_ref[:images, k * shard : (k + 1) * shard]
+        out_ref[k, :images, :] = block
+        out_ref[k ^ 1, images:, :] = block
 
 
 def head_kernel(
-    got_ref, mean_ref, scale_ref, bout_ref, gain_ref, bias_ref, project_ref, out_ref, pooled_ref
+    got_ref, own_ref, other_ref, project_ref, project_other_ref, out_ref, pooled_ref
 ):
-    images, shard = got_ref.shape[1:]
+    images = pooled_ref.shape[0]
     width = project_ref.shape[1]
     mixed = got_ref[0]
     for j in range(1, BLOCKS):
         mixed = mixed + got_ref[j]
-    scale, bias_out = scale_ref[...], bout_ref[...]
-    gain, bias = gain_ref[...], bias_ref[...]
-    pooled = mean_ref[...] + scale * (mixed + bias_out)
-    pooled_ref[...] = pooled
-    head = jnp.concatenate([pooled, scale, bias_out, gain, bias], axis=0)
-    first = jnp.sum(head, axis=1, keepdims=True)
-    second = jnp.sum(head * head, axis=1, keepdims=True)
-    value = jnp.where(iota((8, shard), 0) < images, head * gain, head)
-    high, rest = to_terms(value)
-    middle, low = to_terms(rest)
-    product = jnp.dot(
-        jnp.concatenate([high, middle, low], axis=0).astype(bf16),
-        project_ref[...],
-        preferred_element_type=f32,
-    )
-    out_ref[:, :width] = product[:8] + (product[8:16] + product[16:])
+    first = jnp.zeros((8, 1), f32)
+    second = jnp.zeros((8, 1), f32)
+    product = jnp.zeros((24, width), f32)
+    sides = ((own_ref, project_ref, mixed[:images]), (other_ref, project_other_ref, mixed[images:]))
+    for head_ref, weight_ref, part in sides:
+        gain = head_ref[6:7, :]
+        pooled = head_ref[:images, :] + head_ref[4:5, :] * (part + head_ref[5:6, :])
+        if head_ref is own_ref:
+            pooled_ref[...] = pooled
+        head = jnp.concatenate([pooled, head_ref[images:, :]], axis=0)
+        first = first + jnp.sum(head, axis=1, keepdims=True)
+        second = second + jnp.sum(head * head, axis=1, keepdims=True)
+        value = jnp.where(iota(head.shape, 0) < images, head * gain, head)
+        high, rest = to_terms(value)
+        middle, low = to_terms(rest)
+        product = product + jnp.dot(
+            jnp.concatenate([high, middle, low], axis=0).astype(bf16),
+            weight_ref[...],
+            preferred_element_type=f32,
+        )
+    product = product[:8] + (product[8:16] + product[16:])
     lane = iota((8, 128), 1)
-    out_ref[:, width : width + 128] = jnp.where(
-        lane == 0, first, jnp.where(lane == 1, second, 0.0)
-    )
-
-
-def pair_sum_kernel(mine_ref, other_ref, out_ref):
-    block = mine_ref[...] + other_ref[...]
+    tail = jnp.where(lane == 0, first, jnp.where(lane == 1, second, 0.0))
     for j in range(CHIPS):
-        out_ref[j] = block
+        out_ref[j, :, :width] = product
+        out_ref[j, :, width:] = tail
 
 
 def embed_kernel(got_ref, text_ref, tail_ref, out_ref, own_ref, back_ref, stat_ref):
@@ -300,12 +342,11 @@
     tail = tail_ref[...]
     block = jnp.concatenate([emb[:4], text_ref[...]], axis=0)
     own_ref[...] = block
-    half = width // 2
-    block = jnp.concatenate([block[:, :half], block[:, half:]], axis=0).astype(bf16)
-    tail = jnp.concatenate([tail, tail], axis=0).astype(bf16)
+    block = block.astype(bf16)
+    tail = tail.astype(bf16)
     for d in range(out_ref.shape[0]):
-        out_ref[d, :, :half] = block
-        out_ref[d, :, half:] = tail
+        out_ref[d, :, :width] = block
+        out_ref[d, :, width:] = tail
     stat_ref[0] = jnp.broadcast_to(mean, (8, 128))
     stat_ref[1] = jnp.broadcast_to(inverse, (8, 128))
 
@@ -329,11 +370,8 @@
     width = project_ref.shape[1]
     count = got_ref.shape[0] * 8
     home = pl.ds(pl.multiple_of(lax.axis_index("dp") * 8, 8), 8)
-    half = width // 2
-    got = got_ref[...].astype(f32)
-    raw = jnp.concatenate(
-        [got[:, :8, :half].reshape(count, half), got[:, 8:, :half].reshape(count, half)], axis=1
-    ).astype(bf16)
+    got = got_ref[...].astype(f32).reshape(count, width + 128)
+    raw = got[:, :width].astype(bf16)
     product = lax.dot_general(raw, raw, (((1,), (1,)), ((), ())), preferred_element_type=f32)
     same = iota((count, count), 0) == iota((count, count), 1)
     square = jnp.where(same, product, 0.0)
@@ -345,7 +383,7 @@
     weights = jnp.where(valid, jnp.exp(jnp.where(valid, logits, 0.0)), 0.0)
     row_total = jnp.sum(weights, axis=1, keepdims=True)
     col_total = jnp.sum(weights, axis=0, keepdims=True)
-    target = got[:, :8, half:].reshape(count, 128)[:, 0:1]
+    target = got[:, width : width + 1]
     matched = jnp.where(target == column.astype(f32), 1.0, 0.0)
     grads = loss_scale * (0.5 * (weights / row_total + weights / col_total) - matched)
     grads = jnp.where(valid, grads, 0.0)
@@ -515,14 +553,18 @@
     pairs, width = text_emb.shape
     shards = lax.axis_size("dp")
     (begun,) = run(start_kernel, [shape(8, 128)], flops=START_FLOPS)
-    copies, conv, input_mean = run(
+    copies, conv, head_own = run(
         conv_kernel,
         [
             shape(CHIPS, shard, rows, dtype=bf16),
             shape(shard, rows, dtype=bf16),
-            shape(images, shard),
+            shape(8, shard),
         ],
         Far(begun),
+        layer_scale[None, :],
+        b_out[None, :],
+        head_gain[None, :],
+        head_bias[None, :],
         Far(x_in),
         Far(dw_weight),
         Far(dw_bias[None, :]),
@@ -540,7 +582,7 @@
     conv_other = core_swap(conv_mine)
     conv_mine = conv_mine.reshape(channels // 2, rows)
     conv_other = conv_other.reshape(channels // 2, rows)
-    own_rows, part, vec, w_own, tail = run(
+    own_rows, part, vec, w_own, tail, head_sent, project_sent = run(
         ready_kernel,
         [
             shape(rows, channels // 2, dtype=bf16),
@@ -548,14 +590,21 @@
             shape(8, channels),
             shape(channels, hidden, dtype=bf16),
             shape(8, 128),
+            shape(8, shard),
+            shape(shard, width, dtype=bf16),
         ],
         conv_mine,
         ln_gain[None, :],
         ln_bias[None, :],
         w_in,
         labels,
-        scratch=[pltpu.SemaphoreType.DMA((BLOCKS,))],
-    )
+        head_own,
+        Far(projection),
+        scratch=[pltpu.SemaphoreType.DMA((BLOCKS + 1,))],
+        flops=READY_FLOPS,
+    )
+    head_other = core_swap(head_sent)
+    project_other = core_swap(project_sent)
     slope, hidden_pre, through, row_stat, mixed = run(
         forward_kernel,
         [
@@ -563,7 +612,7 @@
             shape(rows, hidden),
             shape(16, hidden),
             shape(8, rows),
-            shape(BLOCKS, images, shard),
+            shape(8, channels),
         ],
         own_rows,
         conv_other,
@@ -575,24 +624,26 @@
         scratch=[pltpu.VMEM((rows + 16, channels), bf16)],
         flops=2 * rows * channels * hidden,
     )
-    sums, pooled = run(
+    (mixed,) = run(
+        block_kernel,
+        [shape(BLOCKS, 2 * images, shard)],
+        mixed,
+        Far(head_other),
+        Far(project_other),
+    )
+    blocks, pooled = run(
         head_kernel,
-        [shape(8, width + 128), shape(images, shard)],
+        [shape(CHIPS, 8, width + 128), shape(images, shard)],
         shard_exchange(mixed),
-        input_mean,
-        layer_scale[None, :],
-        b_out[None, :],
-        head_gain[None, :],
-        head_bias[None, :],
+        head_own,
+        head_other,
         projection,
-    )
-    (blocks,) = run(
-        pair_sum_kernel, [shape(CHIPS, 8, width + 128)], sums, core_swap(sums)
+        project_other,
     )
     pair_block, own_block, back_rows, head_stat = run(
         embed_kernel,
         [
-            shape(shards, 16, width // 2 + 128, dtype=bf16),
+            shape(shards, 8, width + 128, dtype=bf16),
             shape(8, width),
             shape(8, width),
             shape(2, 8, 128),

time: 112 us -> 111 us (level)
    ppermute x3 -> x4, starting transfers between devices: 3.56 us -> 3.63 us  [core_swap(): return lax.ppermute(array, 'mp', [(i, i ^ 1) for i in range(BLOCKS)])]
  transfers between devices with their start and end apart: 3 -> 4, of which waited for: 2 -> 1; matrix products, arithmetic and copies ran while one was open for 0% -> 0% of each run, Pallas kernels for 3% -> 6%
where the time goes in v8:
time: 111 us; the launch traced here: 110 us
  blocking collectives  89.5 us (81%)
  Pallas kernels  14.1 us (13%)
  starting transfers between devices  3.63 us (3%)
  waiting for transfers between devices  1.15 us (1%)
    all_to_all x3, blocking collectives, chip_exchange(): return lax.all_to_all(array, 'mp', 0, 0, axis_index_groups=groups)  48.4 us
    all_to_all x2, blocking collectives, shard_exchange(): return lax.all_to_all(array, 'mp', 0, 0)  25.1 us
    all_to_all x1, blocking collectives, body(): lax.all_to_all(pair_block, 'dp', 0, 0)  16 us
    pallas_call x12, Pallas kernels, run(): pl.pallas_call(kernel, out_shape=[a.array if isinstance(a, Far) else a fo...  14.1 us
    ppermute x4, starting transfers between devices, core_swap(): return lax.ppermute(array, 'mp', [(i, i ^ 1) for i in range(BLOCKS)])  3.63 us
  transfers between devices with their start and end apart: 4, of which 1 were waited for; matrix products, arithmetic and copies ran while one was open for 0% of the time, Pallas kernels for 6%

profile of v8, /device:TPU:1, one launch (start us, length us, event | category | flops | bytes accessed | tf_op | source)
XLA Modules:
  0.0 110.3 jit_solution(2267393980368142938)
XLA Ops:
  0.6 0.0 copy-start.1
  0.6 0.0 copy-start.10
  0.7 0.0 copy-start.6
  0.7 0.0 copy-start.5
  0.7 0.0 copy-start.9
  0.7 0.0 copy-start.11
  0.7 0.0 copy-start.7
  0.7 0.0 slice-start.2
  0.7 0.7 copy-done.1
  1.5 0.0 copy-done.10
  1.5 0.0 copy-done.6
  1.5 0.0 copy-done.5
  1.5 0.0 copy-done.9
  1.5 0.0 copy-done.11
  1.5 0.2 copy-done.7
  1.7 0.0 copy-start
  1.7 0.0 copy-start.4
  1.7 0.0 slice-start.3
  1.7 0.0 copy-start.8
  1.7 0.0 copy-start.12
  1.7 1.2 %shard_map.159 = (bf16[8,192,256]{2,1,0:T(8,128)(2,1)S(1)}, bf16[192,256]{1,0:T(8,128)(2,1)S(1)}, f32[8,192]{1,0:T(8,128)S(1)}) custom-call(f32[8,128]{1,0:T(8,128)S(1)} %shard_map.158._, f32[1,192]{1,0:T(1,128)S(1)} %bitcast.15, f32[1,192]{1,0:T(1,128)S(1)} %bitcast.22, f32[1,192]{1,0:T(1,128)S(1)} %bitcast.17, f32[1,192]{1,0:T(1,128)S(1)} %bitcast.23, ...), custom_call_target="tpu_custom_call" | custom-call | flops 16000000000 | bytes 143872 | tf_op jit(solution)/shard_map/pallas_call | solution.py:51
  2.9 0.0 slice-start
  2.9 20.3 %all_to_all.30 = bf16[8,192,256]{2,1,0:T(8,128)(2,1)S(1)} all-to-all(bf16[8,192,256]{2,1,0:T(8,128)(2,1)S(1)} %get-tuple-element.29), channel_id=1, replica_groups={{0,2,4,6,8,10,12,14},{1,3,5,7,9,11,13,15},{16,18,20,22,24,26,28,30},{17..., dimensions={0} | all-to-all | bytes 1572864 | tf_op jit(solution)/shard_map/all_to_all | solution.py:32
  23.3 2.5 %collective-permute-start = (bf16[8,192,256]{2,1,0:T(8,128)(2,1)S(1)}, bf16[8,192,256]{2,1,0:T(8,128)(2,1)S(1)}, u32[]{:S(2)}, u32[]{:S(2)}) collective-permute-start(bf16[8,192,256]{2,1,0:T(8,128)(2,1)S(1)} %all_to_all.30), channel_id=1, source_target_pairs={{0,1},{1,0},{2,3},{3,2},{4,5},{5,4},{6,7},{7,6},{8,9},{9,8},{10,11... | collective-permute-start | bytes 2359304 | tf_op jit(solution)/shard_map/ppermute | solution.py:27
  25.8 0.0 slice-done.2
  25.8 0.0 copy-done
  25.8 0.0 copy-done.4
  25.8 0.0 slice-done.3
  25.8 0.0 copy-done.8
  25.8 0.0 copy-done.12
  25.8 0.0 slice-start.1
  25.8 0.0 copy-start.2
  25.8 2.4 %shard_map.160 = (bf16[256,1536]{1,0:T(8,128)(2,1)S(1)}, f32[8,256]{1,0:T(8,128)S(1)}, f32[8,3072]{1,0:T(8,128)S(1)}, bf16[3072,768]{1,0:T(8,128)(2,1)S(1)}, f32...) custom-call(bf16[1536,256]{1,0:T(8,128)(2,1)S(1)} %bitcast.12, f32[1,3072]{1,0:T(1,128)S(1)} %bitcast.13, ...), custom_call_target="tpu_custom_call" | custom-call | flops 12000000000 | bytes 5928976 | tf_op jit(solution)/shard_map/pallas_call | solution.py:51
  28.2 0.1 collective-permute-start.2
  28.3 0.5 collective-permute-start.1
  28.8 0.0 collective-permute-done
  28.8 0.0 slice-done
  28.8 0.0 slice-done.1
  28.8 0.0 copy-done.2
  28.9 0.0 copy-start.3
  28.9 3.0 %shard_map.161 = (f32[256,768]{1,0:T(8,128)S(1)}, f32[256,768]{1,0:T(8,128)S(1)}, f32[16,768]{1,0:T(8,128)S(1)}, f32[8,256]{1,0:T(8,128)S(1)}, f32[8,3072]{1,0:T(8,128)S(1)}) custom-call(bf16[256,1536]{1,0:T(8,128)(2,1)S(1)} %get-tuple-element.32.rows_ref, bf16[1536,256]{1,0:T(8,128)(2,1)S(1)} %bitcast.11, f32[8,256]{1,0:T(8,128)S(1)} %get-tuple-element.33.part_ref, ...), custom_call_target="tpu_custom_call" | custom-call | flops 1207959552 | bytes 11119616 | tf_op jit(solution)/shard_map/pallas_call | solution.py:51
  31.9 0.0 collective-permute-done.1._head.other_ref
  31.9 0.0 collective-permute-done.2._project.project_other_ref
  31.9 0.1 shard_map.162
  32.0 10.4 %all_to_all.31.got_ref = f32[16,8,192]{2,1,0:T(8,128)S(1)} all-to-all(f32[16,8,192]{2,1,0:T(8,128)S(1)} %shard_map.162), channel_id=1, replica_groups=mesh['dp'=16,'mp'=16] {'mp'}, dimensions={0} | all-to-all | bytes 196608 | tf_op jit(solution)/shard_map/all_to_all | solution.py:36
  42.4 0.3 shard_map.163
  42.7 11.0 %all_to_all.32.got_ref = f32[8,8,1152]{2,1,0:T(8,128)S(1)} all-to-all(f32[8,8,1152]{2,1,0:T(8,128)S(1)} %get-tuple-element.38), channel_id=1, replica_groups={{0,2,4,6,8,10,12,14},{1,3,5,7,9,11,13,15},{16,18,20,22,24,26,28,30},{17..., dimensions={0} | all-to-all | bytes 589824 | tf_op jit(solution)/shard_map/all_to_all | solution.py:32
  53.7 0.0 copy-done.3
  53.7 0.2 shard_map.164
  53.9 16.0 %all_to_all.33.got_ref = bf16[16,8,1152]{2,1,0:T(8,128)(2,1)S(1)} all-to-all(bf16[16,8,1152]{2,1,0:T(8,128)(2,1)S(1)} %get-tuple-element.40), channel_id=1, replica_groups=mesh['dp'=16,'mp'=16] {'dp'}, dimensions={0} | all-to-all | bytes 589824 | tf_op jit(solution)/shard_map/all_to_all | solution.py:658
  69.9 1.4 %shard_map.165 = (f32[4,1024]{1,0:T(4,128)}, f32[4,192]{1,0:T(4,128)S(1)}, f32[16,4,192]{2,1,0:T(4,128)S(1)}) custom-call(bf16[16,8,1152]{2,1,0:T(8,128)(2,1)S(1)} %all_to_all.33.got_ref, f32[8,1024]{1,0:T(8,128)S(1)} %get-tuple-element.41.own_ref, f32[8,1024]{1,0:T(8,128)S(1)} %get-tuple-element.42.rows_ref, f32[2,8,128]{2,1,0:T(8,128)S(1)} %get-tuple-element.43.stat_ref, ...), custom_call_target="tpu_custom_call" | custom-call | bytes 766464 | tf_op jit(solution)/shard_map/pallas_call | solution.py:51
  71.4 14.7 %all_to_all.34.got_ref = f32[16,4,192]{2,1,0:T(4,128)S(1)} all-to-all(f32[16,4,192]{2,1,0:T(4,128)S(1)} %get-tuple-element.45), channel_id=1, replica_groups=mesh['dp'=16,'mp'=16] {'mp'}, dimensions={0} | all-to-all | bytes 98304 | tf_op jit(solution)/shard_map/all_to_all | solution.py:36
  86.1 2.4 %shard_map.166 = (bf16[1552,256]{1,0:T(8,128)(2,1)S(1)}, bf16[768,256]{1,0:T(8,128)(2,1)S(1)}, f32[8,256]{1,0:T(8,128)S(1)}) custom-call(f32[16,4,192]{2,1,0:T(4,128)S(1)} %all_to_all.34.got_ref, bf16[768,3072]{1,0:T(8,128)(2,1)S(1)} %bitcast.10, f32[256,768]{1,0:T(8,128)S(1)} %get-tuple-element.46.slope_ref, f32[256,768]{1,0:T(8,128)S(1)} %get-tuple-element.47.hidden_ref, ...), custom_call_target="tpu_custom_call" | custom-call | flops 603979776 | bytes 11111424 | tf_op jit(solution)/shard_map/pallas_call | solution.py:51
  88.5 0.5 collective-permute-start.3
  89.0 0.8 shard_map.167.mine_ref
  89.8 1.1 %collective-permute-done.3.got_ref = bf16[1552,256]{1,0:T(8,128)(2,1)S(1)} collective-permute-done((bf16[1552,256]{1,0:T(8,128)(2,1)S(1)}, bf16[1552,256]{1,0:T(8,128)(2,1)S(1)}, u32[]{:S(2)}, u32[]{:S(2)}) %collective-permute-start.3) | collective-permute-done | bytes 794656 | tf_op jit(solution)/shard_map/ppermute | solution.py:27
  91.0 0.2 shard_map.168
  91.2 17.1 %all_to_all.35.got_ref = bf16[8,208,256]{2,1,0:T(8,128)(2,1)S(1)} all-to-all(bf16[8,208,256]{2,1,0:T(8,128)(2,1)S(1)} %shard_map.168), channel_id=1, replica_groups={{0,2,4,6,8,10,12,14},{1,3,5,7,9,11,13,15},{16,18,20,22,24,26,28,30},{17..., dimensions={0} | all-to-all | bytes 1703936 | tf_op jit(solution)/shard_map/all_to_all | solution.py:32
  108.2 2.1 %shard_map.169 = f32[4,8,8,192]{3,2,1,0:T(8,128)} custom-call(bf16[8,208,256]{2,1,0:T(8,128)(2,1)S(1)} %all_to_all.35.got_ref, bf16[192,256]{1,0:T(8,128)(2,1)S(1)} %get-tuple-element.52.conv_ref, f32[8,256]{1,0:T(8,128)S(1)} %get-tuple-element.53.stat_ref, f32[1,3072]{1,0:T(1,128)S(1)} %bitcast.14, f32[7,7,192]{2,1,0:T(8,128)S(1)} %copy-done.1, ...), custom_call_target="tpu_custom_call" | custom-call | flops 4816896 | bytes 1011456 | tf_op jit(solution)/shard_map/pallas_call | solution.py:51
  (3 shorter events, 0.0 us)
Async XLA Ops:
  0.6 0.8 copy-start.1
  0.6 0.8 copy-start.10
  0.7 0.8 copy-start.6
  0.7 0.8 copy-start.5
  0.7 0.8 copy-start.9
  0.7 0.8 copy-start.11
  0.7 1.0 copy-start.7
  0.7 25.1 %slice-start.2 = ((s8[4718592]{0:T(1024)(128)(4,1)}), s8[4194304]{0:T(1024)(128)(4,1)S(1)}, s32[]{:S(2)}) async-start(s8[4718592]{0:T(1024)(128)(4,1)} %bitcast.19), calls=%async_computation.8 | async-start | bytes 8388608
  1.7 24.1 %copy-start = (bf16[192,1024]{1,0:T(8,128)(2,1)S(1)}, bf16[192,1024]{1,0:T(8,128)(2,1)}, u32[]{:S(2)}) copy-start(bf16[192,1024]{1,0:T(8,128)(2,1)} %project_ref.3) | copy-start | bytes 1179652
  1.7 24.1 %copy-start.4 = (f32[3072]{0:T(1024)S(1)}, f32[3072]{0:T(1024)}, u32[]{:S(2)}) copy-start(f32[3072]{0:T(1024)} %param.18) | copy-start | bytes 36868
  1.7 24.1 %slice-start.3 = ((s8[4718592]{0:T(1024)(128)(4,1)}), s8[524288]{0:T(1024)(128)(4,1)S(1)}, s32[]{:S(2)}) async-start(s8[4718592]{0:T(1024)(128)(4,1)} %bitcast.19), calls=%async_computation.9 | async-start | bytes 1048576
  1.7 24.1 %copy-start.8 = (f32[3072]{0:T(1024)S(1)}, f32[3072]{0:T(1024)}, u32[]{:S(2)}) copy-start(f32[3072]{0:T(1024)} %param.19) | copy-start | bytes 36868
  1.7 24.1 %copy-start.12 = (s32[4]{0:T(128)S(1)}, s32[4]{0:T(128)}, u32[]{:S(2)}) copy-start(s32[4]{0:T(128)} %labels_ref.1) | copy-start | bytes 52
  2.9 25.9 %slice-start = ((s8[4718592]{0:T(1024)(128)(4,1)}), s8[4194304]{0:T(1024)(128)(4,1)S(1)}, s32[]{:S(2)}) async-start(s8[4718592]{0:T(1024)(128)(4,1)} %bitcast.9), calls=%async_computation.6 | async-start | bytes 8388608
  23.3 5.6 %collective-permute-start = (bf16[8,192,256]{2,1,0:T(8,128)(2,1)S(1)}, bf16[8,192,256]{2,1,0:T(8,128)(2,1)S(1)}, u32[]{:S(2)}, u32[]{:S(2)}) collective-permute-start(bf16[8,192,256]{2,1,0:T(8,128)(2,1)S(1)} %all_to_all.30), channel_id=1, source_target_pairs={{0,1},{1,0},{2,3},{3,2},{4,5},{5,4},{6,7},{7,6},{8,9},{9,8},{10,11... | collective-permute-start | bytes 2359304 | tf_op jit(solution)/shard_map/ppermute | solution.py:27
  25.8 3.0 %slice-start.1 = ((s8[4718592]{0:T(1024)(128)(4,1)}), s8[524288]{0:T(1024)(128)(4,1)S(1)}, s32[]{:S(2)}) async-start(s8[4718592]{0:T(1024)(128)(4,1)} %bitcast.9), calls=%async_computation.7 | async-start | bytes 1048576
  25.8 3.0 %copy-start.2 = (f32[768]{0:T(1024)S(1)}, f32[768]{0:T(1024)}, u32[]{:S(2)}) copy-start(f32[768]{0:T(1024)} %b_ref.3) | copy-start | bytes 9220
  28.2 3.6 %collective-permute-start.2 = (bf16[192,1024]{1,0:T(8,128)(2,1)S(1)}, bf16[192,1024]{1,0:T(8,128)(2,1)S(1)}, u32[]{:S(2)}, u32[]{:S(2)}) collective-permute-start(bf16[192,1024]{1,0:T(8,128)(2,1)S(1)} %get-tuple-element.37), channel_id=1, source_target_pairs={{0,1},{1,0},{2,3},{3,2},{4,5},{5,4},{6,7},{7,6},{8,9},{9,8},{10,11... | collective-permute-start | bytes 1179656 | tf_op jit(solution)/shard_map/ppermute | solution.py:27
  28.3 3.5 %collective-permute-start.1 = (f32[8,192]{1,0:T(8,128)S(1)}, f32[8,192]{1,0:T(8,128)S(1)}, u32[]{:S(2)}, u32[]{:S(2)}) collective-permute-start(f32[8,192]{1,0:T(8,128)S(1)} %get-tuple-element.36), channel_id=1, source_target_pairs={{0,1},{1,0},{2,3},{3,2},{4,5},{5,4},{6,7},{7,6},{8,9},{9,8},{10,11... | collective-permute-start | bytes 18440 | tf_op jit(solution)/shard_map/ppermute | solution.py:27
  28.9 24.8 %copy-start.3 = (f32[4,1024]{1,0:T(4,128)S(1)}, f32[4,1024]{1,0:T(4,128)}, u32[]{:S(2)}) copy-start(f32[4,1024]{1,0:T(4,128)} %text_ref.1) | copy-start | bytes 49156
  88.5 2.4 %collective-permute-start.3 = (bf16[1552,256]{1,0:T(8,128)(2,1)S(1)}, bf16[1552,256]{1,0:T(8,128)(2,1)S(1)}, u32[]{:S(2)}, u32[]{:S(2)}) collective-permute-start(bf16[1552,256]{1,0:T(8,128)(2,1)S(1)} %get-tuple-element.50), channel_id=1, source_target_pairs={{0,1},{1,0},{2,3},{3,2},{4,5},{5,4},{6,7},{7,6},{8,9},{9,8},{10,11... | collective-permute-start | bytes 2383880 | tf_op jit(solution)/shard_map/ppermute | solution.py:27

commit v9 on v8

--- a/solution.py
+++ b/solution.py
@@ -108,16 +108,12 @@
 
 def conv_kernel(
     _,
-    scale_ref,
-    bout_ref,
-    gain_ref,
-    shift_ref,
     x_far,
     dw_far,
     bias_far,
     copies_ref,
     conv_ref,
-    head_ref,
+    mean_ref,
     x_ref,
     dw_ref,
     bias_ref,
@@ -136,14 +132,12 @@
     def image(n, carry):
         x = x_ref[n].astype(f32)
         total = jnp.sum(jnp.sum(x, axis=0), axis=0, keepdims=True)
-        head_ref[pl.ds(n, 1), :] = total / positions
+        mean_ref[pl.ds(n, 1), :] = total / positions
         for p, row in enumerate(taps(x, dw_ref, False)):
             rows_ref[pl.ds(pl.multiple_of(n * positions + p * side, side), side), :] = row
         return carry
 
     lax.fori_loop(0, images, image, 0)
-    for i, ref in enumerate((scale_ref, bout_ref, gain_ref, shift_ref)):
-        head_ref[images + i : images + i + 1, :] = ref[...]
     turned = (rows_ref[...] + bias_ref[...]).T.astype(bf16)
     conv_ref[...] = turned
     for j in range(CHIPS):
@@ -155,16 +149,21 @@
     gain_ref,
     bias_ref,
     w_ref,
-    labels_ref,
-    head_ref,
+    labels_far,
+    mean_ref,
+    scale_ref,
+    bout_ref,
+    head_gain_ref,
+    head_bias_ref,
     project_far,
     rows_ref,
     part_ref,
     vec_ref,
     own_ref,
     tail_ref,
-    head_out_ref,
+    head_ref,
     project_ref,
+    labels_ref,
     sems,
 ):
     shard = w_ref.shape[0] // BLOCKS
@@ -178,10 +177,22 @@
                 w_ref.at[source], own_ref.at[k * shard : (k + 1) * shard], sems.at[k]
             )
         )
-    moves.append(pltpu.make_async_copy(project_far, project_ref, sems.at[BLOCKS]))
+    moves.append(
+        pltpu.make_async_copy(project_far, project_ref.at[0:shard], sems.at[BLOCKS])
+    )
+    load = pltpu.make_async_copy(labels_far, labels_ref, sems.at[BLOCKS + 1])
+    load.start()
     for copy in moves:
         copy.start()
-    head_out_ref[...] = head_ref[...]
+    head_ref[0:4, :] = mean_ref[...]
+    for i, ref in enumerate((scale_ref, bout_ref, head_gain_ref, head_bias_ref)):
+        head_ref[4 + i : 5 + i, :] = ref[...]
+    high, rest = to_terms(head_ref[...])
+    middle, low = to_terms(rest)
+    project_ref[shard:, :] = jnp.zeros_like(project_ref[shard:, :])
+    for i, term in enumerate((high, middle, low)):
+        sent = jnp.concatenate([term, jnp.zeros_like(term)], axis=0).astype(bf16)
+        project_ref[shard:, i * 256 : i * 256 + shard] = sent
     half, rows = mine_ref.shape
     step = 256
     first = jnp.zeros((1, rows), f32)
@@ -203,6 +214,7 @@
             vec_ref[i : i + 1, half + j * shard : half + (j + 1) * shard] = jnp.where(
                 core == 0, high, low
             )
+    load.wait()
     pairs = labels_ref.shape[0]
     row = iota((8, 128), 0)
     tail = jnp.zeros((8, 128), f32)
@@ -283,7 +295,7 @@
     mixed_ref[...] = mixed
 
 
-def block_kernel(mixed_ref, _head, _project, out_ref):
+def block_kernel(mixed_ref, _project, out_ref):
     shard = out_ref.shape[2]
     images = out_ref.shape[1] // 2
     for k in range(BLOCKS):
@@ -292,9 +304,7 @@
         out_ref[k ^ 1, images:, :] = block
 
 
-def head_kernel(
-    got_ref, own_ref, other_ref, project_ref, project_other_ref, out_ref, pooled_ref
-):
+def head_kernel(got_ref, own_ref, project_ref, other_ref, out_ref, pooled_ref):
     images = pooled_ref.shape[0]
     width = project_ref.shape[1]
     mixed = got_ref[0]
@@ -303,13 +313,19 @@
     first = jnp.zeros((8, 1), f32)
     second = jnp.zeros((8, 1), f32)
     product = jnp.zeros((24, width), f32)
-    sides = ((own_ref, project_ref, mixed[:images]), (other_ref, project_other_ref, mixed[images:]))
-    for head_ref, weight_ref, part in sides:
-        gain = head_ref[6:7, :]
-        pooled = head_ref[:images, :] + head_ref[4:5, :] * (part + head_ref[5:6, :])
-        if head_ref is own_ref:
+    shard = own_ref.shape[1]
+    sent = other_ref[shard:, :].astype(f32)[:8]
+    other = sent[:, :shard] + (sent[:, 256 : 256 + shard] + sent[:, 512 : 512 + shard])
+    sides = (
+        (own_ref[...], project_ref[...], mixed[:images]),
+        (other, other_ref[:shard, :], mixed[images:]),
+    )
+    for i, (rows, weight, part) in enumerate(sides):
+        gain = rows[6:7, :]
+        pooled = rows[:images, :] + rows[4:5, :] * (part + rows[5:6, :])
+        if i == 0:
             pooled_ref[...] = pooled
-        head = jnp.concatenate([pooled, head_ref[images:, :]], axis=0)
+        head = jnp.concatenate([pooled, rows[images:, :]], axis=0)
         first = first + jnp.sum(head, axis=1, keepdims=True)
         second = second + jnp.sum(head * head, axis=1, keepdims=True)
         value = jnp.where(iota(head.shape, 0) < images, head * gain, head)
@@ -317,7 +333,7 @@
         middle, low = to_terms(rest)
         product = product + jnp.dot(
             jnp.concatenate([high, middle, low], axis=0).astype(bf16),
-            weight_ref[...],
+            weight,
             preferred_element_type=f32,
         )
     product = product[:8] + (product[8:16] + product[16:])
@@ -474,7 +490,18 @@
     ).astype(bf16)
 
 
-def mine_kernel(w_ref, turned_ref, mine_ref):
+def mine_kernel(
+    w_ref, turned_ref, conv_ref, stat_ref, gain_ref, mine_ref, scaled_ref, centred_ref, row_ref
+):
+    shard = conv_ref.shape[0]
+    index = lax.axis_index("mp")
+    pair = gain_ref[:, pl.ds(pl.multiple_of(index // 2 * 2 * shard, 128), 2 * shard)]
+    gain = jnp.where(index % 2 == 0, pair[:, :shard], pair[:, shard:])
+    gain = jnp.broadcast_to(gain, (8, shard)).T[:, 0:1]
+    average, inverse = stat_ref[0:1, :], stat_ref[1:2, :]
+    scaled_ref[...] = gain * inverse
+    centred_ref[...] = (conv_ref[...].astype(f32) - average) * (inverse * inverse)
+    row_ref[...] = jnp.broadcast_to(inverse, row_ref.shape)
     mine_ref[...] = jnp.dot(
         w_ref[: mine_ref.shape[0], :], turned_ref[...], preferred_element_type=f32
     ).astype(bf16)
@@ -496,14 +523,10 @@
 
 
 def final_kernel(
-    got_ref, conv_ref, stat_ref, gain_ref, w_ref, block_ref, out_far, rows_ref, out_ref, sems
+    got_ref, scaled_ref, centred_ref, row_ref, w_ref, block_ref, out_far, rows_ref, out_ref, sems
 ):
-    shard = conv_ref.shape[0]
+    shard = scaled_ref.shape[0]
     channels = shard * BLOCKS
-    index = lax.axis_index("mp")
-    pair = gain_ref[:, pl.ds(pl.multiple_of(index // 2 * 2 * shard, 128), 2 * shard)]
-    gain = jnp.where(index % 2 == 0, pair[:, :shard], pair[:, shard:])
-    gain = jnp.broadcast_to(gain, (8, shard)).T[:, 0:1]
     images, side = out_ref.shape[:2]
     positions = side * side
     total = got_ref[0].astype(f32)
@@ -511,9 +534,8 @@
         total = total + got_ref[j].astype(f32)
     first = (total[shard : shard + 1] + total[shard + 8 : shard + 9]) / channels
     second = (total[shard + 1 : shard + 2] + total[shard + 9 : shard + 10]) / channels
-    average, inverse = stat_ref[0:1, :], stat_ref[1:2, :]
-    centred = (conv_ref[...].astype(f32) - average) * inverse
-    grad = inverse * (total[:shard] * gain - first - centred * second)
+    first = first * row_ref[0:1, :]
+    grad = total[:shard] * scaled_ref[...] - first - centred_ref[...] * second
     rows_ref[...] = grad.T
 
     def image(n, carry):
@@ -553,18 +575,14 @@
     pairs, width = text_emb.shape
     shards = lax.axis_size("dp")
     (begun,) = run(start_kernel, [shape(8, 128)], flops=START_FLOPS)
-    copies, conv, head_own = run(
+    copies, conv, input_mean = run(
         conv_kernel,
         [
             shape(CHIPS, shard, rows, dtype=bf16),
             shape(shard, rows, dtype=bf16),
-            shape(8, shard),
+            shape(images, shard),
         ],
         Far(begun),
-        layer_scale[None, :],
-        b_out[None, :],
-        head_gain[None, :],
-        head_bias[None, :],
         Far(x_in),
         Far(dw_weight),
         Far(dw_bias[None, :]),
@@ -582,7 +600,7 @@
     conv_other = core_swap(conv_mine)
     conv_mine = conv_mine.reshape(channels // 2, rows)
     conv_other = conv_other.reshape(channels // 2, rows)
-    own_rows, part, vec, w_own, tail, head_sent, project_sent = run(
+    own_rows, part, vec, w_own, tail, head_own, project_sent = run(
         ready_kernel,
         [
             shape(rows, channels // 2, dtype=bf16),
@@ -591,19 +609,22 @@
             shape(channels, hidden, dtype=bf16),
             shape(8, 128),
             shape(8, shard),
-            shape(shard, width, dtype=bf16),
+            shape(shard + 16, width, dtype=bf16),
         ],
         conv_mine,
         ln_gain[None, :],
         ln_bias[None, :],
         w_in,
-        labels,
-        head_own,
+        Far(labels),
+        input_mean,
+        layer_scale[None, :],
+        b_out[None, :],
+        head_gain[None, :],
+        head_bias[None, :],
         Far(projection),
-        scratch=[pltpu.SemaphoreType.DMA((BLOCKS + 1,))],
+        scratch=[pltpu.SMEM(labels.shape, jnp.int32), pltpu.SemaphoreType.DMA((BLOCKS + 2,))],
         flops=READY_FLOPS,
     )
-    head_other = core_swap(head_sent)
     project_other = core_swap(project_sent)
     slope, hidden_pre, through, row_stat, mixed = run(
         forward_kernel,
@@ -628,7 +649,6 @@
         block_kernel,
         [shape(BLOCKS, 2 * images, shard)],
         mixed,
-        Far(head_other),
         Far(project_other),
     )
     blocks, pooled = run(
@@ -636,7 +656,6 @@
         [shape(CHIPS, 8, width + 128), shape(images, shard)],
         shard_exchange(mixed),
         head_own,
-        head_other,
         projection,
         project_other,
     )
@@ -687,11 +706,19 @@
         flops=rows * channels * hidden,
     )
     passed = core_swap(other)
-    (mine,) = run(
+    mine, scaled, centred, row_inverse = run(
         mine_kernel,
-        [shape(channels // 2, rows, dtype=bf16)],
+        [
+            shape(channels // 2, rows, dtype=bf16),
+            shape(shard, rows),
+            shape(shard, rows),
+            shape(8, rows),
+        ],
         w_own,
         turned,
+        conv,
+        row_stat,
+        ln_gain[None, :],
         flops=rows * channels * hidden,
     )
     (blocks,) = run(
@@ -701,9 +728,9 @@
         final_kernel,
         [Far(shape(images, side, side, shard))],
         chip_exchange(blocks),
-        conv,
-        row_stat,
-        ln_gain[None, :],
+        scaled,
+        centred,
+        row_inverse,
         dw_weight,
         grad_block,
         scratch=[

time: 111 us -> 110 us (level)
    ppermute x4 -> x3, starting transfers between devices: 3.63 us -> 3.14 us  [core_swap(): return lax.ppermute(array, 'mp', [(i, i ^ 1) for i in range(BLOCKS)])]
  transfers between devices with their start and end apart: 4 -> 3, of which waited for: 1 -> 1; matrix products, arithmetic and copies ran while one was open for 0% -> 0% of each run, Pallas kernels for 6% -> 5%
where the time goes in v9:
time: 110 us
  blocking collectives  89.9 us (82%)
  Pallas kernels  13.5 us (12%)
  starting transfers between devices  3.14 us (3%)
  waiting for transfers between devices  1.13 us (1%)
    all_to_all x3, blocking collectives, chip_exchange(): return lax.all_to_all(array, 'mp', 0, 0, axis_index_groups=groups)  48.4 us
    all_to_all x2, blocking collectives, shard_exchange(): return lax.all_to_all(array, 'mp', 0, 0)  25.4 us
    all_to_all x1, blocking collectives, body(): lax.all_to_all(pair_block, 'dp', 0, 0)  16 us
    pallas_call x12, Pallas kernels, run(): pl.pallas_call(kernel, out_shape=[a.array if isinstance(a, Far) else a fo...  13.5 us
    ppermute x3, starting transfers between devices, core_swap(): return lax.ppermute(array, 'mp', [(i, i ^ 1) for i in range(BLOCKS)])  3.14 us
  transfers between devices with their start and end apart: 3, of which 1 were waited for; matrix products, arithmetic and copies ran while one was open for 0% of the time, Pallas kernels for 5%

profile of v9, /device:TPU:1, one launch (start us, length us, event | category | flops | bytes accessed | tf_op | source)
XLA Modules:
  0.0 109.5 jit_solution(3569737390237296353)
XLA Ops:
  0.6 0.0 copy-start.1
  0.6 0.0 copy-start.9
  0.6 0.0 copy-start.7
  0.7 0.0 slice-start.2
  0.7 0.8 copy-done.1
  1.4 0.0 copy-done.9
  1.5 0.1 copy-done.7
  1.6 0.0 copy-start
  1.6 0.0 copy-start.4
  1.6 0.0 copy-start.5
  1.6 0.0 copy-start.6
  1.6 0.0 slice-start.3
  1.6 0.0 copy-start.8
  1.6 0.0 copy-start.10
  1.6 0.0 copy-start.11
  1.6 0.0 copy-start.12
  1.7 1.2 %shard_map.159 = (bf16[8,192,256]{2,1,0:T(8,128)(2,1)S(1)}, bf16[192,256]{1,0:T(8,128)(2,1)S(1)}, f32[4,192]{1,0:T(4,128)S(1)}) custom-call(f32[8,128]{1,0:T(8,128)S(1)} %shard_map.158._, bf16[4,8,8,192]{3,2,1,0:T(8,128)(2,1)S(1)} %copy-done.7, f32[7,7,192]{2,1,0:T(8,128)S(1)} %copy-done.1, f32[1,192]{1,0:T(1,128)S(1)} %bitcast.22), custom_call_target="tpu_custom_call" | custom-call | flops 16000000000 | bytes 140800 | tf_op jit(solution)/shard_map/pallas_call | solution.py:51
  2.9 0.0 slice-start
  2.9 20.3 %all_to_all.30 = bf16[8,192,256]{2,1,0:T(8,128)(2,1)S(1)} all-to-all(bf16[8,192,256]{2,1,0:T(8,128)(2,1)S(1)} %get-tuple-element.33), channel_id=1, replica_groups={{0,2,4,6,8,10,12,14},{1,3,5,7,9,11,13,15},{16,18,20,22,24,26,28,30},{17..., dimensions={0} | all-to-all | bytes 1572864 | tf_op jit(solution)/shard_map/all_to_all | solution.py:32
  23.2 2.5 %collective-permute-start = (bf16[8,192,256]{2,1,0:T(8,128)(2,1)S(1)}, bf16[8,192,256]{2,1,0:T(8,128)(2,1)S(1)}, u32[]{:S(2)}, u32[]{:S(2)}) collective-permute-start(bf16[8,192,256]{2,1,0:T(8,128)(2,1)S(1)} %all_to_all.30), channel_id=1, source_target_pairs={{0,1},{1,0},{2,3},{3,2},{4,5},{5,4},{6,7},{7,6},{8,9},{9,8},{10,11... | collective-permute-start | bytes 2359304 | tf_op jit(solution)/shard_map/ppermute | solution.py:27
  25.8 0.0 slice-done.2
  25.8 0.0 copy-done
  25.8 0.0 copy-done.4
  25.8 0.0 copy-done.5
  25.8 0.0 copy-done.6
  25.8 0.0 slice-done.3
  25.8 0.0 copy-done.8
  25.8 0.0 copy-done.10
  25.8 0.0 copy-done.11
  25.8 0.0 copy-done.12
  25.8 0.0 slice-start.1
  25.9 0.0 copy-start.2
  25.9 1.9 %shard_map.160 = (bf16[256,1536]{1,0:T(8,128)(2,1)S(1)}, f32[8,256]{1,0:T(8,128)S(1)}, f32[8,3072]{1,0:T(8,128)S(1)}, bf16[3072,768]{1,0:T(8,128)(2,1)S(1)}, f32...) custom-call(bf16[1536,256]{1,0:T(8,128)(2,1)S(1)} %bitcast.12, f32[1,3072]{1,0:T(1,128)S(1)} %bitcast.13, ...), custom_call_target="tpu_custom_call" | custom-call | flops 12000000000 | bytes 5928976 | tf_op jit(solution)/shard_map/pallas_call | solution.py:51
  27.8 0.1 collective-permute-start.1
  27.9 0.0 collective-permute-done
  27.9 0.0 slice-done
  27.9 0.0 slice-done.1
  27.9 0.0 copy-done.2
  27.9 0.0 copy-start.3
  27.9 3.0 %shard_map.161 = (f32[256,768]{1,0:T(8,128)S(1)}, f32[256,768]{1,0:T(8,128)S(1)}, f32[16,768]{1,0:T(8,128)S(1)}, f32[8,256]{1,0:T(8,128)S(1)}, f32[8,3072]{1,0:T(8,128)S(1)}) custom-call(bf16[256,1536]{1,0:T(8,128)(2,1)S(1)} %get-tuple-element.36.rows_ref, bf16[1536,256]{1,0:T(8,128)(2,1)S(1)} %bitcast.11, f32[8,256]{1,0:T(8,128)S(1)} %get-tuple-element.37.part_ref, ...), custom_call_target="tpu_custom_call" | custom-call | flops 1207959552 | bytes 11119616 | tf_op jit(solution)/shard_map/pallas_call | solution.py:51
  30.9 0.0 collective-permute-done.1._project.other_ref
  30.9 0.1 shard_map.162
  31.0 10.7 %all_to_all.31.got_ref = f32[16,8,192]{2,1,0:T(8,128)S(1)} all-to-all(f32[16,8,192]{2,1,0:T(8,128)S(1)} %shard_map.162), channel_id=1, replica_groups=mesh['dp'=16,'mp'=16] {'mp'}, dimensions={0} | all-to-all | bytes 196608 | tf_op jit(solution)/shard_map/all_to_all | solution.py:36
  41.8 0.3 shard_map.163
  42.1 11.0 %all_to_all.32.got_ref = f32[8,8,1152]{2,1,0:T(8,128)S(1)} all-to-all(f32[8,8,1152]{2,1,0:T(8,128)S(1)} %get-tuple-element.42), channel_id=1, replica_groups={{0,2,4,6,8,10,12,14},{1,3,5,7,9,11,13,15},{16,18,20,22,24,26,28,30},{17..., dimensions={0} | all-to-all | bytes 589824 | tf_op jit(solution)/shard_map/all_to_all | solution.py:32
  53.1 0.0 copy-done.3
  53.1 0.2 shard_map.164
  53.3 16.0 %all_to_all.33.got_ref = bf16[16,8,1152]{2,1,0:T(8,128)(2,1)S(1)} all-to-all(bf16[16,8,1152]{2,1,0:T(8,128)(2,1)S(1)} %get-tuple-element.44), channel_id=1, replica_groups=mesh['dp'=16,'mp'=16] {'dp'}, dimensions={0} | all-to-all | bytes 589824 | tf_op jit(solution)/shard_map/all_to_all | solution.py:677
  69.3 1.4 %shard_map.165 = (f32[4,1024]{1,0:T(4,128)}, f32[4,192]{1,0:T(4,128)S(1)}, f32[16,4,192]{2,1,0:T(4,128)S(1)}) custom-call(bf16[16,8,1152]{2,1,0:T(8,128)(2,1)S(1)} %all_to_all.33.got_ref, f32[8,1024]{1,0:T(8,128)S(1)} %get-tuple-element.45.own_ref, f32[8,1024]{1,0:T(8,128)S(1)} %get-tuple-element.46.rows_ref, f32[2,8,128]{2,1,0:T(8,128)S(1)} %get-tuple-element.47.stat_ref, ...), custom_call_target="tpu_custom_call" | custom-call | bytes 766464 | tf_op jit(solution)/shard_map/pallas_call | solution.py:51
  70.8 14.7 %all_to_all.34.got_ref = f32[16,4,192]{2,1,0:T(4,128)S(1)} all-to-all(f32[16,4,192]{2,1,0:T(4,128)S(1)} %get-tuple-element.49), channel_id=1, replica_groups=mesh['dp'=16,'mp'=16] {'mp'}, dimensions={0} | all-to-all | bytes 98304 | tf_op jit(solution)/shard_map/all_to_all | solution.py:36
  85.5 2.5 %shard_map.166 = (bf16[1552,256]{1,0:T(8,128)(2,1)S(1)}, bf16[768,256]{1,0:T(8,128)(2,1)S(1)}, f32[8,256]{1,0:T(8,128)S(1)}) custom-call(f32[16,4,192]{2,1,0:T(4,128)S(1)} %all_to_all.34.got_ref, bf16[768,3072]{1,0:T(8,128)(2,1)S(1)} %bitcast.10, f32[256,768]{1,0:T(8,128)S(1)} %get-tuple-element.50.slope_ref, f32[256,768]{1,0:T(8,128)S(1)} %get-tuple-element.51.hidden_ref, ...), custom_call_target="tpu_custom_call" | custom-call | flops 603979776 | bytes 11111424 | tf_op jit(solution)/shard_map/pallas_call | solution.py:51
  87.9 0.5 collective-permute-start.2
  88.4 0.8 shard_map.167
  89.2 1.1 %collective-permute-done.2.got_ref = bf16[1552,256]{1,0:T(8,128)(2,1)S(1)} collective-permute-done((bf16[1552,256]{1,0:T(8,128)(2,1)S(1)}, bf16[1552,256]{1,0:T(8,128)(2,1)S(1)}, u32[]{:S(2)}, u32[]{:S(2)}) %collective-permute-start.2) | collective-permute-done | bytes 794656 | tf_op jit(solution)/shard_map/ppermute | solution.py:27
  90.4 0.2 shard_map.168
  90.6 17.1 %all_to_all.35.got_ref = bf16[8,208,256]{2,1,0:T(8,128)(2,1)S(1)} all-to-all(bf16[8,208,256]{2,1,0:T(8,128)(2,1)S(1)} %shard_map.168), channel_id=1, replica_groups={{0,2,4,6,8,10,12,14},{1,3,5,7,9,11,13,15},{16,18,20,22,24,26,28,30},{17..., dimensions={0} | all-to-all | bytes 1703936 | tf_op jit(solution)/shard_map/all_to_all | solution.py:32
  107.6 1.9 %shard_map.169 = f32[4,8,8,192]{3,2,1,0:T(8,128)} custom-call(bf16[8,208,256]{2,1,0:T(8,128)(2,1)S(1)} %all_to_all.35.got_ref, f32[192,256]{1,0:T(8,128)S(1)} %get-tuple-element.59.scaled_ref, f32[192,256]{1,0:T(8,128)S(1)} %get-tuple-element.60.centred_ref, f32[8,256]{1,0:T(8,128)S(1)} %get-tuple-element.61.row_ref, f32[7,7,192]{2,1,0:T(8,128)S(1)} %copy-done.1, ...), custom_call_target="tpu_custom_call" | custom-call | flops 4816896 | bytes 1294080 | tf_op jit(solution)/shard_map/pallas_call | solution.py:51
  (3 shorter events, 0.0 us)
Async XLA Ops:
  0.6 0.8 copy-start.1
  0.6 0.8 copy-start.9
  0.6 0.9 copy-start.7
  0.7 25.1 %slice-start.2 = ((s8[4718592]{0:T(1024)(128)(4,1)}), s8[4194304]{0:T(1024)(128)(4,1)S(1)}, s32[]{:S(2)}) async-start(s8[4718592]{0:T(1024)(128)(4,1)} %bitcast.19), calls=%async_computation.8 | async-start | bytes 8388608
  1.6 24.2 %copy-start = (bf16[192,1024]{1,0:T(8,128)(2,1)S(1)}, bf16[192,1024]{1,0:T(8,128)(2,1)}, u32[]{:S(2)}) copy-start(bf16[192,1024]{1,0:T(8,128)(2,1)} %project_ref.3) | copy-start | bytes 1179652
  1.6 24.2 %copy-start.4 = (f32[3072]{0:T(1024)S(1)}, f32[3072]{0:T(1024)}, u32[]{:S(2)}) copy-start(f32[3072]{0:T(1024)} %param.18) | copy-start | bytes 36868
  1.6 24.2 %copy-start.5 = (f32[192]{0:T(256)S(1)}, f32[192]{0:T(256)}, u32[]{:S(2)}) copy-start(f32[192]{0:T(256)} %param.24) | copy-start | bytes 2308
  1.6 24.2 %copy-start.6 = (f32[192]{0:T(256)S(1)}, f32[192]{0:T(256)}, u32[]{:S(2)}) copy-start(f32[192]{0:T(256)} %param.25) | copy-start | bytes 2308
  1.6 24.2 %slice-start.3 = ((s8[4718592]{0:T(1024)(128)(4,1)}), s8[524288]{0:T(1024)(128)(4,1)S(1)}, s32[]{:S(2)}) async-start(s8[4718592]{0:T(1024)(128)(4,1)} %bitcast.19), calls=%async_computation.9 | async-start | bytes 1048576
  1.6 24.2 %copy-start.8 = (f32[3072]{0:T(1024)S(1)}, f32[3072]{0:T(1024)}, u32[]{:S(2)}) copy-start(f32[3072]{0:T(1024)} %param.19) | copy-start | bytes 36868
  1.6 24.2 %copy-start.10 = (f32[192]{0:T(256)S(1)}, f32[192]{0:T(256)}, u32[]{:S(2)}) copy-start(f32[192]{0:T(256)} %param.23) | copy-start | bytes 2308
  1.6 24.2 %copy-start.11 = (f32[192]{0:T(256)S(1)}, f32[192]{0:T(256)}, u32[]{:S(2)}) copy-start(f32[192]{0:T(256)} %param.26) | copy-start | bytes 2308
  1.6 24.2 %copy-start.12 = (s32[4]{0:T(128)S(1)}, s32[4]{0:T(128)}, u32[]{:S(2)}) copy-start(s32[4]{0:T(128)} %labels_far.1) | copy-start | bytes 52
  2.9 25.0 %slice-start = ((s8[4718592]{0:T(1024)(128)(4,1)}), s8[4194304]{0:T(1024)(128)(4,1)S(1)}, s32[]{:S(2)}) async-start(s8[4718592]{0:T(1024)(128)(4,1)} %bitcast.9), calls=%async_computation.6 | async-start | bytes 8388608
  23.2 4.6 %collective-permute-start = (bf16[8,192,256]{2,1,0:T(8,128)(2,1)S(1)}, bf16[8,192,256]{2,1,0:T(8,128)(2,1)S(1)}, u32[]{:S(2)}, u32[]{:S(2)}) collective-permute-start(bf16[8,192,256]{2,1,0:T(8,128)(2,1)S(1)} %all_to_all.30), channel_id=1, source_target_pairs={{0,1},{1,0},{2,3},{3,2},{4,5},{5,4},{6,7},{7,6},{8,9},{9,8},{10,11... | collective-permute-start | bytes 2359304 | tf_op jit(solution)/shard_map/ppermute | solution.py:27
  25.8 2.0 %slice-start.1 = ((s8[4718592]{0:T(1024)(128)(4,1)}), s8[524288]{0:T(1024)(128)(4,1)S(1)}, s32[]{:S(2)}) async-start(s8[4718592]{0:T(1024)(128)(4,1)} %bitcast.9), calls=%async_computation.7 | async-start | bytes 1048576
  25.9 2.0 %copy-start.2 = (f32[768]{0:T(1024)S(1)}, f32[768]{0:T(1024)}, u32[]{:S(2)}) copy-start(f32[768]{0:T(1024)} %b_ref.3) | copy-start | bytes 9220
  27.8 3.1 %collective-permute-start.1 = (bf16[208,1024]{1,0:T(8,128)(2,1)S(1)}, bf16[208,1024]{1,0:T(8,128)(2,1)S(1)}, u32[]{:S(2)}, u32[]{:S(2)}) collective-permute-start(bf16[208,1024]{1,0:T(8,128)(2,1)S(1)} %get-tuple-element.40), channel_id=1, source_target_pairs={{0,1},{1,0},{2,3},{3,2},{4,5},{5,4},{6,7},{7,6},{8,9},{9,8},{10,11... | collective-permute-start | bytes 1277960 | tf_op jit(solution)/shard_map/ppermute | solution.py:27
  27.9 25.2 %copy-start.3 = (f32[4,1024]{1,0:T(4,128)S(1)}, f32[4,1024]{1,0:T(4,128)}, u32[]{:S(2)}) copy-start(f32[4,1024]{1,0:T(4,128)} %text_ref.1) | copy-start | bytes 49156
  87.9 2.4 %collective-permute-start.2 = (bf16[1552,256]{1,0:T(8,128)(2,1)S(1)}, bf16[1552,256]{1,0:T(8,128)(2,1)S(1)}, u32[]{:S(2)}, u32[]{:S(2)}) collective-permute-start(bf16[1552,256]{1,0:T(8,128)(2,1)S(1)} %get-tuple-element.57), channel_id=1, source_target_pairs={{0,1},{1,0},{2,3},{3,2},{4,5},{5,4},{6,7},{7,6},{8,9},{9,8},{10,11... | collective-permute-start | bytes 2383880 | tf_op jit(solution)/shard_map/ppermute | solution.py:27

commit v10 on v9

--- a/solution.py
+++ b/solution.py
@@ -483,15 +483,24 @@
     sums = jnp.where(lane == 0, one, jnp.where(lane == 1, two, 0.0)).T[:8]
     sums_ref[...] = sums
     high, low = to_terms(sums)
-    other_ref[channels // 2 :, :] = jnp.concatenate([high, low], axis=0).astype(bf16)
     half = channels // 2
-    other_ref[:half, :] = jnp.dot(
-        w_ref[half:, :], turned_ref[...], preferred_element_type=f32
+    part = other_ref.shape[0] - 16
+    other_ref[part:, :] = jnp.concatenate([high, low], axis=0).astype(bf16)
+    other_ref[:part, :] = jnp.dot(
+        w_ref[half : half + part, :], turned_ref[...], preferred_element_type=f32
     ).astype(bf16)
 
 
+def rest_kernel(w_ref, turned_ref, other_ref):
+    other_ref[...] = jnp.dot(
+        w_ref[w_ref.shape[0] - other_ref.shape[0] :, :],
+        turned_ref[...],
+        preferred_element_type=f32,
+    ).astype(bf16)
+
+
 def mine_kernel(
-    w_ref, turned_ref, conv_ref, stat_ref, gain_ref, mine_ref, scaled_ref, centred_ref, row_ref
+    _, w_ref, turned_ref, conv_ref, stat_ref, gain_ref, mine_ref, scaled_ref, centred_ref, row_ref
 ):
     shard = conv_ref.shape[0]
     index = lax.axis_index("mp")
@@ -507,15 +516,17 @@
     ).astype(bf16)
 
 
-def pair_kernel(mine_ref, got_ref, sums_ref, out_ref):
-    half = mine_ref.shape[0]
-    shard = half // CHIPS
+def pair_kernel(mine_ref, got_ref, later_ref, sums_ref, out_ref):
+    part = later_ref.shape[0]
+    shard = mine_ref.shape[0] // CHIPS
     for j in range(CHIPS):
         span = slice(j * shard, (j + 1) * shard)
-        out_ref[j, :shard, :] = (mine_ref[span, :].astype(f32) + got_ref[span, :].astype(f32)).astype(
-            bf16
-        )
-    tail = got_ref[half:, :].astype(f32)
+        if j * shard < part:
+            got = got_ref[span, :]
+        else:
+            got = later_ref[j * shard - part : (j + 1) * shard - part, :]
+        out_ref[j, :shard, :] = (mine_ref[span, :].astype(f32) + got.astype(f32)).astype(bf16)
+    tail = got_ref[part:, :].astype(f32)
     high, low = to_terms(sums_ref[...] + (tail[:8] + tail[8:]))
     tail = jnp.concatenate([high, low], axis=0).astype(bf16)
     for j in range(CHIPS):
@@ -691,7 +702,7 @@
     other, turned, row_sums = run(
         backward_kernel,
         [
-            shape(channels // 2 + 16, rows, dtype=bf16),
+            shape(channels // 4 + 16, rows, dtype=bf16),
             shape(hidden, rows, dtype=bf16),
             shape(8, rows),
         ],
@@ -706,6 +717,14 @@
         flops=rows * channels * hidden,
     )
     passed = core_swap(other)
+    (later,) = run(
+        rest_kernel,
+        [shape(channels // 4, rows, dtype=bf16)],
+        w_own,
+        turned,
+        flops=rows * channels * hidden // 2,
+    )
+    passed_later = core_swap(later)
     mine, scaled, centred, row_inverse = run(
         mine_kernel,
         [
@@ -714,6 +733,7 @@
             shape(shard, rows),
             shape(8, rows),
         ],
+        Far(later),
         w_own,
         turned,
         conv,
@@ -722,7 +742,7 @@
         flops=rows * channels * hidden,
     )
     (blocks,) = run(
-        pair_kernel, [shape(CHIPS, shard + 16, rows, dtype=bf16)], mine, passed, row_sums
+        pair_kernel, [shape(CHIPS, shard + 16, rows, dtype=bf16)], mine, passed, passed_later, row_sums
     )
     (grad_input,) = run(
         final_kernel,

time: 110 us -> 110 us (level)
    pallas_call x12 -> x13, Pallas kernels: 13.5 us -> 13.6 us  [run(): pl.pallas_call(kernel, out_shape=[a.array if isinstance(a, Far) else a fo...]
    ppermute x3 -> x4, starting transfers between devices: 3.14 us -> 3.3 us  [core_swap(): return lax.ppermute(array, 'mp', [(i, i ^ 1) for i in range(BLOCKS)])]
  transfers between devices with their start and end apart: 3 -> 4, of which waited for: 1 -> 1; matrix products, arithmetic and copies ran while one was open for 0% -> 0% of each run, Pallas kernels for 5% -> 6%
where the time goes in v10:
time: 110 us
  blocking collectives  90 us (82%)
  Pallas kernels  13.6 us (12%)
  starting transfers between devices  3.3 us (3%)
    all_to_all x3, blocking collectives, chip_exchange(): return lax.all_to_all(array, 'mp', 0, 0, axis_index_groups=groups)  48.6 us
    all_to_all x2, blocking collectives, shard_exchange(): return lax.all_to_all(array, 'mp', 0, 0)  25.4 us
    all_to_all x1, blocking collectives, body(): lax.all_to_all(pair_block, 'dp', 0, 0)  16 us
    pallas_call x13, Pallas kernels, run(): pl.pallas_call(kernel, out_shape=[a.array if isinstance(a, Far) else a fo...  13.6 us
    ppermute x4, starting transfers between devices, core_swap(): return lax.ppermute(array, 'mp', [(i, i ^ 1) for i in range(BLOCKS)])  3.3 us
  transfers between devices with their start and end apart: 4, of which 1 were waited for; matrix products, arithmetic and copies ran while one was open for 0% of the time, Pallas kernels for 6%

profile of v10, /device:TPU:1, one launch (start us, length us, event | category | flops | bytes accessed | tf_op | source)
XLA Modules:
  0.0 109.7 jit_solution(1899916729174755035)
XLA Ops:
  0.6 0.0 copy-start.1
  0.6 0.0 copy-start.9
  0.6 0.0 copy-start.7
  0.7 0.0 slice-start.2
  0.7 0.8 copy-done.1
  1.4 0.0 copy-done.9
  1.5 0.1 copy-done.7
  1.6 0.0 copy-start
  1.6 0.0 copy-start.4
  1.6 0.0 copy-start.5
  1.6 0.0 copy-start.6
  1.6 0.0 slice-start.3
  1.6 0.0 copy-start.8
  1.6 0.0 copy-start.10
  1.6 0.0 copy-start.11
  1.6 0.0 copy-start.12
  1.7 1.2 %shard_map.159 = (bf16[8,192,256]{2,1,0:T(8,128)(2,1)S(1)}, bf16[192,256]{1,0:T(8,128)(2,1)S(1)}, f32[4,192]{1,0:T(4,128)S(1)}) custom-call(f32[8,128]{1,0:T(8,128)S(1)} %shard_map.158._, bf16[4,8,8,192]{3,2,1,0:T(8,128)(2,1)S(1)} %copy-done.7, f32[7,7,192]{2,1,0:T(8,128)S(1)} %copy-done.1, f32[1,192]{1,0:T(1,128)S(1)} %bitcast.22), custom_call_target="tpu_custom_call" | custom-call | flops 16000000000 | bytes 140800 | tf_op jit(solution)/shard_map/pallas_call | solution.py:51
  2.9 0.0 slice-start
  2.9 20.3 %all_to_all.30 = bf16[8,192,256]{2,1,0:T(8,128)(2,1)S(1)} all-to-all(bf16[8,192,256]{2,1,0:T(8,128)(2,1)S(1)} %get-tuple-element.33), channel_id=1, replica_groups={{0,2,4,6,8,10,12,14},{1,3,5,7,9,11,13,15},{16,18,20,22,24,26,28,30},{17..., dimensions={0} | all-to-all | bytes 1572864 | tf_op jit(solution)/shard_map/all_to_all | solution.py:32
  23.2 2.5 %collective-permute-start = (bf16[8,192,256]{2,1,0:T(8,128)(2,1)S(1)}, bf16[8,192,256]{2,1,0:T(8,128)(2,1)S(1)}, u32[]{:S(2)}, u32[]{:S(2)}) collective-permute-start(bf16[8,192,256]{2,1,0:T(8,128)(2,1)S(1)} %all_to_all.30), channel_id=1, source_target_pairs={{0,1},{1,0},{2,3},{3,2},{4,5},{5,4},{6,7},{7,6},{8,9},{9,8},{10,11... | collective-permute-start | bytes 2359304 | tf_op jit(solution)/shard_map/ppermute | solution.py:27
  25.8 0.0 slice-done.2
  25.8 0.0 copy-done
  25.8 0.0 copy-done.4
  25.8 0.0 copy-done.5
  25.8 0.0 copy-done.6
  25.8 0.0 slice-done.3
  25.8 0.0 copy-done.8
  25.8 0.0 copy-done.10
  25.8 0.0 copy-done.11
  25.8 0.0 copy-done.12
  25.8 0.0 slice-start.1
  25.9 0.0 copy-start.2
  25.9 1.9 %shard_map.160 = (bf16[256,1536]{1,0:T(8,128)(2,1)S(1)}, f32[8,256]{1,0:T(8,128)S(1)}, f32[8,3072]{1,0:T(8,128)S(1)}, bf16[3072,768]{1,0:T(8,128)(2,1)S(1)}, f32...) custom-call(bf16[1536,256]{1,0:T(8,128)(2,1)S(1)} %bitcast.12, f32[1,3072]{1,0:T(1,128)S(1)} %bitcast.13, ...), custom_call_target="tpu_custom_call" | custom-call | flops 12000000000 | bytes 5928976 | tf_op jit(solution)/shard_map/pallas_call | solution.py:51
  27.8 0.1 collective-permute-start.1
  27.9 0.0 collective-permute-done
  27.9 0.0 slice-done
  27.9 0.0 slice-done.1
  27.9 0.0 copy-done.2
  27.9 0.0 copy-start.3
  27.9 3.0 %shard_map.161 = (f32[256,768]{1,0:T(8,128)S(1)}, f32[256,768]{1,0:T(8,128)S(1)}, f32[16,768]{1,0:T(8,128)S(1)}, f32[8,256]{1,0:T(8,128)S(1)}, f32[8,3072]{1,0:T(8,128)S(1)}) custom-call(bf16[256,1536]{1,0:T(8,128)(2,1)S(1)} %get-tuple-element.36.rows_ref, bf16[1536,256]{1,0:T(8,128)(2,1)S(1)} %bitcast.11, f32[8,256]{1,0:T(8,128)S(1)} %get-tuple-element.37.part_ref, ...), custom_call_target="tpu_custom_call" | custom-call | flops 1207959552 | bytes 11119616 | tf_op jit(solution)/shard_map/pallas_call | solution.py:51
  30.9 0.0 collective-permute-done.1._project.other_ref
  30.9 0.1 shard_map.162
  31.0 10.7 %all_to_all.31.got_ref = f32[16,8,192]{2,1,0:T(8,128)S(1)} all-to-all(f32[16,8,192]{2,1,0:T(8,128)S(1)} %shard_map.162), channel_id=1, replica_groups=mesh['dp'=16,'mp'=16] {'mp'}, dimensions={0} | all-to-all | bytes 196608 | tf_op jit(solution)/shard_map/all_to_all | solution.py:36
  41.8 0.3 shard_map.163
  42.1 11.0 %all_to_all.32.got_ref = f32[8,8,1152]{2,1,0:T(8,128)S(1)} all-to-all(f32[8,8,1152]{2,1,0:T(8,128)S(1)} %get-tuple-element.42), channel_id=1, replica_groups={{0,2,4,6,8,10,12,14},{1,3,5,7,9,11,13,15},{16,18,20,22,24,26,28,30},{17..., dimensions={0} | all-to-all | bytes 589824 | tf_op jit(solution)/shard_map/all_to_all | solution.py:32
  53.1 0.0 copy-done.3
  53.1 0.2 shard_map.164
  53.3 16.0 %all_to_all.33.got_ref = bf16[16,8,1152]{2,1,0:T(8,128)(2,1)S(1)} all-to-all(bf16[16,8,1152]{2,1,0:T(8,128)(2,1)S(1)} %get-tuple-element.44), channel_id=1, replica_groups=mesh['dp'=16,'mp'=16] {'dp'}, dimensions={0} | all-to-all | bytes 589824 | tf_op jit(solution)/shard_map/all_to_all | solution.py:688
  69.3 1.4 %shard_map.165 = (f32[4,1024]{1,0:T(4,128)}, f32[4,192]{1,0:T(4,128)S(1)}, f32[16,4,192]{2,1,0:T(4,128)S(1)}) custom-call(bf16[16,8,1152]{2,1,0:T(8,128)(2,1)S(1)} %all_to_all.33.got_ref, f32[8,1024]{1,0:T(8,128)S(1)} %get-tuple-element.45.own_ref, f32[8,1024]{1,0:T(8,128)S(1)} %get-tuple-element.46.rows_ref, f32[2,8,128]{2,1,0:T(8,128)S(1)} %get-tuple-element.47.stat_ref, ...), custom_call_target="tpu_custom_call" | custom-call | bytes 766464 | tf_op jit(solution)/shard_map/pallas_call | solution.py:51
  70.8 14.7 %all_to_all.34.got_ref = f32[16,4,192]{2,1,0:T(4,128)S(1)} all-to-all(f32[16,4,192]{2,1,0:T(4,128)S(1)} %get-tuple-element.49), channel_id=1, replica_groups=mesh['dp'=16,'mp'=16] {'mp'}, dimensions={0} | all-to-all | bytes 98304 | tf_op jit(solution)/shard_map/all_to_all | solution.py:36
  85.5 2.1 %shard_map.166 = (bf16[784,256]{1,0:T(8,128)(2,1)S(1)}, bf16[768,256]{1,0:T(8,128)(2,1)S(1)}, f32[8,256]{1,0:T(8,128)S(1)}) custom-call(f32[16,4,192]{2,1,0:T(4,128)S(1)} %all_to_all.34.got_ref, bf16[768,3072]{1,0:T(8,128)(2,1)S(1)} %bitcast.10, f32[256,768]{1,0:T(8,128)S(1)} %get-tuple-element.50.slope_ref, f32[256,768]{1,0:T(8,128)S(1)} %get-tuple-element.51.hidden_ref, ...), custom_call_target="tpu_custom_call" | custom-call | flops 603979776 | bytes 11111424 | tf_op jit(solution)/shard_map/pallas_call | solution.py:51
  87.6 0.5 collective-permute-start.2
  88.1 0.5 shard_map.167._
  88.6 0.2 collective-permute-start.3
  88.8 0.8 shard_map.168
  89.6 0.9 collective-permute-done.3.later_ref
  90.4 0.0 collective-permute-done.2.got_ref
  90.4 0.2 shard_map.169
  90.6 17.2 %all_to_all.35.got_ref = bf16[8,208,256]{2,1,0:T(8,128)(2,1)S(1)} all-to-all(bf16[8,208,256]{2,1,0:T(8,128)(2,1)S(1)} %shard_map.169), channel_id=1, replica_groups={{0,2,4,6,8,10,12,14},{1,3,5,7,9,11,13,15},{16,18,20,22,24,26,28,30},{17..., dimensions={0} | all-to-all | bytes 1703936 | tf_op jit(solution)/shard_map/all_to_all | solution.py:32
  107.8 1.9 %shard_map.170 = f32[4,8,8,192]{3,2,1,0:T(8,128)} custom-call(bf16[8,208,256]{2,1,0:T(8,128)(2,1)S(1)} %all_to_all.35.got_ref, f32[192,256]{1,0:T(8,128)S(1)} %get-tuple-element.59.scaled_ref, f32[192,256]{1,0:T(8,128)S(1)} %get-tuple-element.60.centred_ref, f32[8,256]{1,0:T(8,128)S(1)} %get-tuple-element.61.row_ref, f32[7,7,192]{2,1,0:T(8,128)S(1)} %copy-done.1, ...), custom_call_target="tpu_custom_call" | custom-call | flops 4816896 | bytes 1294080 | tf_op jit(solution)/shard_map/pallas_call | solution.py:51
  (3 shorter events, 0.0 us)
Async XLA Ops:
  0.6 0.8 copy-start.1
  0.6 0.8 copy-start.9
  0.6 0.9 copy-start.7
  0.7 25.1 %slice-start.2 = ((s8[4718592]{0:T(1024)(128)(4,1)}), s8[4194304]{0:T(1024)(128)(4,1)S(1)}, s32[]{:S(2)}) async-start(s8[4718592]{0:T(1024)(128)(4,1)} %bitcast.19), calls=%async_computation.8 | async-start | bytes 8388608
  1.6 24.2 %copy-start = (bf16[192,1024]{1,0:T(8,128)(2,1)S(1)}, bf16[192,1024]{1,0:T(8,128)(2,1)}, u32[]{:S(2)}) copy-start(bf16[192,1024]{1,0:T(8,128)(2,1)} %project_ref.3) | copy-start | bytes 1179652
  1.6 24.2 %copy-start.4 = (f32[3072]{0:T(1024)S(1)}, f32[3072]{0:T(1024)}, u32[]{:S(2)}) copy-start(f32[3072]{0:T(1024)} %param.18) | copy-start | bytes 36868
  1.6 24.2 %copy-start.5 = (f32[192]{0:T(256)S(1)}, f32[192]{0:T(256)}, u32[]{:S(2)}) copy-start(f32[192]{0:T(256)} %param.24) | copy-start | bytes 2308
  1.6 24.2 %copy-start.6 = (f32[192]{0:T(256)S(1)}, f32[192]{0:T(256)}, u32[]{:S(2)}) copy-start(f32[192]{0:T(256)} %param.25) | copy-start | bytes 2308
  1.6 24.2 %slice-start.3 = ((s8[4718592]{0:T(1024)(128)(4,1)}), s8[524288]{0:T(1024)(128)(4,1)S(1)}, s32[]{:S(2)}) async-start(s8[4718592]{0:T(1024)(128)(4,1)} %bitcast.19), calls=%async_computation.9 | async-start | bytes 1048576
  1.6 24.2 %copy-start.8 = (f32[3072]{0:T(1024)S(1)}, f32[3072]{0:T(1024)}, u32[]{:S(2)}) copy-start(f32[3072]{0:T(1024)} %param.19) | copy-start | bytes 36868
  1.6 24.2 %copy-start.10 = (f32[192]{0:T(256)S(1)}, f32[192]{0:T(256)}, u32[]{:S(2)}) copy-start(f32[192]{0:T(256)} %param.23) | copy-start | bytes 2308
  1.6 24.2 %copy-start.11 = (f32[192]{0:T(256)S(1)}, f32[192]{0:T(256)}, u32[]{:S(2)}) copy-start(f32[192]{0:T(256)} %param.26) | copy-start | bytes 2308
  1.6 24.2 %copy-start.12 = (s32[4]{0:T(128)S(1)}, s32[4]{0:T(128)}, u32[]{:S(2)}) copy-start(s32[4]{0:T(128)} %labels_far.1) | copy-start | bytes 52
  2.9 25.0 %slice-start = ((s8[4718592]{0:T(1024)(128)(4,1)}), s8[4194304]{0:T(1024)(128)(4,1)S(1)}, s32[]{:S(2)}) async-start(s8[4718592]{0:T(1024)(128)(4,1)} %bitcast.9), calls=%async_computation.6 | async-start | bytes 8388608
  23.2 4.6 %collective-permute-start = (bf16[8,192,256]{2,1,0:T(8,128)(2,1)S(1)}, bf16[8,192,256]{2,1,0:T(8,128)(2,1)S(1)}, u32[]{:S(2)}, u32[]{:S(2)}) collective-permute-start(bf16[8,192,256]{2,1,0:T(8,128)(2,1)S(1)} %all_to_all.30), channel_id=1, source_target_pairs={{0,1},{1,0},{2,3},{3,2},{4,5},{5,4},{6,7},{7,6},{8,9},{9,8},{10,11... | collective-permute-start | bytes 2359304 | tf_op jit(solution)/shard_map/ppermute | solution.py:27
  25.8 2.0 %slice-start.1 = ((s8[4718592]{0:T(1024)(128)(4,1)}), s8[524288]{0:T(1024)(128)(4,1)S(1)}, s32[]{:S(2)}) async-start(s8[4718592]{0:T(1024)(128)(4,1)} %bitcast.9), calls=%async_computation.7 | async-start | bytes 1048576
  25.9 2.0 %copy-start.2 = (f32[768]{0:T(1024)S(1)}, f32[768]{0:T(1024)}, u32[]{:S(2)}) copy-start(f32[768]{0:T(1024)} %b_ref.3) | copy-start | bytes 9220
  27.8 3.1 %collective-permute-start.1 = (bf16[208,1024]{1,0:T(8,128)(2,1)S(1)}, bf16[208,1024]{1,0:T(8,128)(2,1)S(1)}, u32[]{:S(2)}, u32[]{:S(2)}) collective-permute-start(bf16[208,1024]{1,0:T(8,128)(2,1)S(1)} %get-tuple-element.40), channel_id=1, source_target_pairs={{0,1},{1,0},{2,3},{3,2},{4,5},{5,4},{6,7},{7,6},{8,9},{9,8},{10,11... | collective-permute-start | bytes 1277960 | tf_op jit(solution)/shard_map/ppermute | solution.py:27
  27.9 25.2 %copy-start.3 = (f32[4,1024]{1,0:T(4,128)S(1)}, f32[4,1024]{1,0:T(4,128)}, u32[]{:S(2)}) copy-start(f32[4,1024]{1,0:T(4,128)} %text_ref.1) | copy-start | bytes 49156
  87.6 2.8 %collective-permute-start.2 = (bf16[784,256]{1,0:T(8,128)(2,1)S(1)}, bf16[784,256]{1,0:T(8,128)(2,1)S(1)}, u32[]{:S(2)}, u32[]{:S(2)}) collective-permute-start(bf16[784,256]{1,0:T(8,128)(2,1)S(1)} %get-tuple-element.57), channel_id=1, source_target_pairs={{0,1},{1,0},{2,3},{3,2},{4,5},{5,4},{6,7},{7,6},{8,9},{9,8},{10,11... | collective-permute-start | bytes 1204232 | tf_op jit(solution)/shard_map/ppermute | solution.py:27
  88.6 1.8 %collective-permute-start.3 = (bf16[768,256]{1,0:T(8,128)(2,1)S(1)}, bf16[768,256]{1,0:T(8,128)(2,1)S(1)}, u32[]{:S(2)}, u32[]{:S(2)}) collective-permute-start(bf16[768,256]{1,0:T(8,128)(2,1)S(1)} %shard_map.167._), channel_id=1, source_target_pairs={{0,1},{1,0},{2,3},{3,2},{4,5},{5,4},{6,7},{7,6},{8,9},{9,8},{10,11... | collective-permute-start | bytes 1179656 | tf_op jit(solution)/shard_map/ppermute | solution.py:27

commit v11 on v10

--- a/solution.py
+++ b/solution.py
@@ -517,7 +517,7 @@
 
 
 def pair_kernel(mine_ref, got_ref, later_ref, sums_ref, out_ref):
-    part = later_ref.shape[0]
+    part = mine_ref.shape[0] - later_ref.shape[0]
     shard = mine_ref.shape[0] // CHIPS
     for j in range(CHIPS):
         span = slice(j * shard, (j + 1) * shard)
@@ -702,7 +702,7 @@
     other, turned, row_sums = run(
         backward_kernel,
         [
-            shape(channels // 4 + 16, rows, dtype=bf16),
+            shape(5 * shard + 16, rows, dtype=bf16),
             shape(hidden, rows, dtype=bf16),
             shape(8, rows),
         ],
@@ -719,7 +719,7 @@
     passed = core_swap(other)
     (later,) = run(
         rest_kernel,
-        [shape(channels // 4, rows, dtype=bf16)],
+        [shape(3 * shard, rows, dtype=bf16)],
         w_own,
         turned,
         flops=rows * channels * hidden // 2,

time: 110 us -> 110 us (level)
  no operation moved by 1% of the time
where the time goes in v11:
time: 110 us
  blocking collectives  90 us (82%)
  Pallas kernels  13.7 us (12%)
  starting transfers between devices  3.3 us (3%)
    all_to_all x3, blocking collectives, chip_exchange(): return lax.all_to_all(array, 'mp', 0, 0, axis_index_groups=groups)  48.6 us
    all_to_all x2, blocking collectives, shard_exchange(): return lax.all_to_all(array, 'mp', 0, 0)  25.4 us
    all_to_all x1, blocking collectives, body(): lax.all_to_all(pair_block, 'dp', 0, 0)  16 us
    pallas_call x13, Pallas kernels, run(): pl.pallas_call(kernel, out_shape=[a.array if isinstance(a, Far) else a fo...  13.7 us
    ppermute x4, starting transfers between devices, core_swap(): return lax.ppermute(array, 'mp', [(i, i ^ 1) for i in range(BLOCKS)])  3.3 us
  transfers between devices with their start and end apart: 4, of which 1 were waited for; matrix products, arithmetic and copies ran while one was open for 0% of the time, Pallas kernels for 6%

profile of v11, /device:TPU:1, one launch (start us, length us, event | category | flops | bytes accessed | tf_op | source)
XLA Modules:
  0.0 109.7 jit_solution(11166261697411710111)
XLA Ops:
  0.6 0.0 copy-start.1
  0.6 0.0 copy-start.9
  0.6 0.0 copy-start.7
  0.7 0.0 slice-start.2
  0.7 0.8 copy-done.1
  1.4 0.0 copy-done.9
  1.5 0.1 copy-done.7
  1.6 0.0 copy-start
  1.6 0.0 copy-start.4
  1.6 0.0 copy-start.5
  1.6 0.0 copy-start.6
  1.6 0.0 slice-start.3
  1.6 0.0 copy-start.8
  1.6 0.0 copy-start.10
  1.6 0.0 copy-start.11
  1.6 0.0 copy-start.12
  1.7 1.2 %shard_map.159 = (bf16[8,192,256]{2,1,0:T(8,128)(2,1)S(1)}, bf16[192,256]{1,0:T(8,128)(2,1)S(1)}, f32[4,192]{1,0:T(4,128)S(1)}) custom-call(f32[8,128]{1,0:T(8,128)S(1)} %shard_map.158._, bf16[4,8,8,192]{3,2,1,0:T(8,128)(2,1)S(1)} %copy-done.7, f32[7,7,192]{2,1,0:T(8,128)S(1)} %copy-done.1, f32[1,192]{1,0:T(1,128)S(1)} %bitcast.22), custom_call_target="tpu_custom_call" | custom-call | flops 16000000000 | bytes 140800 | tf_op jit(solution)/shard_map/pallas_call | solution.py:51
  2.9 0.0 slice-start
  2.9 20.3 %all_to_all.30 = bf16[8,192,256]{2,1,0:T(8,128)(2,1)S(1)} all-to-all(bf16[8,192,256]{2,1,0:T(8,128)(2,1)S(1)} %get-tuple-element.33), channel_id=1, replica_groups={{0,2,4,6,8,10,12,14},{1,3,5,7,9,11,13,15},{16,18,20,22,24,26,28,30},{17..., dimensions={0} | all-to-all | bytes 1572864 | tf_op jit(solution)/shard_map/all_to_all | solution.py:32
  23.2 2.5 %collective-permute-start = (bf16[8,192,256]{2,1,0:T(8,128)(2,1)S(1)}, bf16[8,192,256]{2,1,0:T(8,128)(2,1)S(1)}, u32[]{:S(2)}, u32[]{:S(2)}) collective-permute-start(bf16[8,192,256]{2,1,0:T(8,128)(2,1)S(1)} %all_to_all.30), channel_id=1, source_target_pairs={{0,1},{1,0},{2,3},{3,2},{4,5},{5,4},{6,7},{7,6},{8,9},{9,8},{10,11... | collective-permute-start | bytes 2359304 | tf_op jit(solution)/shard_map/ppermute | solution.py:27
  25.8 0.0 slice-done.2
  25.8 0.0 copy-done
  25.8 0.0 copy-done.4
  25.8 0.0 copy-done.5
  25.8 0.0 copy-done.6
  25.8 0.0 slice-done.3
  25.8 0.0 copy-done.8
  25.8 0.0 copy-done.10
  25.8 0.0 copy-done.11
  25.8 0.0 copy-done.12
  25.8 0.0 slice-start.1
  25.9 0.0 copy-start.2
  25.9 1.9 %shard_map.160 = (bf16[256,1536]{1,0:T(8,128)(2,1)S(1)}, f32[8,256]{1,0:T(8,128)S(1)}, f32[8,3072]{1,0:T(8,128)S(1)}, bf16[3072,768]{1,0:T(8,128)(2,1)S(1)}, f32...) custom-call(bf16[1536,256]{1,0:T(8,128)(2,1)S(1)} %bitcast.12, f32[1,3072]{1,0:T(1,128)S(1)} %bitcast.13, ...), custom_call_target="tpu_custom_call" | custom-call | flops 12000000000 | bytes 5928976 | tf_op jit(solution)/shard_map/pallas_call | solution.py:51
  27.8 0.1 collective-permute-start.1
  27.9 0.0 collective-permute-done
  27.9 0.0 slice-done
  27.9 0.0 slice-done.1
  27.9 0.0 copy-done.2
  27.9 0.0 copy-start.3
  27.9 3.0 %shard_map.161 = (f32[256,768]{1,0:T(8,128)S(1)}, f32[256,768]{1,0:T(8,128)S(1)}, f32[16,768]{1,0:T(8,128)S(1)}, f32[8,256]{1,0:T(8,128)S(1)}, f32[8,3072]{1,0:T(8,128)S(1)}) custom-call(bf16[256,1536]{1,0:T(8,128)(2,1)S(1)} %get-tuple-element.36.rows_ref, bf16[1536,256]{1,0:T(8,128)(2,1)S(1)} %bitcast.11, f32[8,256]{1,0:T(8,128)S(1)} %get-tuple-element.37.part_ref, ...), custom_call_target="tpu_custom_call" | custom-call | flops 1207959552 | bytes 11119616 | tf_op jit(solution)/shard_map/pallas_call | solution.py:51
  30.9 0.0 collective-permute-done.1._project.other_ref
  30.9 0.1 shard_map.162
  31.0 10.7 %all_to_all.31.got_ref = f32[16,8,192]{2,1,0:T(8,128)S(1)} all-to-all(f32[16,8,192]{2,1,0:T(8,128)S(1)} %shard_map.162), channel_id=1, replica_groups=mesh['dp'=16,'mp'=16] {'mp'}, dimensions={0} | all-to-all | bytes 196608 | tf_op jit(solution)/shard_map/all_to_all | solution.py:36
  41.8 0.3 shard_map.163
  42.1 11.0 %all_to_all.32.got_ref = f32[8,8,1152]{2,1,0:T(8,128)S(1)} all-to-all(f32[8,8,1152]{2,1,0:T(8,128)S(1)} %get-tuple-element.42), channel_id=1, replica_groups={{0,2,4,6,8,10,12,14},{1,3,5,7,9,11,13,15},{16,18,20,22,24,26,28,30},{17..., dimensions={0} | all-to-all | bytes 589824 | tf_op jit(solution)/shard_map/all_to_all | solution.py:32
  53.1 0.0 copy-done.3
  53.1 0.2 shard_map.164
  53.3 16.0 %all_to_all.33.got_ref = bf16[16,8,1152]{2,1,0:T(8,128)(2,1)S(1)} all-to-all(bf16[16,8,1152]{2,1,0:T(8,128)(2,1)S(1)} %get-tuple-element.44), channel_id=1, replica_groups=mesh['dp'=16,'mp'=16] {'dp'}, dimensions={0} | all-to-all | bytes 589824 | tf_op jit(solution)/shard_map/all_to_all | solution.py:688
  69.3 1.4 %shard_map.165 = (f32[4,1024]{1,0:T(4,128)}, f32[4,192]{1,0:T(4,128)S(1)}, f32[16,4,192]{2,1,0:T(4,128)S(1)}) custom-call(bf16[16,8,1152]{2,1,0:T(8,128)(2,1)S(1)} %all_to_all.33.got_ref, f32[8,1024]{1,0:T(8,128)S(1)} %get-tuple-element.45.own_ref, f32[8,1024]{1,0:T(8,128)S(1)} %get-tuple-element.46.rows_ref, f32[2,8,128]{2,1,0:T(8,128)S(1)} %get-tuple-element.47.stat_ref, ...), custom_call_target="tpu_custom_call" | custom-call | bytes 766464 | tf_op jit(solution)/shard_map/pallas_call | solution.py:51
  70.8 14.7 %all_to_all.34.got_ref = f32[16,4,192]{2,1,0:T(4,128)S(1)} all-to-all(f32[16,4,192]{2,1,0:T(4,128)S(1)} %get-tuple-element.49), channel_id=1, replica_groups=mesh['dp'=16,'mp'=16] {'mp'}, dimensions={0} | all-to-all | bytes 98304 | tf_op jit(solution)/shard_map/all_to_all | solution.py:36
  85.5 2.3 %shard_map.166 = (bf16[976,256]{1,0:T(8,128)(2,1)S(1)}, bf16[768,256]{1,0:T(8,128)(2,1)S(1)}, f32[8,256]{1,0:T(8,128)S(1)}) custom-call(f32[16,4,192]{2,1,0:T(4,128)S(1)} %all_to_all.34.got_ref, bf16[768,3072]{1,0:T(8,128)(2,1)S(1)} %bitcast.10, f32[256,768]{1,0:T(8,128)S(1)} %get-tuple-element.50.slope_ref, f32[256,768]{1,0:T(8,128)S(1)} %get-tuple-element.51.hidden_ref, ...), custom_call_target="tpu_custom_call" | custom-call | flops 603979776 | bytes 11111424 | tf_op jit(solution)/shard_map/pallas_call | solution.py:51
  87.7 0.5 collective-permute-start.2
  88.3 0.4 shard_map.167._
  88.7 0.2 collective-permute-start.3
  88.8 0.8 shard_map.168
  89.6 0.7 collective-permute-done.3.later_ref
  90.3 0.0 collective-permute-done.2.got_ref
  90.3 0.2 shard_map.169
  90.5 17.2 %all_to_all.35.got_ref = bf16[8,208,256]{2,1,0:T(8,128)(2,1)S(1)} all-to-all(bf16[8,208,256]{2,1,0:T(8,128)(2,1)S(1)} %shard_map.169), channel_id=1, replica_groups={{0,2,4,6,8,10,12,14},{1,3,5,7,9,11,13,15},{16,18,20,22,24,26,28,30},{17..., dimensions={0} | all-to-all | bytes 1703936 | tf_op jit(solution)/shard_map/all_to_all | solution.py:32
  107.8 1.9 %shard_map.170 = f32[4,8,8,192]{3,2,1,0:T(8,128)} custom-call(bf16[8,208,256]{2,1,0:T(8,128)(2,1)S(1)} %all_to_all.35.got_ref, f32[192,256]{1,0:T(8,128)S(1)} %get-tuple-element.59.scaled_ref, f32[192,256]{1,0:T(8,128)S(1)} %get-tuple-element.60.centred_ref, f32[8,256]{1,0:T(8,128)S(1)} %get-tuple-element.61.row_ref, f32[7,7,192]{2,1,0:T(8,128)S(1)} %copy-done.1, ...), custom_call_target="tpu_custom_call" | custom-call | flops 4816896 | bytes 1294080 | tf_op jit(solution)/shard_map/pallas_call | solution.py:51
  (3 shorter events, 0.0 us)
Async XLA Ops:
  0.6 0.8 copy-start.1
  0.6 0.8 copy-start.9
  0.6 0.9 copy-start.7
  0.7 25.1 %slice-start.2 = ((s8[4718592]{0:T(1024)(128)(4,1)}), s8[4194304]{0:T(1024)(128)(4,1)S(1)}, s32[]{:S(2)}) async-start(s8[4718592]{0:T(1024)(128)(4,1)} %bitcast.19), calls=%async_computation.8 | async-start | bytes 8388608
  1.6 24.2 %copy-start = (bf16[192,1024]{1,0:T(8,128)(2,1)S(1)}, bf16[192,1024]{1,0:T(8,128)(2,1)}, u32[]{:S(2)}) copy-start(bf16[192,1024]{1,0:T(8,128)(2,1)} %project_ref.3) | copy-start | bytes 1179652
  1.6 24.2 %copy-start.4 = (f32[3072]{0:T(1024)S(1)}, f32[3072]{0:T(1024)}, u32[]{:S(2)}) copy-start(f32[3072]{0:T(1024)} %param.18) | copy-start | bytes 36868
  1.6 24.2 %copy-start.5 = (f32[192]{0:T(256)S(1)}, f32[192]{0:T(256)}, u32[]{:S(2)}) copy-start(f32[192]{0:T(256)} %param.24) | copy-start | bytes 2308
  1.6 24.2 %copy-start.6 = (f32[192]{0:T(256)S(1)}, f32[192]{0:T(256)}, u32[]{:S(2)}) copy-start(f32[192]{0:T(256)} %param.25) | copy-start | bytes 2308
  1.6 24.2 %slice-start.3 = ((s8[4718592]{0:T(1024)(128)(4,1)}), s8[524288]{0:T(1024)(128)(4,1)S(1)}, s32[]{:S(2)}) async-start(s8[4718592]{0:T(1024)(128)(4,1)} %bitcast.19), calls=%async_computation.9 | async-start | bytes 1048576
  1.6 24.2 %copy-start.8 = (f32[3072]{0:T(1024)S(1)}, f32[3072]{0:T(1024)}, u32[]{:S(2)}) copy-start(f32[3072]{0:T(1024)} %param.19) | copy-start | bytes 36868
  1.6 24.2 %copy-start.10 = (f32[192]{0:T(256)S(1)}, f32[192]{0:T(256)}, u32[]{:S(2)}) copy-start(f32[192]{0:T(256)} %param.23) | copy-start | bytes 2308
  1.6 24.2 %copy-start.11 = (f32[192]{0:T(256)S(1)}, f32[192]{0:T(256)}, u32[]{:S(2)}) copy-start(f32[192]{0:T(256)} %param.26) | copy-start | bytes 2308
  1.6 24.2 %copy-start.12 = (s32[4]{0:T(128)S(1)}, s32[4]{0:T(128)}, u32[]{:S(2)}) copy-start(s32[4]{0:T(128)} %labels_far.1) | copy-start | bytes 52
  2.9 25.0 %slice-start = ((s8[4718592]{0:T(1024)(128)(4,1)}), s8[4194304]{0:T(1024)(128)(4,1)S(1)}, s32[]{:S(2)}) async-start(s8[4718592]{0:T(1024)(128)(4,1)} %bitcast.9), calls=%async_computation.6 | async-start | bytes 8388608
  23.2 4.6 %collective-permute-start = (bf16[8,192,256]{2,1,0:T(8,128)(2,1)S(1)}, bf16[8,192,256]{2,1,0:T(8,128)(2,1)S(1)}, u32[]{:S(2)}, u32[]{:S(2)}) collective-permute-start(bf16[8,192,256]{2,1,0:T(8,128)(2,1)S(1)} %all_to_all.30), channel_id=1, source_target_pairs={{0,1},{1,0},{2,3},{3,2},{4,5},{5,4},{6,7},{7,6},{8,9},{9,8},{10,11... | collective-permute-start | bytes 2359304 | tf_op jit(solution)/shard_map/ppermute | solution.py:27
  25.8 2.0 %slice-start.1 = ((s8[4718592]{0:T(1024)(128)(4,1)}), s8[524288]{0:T(1024)(128)(4,1)S(1)}, s32[]{:S(2)}) async-start(s8[4718592]{0:T(1024)(128)(4,1)} %bitcast.9), calls=%async_computation.7 | async-start | bytes 1048576
  25.9 2.0 %copy-start.2 = (f32[768]{0:T(1024)S(1)}, f32[768]{0:T(1024)}, u32[]{:S(2)}) copy-start(f32[768]{0:T(1024)} %b_ref.3) | copy-start | bytes 9220
  27.8 3.1 %collective-permute-start.1 = (bf16[208,1024]{1,0:T(8,128)(2,1)S(1)}, bf16[208,1024]{1,0:T(8,128)(2,1)S(1)}, u32[]{:S(2)}, u32[]{:S(2)}) collective-permute-start(bf16[208,1024]{1,0:T(8,128)(2,1)S(1)} %get-tuple-element.40), channel_id=1, source_target_pairs={{0,1},{1,0},{2,3},{3,2},{4,5},{5,4},{6,7},{7,6},{8,9},{9,8},{10,11... | collective-permute-start | bytes 1277960 | tf_op jit(solution)/shard_map/ppermute | solution.py:27
  27.9 25.2 %copy-start.3 = (f32[4,1024]{1,0:T(4,128)S(1)}, f32[4,1024]{1,0:T(4,128)}, u32[]{:S(2)}) copy-start(f32[4,1024]{1,0:T(4,128)} %text_ref.1) | copy-start | bytes 49156
  87.7 2.6 %collective-permute-start.2 = (bf16[976,256]{1,0:T(8,128)(2,1)S(1)}, bf16[976,256]{1,0:T(8,128)(2,1)S(1)}, u32[]{:S(2)}, u32[]{:S(2)}) collective-permute-start(bf16[976,256]{1,0:T(8,128)(2,1)S(1)} %get-tuple-element.57), channel_id=1, source_target_pairs={{0,1},{1,0},{2,3},{3,2},{4,5},{5,4},{6,7},{7,6},{8,9},{9,8},{10,11... | collective-permute-start | bytes 1499144 | tf_op jit(solution)/shard_map/ppermute | solution.py:27
  88.7 1.7 %collective-permute-start.3 = (bf16[576,256]{1,0:T(8,128)(2,1)S(1)}, bf16[576,256]{1,0:T(8,128)(2,1)S(1)}, u32[]{:S(2)}, u32[]{:S(2)}) collective-permute-start(bf16[576,256]{1,0:T(8,128)(2,1)S(1)} %shard_map.167._), channel_id=1, source_target_pairs={{0,1},{1,0},{2,3},{3,2},{4,5},{5,4},{6,7},{7,6},{8,9},{9,8},{10,11... | collective-permute-start | bytes 884744 | tf_op jit(solution)/shard_map/ppermute | solution.py:27
